TPU v7x, 32 devices: a whole 2x2x4 slice. The times are simulated.
32 devices in a mesh: ctx: 8 (over y, x, core), mem: 4 (over z).
Axes of the slice: x: 2, y: 2, z: 4, core: 2. Of those that a mesh axis runs over, the one named last changes fastest.
Arguments:
- tokens: bfloat16 [8192, 1024], P(('ctx', 'mem')), may hold values from -36 to 36
- routes: int32 [8192, 2], P(('ctx', 'mem')), may hold values from 0 to 3, all different within a row; in each aligned block of 256 rows (0 to 255, 256 to 511, ...) at most 192 rows name the same one
- router: bfloat16 [1024, 4], replicated, may hold values from -0.1875 to 0.1875
- mem_weight: bfloat16 [4, 1024, 1536], P('mem'), may hold values from -0.1875 to 0.1875
- win_weight: bfloat16 [1024, 1536], P('mem'), may hold values from -3 to 3
Outputs:
- mixed: bfloat16 [8192, 512], P(('ctx', 'mem'))
Inputs may be any that keep to these rules, and one draw needn't show every extreme that they name: `routes`: each token names 2 different memories; the 256 tokens of one device name any one memory at most 192 times.
All inputs are finite; a program needn't handle non-finite values.
Results may differ from a plain program's by a relative error of at most 0.009.
Values may be sent and summed in bfloat16 or wider, within the bound.
No kernel may reach another device: no remote copies, remote signals or barrier semaphores. Data moves between devices by JAX's collectives and lax.ppermute only.
A program may use at most 64 MiB of HBM per device.

v0:
```python
import jax
import jax.numpy as jnp
from jax import lax
from jax.sharding import PartitionSpec as P

HEADS = 4
HDIM = 128
WINDOW = 512


norm_eps = 1e-06


def passed_along(x, axis, by):
    devices = lax.axis_size(axis)
    pairs = [(i, i + by) for i in range(devices) if 0 <= i + by < devices]
    return lax.ppermute(x, axis, pairs)


def slot_table(route_rows, mems):
    matches = (route_rows[:, :, None] == jnp.arange(mems, dtype=jnp.int32)[None, None, :]).astype(
        jnp.int32
    )
    flat = matches.reshape(-1, mems)
    earlier = jnp.cumsum(flat, axis=0) - flat
    return jnp.sum(earlier * flat, axis=1).reshape(route_rows.shape)


def memory_local(slot_rows, positions, weight):
    projected = jnp.dot(slot_rows, weight, preferred_element_type=jnp.float32).astype(jnp.bfloat16)
    width = HEADS * HDIM
    causal = positions[None, :] <= positions[:, None]
    intra_list = []
    state_list = []
    for head_index in range(HEADS):
        column_start = head_index * HDIM
        queries = projected[:, column_start : column_start + HDIM]
        key_rows = projected[:, width + column_start : width + column_start + HDIM]
        value_rows = projected[:, 2 * width + column_start : 2 * width + column_start + HDIM]
        scores = lax.dot_general(
            queries, key_rows, (((1,), (1,)), ((), ())), preferred_element_type=jnp.float32
        )
        weights_low = jnp.where(causal, scores, 0.0).astype(jnp.bfloat16)
        intra_list.append(jnp.dot(weights_low, value_rows, preferred_element_type=jnp.float32))
        state_list.append(
            lax.dot_general(
                key_rows, value_rows, (((0,), (0,)), ((), ())), preferred_element_type=jnp.float32
            )
        )
    return (projected[:, :width], jnp.stack(intra_list), jnp.stack(state_list))


def memory_finish(queries, intra, prefix):
    outputs = []
    for head_index in range(HEADS):
        column_start = head_index * HDIM
        inter = jnp.dot(
            queries[:, column_start : column_start + HDIM],
            prefix[head_index].astype(jnp.bfloat16),
            preferred_element_type=jnp.float32,
        )
        summed = intra[head_index] + inter
        factor = lax.rsqrt(jnp.mean(summed * summed, axis=-1, keepdims=True) + norm_eps)
        outputs.append(summed * factor)
    return jnp.concatenate(outputs, axis=-1).astype(jnp.bfloat16)


def window_attend(queries, key_rows, value_rows, first_pos, count):
    distance = (
        jnp.arange(count, dtype=jnp.int32)[:, None]
        + 2 * count
        - jnp.arange(3 * count, dtype=jnp.int32)[None, :]
    )
    key_pos = first_pos - 2 * count + jnp.arange(3 * count, dtype=jnp.int32)
    allowed = (distance >= 0) & (distance < WINDOW) & (key_pos[None, :] >= 0)
    outputs = []
    for head_index in range(HEADS):
        column_start = head_index * HDIM
        scores = lax.dot_general(
            queries[:, column_start : column_start + HDIM],
            key_rows[:, column_start : column_start + HDIM],
            (((1,), (1,)), ((), ())),
            preferred_element_type=jnp.float32,
        ) * HDIM ** (-0.5)
        masked = jnp.where(allowed, scores, -1e30)
        highest = jnp.max(masked, axis=-1, keepdims=True)
        expo = jnp.exp(masked - highest)
        probs = (expo / jnp.sum(expo, axis=-1, keepdims=True)).astype(jnp.bfloat16)
        outputs.append(
            jnp.dot(
                probs,
                value_rows[:, column_start : column_start + HDIM],
                preferred_element_type=jnp.float32,
            )
        )
    return jnp.concatenate(outputs, axis=-1)


def project_window(rows, full_weight):
    return jnp.dot(rows, full_weight, preferred_element_type=jnp.float32).astype(jnp.bfloat16)


def shards(tokens, routes, router, mem_weight, win_weight):
    tok_dev = tokens.shape[0]
    mems = router.shape[1]
    n_mem = lax.axis_size("mem")
    capacity = 3 * tok_dev // mems
    width = HEADS * HDIM
    slots = slot_table(routes, mems)
    row_ids = jnp.broadcast_to(jnp.arange(tok_dev, dtype=jnp.int32)[:, None], routes.shape)
    values = jnp.broadcast_to(tokens[:, None, :], (tok_dev, routes.shape[1], tokens.shape[1]))
    dispatch = (
        jnp.zeros((mems, capacity, tokens.shape[1]), jnp.bfloat16).at[routes, slots].set(values)
    )
    found = jnp.full((mems, capacity), -1, jnp.int32).at[routes, slots].set(row_ids)
    arrived, arrived_ids = (
        lax.all_to_all(dispatch, "mem", split_axis=0, concat_axis=0, tiled=True),
        lax.all_to_all(found, "mem", split_axis=0, concat_axis=0, tiled=True),
    )
    positions = (jnp.arange(n_mem, dtype=jnp.int32)[:, None] * tok_dev + arrived_ids).reshape(-1)
    queries, intra, state = memory_local(
        arrived.reshape(-1, tokens.shape[1]), positions, mem_weight[0]
    )
    my_index = lax.axis_index("ctx")
    shard_states = lax.all_gather(state[None], "ctx", axis=0, tiled=True)
    indices = jnp.arange(shard_states.shape[0], dtype=jnp.int32)
    keep = (indices < my_index).astype(jnp.float32)
    prefix = jnp.einsum("s,shij->hij", keep, shard_states)
    finished = memory_finish(queries, intra, prefix).reshape(n_mem, capacity, width)
    returned = lax.all_to_all(finished, "mem", split_axis=0, concat_axis=0, tiled=True)
    picked = returned[routes, slots].astype(jnp.float32)
    logits = jnp.dot(tokens, router, preferred_element_type=jnp.float32)
    matches = (routes[:, :, None] == jnp.arange(mems, dtype=jnp.int32)[None, None, :]).astype(
        jnp.float32
    )
    chosen = jnp.sum(matches * logits[:, None, :], axis=-1)
    gates = jax.nn.sigmoid(chosen[:, 0] - chosen[:, 1])
    memory_part = gates[:, None] * picked[:, 0] + (1.0 - gates)[:, None] * picked[:, 1]
    full_weight = lax.all_gather(win_weight, "mem", axis=0, tiled=True)
    first_pos = lax.axis_index(("ctx", "mem")) * tok_dev
    earlier_rows = [passed_along(tokens, ("ctx", "mem"), offset) for offset in (2, 1)]
    projected = project_window(jnp.concatenate(earlier_rows + [tokens], axis=0), full_weight)
    key_block = projected[:, width:]
    query_rows = projected[2 * tok_dev :, :width]
    window_part = window_attend(
        query_rows, key_block[:, :width], key_block[:, width:], first_pos, tok_dev
    )
    return (memory_part + window_part).astype(jnp.bfloat16)


def solution(mesh):
    return jax.shard_map(
        shards,
        mesh=mesh,
        in_specs=(
            P(("ctx", "mem"), None),
            P(("ctx", "mem"), None),
            P(),
            P("mem", None, None),
            P("mem", None),
        ),
        out_specs=P(("ctx", "mem"), None),
        check_vma=False,
    )
```

profile of v0, /device:TPU:0, one launch (start us, length us, event | category | flops | bytes accessed | tf_op | source)
XLA Modules:
  0.0 300.1 jit_solution(6576819246935732425)
XLA Ops:
  10.8 2.6 broadcast_in_dim.29
  13.3 2.3 reshape.163
  16.9 76.1 %scatter_fusion.1 = bf16[4,192,1024]{2,1,0:T(8,128)(2,1)} fusion(bf16[4,192,1024]{2,1,0:T(8,128)(2,1)} %broadcast_in_dim.28, s32[512]{0:T(512)S(1)} %reshape.155, bf16[512,1024]{1,0:T(8,128)(2,1)} %reshape.163), kind=kCustom, calls=%fused_computation.2 | custom fusion | bytes 3149824 | tf_op jit(solution)/shard_map/scatter | solution.py:113
  93.1 43.1 %all_to_all.22 = bf16[4,192,1024]{2,1,0:T(8,128)(2,1)S(1)} all-to-all(bf16[4,192,1024]{2,1,0:T(8,128)(2,1)} %scatter_fusion.1), channel_id=1, replica_groups=mesh['ctx'=8,'mem'=4] {'mem'}, dimensions={0} | all-to-all | bytes 3145728 | tf_op jit(solution)/shard_map/all_to_all | solution.py:117
  136.2 2.8 convolution_convert_fusion.1
  141.4 2.9 collective-permute-start.1
  144.3 3.8 %collective-permute-start = (bf16[256,1024]{1,0:T(8,128)(2,1)}, bf16[256,1024]{1,0:T(8,128)(2,1)}, u32[]{:S(2)}, u32[]{:S(2)}) collective-permute-start(bf16[256,1024]{1,0:T(8,128)(2,1)} %param.5), channel_id=1, source_target_pairs={{0,2},{1,3},{2,4},{3,5},{4,6},{5,7},{6,8},{7,9},{8,10},{9,11},{10,... | collective-permute-start | bytes 1572872 | tf_op jit(solution)/shard_map/ppermute | solution.py:17
  148.3 24.7 %scatter_fusion = s32[4,192]{1,0:T(4,128)S(1)} fusion(s32[4,192]{1,0:T(4,128)S(1)} %broadcast_in_dim.25, s32[512]{0:T(512)S(1)} %reshape.155, s32[512]{0:T(512)S(1)} %reshape.157), kind=kCustom, calls=%fused_computation.1 | custom fusion | bytes 10240 | tf_op jit(solution)/shard_map/scatter | solution.py:115
  173.6 3.2 %all-to-all-start = ((s32[4,1,192]{2,1,0:T(1,128)}), s32[4,1,192]{2,1,0:T(1,128)S(1)}, u32[]{:S(2)}, u32[]{:S(2)}) async-start(s32[4,1,192]{2,1,0:T(1,128)} %copy.51), calls=%async_computation | async-start | bytes 8192 | tf_op jit(solution)/shard_map/all_to_all | solution.py:118
  182.5 2.0 fusion.5
  184.5 1.9 fusion.58
  186.4 3.0 multiply_reduce_fusion
  191.3 2.9 multiply_reduce_fusion.1
  196.0 2.8 multiply_reduce_fusion.2
  204.9 2.9 multiply_reduce_fusion.3
  209.0 1.9 pad_maximum_fusion
  210.9 4.4 %all-to-all-start.2 = ((bf16[4,192,512]{2,1,0:T(8,128)(2,1)}), bf16[4,192,512]{2,1,0:T(8,128)(2,1)}, u32[]{:S(2)}, u32[]{:S(2)}) async-start(bf16[4,192,512]{2,1,0:T(8,128)(2,1)} %pad_maximum_fusion), calls=%async_computation.2 | async-start | bytes 1572864 | tf_op jit(solution)/shard_map/all_to_all | solution.py:130
  215.3 44.1 %all-gather.4.cloned.1.call-done = bf16[1024,1536]{1,0:T(8,128)(2,1)} async-done(((bf16[256,1536]{1,0:T(8,128)(2,1)}), bf16[1024,1536]{1,0:T(8,128)(2,1)}) %all-gather.4.cloned.1.call-update) | async-done | bytes 3145744 | tf_op jit(solution)/shard_map/all_gather | solution.py:139
  259.5 5.0 %convolution_convert_fusion = bf16[768,1536]{1,0:T(8,128)(2,1)S(1)} fusion(bf16[1024,1536]{1,0:T(8,128)(2,1)} %all-gather.4.cloned.1.call-done, bf16[256,1024]{1,0:T(8,128)(2,1)} %param.5, bf16[256,1024]{1,0:T(8,128)(2,1)} %collective-permute-done.1, bf16[256,1024]{1,0:T(8,128)(2,1)} %collective-permute-done), kind=kOutput, calls=%fused_computation.7 | convolution fusion | flops 2421817344 | bytes 7077888 | tf_op jit(solution)/shard_map/dot_general | solution.py:100
  271.2 9.7 %gather_fusion = bf16[512,512]{1,0:T(8,128)(2,1)} fusion(bf16[4,192,512]{2,1,0:T(8,128)(2,1)} %all-to-all-done.2, s32[512]{0:T(512)S(1)} %reshape.149), kind=kCustom, calls=%fused_computation | custom fusion | bytes 1052672 | tf_op jit(solution)/shard_map/gather | solution.py:131
  280.9 2.7 reshape.168
  283.6 3.5 %fusion.114 = (f32[256,1,512]{2,1,0:T(1,128)}, f32[256,1,512]{2,1,0:T(1,128)}) fusion(f32[256,2,512]{2,1,0:T(2,128)} %reshape.168), kind=kLoop, calls=%fused_computation.171 | loop fusion | bytes 2097152 | tf_op jit(solution)/shard_map/slice | solution.py:138
  287.0 1.9 copy.60
  289.0 1.9 copy.59
  (88 shorter events, 34.3 us)
Async XLA Ops:
  6.5 129.6 %copy-start = (bf16[1,1024,1536]{2,1,0:T(8,128)(2,1)S(1)}, bf16[1,1024,1536]{2,1,0:T(8,128)(2,1)}, u32[]{:S(2)}) copy-start(bf16[1,1024,1536]{2,1,0:T(8,128)(2,1)} %param.8) | copy-start | bytes 9437188
  6.5 175.9 %all-gather.6.cloned.1.call-start = ((), (), s32[]{:S(2)}) async-start(), calls=%async_computation.4 | async-start | bytes 1179648 | tf_op jit(solution)/shard_map/all_gather | solution.py:125
  139.0 1.4 copy-start.2
  141.4 73.9 %collective-permute-start.1 = (bf16[256,1024]{1,0:T(8,128)(2,1)}, bf16[256,1024]{1,0:T(8,128)(2,1)}, u32[]{:S(2)}, u32[]{:S(2)}) collective-permute-start(bf16[256,1024]{1,0:T(8,128)(2,1)} %param.5), channel_id=1, source_target_pairs={{0,1},{1,2},{2,3},{3,4},{4,5},{5,6},{6,7},{7,8},{8,9},{9,10},{10,1... | collective-permute-start | bytes 1572872 | tf_op jit(solution)/shard_map/ppermute | solution.py:17
  144.3 71.0 %collective-permute-start = (bf16[256,1024]{1,0:T(8,128)(2,1)}, bf16[256,1024]{1,0:T(8,128)(2,1)}, u32[]{:S(2)}, u32[]{:S(2)}) collective-permute-start(bf16[256,1024]{1,0:T(8,128)(2,1)} %param.5), channel_id=1, source_target_pairs={{0,2},{1,3},{2,4},{3,5},{4,6},{5,7},{6,8},{7,9},{8,10},{9,11},{10,... | collective-permute-start | bytes 1572872 | tf_op jit(solution)/shard_map/ppermute | solution.py:17
  148.2 29.9 %copy-start.4 = (bf16[1024,4]{0,1:T(4,128)(2,1)S(1)}, bf16[1024,4]{0,1:T(4,128)(2,1)}, u32[]{:S(2)}) copy-start(bf16[1024,4]{0,1:T(4,128)(2,1)} %param.7) | copy-start | bytes 24580
  148.2 31.8 %copy-start.3 = (s32[256,2]{0,1:T(2,128)S(1)}, s32[256,2]{0,1:T(2,128)}, u32[]{:S(2)}) copy-start(s32[256,2]{0,1:T(2,128)} %param.6) | copy-start | bytes 6148
  173.6 8.8 %all-to-all-start = ((s32[4,1,192]{2,1,0:T(1,128)}), s32[4,1,192]{2,1,0:T(1,128)S(1)}, u32[]{:S(2)}, u32[]{:S(2)}) async-start(s32[4,1,192]{2,1,0:T(1,128)} %copy.51), calls=%async_computation | async-start | bytes 8192 | tf_op jit(solution)/shard_map/all_to_all | solution.py:118
  176.8 82.6 %all-gather.4.cloned.1.call-start = ((), (), s32[]{:S(2)}) async-start(), calls=%async_computation.3 | async-start | bytes 3932160 | tf_op jit(solution)/shard_map/all_gather | solution.py:139
  182.5 13.6 %copy-start.5 = (s32[768]{0:T(1024)}, s32[768]{0:T(1024)S(1)}, u32[]{:S(2)}) copy-start(s32[768]{0:T(1024)S(1)} %add.120) | copy-start | bytes 9220
  184.5 9.7 %copy-start.1 = (bf16[4,128,128]{2,1,0:T(8,128)(2,1)}, bf16[4,128,128]{2,1,0:T(8,128)(2,1)S(1)}, u32[]{:S(2)}) copy-start(bf16[4,128,128]{2,1,0:T(8,128)(2,1)S(1)} %convert.22) | copy-start | bytes 393220
  210.9 60.2 %all-to-all-start.2 = ((bf16[4,192,512]{2,1,0:T(8,128)(2,1)}), bf16[4,192,512]{2,1,0:T(8,128)(2,1)}, u32[]{:S(2)}, u32[]{:S(2)}) async-start(bf16[4,192,512]{2,1,0:T(8,128)(2,1)} %pad_maximum_fusion), calls=%async_computation.2 | async-start | bytes 1572864 | tf_op jit(solution)/shard_map/all_to_all | solution.py:130
  215.3 49.1 %copy-start.6 = (pred[768]{0:T(1024)(128)(4,1)S(1)}, pred[768]{0:T(1024)(128)(4,1)}, u32[]{:S(2)}) copy-start(pred[768]{0:T(1024)(128)(4,1)} %add_compare_fusion) | copy-start | bytes 2308
  215.3 49.1 %copy-start.7 = (s32[256]{0:T(256)S(1)}, s32[256]{0:T(256)}, u32[]{:S(2)}) copy-start(s32[256]{0:T(256)} %iota_add_fusion) | copy-start | bytes 3076
Sparse Core Ops, SparseCore 0:
  141.5 23.0 all-gather.5
  179.2 80.1 all-gather.3
where the time goes:
time: 304 us; the launch traced here: 300 us
  local copies, waits for them, and re-layouts  132 us (43%)
  waiting for transfers between devices  46.7 us (15%)
  blocking collectives  43.1 us (14%)
  matrix products  36.8 us (12%)
  starting transfers between devices  14.3 us (5%)
  other arithmetic  14 us (5%)
  between operations  13.7 us (5%)
    scatter x1, local copies, waits for them, and re-layouts, shards(): jnp.zeros((mems, capacity, tokens.shape[1]), jnp.bfloat16).at[routes, slots]  76.1 us
    all_gather x1, waiting for transfers between devices, shards(): full_weight = lax.all_gather(win_weight, 'mem', axis=0, tiled=True)  44.1 us
    all_to_all x1, blocking collectives, shards(): lax.all_to_all(dispatch, 'mem', split_axis=0, concat_axis=0, tiled=True)  43.1 us
    scatter x1, local copies, waits for them, and re-layouts, shards(): jnp.full((mems, capacity), -1, jnp.int32).at[routes, slots].set(row_ids)  24.7 us
    dot_general x4, matrix products, memory_local(): jnp.dot(weights_low, value_rows, preferred_element_type=jnp.float32)  11.6 us
    gather x1, local copies, waits for them, and re-layouts, shards(): picked = returned[routes, slots].astype(jnp.float32)  9.71 us
    dot_general x4, matrix products, memory_finish(): jnp.dot(queries[:, column_start:column_start + HDIM], prefix[head_index]....  7.55 us
    another operation x7, other arithmetic  6.77 us
  transfers between devices with their start and end apart: 6, of which 2 were waited for; matrix products, arithmetic and copies ran while one was open for 23% of the time, Pallas kernels for 0%

commit v1 on v0

--- a/solution.py
+++ b/solution.py
@@ -1,6 +1,10 @@
+import functools
+
 import jax
 import jax.numpy as jnp
 from jax import lax
+from jax.experimental import pallas as pl
+from jax.experimental.pallas import tpu as pltpu
 from jax.sharding import PartitionSpec as P
 
 HEADS = 4
@@ -100,7 +104,7 @@
     return jnp.dot(rows, full_weight, preferred_element_type=jnp.float32).astype(jnp.bfloat16)
 
 
-def shards(tokens, routes, router, mem_weight, win_weight):
+def sparse_shards(tokens, routes, router, mem_weight, win_weight):
     tok_dev = tokens.shape[0]
     mems = router.shape[1]
     n_mem = lax.axis_size("mem")
@@ -146,6 +150,279 @@
         query_rows, key_block[:, :width], key_block[:, width:], first_pos, tok_dev
     )
     return (memory_part + window_part).astype(jnp.bfloat16)
+
+def kernel_call(body, name, out_shape, flops, moved, **kwargs):
+    return pl.pallas_call(
+        body,
+        name=name,
+        out_shape=out_shape,
+        cost_estimate=pl.CostEstimate(flops=flops, bytes_accessed=moved, transcendentals=0),
+        compiler_params=pltpu.CompilerParams(vmem_limit_bytes=48 * 1024 * 1024),
+        **kwargs,
+    )
+
+
+def as_column(row, count):
+    diagonal = lax.broadcasted_iota(jnp.int32, (count, count), 0) == lax.broadcasted_iota(
+        jnp.int32, (count, count), 1
+    )
+    return jnp.sum(jnp.where(diagonal, row, 0.0), axis=1, keepdims=True)
+
+
+def project_body(n_mem, *refs):
+    rows = refs[:n_mem]
+    routes_ref, router_ref, weight_ref, proj_ref, coef_ref, state_ref = refs[n_mem:]
+    count = rows[0].shape[0]
+    width = HEADS * HDIM
+    mine = lax.axis_index("mem")
+    for step in range(n_mem):
+        group = lax.rem(mine + n_mem - step, n_mem)
+        place = pl.ds(pl.multiple_of(group * count, count), count)
+        tokens = rows[step][...]
+        named = routes_ref[group].astype(jnp.float32)
+        first = as_column(named[0:1, :], count)
+        second = as_column(named[1:2, :], count)
+        me = mine.astype(jnp.float32)
+        is_first = first == me
+        is_second = second == me
+        logits = lax.dot_general(
+            tokens, router_ref[...], (((1,), (1,)), ((), ())), preferred_element_type=jnp.float32
+        )
+        lane = lax.broadcasted_iota(jnp.int32, logits.shape, 1).astype(jnp.float32)
+        difference = jnp.sum(
+            jnp.where(lane == first, logits, 0.0) - jnp.where(lane == second, logits, 0.0),
+            axis=1,
+            keepdims=True,
+        )
+        gate = jax.nn.sigmoid(difference)
+        coef = jnp.where(is_first, gate, jnp.where(is_second, 1.0 - gate, 0.0))
+        coef_ref[place, :] = jnp.broadcast_to(coef, (count, HDIM))
+        projected = jnp.dot(tokens, weight_ref[...], preferred_element_type=jnp.float32)
+        proj_ref[place, :] = jnp.where(is_first | is_second, projected, 0.0).astype(jnp.bfloat16)
+    for head in range(HEADS):
+        keys = proj_ref[:, width + head * HDIM : width + (head + 1) * HDIM]
+        values = proj_ref[:, 2 * width + head * HDIM : 2 * width + (head + 1) * HDIM]
+        state_ref[head * HDIM : (head + 1) * HDIM, :] = lax.dot_general(
+            keys, values, (((0,), (0,)), ((), ())), preferred_element_type=jnp.float32
+        )
+
+
+def intra_body(count, proj_ref, intra_ref):
+    width = HEADS * HDIM
+    blocks = proj_ref.shape[0] // count
+    causal = lax.broadcasted_iota(jnp.int32, (count, count), 1) <= lax.broadcasted_iota(
+        jnp.int32, (count, count), 0
+    )
+    for head in range(HEADS):
+        columns = slice(head * HDIM, (head + 1) * HDIM)
+        key_columns = slice(width + head * HDIM, width + (head + 1) * HDIM)
+        value_columns = slice(2 * width + head * HDIM, 2 * width + (head + 1) * HDIM)
+        for block in range(blocks):
+            here = slice(block * count, (block + 1) * count)
+            queries = proj_ref[here, columns]
+            scores = lax.dot_general(
+                queries,
+                proj_ref[here, key_columns],
+                (((1,), (1,)), ((), ())),
+                preferred_element_type=jnp.float32,
+            )
+            weights = jnp.where(causal, scores, 0.0).astype(jnp.bfloat16)
+            total = jnp.dot(
+                weights, proj_ref[here, value_columns], preferred_element_type=jnp.float32
+            )
+            if block:
+                before = slice(0, block * count)
+                scores = lax.dot_general(
+                    queries,
+                    proj_ref[before, key_columns],
+                    (((1,), (1,)), ((), ())),
+                    preferred_element_type=jnp.float32,
+                )
+                total += jnp.dot(
+                    scores.astype(jnp.bfloat16),
+                    proj_ref[before, value_columns],
+                    preferred_element_type=jnp.float32,
+                )
+            intra_ref[here, columns] = total
+
+
+def window_project_body(n_mem, *refs):
+    rows = refs[:n_mem]
+    weight_ref, win_ref, tail_ref, full_ref = refs[n_mem:]
+    pieces, sources, depth, _ = weight_ref.shape
+    count = rows[0].shape[0]
+    mine = lax.axis_index("mem")
+    for source in range(sources):
+        for piece in range(pieces):
+            start = (source * pieces + piece) * depth
+            full_ref[start : start + depth, :] = weight_ref[piece, source]
+    for step in range(n_mem):
+        group = lax.rem(mine + n_mem - step, n_mem)
+        place = pl.ds(pl.multiple_of(group * count, count), count)
+        win_ref[place, :] = jnp.dot(
+            rows[step][...], full_ref[...], preferred_element_type=jnp.float32
+        ).astype(jnp.bfloat16)
+    total = n_mem * count
+    tail_ref[...] = win_ref[total - WINDOW : total, HDIM:]
+
+
+def window_attend_body(count, win_ref, halo_ref, out_ref, keys_ref):
+    total = win_ref.shape[0]
+    keys_ref[0:WINDOW, :] = halo_ref[...]
+    keys_ref[WINDOW:, :] = win_ref[:, HDIM:]
+    span = count + WINDOW
+    row = lax.broadcasted_iota(jnp.int32, (count, span), 0)
+    column = lax.broadcasted_iota(jnp.int32, (count, span), 1)
+    distance = row + WINDOW - column
+    within = (distance >= 0) & (distance < WINDOW)
+    missing = jnp.where(lax.axis_index("ctx") == 0, WINDOW, 0)
+    for block in range(total // count):
+        start = block * count
+        keys = keys_ref[start : start + span, :HDIM]
+        values = keys_ref[start : start + span, HDIM:]
+        scores = lax.dot_general(
+            win_ref[start : start + count, :HDIM],
+            keys,
+            (((1,), (1,)), ((), ())),
+            preferred_element_type=jnp.float32,
+        ) * HDIM ** (-0.5)
+        allowed = within & (column + start >= missing) if start < WINDOW else within
+        masked = jnp.where(allowed, scores, -1e30)
+        highest = jnp.max(masked, axis=-1, keepdims=True)
+        expo = jnp.exp(masked - highest)
+        probs = (expo / jnp.sum(expo, axis=-1, keepdims=True)).astype(jnp.bfloat16)
+        out_ref[start : start + count, :] = jnp.dot(
+            probs, values, preferred_element_type=jnp.float32
+        )
+
+
+def finish_body(count, proj_ref, intra_ref, prefix_ref, coef_ref, window_ref, out_ref):
+    mine = lax.axis_index("mem")
+    for block in range(proj_ref.shape[0] // count):
+        here = slice(block * count, (block + 1) * count)
+        coef = coef_ref[here, :]
+        for head in range(HEADS):
+            columns = slice(head * HDIM, (head + 1) * HDIM)
+            summed = intra_ref[here, columns] + jnp.dot(
+                proj_ref[here, columns], prefix_ref[columns, :], preferred_element_type=jnp.float32
+            )
+            factor = lax.rsqrt(jnp.mean(summed * summed, axis=-1, keepdims=True) + norm_eps)
+            memory_out = (summed * factor).astype(jnp.bfloat16).astype(jnp.float32)
+            window = jnp.where(mine == head, window_ref[here, :], 0.0)
+            out_ref[block, :, columns] = (coef * memory_out + window).astype(jnp.bfloat16)
+
+
+def add_body(parts_ref, out_ref):
+    total = parts_ref[0].astype(jnp.float32)
+    for part in range(1, parts_ref.shape[0]):
+        total += parts_ref[part].astype(jnp.float32)
+    out_ref[...] = total.astype(jnp.bfloat16)
+
+
+def exclusive_prefix(state):
+    devices = lax.axis_size("ctx")
+    pieces = state.reshape(devices, -1, state.shape[1])
+    pieces = lax.all_to_all(pieces, "ctx", split_axis=0, concat_axis=0, tiled=True)
+    earlier = [jnp.zeros_like(pieces[0])]
+    for index in range(devices - 1):
+        earlier.append(earlier[-1] + pieces[index])
+    sums = jnp.stack(earlier).astype(jnp.bfloat16)
+    return lax.all_to_all(sums, "ctx", split_axis=0, concat_axis=0, tiled=True).reshape(state.shape)
+
+
+def dense_shards(tokens, routes, router, mem_weight, win_weight):
+    count, depth = tokens.shape
+    n_mem = lax.axis_size("mem")
+    n_ctx = lax.axis_size("ctx")
+    total = n_mem * count
+    width = HEADS * HDIM
+    rows = [tokens]
+    for shift in range(1, n_mem):
+        rows.append(lax.ppermute(tokens, "mem", [(i, (i + shift) % n_mem) for i in range(n_mem)]))
+    all_routes = lax.all_gather(routes.T, "mem", axis=0, tiled=False)
+
+    cut = win_weight.shape[0] // n_ctx
+    piece = lax.dynamic_slice_in_dim(win_weight, lax.axis_index("ctx") * cut, cut, 0)
+    piece = jnp.concatenate(
+        [
+            jnp.concatenate(
+                [piece[:, p * width + h * HDIM : p * width + (h + 1) * HDIM] for p in range(3)],
+                axis=1,
+            )[None]
+            for h in range(HEADS)
+        ],
+        axis=0,
+    )
+    piece = lax.all_to_all(piece, "mem", split_axis=0, concat_axis=0, tiled=True)
+    head_weight = lax.all_gather(piece, "ctx", axis=0, tiled=False)
+
+    proj, coef, state = kernel_call(
+        functools.partial(project_body, n_mem),
+        "project",
+        (
+            jax.ShapeDtypeStruct((total, 3 * width), jnp.bfloat16),
+            jax.ShapeDtypeStruct((total, HDIM), jnp.float32),
+            jax.ShapeDtypeStruct((width, HDIM), jnp.float32),
+        ),
+        2 * total * depth * 3 * width,
+        8 << 20,
+    )(*rows, all_routes, router.T, mem_weight[0])
+    prefix = exclusive_prefix(state)
+    win, tail = kernel_call(
+        functools.partial(window_project_body, n_mem),
+        "window_project",
+        (
+            jax.ShapeDtypeStruct((total, 3 * HDIM), jnp.bfloat16),
+            jax.ShapeDtypeStruct((WINDOW, 2 * HDIM), jnp.bfloat16),
+        ),
+        2 * total * depth * 3 * HDIM,
+        4 << 20,
+        scratch_shapes=[pltpu.VMEM((depth, 3 * HDIM), jnp.bfloat16)],
+    )(*rows, head_weight)
+    halo = passed_along(tail, "ctx", 1)
+    intra = kernel_call(
+        functools.partial(intra_body, count),
+        "intra",
+        jax.ShapeDtypeStruct((total, width), jnp.float32),
+        3 * total * total * width,
+        5 << 20,
+    )(proj)
+    window_part = kernel_call(
+        functools.partial(window_attend_body, count),
+        "window_attend",
+        jax.ShapeDtypeStruct((total, HDIM), jnp.float32),
+        4 * total * (count + WINDOW) * HDIM,
+        2 << 20,
+        scratch_shapes=[pltpu.VMEM((total + WINDOW, 2 * HDIM), jnp.bfloat16)],
+    )(win, halo)
+    partial_sums = kernel_call(
+        functools.partial(finish_body, count),
+        "finish",
+        jax.ShapeDtypeStruct((n_mem, count, width), jnp.bfloat16),
+        2 * total * width * HDIM,
+        6 << 20,
+    )(proj, intra, prefix, coef, window_part)
+    parts = lax.all_to_all(partial_sums, "mem", split_axis=0, concat_axis=0, tiled=True)
+    return kernel_call(
+        add_body,
+        "add_parts",
+        jax.ShapeDtypeStruct((count, width), jnp.bfloat16),
+        n_mem * count * width,
+        2 << 20,
+    )(parts)
+
+
+def shards(tokens, routes, router, mem_weight, win_weight):
+    n_mem = lax.axis_size("mem")
+    n_ctx = lax.axis_size("ctx")
+    dense = (
+        n_mem == HEADS
+        and router.shape[1] == n_mem
+        and win_weight.shape[0] % (16 * n_ctx) == 0
+        and n_mem * tokens.shape[0] >= WINDOW
+    )
+    body = dense_shards if dense else sparse_shards
+    return body(tokens, routes, router, mem_weight, win_weight)
 
 
 def solution(mesh):

time: 304 us -> 159 us (0.52)
  local copies, waits for them, and re-layouts: 132 us -> 19.9 us
  waiting for transfers between devices: 46.7 us -> 0.02 us
  blocking collectives: 43.1 us -> 89.4 us
  matrix products: 36.8 us -> 0 us
  Pallas kernels: 0 us -> 19.1 us
  between operations: 13.7 us -> 0.14 us
  starting transfers between devices: 14.3 us -> 20 us
  other arithmetic: 14 us -> 9.03 us
    scatter x2 -> x0, local copies, waits for them, and re-layouts: 101 us -> none  [the longest x1 76.1 us: shards(): jnp.zeros((mems, capacity, tokens.shape[1]), jnp.bfloat16).at[routes, slots]]
    all_gather x0 -> x2, blocking collectives: none -> 60.3 us  [the longest x1 48.1 us: dense_shards(): all_routes = lax.all_gather(routes.T, 'mem', axis=0, tiled=False)]
    all_gather x2 -> x0, waiting for transfers between devices: 44.1 us -> none  [the longest x1 44.1 us: shards(): full_weight = lax.all_gather(win_weight, 'mem', axis=0, tiled=True)]
    dot_general x24 -> x0, matrix products: 36.8 us -> none  [the longest x4 11.6 us: memory_local(): jnp.dot(weights_low, value_rows, preferred_element_type=jnp.float32)]
    pallas_call x0 -> x6, Pallas kernels: none -> 19.1 us  [the longest x1 7.17 us: dense_shards(): kernel_call(functools.partial(project_body, n_mem), 'project', (jax.Shape...]
    all_to_all x1, blocking collectives: 43.1 us -> 29.1 us  [dense_shards(): lax.all_to_all(partial_sums, 'mem', split_axis=0, concat_axis=0, tiled=True)]
    unnamed x19 -> x40, local copies, waits for them, and re-layouts: 5.5 us -> 19.1 us
    gather x1 -> x0, local copies, waits for them, and re-layouts: 9.71 us -> none  [shards(): picked = returned[routes, slots].astype(jnp.float32)]
  transfers between devices with their start and end apart: 6 -> 7, of which waited for: 2 -> 0; matrix products, arithmetic and copies ran while one was open for 23% -> 8% of each run, Pallas kernels for 0% -> 10%
where the time goes in v1:
time: 159 us; the launch traced here: 158 us
  blocking collectives  89.4 us (56%)
  starting transfers between devices  20 us (13%)
  local copies, waits for them, and re-layouts  19.9 us (13%)
  Pallas kernels  19.1 us (12%)
  other arithmetic  9.03 us (6%)
    all_gather x1, blocking collectives, dense_shards(): all_routes = lax.all_gather(routes.T, 'mem', axis=0, tiled=False)  48.1 us
    all_to_all x1, blocking collectives, dense_shards(): lax.all_to_all(partial_sums, 'mem', split_axis=0, concat_axis=0, tiled=True)  29.1 us
    unnamed x40, local copies, waits for them, and re-layouts  19.1 us
    all_gather x1, blocking collectives, dense_shards(): head_weight = lax.all_gather(piece, 'ctx', axis=0, tiled=False)  12.2 us
    pallas_call x1, Pallas kernels, dense_shards(): kernel_call(functools.partial(project_body, n_mem), 'project', (jax.Shape...  7.17 us
    unnamed x5, other arithmetic  6.93 us
    ppermute x3, starting transfers between devices, dense_shards(): lax.ppermute(tokens, 'mem', [(i, (i + shift) % n_mem) for i in range(n_me...  6.06 us
    all_to_all x1, starting transfers between devices, dense_shards(): lax.all_to_all(piece, 'mem', split_axis=0, concat_axis=0, tiled=True)  4.08 us
  transfers between devices with their start and end apart: 7, of which 0 were waited for; matrix products, arithmetic and copies ran while one was open for 8% of the time, Pallas kernels for 10%

profile of v1, /device:TPU:0, one launch (start us, length us, event | category | flops | bytes accessed | tf_op | source)
XLA Modules:
  0.0 157.6 jit_solution(8405644597925636226)
XLA Ops:
  0.0 5.0 %collective-permute-start.2 = (bf16[256,1024]{1,0:T(8,128)(2,1)}, bf16[256,1024]{1,0:T(8,128)(2,1)S(1)}, u32[]{:S(2)}, u32[]{:S(2)}) collective-permute-start(bf16[256,1024]{1,0:T(8,128)(2,1)} %refs_0_.3), channel_id=1, source_target_pairs={{0,3},{1,0},{2,1},{3,2},{4,7},{5,4},{6,5},{7,6},{8,11},{9,8},{10,9... | collective-permute-start | bytes 1572872 | tf_op jit(solution)/shard_map/ppermute | solution.py:341
  7.6 4.1 %all-to-all-start.2 = ((bf16[4,32,384]{2,1,0:T(8,128)(2,1)}), bf16[4,32,384]{2,1,0:T(8,128)(2,1)S(1)}, u32[]{:S(2)}, u32[]{:S(2)}) async-start(bf16[4,32,384]{2,1,0:T(8,128)(2,1)} %pad_maximum_fusion), calls=%async_computation.2 | async-start | bytes 196608 | tf_op jit(solution)/shard_map/all_to_all | solution.py:356
  11.7 48.1 %all-gather.2.refs_4_ = s32[4,2,256]{2,1,0:T(2,128)S(1)} all-gather(s32[1,2,256]{2,1,0:T(2,128)} %bitcast.19), channel_id=2, replica_groups=mesh['ctx'=8,'mem'=4] {'mem'}, dimensions={0}, use_global_device_ids=true | all-gather | bytes 10240 | tf_op jit(solution)/shard_map/all_gather | solution.py:342
  63.9 1.0 copy-done.10
  64.9 1.0 copy-done.13
  67.7 7.2 %project.1 = (bf16[1024,1536]{1,0:T(8,128)(2,1)S(1)}, f32[1024,128]{1,0:T(8,128)S(1)}, f32[512,128]{1,0:T(8,128)}) custom-call(bf16[256,1024]{1,0:T(8,128)(2,1)S(1)} %copy-done.7, bf16[256,1024]{1,0:T(8,128)(2,1)S(1)} %copy-done.16, bf16[256,1024]{1,0:T(8,128)(2,1)S(1)} %copy-done.13, bf16[256,1024]{1,0:T(8,128)(2,1)S(1)} %copy-done.10, ...), custom_call_target="tpu_custom_call" | custom-call | flops 3221225472 | bytes 8388608 | tf_op jit(solution)/shard_map/project/pallas_call | solution.py:359
  75.6 4.1 %all-to-all-start = ((f32[8,64,128]{2,1,0:T(8,128)}), f32[8,64,128]{2,1,0:T(8,128)}, u32[]{:S(2)}, u32[]{:S(2)}) async-start(f32[8,64,128]{2,1,0:T(8,128)} %bitcast.4), calls=%async_computation | async-start | bytes 524288 | tf_op jit(solution)/shard_map/all_to_all | solution.py:325
  79.7 12.2 %all-gather.1 = bf16[32,32,384]{2,1,0:T(8,128)(2,1)S(1)} all-gather(bf16[4,32,384]{2,1,0:T(8,128)(2,1)S(1)} %all-to-all-done.2), channel_id=3, replica_groups=mesh['ctx'=8,'mem'=4] {'ctx'}, dimensions={0}, use_global_device_ids=true | all-gather | bytes 884736 | tf_op jit(solution)/shard_map/all_gather | solution.py:357
  96.1 2.0 %window_project.1 = (bf16[1024,384]{1,0:T(8,128)(2,1)S(1)}, bf16[512,256]{1,0:T(8,128)(2,1)}) custom-call(bf16[256,1024]{1,0:T(8,128)(2,1)S(1)} %copy-done.8, bf16[256,1024]{1,0:T(8,128)(2,1)S(1)} %copy-done.17, bf16[256,1024]{1,0:T(8,128)(2,1)S(1)} %copy-done.14, bf16[256,1024]{1,0:T(8,128)(2,1)S(1)} %copy-done.11, bf16[8,4,32,384]{3,2,1,0:T(8,128)(2,1)S(1)} %bitcast.16), custom_call_target="tpu_custom_call" | custom-call | flops 805306368 | bytes 4194304 | tf_op jit(solution)/shard_map/window_project/pallas_call | solution.py:371
  99.0 2.3 %collective-permute-start.3 = (bf16[512,256]{1,0:T(8,128)(2,1)}, bf16[512,256]{1,0:T(8,128)(2,1)S(1)}, u32[]{:S(2)}, u32[]{:S(2)}) collective-permute-start(bf16[512,256]{1,0:T(8,128)(2,1)} %get-tuple-element.14), channel_id=1, source_target_pairs={{0,4},{4,8},{8,12},{12,16},{16,20},{20,24},{24,28},{1,5},{5,9},{9,... | collective-permute-start | bytes 786440 | tf_op jit(solution)/shard_map/ppermute | solution.py:21
  101.3 1.4 constant_dynamic-update-slice_fusion.6
  102.7 1.4 constant_dynamic-update-slice_fusion.5
  104.0 1.4 constant_dynamic-update-slice_fusion.4
  105.4 1.4 constant_dynamic-update-slice_fusion.3
  106.9 1.4 constant_dynamic-update-slice_fusion.2
  108.2 1.4 constant_dynamic-update-slice_fusion.1
  109.6 1.4 constant_dynamic-update-slice_fusion
  111.0 3.5 %all-to-all-start.1 = ((bf16[8,64,128]{2,1,0:T(8,128)(2,1)}), bf16[8,64,128]{2,1,0:T(8,128)(2,1)S(1)}, u32[]{:S(2)}, u32[]{:S(2)}) async-start(bf16[8,64,128]{2,1,0:T(8,128)(2,1)} %constant_dynamic-update-slice_fusion), calls=%async_computation.1 | async-start | bytes 262144 | tf_op jit(solution)/shard_map/all_to_all | solution.py:330
  114.6 3.8 %intra.1.intra_ref = f32[1024,512]{1,0:T(8,128)S(1)} custom-call(bf16[1024,1536]{1,0:T(8,128)(2,1)S(1)} %get-tuple-element.10.proj_ref), custom_call_target="tpu_custom_call" | custom-call | flops 1610612736 | bytes 5242880 | tf_op jit(solution)/shard_map/intra/pallas_call | solution.py:383
  118.4 1.3 copy-done.1
  119.8 2.3 %window_attend.1.window_ref = f32[1024,128]{1,0:T(8,128)S(1)} custom-call(bf16[1024,384]{1,0:T(8,128)(2,1)S(1)} %copy-done.4, bf16[512,256]{1,0:T(8,128)(2,1)S(1)} %collective-permute-done.3.halo_ref), custom_call_target="tpu_custom_call" | custom-call | flops 402653184 | bytes 2097152 | tf_op jit(solution)/shard_map/window_attend/pallas_call | solution.py:390
  122.1 1.6 %copy-done.2 = f32[1024,512]{1,0:T(8,128)S(1)} copy-done((f32[1024,512]{1,0:T(8,128)S(1)}, f32[1024,512]{1,0:T(8,128)}, u32[]{:S(2)}) %copy-start.2) | copy-done | bytes 2097176
  124.8 2.9 %finish.1 = bf16[4,256,512]{2,1,0:T(8,128)(2,1)S(1)} custom-call(bf16[1024,1536]{1,0:T(8,128)(2,1)} %copy-done, f32[1024,512]{1,0:T(8,128)S(1)} %copy-done.2, bf16[512,128]{1,0:T(8,128)(2,1)S(1)} %bitcast.17, f32[1024,128]{1,0:T(8,128)S(1)} %copy-done.6, f32[1024,128]{1,0:T(8,128)S(1)} %window_attend.1.window_ref), custom_call_target="tpu_custom_call" | custom-call | flops 134217728 | bytes 6291456 | tf_op jit(solution)/shard_map/finish/pallas_call | solution.py:398
  127.7 29.1 %all_to_all.20.parts_ref = bf16[4,256,512]{2,1,0:T(8,128)(2,1)S(1)} all-to-all(bf16[4,256,512]{2,1,0:T(8,128)(2,1)S(1)} %finish.1), channel_id=1, replica_groups=mesh['ctx'=8,'mem'=4] {'mem'}, dimensions={0} | all-to-all | bytes 2097152 | tf_op jit(solution)/shard_map/all_to_all | solution.py:405
  (49 shorter events, 16.1 us)
Async XLA Ops:
  0.0 60.4 %collective-permute-start.2 = (bf16[256,1024]{1,0:T(8,128)(2,1)}, bf16[256,1024]{1,0:T(8,128)(2,1)S(1)}, u32[]{:S(2)}, u32[]{:S(2)}) collective-permute-start(bf16[256,1024]{1,0:T(8,128)(2,1)} %refs_0_.3), channel_id=1, source_target_pairs={{0,3},{1,0},{2,1},{3,2},{4,7},{5,4},{6,5},{7,6},{8,11},{9,8},{10,9... | collective-permute-start | bytes 1572872 | tf_op jit(solution)/shard_map/ppermute | solution.py:341
  5.0 56.2 %collective-permute-start.1 = (bf16[256,1024]{1,0:T(8,128)(2,1)}, bf16[256,1024]{1,0:T(8,128)(2,1)S(1)}, u32[]{:S(2)}, u32[]{:S(2)}) collective-permute-start(bf16[256,1024]{1,0:T(8,128)(2,1)} %refs_0_.3), channel_id=1, source_target_pairs={{0,2},{1,3},{2,0},{3,1},{4,6},{5,7},{6,4},{7,5},{8,10},{9,11},{10,... | collective-permute-start | bytes 1572872 | tf_op jit(solution)/shard_map/ppermute | solution.py:341
  5.1 57.0 %collective-permute-start = (bf16[256,1024]{1,0:T(8,128)(2,1)}, bf16[256,1024]{1,0:T(8,128)(2,1)S(1)}, u32[]{:S(2)}, u32[]{:S(2)}) collective-permute-start(bf16[256,1024]{1,0:T(8,128)(2,1)} %refs_0_.3), channel_id=1, source_target_pairs={{0,1},{1,2},{2,3},{3,0},{4,5},{5,6},{6,7},{7,4},{8,9},{9,10},{10,1... | collective-permute-start | bytes 1572872 | tf_op jit(solution)/shard_map/ppermute | solution.py:341
  7.6 68.0 %all-to-all-start.2 = ((bf16[4,32,384]{2,1,0:T(8,128)(2,1)}), bf16[4,32,384]{2,1,0:T(8,128)(2,1)S(1)}, u32[]{:S(2)}, u32[]{:S(2)}) async-start(bf16[4,32,384]{2,1,0:T(8,128)(2,1)} %pad_maximum_fusion), calls=%async_computation.2 | async-start | bytes 196608 | tf_op jit(solution)/shard_map/all_to_all | solution.py:356
  60.4 0.8 copy-start.9
  62.0 0.8 copy-start.15
  62.8 1.0 copy-start.7
  63.9 1.0 copy-start.10
  64.9 1.0 copy-start.13
  65.9 1.0 copy-start.16
  74.8 0.8 copy-start.5
  75.6 42.8 %copy-start = (bf16[1024,1536]{1,0:T(8,128)(2,1)}, bf16[1024,1536]{1,0:T(8,128)(2,1)S(1)}, u32[]{:S(2)}) copy-start(bf16[1024,1536]{1,0:T(8,128)(2,1)S(1)} %get-tuple-element.10.proj_ref) | copy-start | bytes 9437188
  75.6 25.7 %all-to-all-start = ((f32[8,64,128]{2,1,0:T(8,128)}), f32[8,64,128]{2,1,0:T(8,128)}, u32[]{:S(2)}, u32[]{:S(2)}) async-start(f32[8,64,128]{2,1,0:T(8,128)} %bitcast.4), calls=%async_computation | async-start | bytes 524288 | tf_op jit(solution)/shard_map/all_to_all | solution.py:325
  91.9 1.0 copy-start.8
  93.0 1.0 copy-start.11
  94.0 1.0 copy-start.14
  95.1 1.0 copy-start.17
  98.1 0.9 copy-start.3
  99.0 20.8 %collective-permute-start.3 = (bf16[512,256]{1,0:T(8,128)(2,1)}, bf16[512,256]{1,0:T(8,128)(2,1)S(1)}, u32[]{:S(2)}, u32[]{:S(2)}) collective-permute-start(bf16[512,256]{1,0:T(8,128)(2,1)} %get-tuple-element.14), channel_id=1, source_target_pairs={{0,4},{4,8},{8,12},{12,16},{16,20},{20,24},{24,28},{1,5},{5,9},{9,... | collective-permute-start | bytes 786440 | tf_op jit(solution)/shard_map/ppermute | solution.py:21
  111.0 11.1 %all-to-all-start.1 = ((bf16[8,64,128]{2,1,0:T(8,128)(2,1)}), bf16[8,64,128]{2,1,0:T(8,128)(2,1)S(1)}, u32[]{:S(2)}, u32[]{:S(2)}) async-start(bf16[8,64,128]{2,1,0:T(8,128)(2,1)} %constant_dynamic-update-slice_fusion), calls=%async_computation.1 | async-start | bytes 262144 | tf_op jit(solution)/shard_map/all_to_all | solution.py:330
  114.6 5.2 %copy-start.4 = (bf16[1024,384]{1,0:T(8,128)(2,1)S(1)}, bf16[1024,384]{1,0:T(8,128)(2,1)}, u32[]{:S(2)}) copy-start(bf16[1024,384]{1,0:T(8,128)(2,1)} %copy-done.3) | copy-start | bytes 2359300
  118.4 1.4 copy-start.1
  122.1 1.6 %copy-start.2 = (f32[1024,512]{1,0:T(8,128)S(1)}, f32[1024,512]{1,0:T(8,128)}, u32[]{:S(2)}) copy-start(f32[1024,512]{1,0:T(8,128)} %copy-done.1) | copy-start | bytes 6291460
  123.7 1.0 copy-start.6
  (2 other events, 1.5 us)

commit v2 on v0

--- a/solution.py
+++ b/solution.py
@@ -1,6 +1,10 @@
+import functools
+
 import jax
 import jax.numpy as jnp
 from jax import lax
+from jax.experimental import pallas as pl
+from jax.experimental.pallas import tpu as pltpu
 from jax.sharding import PartitionSpec as P
 
 HEADS = 4
@@ -100,7 +104,7 @@
     return jnp.dot(rows, full_weight, preferred_element_type=jnp.float32).astype(jnp.bfloat16)
 
 
-def shards(tokens, routes, router, mem_weight, win_weight):
+def sparse_shards(tokens, routes, router, mem_weight, win_weight):
     tok_dev = tokens.shape[0]
     mems = router.shape[1]
     n_mem = lax.axis_size("mem")
@@ -146,6 +150,661 @@
         query_rows, key_block[:, :width], key_block[:, width:], first_pos, tok_dev
     )
     return (memory_part + window_part).astype(jnp.bfloat16)
+
+HBM = pl.BlockSpec(memory_space=pltpu.HBM)
+WHOLE = pl.BlockSpec()
+ROUTE_ROWS = 16
+
+
+def kernel_call(body, name, out_shape, flops, moved, grant=16, **kwargs):
+    return pl.pallas_call(
+        body,
+        name=name,
+        out_shape=out_shape,
+        cost_estimate=pl.CostEstimate(flops=flops, bytes_accessed=moved, transcendentals=0),
+        compiler_params=pltpu.CompilerParams(vmem_limit_bytes=grant * 1024 * 1024),
+        **kwargs,
+    )
+
+
+def rows_of(group, count):
+    return pl.ds(pl.multiple_of(group * count, count), count)
+
+
+def begin(source, target, sem):
+    copy = pltpu.make_async_copy(source, target, sem)
+    copy.start()
+    return copy
+
+
+def pack_body(weight_ref, routes_ref, *refs):
+    outs, (rows_ref, sem) = refs[:-2], refs[-2:]
+    cut, _ = rows_ref.shape
+    width = HEADS * HDIM
+    n_mem = len(outs)
+    copy = begin(weight_ref.at[rows_of(lax.axis_index("ctx"), cut), :], rows_ref, sem)
+    routes = routes_ref[...].astype(jnp.float32)
+    count = routes.shape[1]
+    row = lax.broadcasted_iota(jnp.int32, (ROUTE_ROWS, count), 0)
+    named = jnp.where(row == 0, routes[0:1, :], jnp.where(row == 1, routes[1:2, :], 0.0))
+    named = named.astype(jnp.bfloat16)
+    rest = outs[0].shape[1] - count
+    for out_ref in outs:
+        out_ref[cut : cut + ROUTE_ROWS, 0:count] = named
+        if rest:
+            out_ref[cut : cut + ROUTE_ROWS, count:] = jnp.zeros((ROUTE_ROWS, rest), jnp.bfloat16)
+    copy.wait()
+    mine = lax.axis_index("mem")
+    for shift, out_ref in enumerate(outs):
+        head = lax.rem(mine + shift, n_mem)
+        for part in range(3):
+            at = pl.ds(pl.multiple_of(part * width + head * HDIM, HDIM), HDIM)
+            out_ref[0:cut, part * HDIM : (part + 1) * HDIM] = rows_ref[:, at]
+
+
+def arrange_body(*refs):
+    pieces, out_ref = refs[:-1], refs[-1]
+    mine = lax.axis_index("mem")
+    for shift, piece_ref in enumerate(pieces):
+        out_ref[lax.rem(mine + len(pieces) - shift, len(pieces))] = piece_ref[...]
+
+
+def as_column(row, count):
+    diagonal = lax.broadcasted_iota(jnp.int32, (count, count), 0) == lax.broadcasted_iota(
+        jnp.int32, (count, count), 1
+    )
+    return jnp.sum(jnp.where(diagonal, row, 0.0), axis=1, keepdims=True)
+
+
+def members(group, packed_ref, count):
+    cut = packed_ref.shape[1] - ROUTE_ROWS
+    mine = lax.axis_index("mem").astype(jnp.float32)
+    named = packed_ref[group, cut : cut + ROUTE_ROWS, 0:count].astype(jnp.float32)
+    first = as_column(named[0:1, :], count)
+    second = as_column(named[1:2, :], count)
+    return first, second, first == mine, second == mine
+
+
+def coefficients(tokens, router, first, second, is_first, is_second):
+    logits = lax.dot_general(
+        tokens, router, (((1,), (1,)), ((), ())), preferred_element_type=jnp.float32
+    )
+    lane = lax.broadcasted_iota(jnp.int32, logits.shape, 1).astype(jnp.float32)
+    difference = jnp.sum(
+        jnp.where(lane == first, logits, 0.0) - jnp.where(lane == second, logits, 0.0),
+        axis=1,
+        keepdims=True,
+    )
+    gate = jax.nn.sigmoid(difference)
+    coef = jnp.where(is_first, gate, jnp.where(is_second, 1.0 - gate, 0.0))
+    return jnp.broadcast_to(coef, (tokens.shape[0], HDIM))
+
+
+def outer_sum(keys, values):
+    return lax.dot_general(
+        keys, values, (((0,), (0,)), ((), ())), preferred_element_type=jnp.float32
+    )
+
+
+def pair(queries, keys, values, causal=None):
+    scores = lax.dot_general(
+        queries, keys, (((1,), (1,)), ((), ())), preferred_element_type=jnp.float32
+    )
+    if causal is not None:
+        scores = jnp.where(causal, scores, 0.0)
+    return jnp.dot(scores.astype(jnp.bfloat16), values, preferred_element_type=jnp.float32)
+
+
+def triangle(count):
+    return lax.broadcasted_iota(jnp.int32, (count, count), 1) <= lax.broadcasted_iota(
+        jnp.int32, (count, count), 0
+    )
+
+
+def slot_group(slot):
+    hop = (slot + 1) // 2
+    return lax.axis_index("mem") + jnp.where(lax.rem(slot, 2) == 1, -hop, hop)
+
+
+def early_body(n_mem, hops, *refs):
+    slots = 1 + 2 * hops
+    sources = refs[:slots]
+    packed_ref, router_ref, weight_ref = refs[slots : slots + 3]
+    proj_ref, intra_ref, coef_ref, state_ref = refs[slots + 3 : slots + 7]
+    rows_ref, held_ref, made_ref, sum_ref, sems, weight_sem, out_sems = refs[slots + 7 :]
+    count = sources[0].shape[0]
+    width = HEADS * HDIM
+    load = begin(weight_ref, held_ref, weight_sem)
+
+    def here(group):
+        return (group >= 0) & (group < n_mem)
+
+    for slot in range(slots):
+
+        @pl.when(here(slot_group(slot)))
+        def _(slot=slot):
+            begin(sources[slot], rows_ref.at[slot], sems.at[slot])
+
+    state_ref[...] = jnp.zeros_like(state_ref)
+    for slot in range(slots):
+
+        @pl.when(here(slot_group(slot)))
+        def _(slot=slot):
+            pltpu.make_async_copy(sources[slot], rows_ref.at[slot], sems.at[slot]).wait()
+
+    load.wait()
+
+    @pl.loop(0, slots)
+    def _(slot):
+        group = slot_group(slot)
+
+        @pl.when(here(group))
+        def _():
+            place = rows_of(group, count)
+            tokens = rows_ref[slot]
+            first, second, is_first, is_second = members(group, packed_ref, count)
+            projected = jnp.dot(tokens, held_ref[...], preferred_element_type=jnp.float32)
+            projected = jnp.where(is_first | is_second, projected, 0.0).astype(jnp.bfloat16)
+            made_ref[place, :] = projected
+            coef_ref[place, :] = coefficients(
+                tokens, router_ref[...], first, second, is_first, is_second
+            )
+            for head in range(HEADS):
+                columns = slice(head * HDIM, (head + 1) * HDIM)
+                state_ref[columns, :] += outer_sum(
+                    projected[:, width + head * HDIM : width + (head + 1) * HDIM],
+                    projected[:, 2 * width + head * HDIM : 2 * width + (head + 1) * HDIM],
+                )
+
+    stored = begin(made_ref, proj_ref, out_sems.at[0])
+    mine = lax.axis_index("mem")
+
+    def present(group):
+        return jnp.abs(mine - group) <= hops
+
+    def block(queries_at, keys_at, head, causal=None):
+        return pair(
+            made_ref[rows_of(queries_at, count), head * HDIM : (head + 1) * HDIM],
+            made_ref[rows_of(keys_at, count), width + head * HDIM : width + (head + 1) * HDIM],
+            made_ref[
+                rows_of(keys_at, count), 2 * width + head * HDIM : 2 * width + (head + 1) * HDIM
+            ],
+            causal,
+        )
+
+    @pl.loop(0, n_mem)
+    def _(group):
+        @pl.when(present(group))
+        def _():
+            for head in range(HEADS):
+                sum_ref[rows_of(group, count), head * HDIM : (head + 1) * HDIM] = block(
+                    group, group, head, triangle(count)
+                )
+
+        @pl.loop(0, group)
+        def _(other):
+            @pl.when(present(group) & present(other))
+            def _():
+                for head in range(HEADS):
+                    sum_ref[rows_of(group, count), head * HDIM : (head + 1) * HDIM] += block(
+                        group, other, head
+                    )
+
+    summed = begin(sum_ref, intra_ref, out_sems.at[1])
+    stored.wait()
+    summed.wait()
+
+
+def last_keys_body(n_mem, below_ref, above_ref, packed_ref, weight_ref, before_ref, *refs):
+    kv_ref, state_ref, rows_ref, held_ref, sems = refs
+    count = rows_ref.shape[0]
+    width = HEADS * HDIM
+    mine = lax.axis_index("mem")
+    state_ref[...] = before_ref[...]
+    load = pltpu.make_async_copy(weight_ref.at[:, pl.ds(width, 2 * width)], held_ref, sems.at[0])
+    from_below = pltpu.make_async_copy(below_ref, rows_ref, sems.at[1])
+    from_above = pltpu.make_async_copy(above_ref, rows_ref, sems.at[2])
+    at_end = (mine == 0) | (mine == n_mem - 1)
+
+    @pl.when(at_end)
+    def _():
+        load.start()
+
+    @pl.when(mine == 0)
+    def _():
+        from_above.start()
+        from_above.wait()
+
+    @pl.when(mine == n_mem - 1)
+    def _():
+        from_below.start()
+        from_below.wait()
+
+    @pl.when(at_end)
+    def _():
+        _, _, is_first, is_second = members(n_mem - 1 - mine, packed_ref, count)
+        load.wait()
+        projected = jnp.dot(rows_ref[...], held_ref[...], preferred_element_type=jnp.float32)
+        projected = jnp.where(is_first | is_second, projected, 0.0).astype(jnp.bfloat16)
+        kv_ref[...] = projected
+        for head in range(HEADS):
+            columns = slice(head * HDIM, (head + 1) * HDIM)
+            state_ref[columns, :] += outer_sum(
+                projected[:, columns], projected[:, width + head * HDIM : width + (head + 1) * HDIM]
+            )
+
+
+def last_queries_body(n_mem, below_ref, above_ref, packed_ref, router_ref, weight_ref, proj_ref, kv_ref, *refs):
+    query_ref, coef_ref, extra_ref, rows_ref, held_ref, made_ref, sum_ref, sems = refs
+    count = rows_ref.shape[0]
+    total = made_ref.shape[0]
+    width = HEADS * HDIM
+    mine = lax.axis_index("mem")
+    load = pltpu.make_async_copy(weight_ref.at[:, pl.ds(0, width)], held_ref, sems.at[0])
+    from_below = pltpu.make_async_copy(below_ref, rows_ref, sems.at[1])
+    from_above = pltpu.make_async_copy(above_ref, rows_ref, sems.at[2])
+    made = pltpu.make_async_copy(proj_ref, made_ref, sems.at[3])
+    own = slice(0, count)
+    last = slice(total - count, total)
+    store_all = pltpu.make_async_copy(sum_ref, extra_ref, sems.at[4])
+    store_last = pltpu.make_async_copy(sum_ref.at[last, :], extra_ref.at[last, :], sems.at[5])
+    at_end = (mine == 0) | (mine == n_mem - 1)
+
+    @pl.when(at_end)
+    def _():
+        load.start()
+        made.start()
+
+    @pl.when(mine == 0)
+    def _():
+        from_above.start()
+        from_above.wait()
+
+    @pl.when(mine == n_mem - 1)
+    def _():
+        from_below.start()
+        from_below.wait()
+
+    @pl.when(at_end)
+    def _():
+        tokens = rows_ref[...]
+        first, second, is_first, is_second = members(n_mem - 1 - mine, packed_ref, count)
+        coef_ref[...] = coefficients(tokens, router_ref[...], first, second, is_first, is_second)
+        load.wait()
+        queries = jnp.dot(tokens, held_ref[...], preferred_element_type=jnp.float32)
+        query_ref[...] = jnp.where(is_first | is_second, queries, 0.0).astype(jnp.bfloat16)
+        made.wait()
+        causal = triangle(count)
+        at = jnp.where(mine == 0, n_mem - 1, 0)
+        for head in range(HEADS):
+            columns = slice(head * HDIM, (head + 1) * HDIM)
+            value_columns = slice(width + head * HDIM, width + (head + 1) * HDIM)
+            sum_ref[rows_of(at, count), columns] = pair(
+                query_ref[:, columns], kv_ref[:, columns], kv_ref[:, value_columns], causal
+            )
+
+    @pl.when(mine == 0)
+    def _():
+        for head in range(HEADS):
+            columns = slice(head * HDIM, (head + 1) * HDIM)
+            key_columns = slice(width + head * HDIM, width + (head + 1) * HDIM)
+            value_columns = slice(2 * width + head * HDIM, 2 * width + (head + 1) * HDIM)
+            sum_ref[last, columns] += pair(
+                query_ref[:, columns],
+                made_ref[0 : total - count, key_columns],
+                made_ref[0 : total - count, value_columns],
+            )
+        store_last.start()
+        store_last.wait()
+
+    @pl.when(mine == n_mem - 1)
+    def _():
+        for head in range(HEADS):
+            columns = slice(head * HDIM, (head + 1) * HDIM)
+            value_columns = slice(width + head * HDIM, width + (head + 1) * HDIM)
+            for group in range(1, n_mem):
+                here = slice(group * count, (group + 1) * count)
+                sum_ref[here, columns] = pair(
+                    made_ref[here, columns], kv_ref[:, columns], kv_ref[:, value_columns]
+                )
+        store_all.start()
+        store_all.wait()
+
+
+def window_project_body(n_mem, *refs):
+    slots = 2 * n_mem - 1
+    sources = refs[:slots]
+    pieces_ref, win_ref, tail_ref, rows_ref, full_ref, made_ref, sems, out_sem = refs[slots:]
+    pieces, origins, depth, _ = pieces_ref.shape
+    depth = depth - ROUTE_ROWS
+    count = sources[0].shape[0]
+    total = n_mem * count
+
+    def here(slot):
+        group = slot_group(slot)
+        return (group >= 0) & (group < n_mem)
+
+    for slot in range(slots):
+
+        @pl.when(here(slot))
+        def _(slot=slot):
+            place = rows_of(slot_group(slot), count)
+            begin(sources[slot], rows_ref.at[place, :], sems.at[slot])
+
+    for origin in range(origins):
+        for piece in range(pieces):
+            start = (origin * pieces + piece) * depth
+            full_ref[start : start + depth, :] = pieces_ref[piece, origin, 0:depth, :]
+    for slot in range(slots):
+
+        @pl.when(here(slot))
+        def _(slot=slot):
+            place = rows_of(slot_group(slot), count)
+            pltpu.make_async_copy(sources[slot], rows_ref.at[place, :], sems.at[slot]).wait()
+
+    for group in range(n_mem):
+        place = slice(group * count, (group + 1) * count)
+        made_ref[place, :] = jnp.dot(
+            rows_ref[place, :], full_ref[...], preferred_element_type=jnp.float32
+        ).astype(jnp.bfloat16)
+    stored = begin(made_ref, win_ref, out_sem)
+    tail_ref[...] = made_ref[total - WINDOW : total, HDIM:]
+    stored.wait()
+
+
+def window_attend_body(count, win_ref, halo_ref, out_ref, held_ref, keys_ref, sem):
+    load = begin(win_ref, held_ref, sem)
+    total = held_ref.shape[0]
+    keys_ref[0:WINDOW, :] = halo_ref[...]
+    span = count + WINDOW
+    row = lax.broadcasted_iota(jnp.int32, (count, span), 0)
+    column = lax.broadcasted_iota(jnp.int32, (count, span), 1)
+    distance = row + WINDOW - column
+    within = (distance >= 0) & (distance < WINDOW)
+    missing = jnp.where(lax.axis_index("ctx") == 0, WINDOW, 0)
+    load.wait()
+    keys_ref[WINDOW:, :] = held_ref[:, HDIM:]
+    for block in range(total // count):
+        start = block * count
+        keys = keys_ref[start : start + span, :HDIM]
+        values = keys_ref[start : start + span, HDIM:]
+        scores = lax.dot_general(
+            held_ref[start : start + count, :HDIM],
+            keys,
+            (((1,), (1,)), ((), ())),
+            preferred_element_type=jnp.float32,
+        ) * HDIM ** (-0.5)
+        allowed = within & (column + start >= missing) if start < WINDOW else within
+        masked = jnp.where(allowed, scores, -1e30)
+        highest = jnp.max(masked, axis=-1, keepdims=True)
+        expo = jnp.exp(masked - highest)
+        probs = (expo / jnp.sum(expo, axis=-1, keepdims=True)).astype(jnp.bfloat16)
+        out_ref[start : start + count, :] = jnp.dot(
+            probs, values, preferred_element_type=jnp.float32
+        )
+
+
+def finish_body(n_mem, shift, *refs):
+    proj_ref, intra_ref, coef_ref, last_query_ref, last_coef_ref, extra_ref = refs[:6]
+    window_ref, prefix_ref, out_ref = refs[6:9]
+    query_s, intra_s, extra_s, coef_s, window_s, sems = refs[9:]
+    mine = lax.axis_index("mem")
+    count, width = out_ref.shape
+    group = lax.rem(mine + shift, n_mem)
+    here = rows_of(group, count)
+    is_last = ((mine == 0) & (group == n_mem - 1)) | ((mine == n_mem - 1) & (group == 0))
+    has_extra = (mine == n_mem - 1) | is_last
+    early = [
+        pltpu.make_async_copy(proj_ref.at[here, pl.ds(0, width)], query_s, sems.at[0]),
+        pltpu.make_async_copy(intra_ref.at[here, :], intra_s, sems.at[1]),
+        pltpu.make_async_copy(coef_ref.at[here, :], coef_s, sems.at[2]),
+    ]
+    late = [
+        pltpu.make_async_copy(last_query_ref, query_s, sems.at[3]),
+        pltpu.make_async_copy(last_coef_ref, coef_s, sems.at[4]),
+    ]
+    extra = pltpu.make_async_copy(extra_ref.at[here, :], extra_s, sems.at[5])
+    window = begin(window_ref.at[here, :], window_s, sems.at[6])
+
+    @pl.when(has_extra)
+    def _():
+        extra.start()
+
+    @pl.when(is_last)
+    def _():
+        for copy in late:
+            copy.start()
+        intra_s[...] = jnp.zeros_like(intra_s)
+        for copy in late:
+            copy.wait()
+
+    @pl.when(jnp.logical_not(is_last))
+    def _():
+        for copy in early:
+            copy.start()
+        for copy in early:
+            copy.wait()
+
+    @pl.when(has_extra)
+    def _():
+        extra.wait()
+        intra_s[...] += extra_s[...]
+
+    window.wait()
+    coef = coef_s[...]
+    for head in range(HEADS):
+        columns = slice(head * HDIM, (head + 1) * HDIM)
+        summed = intra_s[:, columns] + jnp.dot(
+            query_s[:, columns], prefix_ref[columns, :], preferred_element_type=jnp.float32
+        )
+        factor = lax.rsqrt(jnp.mean(summed * summed, axis=-1, keepdims=True) + norm_eps)
+        memory_out = (summed * factor).astype(jnp.bfloat16).astype(jnp.float32)
+        window_part = jnp.where(mine == head, window_s[...], 0.0)
+        out_ref[:, columns] = (coef * memory_out + window_part).astype(out_ref.dtype)
+
+
+def add_body(*refs):
+    total = refs[0][...]
+    for part_ref in refs[1:-1]:
+        total += part_ref[...].astype(jnp.float32)
+    refs[-1][...] = total.astype(jnp.bfloat16)
+
+
+def running_sums_body(pieces_ref, sums_ref):
+    total = jnp.zeros(pieces_ref.shape[1:], jnp.float32)
+    for index in range(pieces_ref.shape[0]):
+        sums_ref[index] = total.astype(jnp.bfloat16)
+        total += pieces_ref[index]
+
+
+def exclusive_prefix(state):
+    devices = lax.axis_size("ctx")
+    pieces = state.reshape(devices, -1, state.shape[1])
+    pieces = lax.all_to_all(pieces, "ctx", split_axis=0, concat_axis=0, tiled=True)
+    sums = kernel_call(
+        running_sums_body,
+        "running_sums",
+        jax.ShapeDtypeStruct(pieces.shape, jnp.bfloat16),
+        pieces.size,
+        6 * pieces.size,
+    )(pieces)
+    return lax.all_to_all(sums, "ctx", split_axis=0, concat_axis=0, tiled=True).reshape(state.shape)
+
+
+def dense_shards(tokens, routes, router, mem_weight, win_weight):
+    count, depth = tokens.shape
+    n_mem = lax.axis_size("mem")
+    n_ctx = lax.axis_size("ctx")
+    total = n_mem * count
+    width = HEADS * HDIM
+    cut = win_weight.shape[0] // n_ctx
+    low, full = jnp.bfloat16, jnp.float32
+    dma = pltpu.SemaphoreType.DMA
+
+    def shape(rows, columns, kind=low):
+        return jax.ShapeDtypeStruct((rows, columns), kind)
+
+    below, above = [tokens], [tokens]
+    for hop in range(1, n_mem):
+        up = [(i, i + 1) for i in range(hop - 1, n_mem - 1)]
+        down = [(n_mem - 1 - i, n_mem - 1 - j) for i, j in up]
+        below.append(lax.ppermute(below[-1], "mem", up))
+        above.append(lax.ppermute(above[-1], "mem", down))
+    slots = [tokens]
+    for hop in range(1, n_mem):
+        slots += [below[hop], above[hop]]
+
+    packed = kernel_call(
+        pack_body,
+        "pack",
+        [shape(cut + ROUTE_ROWS, 3 * HDIM)] * n_mem,
+        1 << 20,
+        1 << 20,
+        in_specs=[HBM, WHOLE],
+        scratch_shapes=[pltpu.VMEM((cut, 3 * width), low), dma],
+    )(win_weight, routes.T)
+    packed = [packed[0]] + [
+        lax.ppermute(packed[s], "mem", [(i, (i + s) % n_mem) for i in range(n_mem)])
+        for s in range(1, n_mem)
+    ]
+    packed = kernel_call(
+        arrange_body,
+        "arrange",
+        jax.ShapeDtypeStruct((n_mem,) + packed[0].shape, low),
+        1 << 20,
+        1 << 20,
+    )(*packed)
+    pieces = lax.all_gather(packed, "ctx", axis=0, tiled=False)
+
+    weight = mem_weight[0]
+    router_rows = router.T
+    hops = n_mem - 2
+    early = 1 + 2 * hops
+    proj, intra, coef, state = kernel_call(
+        functools.partial(early_body, n_mem, hops),
+        "early_rows",
+        (
+            shape(total, 3 * width),
+            shape(total, width, full),
+            shape(total, HDIM, full),
+            shape(width, HDIM, full),
+        ),
+        2 * total * depth * 3 * width,
+        10 << 20,
+        grant=24,
+        in_specs=[HBM] * early + [WHOLE, WHOLE, HBM],
+        out_specs=[HBM, HBM, WHOLE, WHOLE],
+        scratch_shapes=[
+            pltpu.VMEM((early, count, depth), low),
+            pltpu.VMEM((depth, 3 * width), low),
+            pltpu.VMEM((total, 3 * width), low),
+            pltpu.VMEM((total, width), full),
+            dma((early,)),
+            dma,
+            dma((2,)),
+        ],
+    )(*slots[:early], packed, router_rows, weight)
+    last_kv, state = kernel_call(
+        functools.partial(last_keys_body, n_mem),
+        "last_keys",
+        (shape(count, 2 * width), shape(width, HDIM, full)),
+        2 * count * depth * 2 * width,
+        3 << 20,
+        in_specs=[HBM, HBM, WHOLE, HBM, WHOLE],
+        scratch_shapes=[
+            pltpu.VMEM((count, depth), low),
+            pltpu.VMEM((depth, 2 * width), low),
+            dma((3,)),
+        ],
+    )(below[-1], above[-1], packed, weight, state)
+    prefix = exclusive_prefix(state)
+
+    win, tail = kernel_call(
+        functools.partial(window_project_body, n_mem),
+        "window_project",
+        (shape(total, 3 * HDIM), shape(WINDOW, 2 * HDIM)),
+        2 * total * depth * 3 * HDIM,
+        5 << 20,
+        in_specs=[HBM] * len(slots) + [WHOLE],
+        out_specs=[HBM, WHOLE],
+        scratch_shapes=[
+            pltpu.VMEM((total, depth), low),
+            pltpu.VMEM((depth, 3 * HDIM), low),
+            pltpu.VMEM((total, 3 * HDIM), low),
+            dma((len(slots),)),
+            dma,
+        ],
+    )(*slots, pieces)
+    halo = passed_along(tail, "ctx", 1)
+    last_query, last_coef, extra = kernel_call(
+        functools.partial(last_queries_body, n_mem),
+        "last_queries",
+        (shape(count, width), shape(count, HDIM, full), shape(total, width, full)),
+        8 * count * depth * width,
+        8 << 20,
+        in_specs=[HBM, HBM, WHOLE, WHOLE, HBM, HBM, WHOLE],
+        out_specs=[WHOLE, WHOLE, HBM],
+        scratch_shapes=[
+            pltpu.VMEM((count, depth), low),
+            pltpu.VMEM((depth, width), low),
+            pltpu.VMEM((total, 3 * width), low),
+            pltpu.VMEM((total, width), full),
+            dma((6,)),
+        ],
+    )(below[-1], above[-1], packed, router_rows, weight, proj, last_kv)
+    window_part = kernel_call(
+        functools.partial(window_attend_body, count),
+        "window_attend",
+        shape(total, HDIM, full),
+        4 * total * (count + WINDOW) * HDIM,
+        3 << 20,
+        in_specs=[HBM, WHOLE],
+        scratch_shapes=[
+            pltpu.VMEM((total, 3 * HDIM), low),
+            pltpu.VMEM((total + WINDOW, 2 * HDIM), low),
+            dma,
+        ],
+    )(win, halo)
+
+    def finish(shift):
+        return kernel_call(
+            functools.partial(finish_body, n_mem, shift),
+            f"finish{shift}",
+            shape(count, width, low if shift else full),
+            2 * count * width * HDIM,
+            2 << 20,
+            in_specs=[HBM] * 7 + [WHOLE],
+            scratch_shapes=[
+                pltpu.VMEM((count, width), low),
+                pltpu.VMEM((count, width), full),
+                pltpu.VMEM((count, width), full),
+                pltpu.VMEM((count, HDIM), full),
+                pltpu.VMEM((count, HDIM), full),
+                dma((7,)),
+            ],
+        )(proj, intra, coef, last_query, last_coef, extra, window_part, prefix)
+
+    parts = []
+    for shift in sorted(range(1, n_mem), key=lambda s: abs(2 * s - n_mem)):
+        pairs = [(i, (i + shift) % n_mem) for i in range(n_mem)]
+        parts.append(lax.ppermute(finish(shift), "mem", pairs))
+    return kernel_call(
+        add_body, "add_parts", shape(count, width), n_mem * count * width, 2 << 20
+    )(finish(0), *parts)
+
+
+def shards(tokens, routes, router, mem_weight, win_weight):
+    n_mem = lax.axis_size("mem")
+    n_ctx = lax.axis_size("ctx")
+    dense = (
+        n_mem == HEADS
+        and router.shape[1] == n_mem
+        and win_weight.shape[0] % (16 * n_ctx) == 0
+        and tokens.shape[0] <= 3 * HDIM
+        and n_mem * tokens.shape[0] >= WINDOW
+    )
+    body = dense_shards if dense else sparse_shards
+    return body(tokens, routes, router, mem_weight, win_weight)
 
 
 def solution(mesh):

time: 304 us -> 148 us (0.49)
  the two profiles are of different devices: /device:TPU:0 before, /device:TPU:9 now
where the time goes in v2:
time: 148 us; the launch traced here: 147 us
  waiting for transfers between devices  39.1 us (26%)
  starting transfers between devices  35.8 us (24%)
  local copies, waits for them, and re-layouts  31 us (21%)
  Pallas kernels  27.1 us (18%)
  between operations  13.7 us (9%)
    unnamed x76, local copies, waits for them, and re-layouts  31 us
    ppermute x3, waiting for transfers between devices, dense_shards(): parts.append(lax.ppermute(finish(shift), 'mem', pairs))  21.3 us
    ppermute x3, waiting for transfers between devices, dense_shards(): above.append(lax.ppermute(above[-1], 'mem', down))  15.8 us
    pallas_call x1, Pallas kernels, dense_shards(): kernel_call(functools.partial(early_body, n_mem, hops), 'early_rows', (sh...  13.6 us
    ppermute x3, starting transfers between devices, dense_shards(): above.append(lax.ppermute(above[-1], 'mem', down))  10.5 us
    all_to_all x1, starting transfers between devices, exclusive_prefix(): lax.all_to_all(pieces, 'ctx', split_axis=0, concat_axis=0, tiled=True)  7.1 us
    ppermute x3, starting transfers between devices, dense_shards(): below.append(lax.ppermute(below[-1], 'mem', up))  4.45 us
    ppermute x3, starting transfers between devices, dense_shards(): lax.ppermute(packed[s], 'mem', [(i, (i + s) % n_mem) for i in range(n_mem)])  3.83 us
  transfers between devices with their start and end apart: 16, of which 7 were waited for; matrix products, arithmetic and copies ran while one was open for 0% of the time, Pallas kernels for 16%

profile of v2, /device:TPU:9, one launch (start us, length us, event | category | flops | bytes accessed | tf_op | source)
XLA Modules:
  0.0 146.8 jit_solution(4528058379401848025)
XLA Ops:
  8.5 1.3 collective-permute-start.4
  10.9 1.4 collective-permute-start.6
  15.0 3.4 %collective-permute-start.1 = (bf16[256,1024]{1,0:T(8,128)(2,1)}, bf16[256,1024]{1,0:T(8,128)(2,1)S(1)}, u32[]{:S(2)}, u32[]{:S(2)}) collective-permute-start(bf16[256,1024]{1,0:T(8,128)(2,1)} %refs_0_.3), channel_id=1, source_target_pairs={{3,2},{2,1},{1,0},{7,6},{6,5},{5,4},{11,10},{10,9},{9,8},{15,14},{... | collective-permute-start | bytes 1572872 | tf_op jit(solution)/shard_map/ppermute | solution.py:652
  18.4 1.9 %collective-permute-start = (bf16[256,1024]{1,0:T(8,128)(2,1)}, bf16[256,1024]{1,0:T(8,128)(2,1)S(1)}, u32[]{:S(2)}, u32[]{:S(2)}) collective-permute-start(bf16[256,1024]{1,0:T(8,128)(2,1)} %refs_0_.3), channel_id=1, source_target_pairs={{0,1},{1,2},{2,3},{4,5},{5,6},{6,7},{8,9},{9,10},{10,11},{12,13},{... | collective-permute-start | bytes 1572872 | tf_op jit(solution)/shard_map/ppermute | solution.py:651
  20.4 8.5 %collective-permute-done.1.refs_2_ = bf16[256,1024]{1,0:T(8,128)(2,1)S(1)} collective-permute-done((bf16[256,1024]{1,0:T(8,128)(2,1)}, bf16[256,1024]{1,0:T(8,128)(2,1)S(1)}, u32[]{:S(2)}, u32[]{:S(2)}) %collective-permute-start.1) | collective-permute-done | bytes 524320 | tf_op jit(solution)/shard_map/ppermute | solution.py:652
  28.8 3.5 %collective-permute-start.3 = (bf16[256,1024]{1,0:T(8,128)(2,1)S(1)}, bf16[256,1024]{1,0:T(8,128)(2,1)S(1)}, u32[]{:S(2)}, u32[]{:S(2)}) collective-permute-start(bf16[256,1024]{1,0:T(8,128)(2,1)S(1)} %collective-permute-done.1.refs_2_), channel_id=1, source_target_pairs={{2,1},{1,0},{6,5},{5,4},{10,9},{9,8},{14,13},{13,12},{18,17},{17,1... | collective-permute-start | bytes 1572872 | tf_op jit(solution)/shard_map/ppermute | solution.py:652
  32.3 1.8 %collective-permute-start.2 = (bf16[256,1024]{1,0:T(8,128)(2,1)S(1)}, bf16[256,1024]{1,0:T(8,128)(2,1)S(1)}, u32[]{:S(2)}, u32[]{:S(2)}) collective-permute-start(bf16[256,1024]{1,0:T(8,128)(2,1)S(1)} %collective-permute-done.refs_1_), channel_id=1, source_target_pairs={{1,2},{2,3},{5,6},{6,7},{9,10},{10,11},{13,14},{14,15},{17,18},{18... | collective-permute-start | bytes 1572872 | tf_op jit(solution)/shard_map/ppermute | solution.py:651
  34.2 7.3 %collective-permute-done.3.refs_4_ = bf16[256,1024]{1,0:T(8,128)(2,1)S(1)} collective-permute-done((bf16[256,1024]{1,0:T(8,128)(2,1)S(1)}, bf16[256,1024]{1,0:T(8,128)(2,1)S(1)}, u32[]{:S(2)}, u32[]{:S(2)}) %collective-permute-start.3) | collective-permute-done | bytes 524320 | tf_op jit(solution)/shard_map/ppermute | solution.py:652
  41.5 3.6 %collective-permute-start.8 = (bf16[256,1024]{1,0:T(8,128)(2,1)S(1)}, bf16[256,1024]{1,0:T(8,128)(2,1)S(1)}, u32[]{:S(2)}, u32[]{:S(2)}) collective-permute-start(bf16[256,1024]{1,0:T(8,128)(2,1)S(1)} %collective-permute-done.3.refs_4_), channel_id=1, source_target_pairs={{1,0},{5,4},{9,8},{13,12},{17,16},{21,20},{25,24},{29,28}} | collective-permute-start | bytes 1572872 | tf_op jit(solution)/shard_map/ppermute | solution.py:652
  45.9 1.9 %copy-done.6 = bf16[1,1024,1536]{2,1,0:T(8,128)(2,1)S(1)} copy-done((bf16[1,1024,1536]{2,1,0:T(8,128)(2,1)S(1)}, bf16[1,1024,1536]{2,1,0:T(8,128)(2,1)}, u32[]{:S(2)}) %copy-start.6) | copy-done | bytes 3145752
  49.5 13.6 %early_rows.1 = (bf16[1024,1536]{1,0:T(8,128)(2,1)S(1)}, f32[1024,512]{1,0:T(8,128)S(1)}, f32[1024,128]{1,0:T(8,128)S(1)}, f32[512,128]{1,0:T(8,128)S(1)}) custom-call(bf16[256,1024]{1,0:T(8,128)(2,1)S(1)} %copy-done.22, bf16[256,1024]{1,0:T(8,128)(2,1)S(1)} %collective-permute-done.refs_1_, bf16[256,1024]{1,0:T(8,128)(2,1)S(1)} %collective-permute-done.1.refs_2_, ...), custom_call_target="tpu_custom_call" | custom-call | flops 3221225472 | bytes 10485760 | tf_op jit(solution)/shard_map/early_rows/pallas_call | solution.py:683
  66.4 7.1 %all-to-all-start = ((f32[8,64,128]{2,1,0:T(8,128)}), f32[8,64,128]{2,1,0:T(8,128)S(1)}, u32[]{:S(2)}, u32[]{:S(2)}) async-start(f32[8,64,128]{2,1,0:T(8,128)} %bitcast.14), calls=%async_computation | async-start | bytes 524288 | tf_op jit(solution)/shard_map/all_to_all | solution.py:623
  75.6 1.3 copy-done.18
  82.1 2.3 %window_project.1 = (bf16[1024,384]{1,0:T(8,128)(2,1)S(1)}, bf16[512,256]{1,0:T(8,128)(2,1)}) custom-call(bf16[256,1024]{1,0:T(8,128)(2,1)S(1)} %copy-done.23, bf16[256,1024]{1,0:T(8,128)(2,1)S(1)} %copy-done.27, bf16[256,1024]{1,0:T(8,128)(2,1)S(1)} %copy-done.25, bf16[256,1024]{1,0:T(8,128)(2,1)S(1)} %copy-done.31, bf16[256,1024]{1,0:T(8,128)(2,1)S(1)} %copy-done.29, ...), custom_call_target="tpu_custom_call" | custom-call | flops 805306368 | bytes 5242880 | tf_op jit(solution)/shard_map/window_project/pallas_call | solution.py:722
  85.3 3.5 %collective-permute-start.9 = (bf16[512,256]{1,0:T(8,128)(2,1)}, bf16[512,256]{1,0:T(8,128)(2,1)}, u32[]{:S(2)}, u32[]{:S(2)}) collective-permute-start(bf16[512,256]{1,0:T(8,128)(2,1)} %get-tuple-element.33), channel_id=1, source_target_pairs={{0,4},{4,8},{8,12},{12,16},{16,20},{20,24},{24,28},{1,5},{5,9},{9,... | collective-permute-start | bytes 786440 | tf_op jit(solution)/shard_map/ppermute | solution.py:21
  89.6 3.3 %all-to-all-start.1 = ((bf16[8,64,128]{2,1,0:T(8,128)(2,1)}), bf16[8,64,128]{2,1,0:T(8,128)(2,1)S(1)}, u32[]{:S(2)}, u32[]{:S(2)}) async-start(bf16[8,64,128]{2,1,0:T(8,128)(2,1)} %running_sums.1), calls=%async_computation.1 | async-start | bytes 262144 | tf_op jit(solution)/shard_map/all_to_all | solution.py:631
  92.9 1.9 %copy-done.7 = bf16[1,1024,1536]{2,1,0:T(8,128)(2,1)S(1)} copy-done((bf16[1,1024,1536]{2,1,0:T(8,128)(2,1)S(1)}, bf16[1,1024,1536]{2,1,0:T(8,128)(2,1)}, u32[]{:S(2)}) %copy-start.7) | copy-done | bytes 3145752
  99.0 1.3 copy-done.2
  101.0 3.3 %window_attend.1.refs_6_ = f32[1024,128]{1,0:T(8,128)S(1)} custom-call(bf16[1024,384]{1,0:T(8,128)(2,1)S(1)} %copy-done.21, bf16[512,256]{1,0:T(8,128)(2,1)} %collective-permute-done.9.halo_ref), custom_call_target="tpu_custom_call" | custom-call | flops 402653184 | bytes 3145728 | tf_op jit(solution)/shard_map/window_attend/pallas_call | solution.py:755
  105.1 1.6 %copy-done.1 = f32[1024,512]{1,0:T(8,128)S(1)} copy-done((f32[1024,512]{1,0:T(8,128)S(1)}, f32[1024,512]{1,0:T(8,128)}, u32[]{:S(2)}) %copy-start.1) | copy-done | bytes 2097176
  106.7 1.6 %copy-done.3 = f32[1024,512]{1,0:T(8,128)S(1)} copy-done((f32[1024,512]{1,0:T(8,128)S(1)}, f32[1024,512]{1,0:T(8,128)}, u32[]{:S(2)}) %copy-start.3) | copy-done | bytes 2097176
  113.9 1.3 collective-permute-start.10
  117.8 9.0 %collective-permute-done.10.refs_1_ = bf16[256,512]{1,0:T(8,128)(2,1)S(1)} collective-permute-done((bf16[256,512]{1,0:T(8,128)(2,1)S(1)}, bf16[256,512]{1,0:T(8,128)(2,1)S(1)}, u32[]{:S(2)}, u32[]{:S(2)}) %collective-permute-start.10) | collective-permute-done | bytes 262176 | tf_op jit(solution)/shard_map/ppermute | solution.py:790
  126.8 11.2 %collective-permute-done.11.refs_2_ = bf16[256,512]{1,0:T(8,128)(2,1)S(1)} collective-permute-done((bf16[256,512]{1,0:T(8,128)(2,1)S(1)}, bf16[256,512]{1,0:T(8,128)(2,1)S(1)}, u32[]{:S(2)}, u32[]{:S(2)}) %collective-permute-start.11) | collective-permute-done | bytes 262176 | tf_op jit(solution)/shard_map/ppermute | solution.py:790
  (98 shorter events, 36.0 us)
Async XLA Ops:
  6.5 67.0 %all-gather.3.cloned.1.call-start = ((), (), s32[]{:S(2)}) async-start(), calls=%async_computation.2 | async-start | bytes 1327104 | tf_op jit(solution)/shard_map/all_gather | solution.py:677
  8.5 3.8 %collective-permute-start.4 = (bf16[48,384]{1,0:T(8,128)(2,1)S(1)}, bf16[48,384]{1,0:T(8,128)(2,1)S(1)}, u32[]{:S(2)}, u32[]{:S(2)}) collective-permute-start(bf16[48,384]{1,0:T(8,128)(2,1)S(1)} %get-tuple-element.21), channel_id=1, source_target_pairs={{0,1},{1,2},{2,3},{3,0},{4,5},{5,6},{6,7},{7,4},{8,9},{9,10},{10,1... | collective-permute-start | bytes 110600 | tf_op jit(solution)/shard_map/ppermute | solution.py:667
  9.9 3.7 %collective-permute-start.5 = (bf16[48,384]{1,0:T(8,128)(2,1)S(1)}, bf16[48,384]{1,0:T(8,128)(2,1)S(1)}, u32[]{:S(2)}, u32[]{:S(2)}) collective-permute-start(bf16[48,384]{1,0:T(8,128)(2,1)S(1)} %get-tuple-element.22), channel_id=1, source_target_pairs={{0,2},{1,3},{2,0},{3,1},{4,6},{5,7},{6,4},{7,5},{8,10},{9,11},{10,... | collective-permute-start | bytes 110600 | tf_op jit(solution)/shard_map/ppermute | solution.py:667
  10.9 3.4 %collective-permute-start.6 = (bf16[48,384]{1,0:T(8,128)(2,1)S(1)}, bf16[48,384]{1,0:T(8,128)(2,1)S(1)}, u32[]{:S(2)}, u32[]{:S(2)}) collective-permute-start(bf16[48,384]{1,0:T(8,128)(2,1)S(1)} %get-tuple-element.23), channel_id=1, source_target_pairs={{0,3},{1,0},{2,1},{3,2},{4,7},{5,4},{6,5},{7,6},{8,11},{9,8},{10,9... | collective-permute-start | bytes 110600 | tf_op jit(solution)/shard_map/ppermute | solution.py:667
  15.0 13.8 %collective-permute-start.1 = (bf16[256,1024]{1,0:T(8,128)(2,1)}, bf16[256,1024]{1,0:T(8,128)(2,1)S(1)}, u32[]{:S(2)}, u32[]{:S(2)}) collective-permute-start(bf16[256,1024]{1,0:T(8,128)(2,1)} %refs_0_.3), channel_id=1, source_target_pairs={{3,2},{2,1},{1,0},{7,6},{6,5},{5,4},{11,10},{10,9},{9,8},{15,14},{... | collective-permute-start | bytes 1572872 | tf_op jit(solution)/shard_map/ppermute | solution.py:652
  18.4 13.9 %collective-permute-start = (bf16[256,1024]{1,0:T(8,128)(2,1)}, bf16[256,1024]{1,0:T(8,128)(2,1)S(1)}, u32[]{:S(2)}, u32[]{:S(2)}) collective-permute-start(bf16[256,1024]{1,0:T(8,128)(2,1)} %refs_0_.3), channel_id=1, source_target_pairs={{0,1},{1,2},{2,3},{4,5},{5,6},{6,7},{8,9},{9,10},{10,11},{12,13},{... | collective-permute-start | bytes 1572872 | tf_op jit(solution)/shard_map/ppermute | solution.py:651
  28.8 34.2 %copy-start.24 = (bf16[256,1024]{1,0:T(8,128)(2,1)}, bf16[256,1024]{1,0:T(8,128)(2,1)S(1)}, u32[]{:S(2)}) copy-start(bf16[256,1024]{1,0:T(8,128)(2,1)S(1)} %collective-permute-done.1.refs_2_) | copy-start | bytes 1572868
  28.8 12.7 %collective-permute-start.3 = (bf16[256,1024]{1,0:T(8,128)(2,1)S(1)}, bf16[256,1024]{1,0:T(8,128)(2,1)S(1)}, u32[]{:S(2)}, u32[]{:S(2)}) collective-permute-start(bf16[256,1024]{1,0:T(8,128)(2,1)S(1)} %collective-permute-done.1.refs_2_), channel_id=1, source_target_pairs={{2,1},{1,0},{6,5},{5,4},{10,9},{9,8},{14,13},{13,12},{18,17},{17,1... | collective-permute-start | bytes 1572872 | tf_op jit(solution)/shard_map/ppermute | solution.py:652
  32.3 30.7 %copy-start.26 = (bf16[256,1024]{1,0:T(8,128)(2,1)}, bf16[256,1024]{1,0:T(8,128)(2,1)S(1)}, u32[]{:S(2)}) copy-start(bf16[256,1024]{1,0:T(8,128)(2,1)S(1)} %collective-permute-done.refs_1_) | copy-start | bytes 1572868
  32.3 12.8 %collective-permute-start.2 = (bf16[256,1024]{1,0:T(8,128)(2,1)S(1)}, bf16[256,1024]{1,0:T(8,128)(2,1)S(1)}, u32[]{:S(2)}, u32[]{:S(2)}) collective-permute-start(bf16[256,1024]{1,0:T(8,128)(2,1)S(1)} %collective-permute-done.refs_1_), channel_id=1, source_target_pairs={{1,2},{2,3},{5,6},{6,7},{9,10},{10,11},{13,14},{14,15},{17,18},{18... | collective-permute-start | bytes 1572872 | tf_op jit(solution)/shard_map/ppermute | solution.py:651
  41.5 21.6 %copy-start.28 = (bf16[256,1024]{1,0:T(8,128)(2,1)}, bf16[256,1024]{1,0:T(8,128)(2,1)S(1)}, u32[]{:S(2)}) copy-start(bf16[256,1024]{1,0:T(8,128)(2,1)S(1)} %collective-permute-done.3.refs_4_) | copy-start | bytes 1572868
  41.5 21.6 %collective-permute-start.8 = (bf16[256,1024]{1,0:T(8,128)(2,1)S(1)}, bf16[256,1024]{1,0:T(8,128)(2,1)S(1)}, u32[]{:S(2)}, u32[]{:S(2)}) collective-permute-start(bf16[256,1024]{1,0:T(8,128)(2,1)S(1)} %collective-permute-done.3.refs_4_), channel_id=1, source_target_pairs={{1,0},{5,4},{9,8},{13,12},{17,16},{21,20},{25,24},{29,28}} | collective-permute-start | bytes 1572872 | tf_op jit(solution)/shard_map/ppermute | solution.py:652
  45.1 17.9 %copy-start.30 = (bf16[256,1024]{1,0:T(8,128)(2,1)}, bf16[256,1024]{1,0:T(8,128)(2,1)S(1)}, u32[]{:S(2)}) copy-start(bf16[256,1024]{1,0:T(8,128)(2,1)S(1)} %collective-permute-done.2.refs_3_) | copy-start | bytes 1572868
  45.1 18.0 %collective-permute-start.7 = (bf16[256,1024]{1,0:T(8,128)(2,1)S(1)}, bf16[256,1024]{1,0:T(8,128)(2,1)S(1)}, u32[]{:S(2)}, u32[]{:S(2)}) collective-permute-start(bf16[256,1024]{1,0:T(8,128)(2,1)S(1)} %collective-permute-done.2.refs_3_), channel_id=1, source_target_pairs={{2,3},{6,7},{10,11},{14,15},{18,19},{22,23},{26,27},{30,31}} | collective-permute-start | bytes 1572872 | tf_op jit(solution)/shard_map/ppermute | solution.py:651
  45.9 1.9 %copy-start.6 = (bf16[1,1024,1536]{2,1,0:T(8,128)(2,1)S(1)}, bf16[1,1024,1536]{2,1,0:T(8,128)(2,1)}, u32[]{:S(2)}) copy-start(bf16[1,1024,1536]{2,1,0:T(8,128)(2,1)} %param.8) | copy-start | bytes 9437188
  66.4 22.5 %all-to-all-start = ((f32[8,64,128]{2,1,0:T(8,128)}), f32[8,64,128]{2,1,0:T(8,128)S(1)}, u32[]{:S(2)}, u32[]{:S(2)}) async-start(f32[8,64,128]{2,1,0:T(8,128)} %bitcast.14), calls=%async_computation | async-start | bytes 524288 | tf_op jit(solution)/shard_map/all_to_all | solution.py:623
  82.1 10.8 %copy-start.36 = (bf16[1024,4]{0,1:T(4,128)(2,1)S(1)}, bf16[1024,4]{0,1:T(4,128)(2,1)}, u32[]{:S(2)}) copy-start(bf16[1024,4]{0,1:T(4,128)(2,1)} %param.7) | copy-start | bytes 24580
  85.3 15.6 %collective-permute-start.9 = (bf16[512,256]{1,0:T(8,128)(2,1)}, bf16[512,256]{1,0:T(8,128)(2,1)}, u32[]{:S(2)}, u32[]{:S(2)}) collective-permute-start(bf16[512,256]{1,0:T(8,128)(2,1)} %get-tuple-element.33), channel_id=1, source_target_pairs={{0,4},{4,8},{8,12},{12,16},{16,20},{20,24},{24,28},{1,5},{5,9},{9,... | collective-permute-start | bytes 786440 | tf_op jit(solution)/shard_map/ppermute | solution.py:21
  89.6 15.5 %all-to-all-start.1 = ((bf16[8,64,128]{2,1,0:T(8,128)(2,1)}), bf16[8,64,128]{2,1,0:T(8,128)(2,1)S(1)}, u32[]{:S(2)}, u32[]{:S(2)}) async-start(bf16[8,64,128]{2,1,0:T(8,128)(2,1)} %running_sums.1), calls=%async_computation.1 | async-start | bytes 262144 | tf_op jit(solution)/shard_map/all_to_all | solution.py:631
  92.9 1.9 %copy-start.7 = (bf16[1,1024,1536]{2,1,0:T(8,128)(2,1)S(1)}, bf16[1,1024,1536]{2,1,0:T(8,128)(2,1)}, u32[]{:S(2)}) copy-start(bf16[1,1024,1536]{2,1,0:T(8,128)(2,1)} %param.8) | copy-start | bytes 9437188
  97.9 3.0 %copy-start.21 = (bf16[1024,384]{1,0:T(8,128)(2,1)S(1)}, bf16[1024,384]{1,0:T(8,128)(2,1)}, u32[]{:S(2)}) copy-start(bf16[1024,384]{1,0:T(8,128)(2,1)} %copy-done.20) | copy-start | bytes 2359300
  113.9 12.9 %collective-permute-start.10 = (bf16[256,512]{1,0:T(8,128)(2,1)S(1)}, bf16[256,512]{1,0:T(8,128)(2,1)S(1)}, u32[]{:S(2)}, u32[]{:S(2)}) collective-permute-start(bf16[256,512]{1,0:T(8,128)(2,1)S(1)} %finish2.1), channel_id=1, source_target_pairs={{0,2},{1,3},{2,0},{3,1},{4,6},{5,7},{6,4},{7,5},{8,10},{9,11},{10,... | collective-permute-start | bytes 786440 | tf_op jit(solution)/shard_map/ppermute | solution.py:790
  115.2 22.9 %collective-permute-start.11 = (bf16[256,512]{1,0:T(8,128)(2,1)S(1)}, bf16[256,512]{1,0:T(8,128)(2,1)S(1)}, u32[]{:S(2)}, u32[]{:S(2)}) collective-permute-start(bf16[256,512]{1,0:T(8,128)(2,1)S(1)} %finish1.1), channel_id=1, source_target_pairs={{0,1},{1,2},{2,3},{3,0},{4,5},{5,6},{6,7},{7,4},{8,9},{9,10},{10,1... | collective-permute-start | bytes 786440 | tf_op jit(solution)/shard_map/ppermute | solution.py:790
  115.9 23.3 %collective-permute-start.12 = (bf16[256,512]{1,0:T(8,128)(2,1)S(1)}, bf16[256,512]{1,0:T(8,128)(2,1)S(1)}, u32[]{:S(2)}, u32[]{:S(2)}) collective-permute-start(bf16[256,512]{1,0:T(8,128)(2,1)S(1)} %finish3.1), channel_id=1, source_target_pairs={{0,3},{1,0},{2,1},{3,2},{4,7},{5,4},{6,5},{7,6},{8,11},{9,8},{10,9... | collective-permute-start | bytes 786440 | tf_op jit(solution)/shard_map/ppermute | solution.py:790
  (30 other events, 32.8 us)
Sparse Core Ops, SparseCore 0:
  15.1 27.5 all-gather.2

commit v3 on v2

--- a/solution.py
+++ b/solution.py
@@ -156,7 +156,8 @@
 ROUTE_ROWS = 16
 
 
-def kernel_call(body, name, out_shape, flops, moved, grant=16, **kwargs):
+def kernel_call(body, name, out_shape, flops, moved, **kwargs):
+    grant = 60 if "in_specs" in kwargs else 8
     return pl.pallas_call(
         body,
         name=name,
@@ -691,7 +692,6 @@
         ),
         2 * total * depth * 3 * width,
         10 << 20,
-        grant=24,
         in_specs=[HBM] * early + [WHOLE, WHOLE, HBM],
         out_specs=[HBM, HBM, WHOLE, WHOLE],
         scratch_shapes=[

time: 148 us -> 145 us (0.980)
  local copies, waits for them, and re-layouts: 31 us -> 4.14 us
  Pallas kernels: 27.1 us -> 50.2 us
  starting transfers between devices: 35.8 us -> 40.5 us
  waiting for transfers between devices: 39.1 us -> 35.7 us
    unnamed x76 -> x24, local copies, waits for them, and re-layouts: 31 us -> 4.14 us
    pallas_call x4, Pallas kernels: 3.42 us -> 13.3 us  [finish(): kernel_call(functools.partial(finish_body, n_mem, shift), f'finish{shift}...]
    ppermute x3, starting transfers between devices: 3.09 us -> 7.7 us  [dense_shards(): parts.append(lax.ppermute(finish(shift), 'mem', pairs))]
    pallas_call x1, Pallas kernels: 13.6 us -> 17.5 us  [dense_shards(): kernel_call(functools.partial(early_body, n_mem, hops), 'early_rows', (sh...]
    ppermute x3, waiting for transfers between devices: 21.3 us -> 17.7 us  [dense_shards(): parts.append(lax.ppermute(finish(shift), 'mem', pairs))]
    pallas_call x1, Pallas kernels: 2.34 us -> 5.84 us  [dense_shards(): kernel_call(functools.partial(window_project_body, n_mem), 'window_projec...]
    pallas_call x1, Pallas kernels: 0.14 us -> 2.27 us  [dense_shards(): kernel_call(pack_body, 'pack', [shape(cut + ROUTE_ROWS, 3 * HDIM)] * n_me...]
    pallas_call x1, Pallas kernels: 3.32 us -> 5.17 us  [dense_shards(): kernel_call(functools.partial(window_attend_body, count), 'window_attend'...]
  transfers between devices with their start and end apart: 16 -> 16, of which waited for: 7 -> 7; matrix products, arithmetic and copies ran while one was open for 0% -> 0% of each run, Pallas kernels for 16% -> 25%
where the time goes in v3:
time: 145 us; the launch traced here: 144 us
  Pallas kernels  50.2 us (35%)
  starting transfers between devices  40.5 us (28%)
  waiting for transfers between devices  35.7 us (25%)
  between operations  13.7 us (9%)
  local copies, waits for them, and re-layouts  4.14 us (3%)
    ppermute x3, waiting for transfers between devices, dense_shards(): parts.append(lax.ppermute(finish(shift), 'mem', pairs))  17.7 us
    pallas_call x1, Pallas kernels, dense_shards(): kernel_call(functools.partial(early_body, n_mem, hops), 'early_rows', (sh...  17.5 us
    ppermute x3, waiting for transfers between devices, dense_shards(): above.append(lax.ppermute(above[-1], 'mem', down))  15.8 us
    pallas_call x4, Pallas kernels, finish(): kernel_call(functools.partial(finish_body, n_mem, shift), f'finish{shift}...  13.3 us
    ppermute x3, starting transfers between devices, dense_shards(): above.append(lax.ppermute(above[-1], 'mem', down))  10.5 us
    ppermute x3, starting transfers between devices, dense_shards(): parts.append(lax.ppermute(finish(shift), 'mem', pairs))  7.7 us
    all_to_all x1, starting transfers between devices, exclusive_prefix(): lax.all_to_all(pieces, 'ctx', split_axis=0, concat_axis=0, tiled=True)  7.11 us
    pallas_call x1, Pallas kernels, dense_shards(): kernel_call(functools.partial(window_project_body, n_mem), 'window_projec...  5.84 us
  transfers between devices with their start and end apart: 16, of which 7 were waited for; matrix products, arithmetic and copies ran while one was open for 0% of the time, Pallas kernels for 25%

profile of v3, /device:TPU:9, one launch (start us, length us, event | category | flops | bytes accessed | tf_op | source)
XLA Modules:
  0.0 144.2 jit_solution(3249785752313751940)
XLA Ops:
  6.5 2.3 %pack.1 = (bf16[48,384]{1,0:T(8,128)(2,1)}, bf16[48,384]{1,0:T(8,128)(2,1)}, bf16[48,384]{1,0:T(8,128)(2,1)}, bf16[48,384]{1,0:T(8,128)(2,1)}) custom-call(bf16[256,1536]{1,0:T(8,128)(2,1)} %weight_ref.1, s32[2,256]{1,0:T(2,128)} %bitcast.17), custom_call_target="tpu_custom_call" | custom-call | flops 1048576 | bytes 1048576 | tf_op jit(solution)/shard_map/pack/pallas_call | solution.py:658
  16.3 3.4 %collective-permute-start.1 = (bf16[256,1024]{1,0:T(8,128)(2,1)}, bf16[256,1024]{1,0:T(8,128)(2,1)S(1)}, u32[]{:S(2)}, u32[]{:S(2)}) collective-permute-start(bf16[256,1024]{1,0:T(8,128)(2,1)} %refs_0_.3), channel_id=1, source_target_pairs={{3,2},{2,1},{1,0},{7,6},{6,5},{5,4},{11,10},{10,9},{9,8},{15,14},{... | collective-permute-start | bytes 1572872 | tf_op jit(solution)/shard_map/ppermute | solution.py:653
  19.7 1.9 %collective-permute-start = (bf16[256,1024]{1,0:T(8,128)(2,1)}, bf16[256,1024]{1,0:T(8,128)(2,1)S(1)}, u32[]{:S(2)}, u32[]{:S(2)}) collective-permute-start(bf16[256,1024]{1,0:T(8,128)(2,1)} %refs_0_.3), channel_id=1, source_target_pairs={{0,1},{1,2},{2,3},{4,5},{5,6},{6,7},{8,9},{9,10},{10,11},{12,13},{... | collective-permute-start | bytes 1572872 | tf_op jit(solution)/shard_map/ppermute | solution.py:652
  21.7 8.5 %collective-permute-done.1.refs_2_ = bf16[256,1024]{1,0:T(8,128)(2,1)S(1)} collective-permute-done((bf16[256,1024]{1,0:T(8,128)(2,1)}, bf16[256,1024]{1,0:T(8,128)(2,1)S(1)}, u32[]{:S(2)}, u32[]{:S(2)}) %collective-permute-start.1) | collective-permute-done | bytes 524320 | tf_op jit(solution)/shard_map/ppermute | solution.py:653
  30.1 3.5 %collective-permute-start.3 = (bf16[256,1024]{1,0:T(8,128)(2,1)S(1)}, bf16[256,1024]{1,0:T(8,128)(2,1)S(1)}, u32[]{:S(2)}, u32[]{:S(2)}) collective-permute-start(bf16[256,1024]{1,0:T(8,128)(2,1)S(1)} %collective-permute-done.1.refs_2_), channel_id=1, source_target_pairs={{2,1},{1,0},{6,5},{5,4},{10,9},{9,8},{14,13},{13,12},{18,17},{17,1... | collective-permute-start | bytes 1572872 | tf_op jit(solution)/shard_map/ppermute | solution.py:653
  33.7 1.8 %collective-permute-start.2 = (bf16[256,1024]{1,0:T(8,128)(2,1)S(1)}, bf16[256,1024]{1,0:T(8,128)(2,1)S(1)}, u32[]{:S(2)}, u32[]{:S(2)}) collective-permute-start(bf16[256,1024]{1,0:T(8,128)(2,1)S(1)} %collective-permute-done.refs_1_), channel_id=1, source_target_pairs={{1,2},{2,3},{5,6},{6,7},{9,10},{10,11},{13,14},{14,15},{17,18},{18... | collective-permute-start | bytes 1572872 | tf_op jit(solution)/shard_map/ppermute | solution.py:652
  35.5 7.3 %collective-permute-done.3.refs_4_ = bf16[256,1024]{1,0:T(8,128)(2,1)S(1)} collective-permute-done((bf16[256,1024]{1,0:T(8,128)(2,1)S(1)}, bf16[256,1024]{1,0:T(8,128)(2,1)S(1)}, u32[]{:S(2)}, u32[]{:S(2)}) %collective-permute-start.3) | collective-permute-done | bytes 524320 | tf_op jit(solution)/shard_map/ppermute | solution.py:653
  42.8 3.6 %collective-permute-start.8 = (bf16[256,1024]{1,0:T(8,128)(2,1)S(1)}, bf16[256,1024]{1,0:T(8,128)(2,1)S(1)}, u32[]{:S(2)}, u32[]{:S(2)}) collective-permute-start(bf16[256,1024]{1,0:T(8,128)(2,1)S(1)} %collective-permute-done.3.refs_4_), channel_id=1, source_target_pairs={{1,0},{5,4},{9,8},{13,12},{17,16},{21,20},{25,24},{29,28}} | collective-permute-start | bytes 1572872 | tf_op jit(solution)/shard_map/ppermute | solution.py:653
  47.2 17.5 %early_rows.1 = (bf16[1024,1536]{1,0:T(8,128)(2,1)}, f32[1024,512]{1,0:T(8,128)}, f32[1024,128]{1,0:T(8,128)}, f32[512,128]{1,0:T(8,128)}) custom-call(bf16[256,1024]{1,0:T(8,128)(2,1)} %refs_0_.3, bf16[256,1024]{1,0:T(8,128)(2,1)} %copy-done.6, bf16[256,1024]{1,0:T(8,128)(2,1)} %copy-done.5, bf16[256,1024]{1,0:T(8,128)(2,1)} %copy-done.8, ...), custom_call_target="tpu_custom_call" | custom-call | flops 3221225472 | bytes 10485760 | tf_op jit(solution)/shard_map/early_rows/pallas_call | solution.py:684
  65.7 2.0 %last_keys.1 = (bf16[256,1024]{1,0:T(8,128)(2,1)}, f32[512,128]{1,0:T(8,128)}) custom-call(bf16[256,1024]{1,0:T(8,128)(2,1)} %copy-done.3, bf16[256,1024]{1,0:T(8,128)(2,1)} %copy-done.2, bf16[4,48,384]{2,1,0:T(8,128)(2,1)} %arrange.1.refs_5_.packed_ref, bf16[1024,1536]{1,0:T(8,128)(2,1)} %bitcast.7, f32[512,128]{1,0:T(8,128)} %get-tuple-element.27.before_ref), custom_call_target="tpu_custom_call" | custom-call | flops 536870912 | bytes 3145728 | tf_op jit(solution)/shard_map/last_keys/pallas_call | solution.py:707
  67.7 7.1 %all-to-all-start = ((f32[8,64,128]{2,1,0:T(8,128)}), f32[8,64,128]{2,1,0:T(8,128)S(1)}, u32[]{:S(2)}, u32[]{:S(2)}) async-start(f32[8,64,128]{2,1,0:T(8,128)} %bitcast.14), calls=%async_computation | async-start | bytes 524288 | tf_op jit(solution)/shard_map/all_to_all | solution.py:624
  74.8 5.8 %window_project.1 = (bf16[1024,384]{1,0:T(8,128)(2,1)}, bf16[512,256]{1,0:T(8,128)(2,1)}) custom-call(bf16[256,1024]{1,0:T(8,128)(2,1)} %refs_0_.3, bf16[256,1024]{1,0:T(8,128)(2,1)} %copy-done.6, bf16[256,1024]{1,0:T(8,128)(2,1)} %copy-done.5, bf16[256,1024]{1,0:T(8,128)(2,1)} %copy-done.8, bf16[256,1024]{1,0:T(8,128)(2,1)} %copy-done.7, ...), custom_call_target="tpu_custom_call" | custom-call | flops 805306368 | bytes 5242880 | tf_op jit(solution)/shard_map/window_project/pallas_call | solution.py:722
  80.7 3.5 %collective-permute-start.9 = (bf16[512,256]{1,0:T(8,128)(2,1)}, bf16[512,256]{1,0:T(8,128)(2,1)S(1)}, u32[]{:S(2)}, u32[]{:S(2)}) collective-permute-start(bf16[512,256]{1,0:T(8,128)(2,1)} %get-tuple-element.33), channel_id=1, source_target_pairs={{0,4},{4,8},{8,12},{12,16},{16,20},{20,24},{24,28},{1,5},{5,9},{9,... | collective-permute-start | bytes 786440 | tf_op jit(solution)/shard_map/ppermute | solution.py:21
  84.9 3.3 %all-to-all-start.1 = ((bf16[8,64,128]{2,1,0:T(8,128)(2,1)}), bf16[8,64,128]{2,1,0:T(8,128)(2,1)S(1)}, u32[]{:S(2)}, u32[]{:S(2)}) async-start(bf16[8,64,128]{2,1,0:T(8,128)(2,1)} %running_sums.1), calls=%async_computation.1 | async-start | bytes 262144 | tf_op jit(solution)/shard_map/all_to_all | solution.py:632
  88.2 1.9 %last_queries.1 = (bf16[256,512]{1,0:T(8,128)(2,1)}, f32[256,128]{1,0:T(8,128)}, f32[1024,512]{1,0:T(8,128)}) custom-call(bf16[256,1024]{1,0:T(8,128)(2,1)} %copy-done.3, bf16[256,1024]{1,0:T(8,128)(2,1)} %copy-done.2, bf16[4,48,384]{2,1,0:T(8,128)(2,1)} %arrange.1.refs_5_.packed_ref, bf16[4,1024]{1,0:T(4,128)(2,1)} %bitcast.16, bf16[1024,1536]{1,0:T(8,128)(2,1)} %bitcast.8, ...), custom_call_target="tpu_custom_call" | custom-call | flops 1073741824 | bytes 8388608 | tf_op jit(solution)/shard_map/last_queries/pallas_call | solution.py:739
  90.9 5.2 %window_attend.1.refs_6_ = f32[1024,128]{1,0:T(8,128)} custom-call(bf16[1024,384]{1,0:T(8,128)(2,1)} %get-tuple-element.32.win_ref, bf16[512,256]{1,0:T(8,128)(2,1)} %copy-done.11), custom_call_target="tpu_custom_call" | custom-call | flops 402653184 | bytes 3145728 | tf_op jit(solution)/shard_map/window_attend/pallas_call | solution.py:755
  96.7 3.3 %finish3.1 = bf16[256,512]{1,0:T(8,128)(2,1)} custom-call(bf16[1024,1536]{1,0:T(8,128)(2,1)} %get-tuple-element.24.proj_ref.refs_0_, f32[1024,512]{1,0:T(8,128)} %get-tuple-element.25.refs_1_, f32[1024,128]{1,0:T(8,128)} %get-tuple-element.26.refs_2_, bf16[256,512]{1,0:T(8,128)(2,1)} %get-tuple-element.29.refs_3_, f32[256,128]{1,0:T(8,128)} %get-tuple-element.30.refs_4_, ...), custom_call_target="tpu_custom_call" | custom-call | flops 33554432 | bytes 2097152 | tf_op jit(solution)/shard_map/finish3/pallas_call | solution.py:770
  100.0 3.3 %finish1.1 = bf16[256,512]{1,0:T(8,128)(2,1)} custom-call(bf16[1024,1536]{1,0:T(8,128)(2,1)} %get-tuple-element.24.proj_ref.refs_0_, f32[1024,512]{1,0:T(8,128)} %get-tuple-element.25.refs_1_, f32[1024,128]{1,0:T(8,128)} %get-tuple-element.26.refs_2_, bf16[256,512]{1,0:T(8,128)(2,1)} %get-tuple-element.29.refs_3_, f32[256,128]{1,0:T(8,128)} %get-tuple-element.30.refs_4_, ...), custom_call_target="tpu_custom_call" | custom-call | flops 33554432 | bytes 2097152 | tf_op jit(solution)/shard_map/finish1/pallas_call | solution.py:770
  103.3 3.3 %finish2.1 = bf16[256,512]{1,0:T(8,128)(2,1)} custom-call(bf16[1024,1536]{1,0:T(8,128)(2,1)} %get-tuple-element.24.proj_ref.refs_0_, f32[1024,512]{1,0:T(8,128)} %get-tuple-element.25.refs_1_, f32[1024,128]{1,0:T(8,128)} %get-tuple-element.26.refs_2_, bf16[256,512]{1,0:T(8,128)(2,1)} %get-tuple-element.29.refs_3_, f32[256,128]{1,0:T(8,128)} %get-tuple-element.30.refs_4_, ...), custom_call_target="tpu_custom_call" | custom-call | flops 33554432 | bytes 2097152 | tf_op jit(solution)/shard_map/finish2/pallas_call | solution.py:770
  106.7 6.2 %collective-permute-start.10 = (bf16[256,512]{1,0:T(8,128)(2,1)}, bf16[256,512]{1,0:T(8,128)(2,1)S(1)}, u32[]{:S(2)}, u32[]{:S(2)}) collective-permute-start(bf16[256,512]{1,0:T(8,128)(2,1)} %finish2.1), channel_id=1, source_target_pairs={{0,2},{1,3},{2,0},{3,1},{4,6},{5,7},{6,4},{7,5},{8,10},{9,11},{10,... | collective-permute-start | bytes 786440 | tf_op jit(solution)/shard_map/ppermute | solution.py:790
  114.4 3.4 %finish0.1.refs_0_ = f32[256,512]{1,0:T(8,128)} custom-call(bf16[1024,1536]{1,0:T(8,128)(2,1)} %get-tuple-element.24.proj_ref.refs_0_, f32[1024,512]{1,0:T(8,128)} %get-tuple-element.25.refs_1_, f32[1024,128]{1,0:T(8,128)} %get-tuple-element.26.refs_2_, bf16[256,512]{1,0:T(8,128)(2,1)} %get-tuple-element.29.refs_3_, f32[256,128]{1,0:T(8,128)} %get-tuple-element.30.refs_4_, ...), custom_call_target="tpu_custom_call" | custom-call | flops 33554432 | bytes 2097152 | tf_op jit(solution)/shard_map/finish0/pallas_call | solution.py:770
  117.8 4.2 %collective-permute-done.10.refs_1_ = bf16[256,512]{1,0:T(8,128)(2,1)S(1)} collective-permute-done((bf16[256,512]{1,0:T(8,128)(2,1)}, bf16[256,512]{1,0:T(8,128)(2,1)S(1)}, u32[]{:S(2)}, u32[]{:S(2)}) %collective-permute-start.10) | collective-permute-done | bytes 262176 | tf_op jit(solution)/shard_map/ppermute | solution.py:790
  122.0 11.0 %collective-permute-done.11.refs_2_ = bf16[256,512]{1,0:T(8,128)(2,1)S(1)} collective-permute-done((bf16[256,512]{1,0:T(8,128)(2,1)S(1)}, bf16[256,512]{1,0:T(8,128)(2,1)S(1)}, u32[]{:S(2)}, u32[]{:S(2)}) %collective-permute-start.11) | collective-permute-done | bytes 262176 | tf_op jit(solution)/shard_map/ppermute | solution.py:790
  133.0 2.5 %collective-permute-done.12.refs_3_ = bf16[256,512]{1,0:T(8,128)(2,1)S(1)} collective-permute-done((bf16[256,512]{1,0:T(8,128)(2,1)S(1)}, bf16[256,512]{1,0:T(8,128)(2,1)S(1)}, u32[]{:S(2)}, u32[]{:S(2)}) %collective-permute-start.12) | collective-permute-done | bytes 262176 | tf_op jit(solution)/shard_map/ppermute | solution.py:790
  (46 shorter events, 14.6 us)
Async XLA Ops:
  6.5 68.3 %all-gather.3.cloned.1.call-start = ((), (), s32[]{:S(2)}) async-start(), calls=%async_computation.2 | async-start | bytes 1327104 | tf_op jit(solution)/shard_map/all_gather | solution.py:678
  8.8 3.8 %collective-permute-start.4 = (bf16[48,384]{1,0:T(8,128)(2,1)}, bf16[48,384]{1,0:T(8,128)(2,1)S(1)}, u32[]{:S(2)}, u32[]{:S(2)}) collective-permute-start(bf16[48,384]{1,0:T(8,128)(2,1)} %get-tuple-element.21), channel_id=1, source_target_pairs={{0,1},{1,2},{2,3},{3,0},{4,5},{5,6},{6,7},{7,4},{8,9},{9,10},{10,1... | collective-permute-start | bytes 110600 | tf_op jit(solution)/shard_map/ppermute | solution.py:668
  10.2 3.9 %collective-permute-start.5 = (bf16[48,384]{1,0:T(8,128)(2,1)}, bf16[48,384]{1,0:T(8,128)(2,1)S(1)}, u32[]{:S(2)}, u32[]{:S(2)}) collective-permute-start(bf16[48,384]{1,0:T(8,128)(2,1)} %get-tuple-element.22), channel_id=1, source_target_pairs={{0,2},{1,3},{2,0},{3,1},{4,6},{5,7},{6,4},{7,5},{8,10},{9,11},{10,... | collective-permute-start | bytes 110600 | tf_op jit(solution)/shard_map/ppermute | solution.py:668
  11.3 3.6 %collective-permute-start.6 = (bf16[48,384]{1,0:T(8,128)(2,1)}, bf16[48,384]{1,0:T(8,128)(2,1)S(1)}, u32[]{:S(2)}, u32[]{:S(2)}) collective-permute-start(bf16[48,384]{1,0:T(8,128)(2,1)} %get-tuple-element.23), channel_id=1, source_target_pairs={{0,3},{1,0},{2,1},{3,2},{4,7},{5,4},{6,5},{7,6},{8,11},{9,8},{10,9... | collective-permute-start | bytes 110600 | tf_op jit(solution)/shard_map/ppermute | solution.py:668
  16.3 13.8 %collective-permute-start.1 = (bf16[256,1024]{1,0:T(8,128)(2,1)}, bf16[256,1024]{1,0:T(8,128)(2,1)S(1)}, u32[]{:S(2)}, u32[]{:S(2)}) collective-permute-start(bf16[256,1024]{1,0:T(8,128)(2,1)} %refs_0_.3), channel_id=1, source_target_pairs={{3,2},{2,1},{1,0},{7,6},{6,5},{5,4},{11,10},{10,9},{9,8},{15,14},{... | collective-permute-start | bytes 1572872 | tf_op jit(solution)/shard_map/ppermute | solution.py:653
  19.7 13.9 %collective-permute-start = (bf16[256,1024]{1,0:T(8,128)(2,1)}, bf16[256,1024]{1,0:T(8,128)(2,1)S(1)}, u32[]{:S(2)}, u32[]{:S(2)}) collective-permute-start(bf16[256,1024]{1,0:T(8,128)(2,1)} %refs_0_.3), channel_id=1, source_target_pairs={{0,1},{1,2},{2,3},{4,5},{5,6},{6,7},{8,9},{9,10},{10,11},{12,13},{... | collective-permute-start | bytes 1572872 | tf_op jit(solution)/shard_map/ppermute | solution.py:652
  30.1 17.0 %copy-start.5 = (bf16[256,1024]{1,0:T(8,128)(2,1)}, bf16[256,1024]{1,0:T(8,128)(2,1)S(1)}, u32[]{:S(2)}) copy-start(bf16[256,1024]{1,0:T(8,128)(2,1)S(1)} %collective-permute-done.1.refs_2_) | copy-start | bytes 1572868
  30.1 12.7 %collective-permute-start.3 = (bf16[256,1024]{1,0:T(8,128)(2,1)S(1)}, bf16[256,1024]{1,0:T(8,128)(2,1)S(1)}, u32[]{:S(2)}, u32[]{:S(2)}) collective-permute-start(bf16[256,1024]{1,0:T(8,128)(2,1)S(1)} %collective-permute-done.1.refs_2_), channel_id=1, source_target_pairs={{2,1},{1,0},{6,5},{5,4},{10,9},{9,8},{14,13},{13,12},{18,17},{17,1... | collective-permute-start | bytes 1572872 | tf_op jit(solution)/shard_map/ppermute | solution.py:653
  33.6 13.5 %copy-start.6 = (bf16[256,1024]{1,0:T(8,128)(2,1)}, bf16[256,1024]{1,0:T(8,128)(2,1)S(1)}, u32[]{:S(2)}) copy-start(bf16[256,1024]{1,0:T(8,128)(2,1)S(1)} %collective-permute-done.refs_1_) | copy-start | bytes 1572868
  33.7 12.8 %collective-permute-start.2 = (bf16[256,1024]{1,0:T(8,128)(2,1)S(1)}, bf16[256,1024]{1,0:T(8,128)(2,1)S(1)}, u32[]{:S(2)}, u32[]{:S(2)}) collective-permute-start(bf16[256,1024]{1,0:T(8,128)(2,1)S(1)} %collective-permute-done.refs_1_), channel_id=1, source_target_pairs={{1,2},{2,3},{5,6},{6,7},{9,10},{10,11},{13,14},{14,15},{17,18},{18... | collective-permute-start | bytes 1572872 | tf_op jit(solution)/shard_map/ppermute | solution.py:652
  42.8 4.4 %copy-start.7 = (bf16[256,1024]{1,0:T(8,128)(2,1)}, bf16[256,1024]{1,0:T(8,128)(2,1)S(1)}, u32[]{:S(2)}) copy-start(bf16[256,1024]{1,0:T(8,128)(2,1)S(1)} %collective-permute-done.3.refs_4_) | copy-start | bytes 1572868
  42.8 22.0 %collective-permute-start.8 = (bf16[256,1024]{1,0:T(8,128)(2,1)S(1)}, bf16[256,1024]{1,0:T(8,128)(2,1)S(1)}, u32[]{:S(2)}, u32[]{:S(2)}) collective-permute-start(bf16[256,1024]{1,0:T(8,128)(2,1)S(1)} %collective-permute-done.3.refs_4_), channel_id=1, source_target_pairs={{1,0},{5,4},{9,8},{13,12},{17,16},{21,20},{25,24},{29,28}} | collective-permute-start | bytes 1572872 | tf_op jit(solution)/shard_map/ppermute | solution.py:653
  46.4 0.8 copy-start.8
  46.5 18.3 %collective-permute-start.7 = (bf16[256,1024]{1,0:T(8,128)(2,1)S(1)}, bf16[256,1024]{1,0:T(8,128)(2,1)S(1)}, u32[]{:S(2)}, u32[]{:S(2)}) collective-permute-start(bf16[256,1024]{1,0:T(8,128)(2,1)S(1)} %collective-permute-done.2.refs_3_), channel_id=1, source_target_pairs={{2,3},{6,7},{10,11},{14,15},{18,19},{22,23},{26,27},{30,31}} | collective-permute-start | bytes 1572872 | tf_op jit(solution)/shard_map/ppermute | solution.py:652
  64.8 0.9 copy-start.3
  67.7 16.5 %all-to-all-start = ((f32[8,64,128]{2,1,0:T(8,128)}), f32[8,64,128]{2,1,0:T(8,128)S(1)}, u32[]{:S(2)}, u32[]{:S(2)}) async-start(f32[8,64,128]{2,1,0:T(8,128)} %bitcast.14), calls=%async_computation | async-start | bytes 524288 | tf_op jit(solution)/shard_map/all_to_all | solution.py:624
  80.7 9.5 %collective-permute-start.9 = (bf16[512,256]{1,0:T(8,128)(2,1)}, bf16[512,256]{1,0:T(8,128)(2,1)S(1)}, u32[]{:S(2)}, u32[]{:S(2)}) collective-permute-start(bf16[512,256]{1,0:T(8,128)(2,1)} %get-tuple-element.33), channel_id=1, source_target_pairs={{0,4},{4,8},{8,12},{12,16},{16,20},{20,24},{24,28},{1,5},{5,9},{9,... | collective-permute-start | bytes 786440 | tf_op jit(solution)/shard_map/ppermute | solution.py:21
  84.9 11.2 %all-to-all-start.1 = ((bf16[8,64,128]{2,1,0:T(8,128)(2,1)}), bf16[8,64,128]{2,1,0:T(8,128)(2,1)S(1)}, u32[]{:S(2)}, u32[]{:S(2)}) async-start(bf16[8,64,128]{2,1,0:T(8,128)(2,1)} %running_sums.1), calls=%async_computation.1 | async-start | bytes 262144 | tf_op jit(solution)/shard_map/all_to_all | solution.py:632
  103.3 9.6 %copy-start.10 = (bf16[256,512]{1,0:T(8,128)(2,1)S(1)}, bf16[256,512]{1,0:T(8,128)(2,1)}, u32[]{:S(2)}) copy-start(bf16[256,512]{1,0:T(8,128)(2,1)} %finish1.1) | copy-start | bytes 786436
  103.3 9.6 %copy-start.9 = (bf16[256,512]{1,0:T(8,128)(2,1)S(1)}, bf16[256,512]{1,0:T(8,128)(2,1)}, u32[]{:S(2)}) copy-start(bf16[256,512]{1,0:T(8,128)(2,1)} %finish3.1) | copy-start | bytes 786436
  106.7 15.3 %collective-permute-start.10 = (bf16[256,512]{1,0:T(8,128)(2,1)}, bf16[256,512]{1,0:T(8,128)(2,1)S(1)}, u32[]{:S(2)}, u32[]{:S(2)}) collective-permute-start(bf16[256,512]{1,0:T(8,128)(2,1)} %finish2.1), channel_id=1, source_target_pairs={{0,2},{1,3},{2,0},{3,1},{4,6},{5,7},{6,4},{7,5},{8,10},{9,11},{10,... | collective-permute-start | bytes 786440 | tf_op jit(solution)/shard_map/ppermute | solution.py:790
  112.9 20.1 %collective-permute-start.11 = (bf16[256,512]{1,0:T(8,128)(2,1)S(1)}, bf16[256,512]{1,0:T(8,128)(2,1)S(1)}, u32[]{:S(2)}, u32[]{:S(2)}) collective-permute-start(bf16[256,512]{1,0:T(8,128)(2,1)S(1)} %copy-done.10), channel_id=1, source_target_pairs={{0,1},{1,2},{2,3},{3,0},{4,5},{5,6},{6,7},{7,4},{8,9},{9,10},{10,1... | collective-permute-start | bytes 786440 | tf_op jit(solution)/shard_map/ppermute | solution.py:790
  112.9 22.6 %collective-permute-start.12 = (bf16[256,512]{1,0:T(8,128)(2,1)S(1)}, bf16[256,512]{1,0:T(8,128)(2,1)S(1)}, u32[]{:S(2)}, u32[]{:S(2)}) collective-permute-start(bf16[256,512]{1,0:T(8,128)(2,1)S(1)} %copy-done.9), channel_id=1, source_target_pairs={{0,3},{1,0},{2,1},{3,2},{4,7},{5,4},{6,5},{7,6},{8,11},{9,8},{10,9... | collective-permute-start | bytes 786440 | tf_op jit(solution)/shard_map/ppermute | solution.py:790
  135.5 1.0 copy-start
  (4 other events, 2.9 us)
Sparse Core Ops, SparseCore 0:
  16.4 27.5 all-gather.2

commit v4 on v3

--- a/solution.py
+++ b/solution.py
@@ -156,8 +156,7 @@
 ROUTE_ROWS = 16
 
 
-def kernel_call(body, name, out_shape, flops, moved, **kwargs):
-    grant = 60 if "in_specs" in kwargs else 8
+def kernel_call(body, name, out_shape, flops, moved, grant=12, **kwargs):
     return pl.pallas_call(
         body,
         name=name,
@@ -178,7 +177,7 @@
     return copy
 
 
-def pack_body(weight_ref, routes_ref, *refs):
+def pack_body(weight_ref, routes_ref, _, *refs):
     outs, (rows_ref, sem) = refs[:-2], refs[-2:]
     cut, _ = rows_ref.shape
     width = HEADS * HDIM
@@ -264,72 +263,53 @@
 
 def slot_group(slot):
     hop = (slot + 1) // 2
-    return lax.axis_index("mem") + jnp.where(lax.rem(slot, 2) == 1, -hop, hop)
+    return lax.axis_index("mem") + (-hop if slot % 2 else hop)
+
+
+def in_line(group, n_mem):
+    return (group >= 0) & (group < n_mem)
+
+
+def head_columns(head, part=0):
+    return slice((part * HEADS + head) * HDIM, (part * HEADS + head + 1) * HDIM)
 
 
 def early_body(n_mem, hops, *refs):
     slots = 1 + 2 * hops
     sources = refs[:slots]
     packed_ref, router_ref, weight_ref = refs[slots : slots + 3]
-    proj_ref, intra_ref, coef_ref, state_ref = refs[slots + 3 : slots + 7]
-    rows_ref, held_ref, made_ref, sum_ref, sems, weight_sem, out_sems = refs[slots + 7 :]
+    proj_ref, intra_ref, coef_ref, state_ref = refs[slots + 3 :]
     count = sources[0].shape[0]
     width = HEADS * HDIM
-    load = begin(weight_ref, held_ref, weight_sem)
-
-    def here(group):
-        return (group >= 0) & (group < n_mem)
-
-    for slot in range(slots):
-
-        @pl.when(here(slot_group(slot)))
-        def _(slot=slot):
-            begin(sources[slot], rows_ref.at[slot], sems.at[slot])
-
+    mine = lax.axis_index("mem")
     state_ref[...] = jnp.zeros_like(state_ref)
     for slot in range(slots):
-
-        @pl.when(here(slot_group(slot)))
-        def _(slot=slot):
-            pltpu.make_async_copy(sources[slot], rows_ref.at[slot], sems.at[slot]).wait()
-
-    load.wait()
-
-    @pl.loop(0, slots)
-    def _(slot):
         group = slot_group(slot)
 
-        @pl.when(here(group))
-        def _():
+        @pl.when(in_line(group, n_mem))
+        def _(slot=slot, group=group):
             place = rows_of(group, count)
-            tokens = rows_ref[slot]
+            tokens = sources[slot][...]
             first, second, is_first, is_second = members(group, packed_ref, count)
-            projected = jnp.dot(tokens, held_ref[...], preferred_element_type=jnp.float32)
+            projected = jnp.dot(tokens, weight_ref[...], preferred_element_type=jnp.float32)
             projected = jnp.where(is_first | is_second, projected, 0.0).astype(jnp.bfloat16)
-            made_ref[place, :] = projected
+            proj_ref[place, :] = projected
             coef_ref[place, :] = coefficients(
                 tokens, router_ref[...], first, second, is_first, is_second
             )
             for head in range(HEADS):
-                columns = slice(head * HDIM, (head + 1) * HDIM)
-                state_ref[columns, :] += outer_sum(
-                    projected[:, width + head * HDIM : width + (head + 1) * HDIM],
-                    projected[:, 2 * width + head * HDIM : 2 * width + (head + 1) * HDIM],
+                state_ref[head_columns(head), :] += outer_sum(
+                    projected[:, head_columns(head, 1)], projected[:, head_columns(head, 2)]
                 )
-
-    stored = begin(made_ref, proj_ref, out_sems.at[0])
-    mine = lax.axis_index("mem")
 
     def present(group):
         return jnp.abs(mine - group) <= hops
 
     def block(queries_at, keys_at, head, causal=None):
         return pair(
-            made_ref[rows_of(queries_at, count), head * HDIM : (head + 1) * HDIM],
-            made_ref[rows_of(keys_at, count), width + head * HDIM : width + (head + 1) * HDIM],
-            made_ref[
-                rows_of(keys_at, count), 2 * width + head * HDIM : 2 * width + (head + 1) * HDIM
-            ],
+            proj_ref[rows_of(queries_at, count), head_columns(head)],
+            proj_ref[rows_of(keys_at, count), head_columns(head, 1)],
+            proj_ref[rows_of(keys_at, count), head_columns(head, 2)],
             causal,
         )
 
@@ -338,7 +318,7 @@
         @pl.when(present(group))
         def _():
             for head in range(HEADS):
-                sum_ref[rows_of(group, count), head * HDIM : (head + 1) * HDIM] = block(
+                intra_ref[rows_of(group, count), head_columns(head)] = block(
                     group, group, head, triangle(count)
                 )
 
@@ -347,175 +327,106 @@
             @pl.when(present(group) & present(other))
             def _():
                 for head in range(HEADS):
-                    sum_ref[rows_of(group, count), head * HDIM : (head + 1) * HDIM] += block(
+                    intra_ref[rows_of(group, count), head_columns(head)] += block(
                         group, other, head
                     )
 
-    summed = begin(sum_ref, intra_ref, out_sems.at[1])
-    stored.wait()
-    summed.wait()
-
 
 def last_keys_body(n_mem, below_ref, above_ref, packed_ref, weight_ref, before_ref, *refs):
-    kv_ref, state_ref, rows_ref, held_ref, sems = refs
-    count = rows_ref.shape[0]
+    kv_ref, state_ref, sent_ref = refs
+    count = below_ref.shape[0]
     width = HEADS * HDIM
     mine = lax.axis_index("mem")
     state_ref[...] = before_ref[...]
-    load = pltpu.make_async_copy(weight_ref.at[:, pl.ds(width, 2 * width)], held_ref, sems.at[0])
-    from_below = pltpu.make_async_copy(below_ref, rows_ref, sems.at[1])
-    from_above = pltpu.make_async_copy(above_ref, rows_ref, sems.at[2])
-    at_end = (mine == 0) | (mine == n_mem - 1)
-
-    @pl.when(at_end)
-    def _():
-        load.start()
-
-    @pl.when(mine == 0)
-    def _():
-        from_above.start()
-        from_above.wait()
-
-    @pl.when(mine == n_mem - 1)
-    def _():
-        from_below.start()
-        from_below.wait()
-
-    @pl.when(at_end)
+
+    @pl.when((mine == 0) | (mine == n_mem - 1))
     def _():
         _, _, is_first, is_second = members(n_mem - 1 - mine, packed_ref, count)
-        load.wait()
-        projected = jnp.dot(rows_ref[...], held_ref[...], preferred_element_type=jnp.float32)
+        tokens = jnp.where(mine == 0, above_ref[...], below_ref[...])
+        projected = jnp.dot(tokens, weight_ref[:, width:], preferred_element_type=jnp.float32)
         projected = jnp.where(is_first | is_second, projected, 0.0).astype(jnp.bfloat16)
         kv_ref[...] = projected
         for head in range(HEADS):
-            columns = slice(head * HDIM, (head + 1) * HDIM)
-            state_ref[columns, :] += outer_sum(
-                projected[:, columns], projected[:, width + head * HDIM : width + (head + 1) * HDIM]
+            state_ref[head_columns(head), :] += outer_sum(
+                projected[:, head_columns(head)], projected[:, head_columns(head, 1)]
             )
 
+    sent_ref[...] = state_ref[...].astype(jnp.bfloat16)
+
 
 def last_queries_body(n_mem, below_ref, above_ref, packed_ref, router_ref, weight_ref, proj_ref, kv_ref, *refs):
-    query_ref, coef_ref, extra_ref, rows_ref, held_ref, made_ref, sum_ref, sems = refs
-    count = rows_ref.shape[0]
-    total = made_ref.shape[0]
+    query_ref, coef_ref, extra_ref = refs
+    count = below_ref.shape[0]
+    total = extra_ref.shape[0]
     width = HEADS * HDIM
     mine = lax.axis_index("mem")
-    load = pltpu.make_async_copy(weight_ref.at[:, pl.ds(0, width)], held_ref, sems.at[0])
-    from_below = pltpu.make_async_copy(below_ref, rows_ref, sems.at[1])
-    from_above = pltpu.make_async_copy(above_ref, rows_ref, sems.at[2])
-    made = pltpu.make_async_copy(proj_ref, made_ref, sems.at[3])
-    own = slice(0, count)
     last = slice(total - count, total)
-    store_all = pltpu.make_async_copy(sum_ref, extra_ref, sems.at[4])
-    store_last = pltpu.make_async_copy(sum_ref.at[last, :], extra_ref.at[last, :], sems.at[5])
-    at_end = (mine == 0) | (mine == n_mem - 1)
-
-    @pl.when(at_end)
+
+    @pl.when((mine == 0) | (mine == n_mem - 1))
     def _():
-        load.start()
-        made.start()
-
-    @pl.when(mine == 0)
-    def _():
-        from_above.start()
-        from_above.wait()
-
-    @pl.when(mine == n_mem - 1)
-    def _():
-        from_below.start()
-        from_below.wait()
-
-    @pl.when(at_end)
-    def _():
-        tokens = rows_ref[...]
+        tokens = jnp.where(mine == 0, above_ref[...], below_ref[...])
         first, second, is_first, is_second = members(n_mem - 1 - mine, packed_ref, count)
         coef_ref[...] = coefficients(tokens, router_ref[...], first, second, is_first, is_second)
-        load.wait()
-        queries = jnp.dot(tokens, held_ref[...], preferred_element_type=jnp.float32)
+        queries = jnp.dot(tokens, weight_ref[:, 0:width], preferred_element_type=jnp.float32)
         query_ref[...] = jnp.where(is_first | is_second, queries, 0.0).astype(jnp.bfloat16)
-        made.wait()
         causal = triangle(count)
         at = jnp.where(mine == 0, n_mem - 1, 0)
         for head in range(HEADS):
-            columns = slice(head * HDIM, (head + 1) * HDIM)
-            value_columns = slice(width + head * HDIM, width + (head + 1) * HDIM)
-            sum_ref[rows_of(at, count), columns] = pair(
-                query_ref[:, columns], kv_ref[:, columns], kv_ref[:, value_columns], causal
+            extra_ref[rows_of(at, count), head_columns(head)] = pair(
+                query_ref[:, head_columns(head)],
+                kv_ref[:, head_columns(head)],
+                kv_ref[:, head_columns(head, 1)],
+                causal,
             )
 
     @pl.when(mine == 0)
     def _():
         for head in range(HEADS):
-            columns = slice(head * HDIM, (head + 1) * HDIM)
-            key_columns = slice(width + head * HDIM, width + (head + 1) * HDIM)
-            value_columns = slice(2 * width + head * HDIM, 2 * width + (head + 1) * HDIM)
-            sum_ref[last, columns] += pair(
-                query_ref[:, columns],
-                made_ref[0 : total - count, key_columns],
-                made_ref[0 : total - count, value_columns],
+            extra_ref[last, head_columns(head)] += pair(
+                query_ref[:, head_columns(head)],
+                proj_ref[0 : total - count, head_columns(head, 1)],
+                proj_ref[0 : total - count, head_columns(head, 2)],
             )
-        store_last.start()
-        store_last.wait()
 
     @pl.when(mine == n_mem - 1)
     def _():
         for head in range(HEADS):
-            columns = slice(head * HDIM, (head + 1) * HDIM)
-            value_columns = slice(width + head * HDIM, width + (head + 1) * HDIM)
             for group in range(1, n_mem):
                 here = slice(group * count, (group + 1) * count)
-                sum_ref[here, columns] = pair(
-                    made_ref[here, columns], kv_ref[:, columns], kv_ref[:, value_columns]
+                extra_ref[here, head_columns(head)] = pair(
+                    proj_ref[here, head_columns(head)],
+                    kv_ref[:, head_columns(head)],
+                    kv_ref[:, head_columns(head, 1)],
                 )
-        store_all.start()
-        store_all.wait()
-
-
-def window_project_body(n_mem, *refs):
+
+
+def window_project_body(n_mem, n_ctx, *refs):
     slots = 2 * n_mem - 1
-    sources = refs[:slots]
-    pieces_ref, win_ref, tail_ref, rows_ref, full_ref, made_ref, sems, out_sem = refs[slots:]
-    pieces, origins, depth, _ = pieces_ref.shape
+    sources, pieces = refs[:slots], refs[slots : slots + n_ctx]
+    win_ref, tail_ref, full_ref = refs[slots + n_ctx :]
+    origins, depth, _ = pieces[0].shape
     depth = depth - ROUTE_ROWS
     count = sources[0].shape[0]
+    my_ctx = lax.axis_index("ctx")
+    for shift, piece_ref in enumerate(pieces):
+        piece = lax.rem(my_ctx + n_ctx - shift, n_ctx)
+        for origin in range(origins):
+            full_ref[rows_of(origin * n_ctx + piece, depth), :] = piece_ref[origin, 0:depth, :]
+    for slot in range(slots):
+        group = slot_group(slot)
+
+        @pl.when(in_line(group, n_mem))
+        def _(slot=slot, group=group):
+            win_ref[rows_of(group, count), :] = jnp.dot(
+                sources[slot][...], full_ref[...], preferred_element_type=jnp.float32
+            ).astype(jnp.bfloat16)
+
     total = n_mem * count
-
-    def here(slot):
-        group = slot_group(slot)
-        return (group >= 0) & (group < n_mem)
-
-    for slot in range(slots):
-
-        @pl.when(here(slot))
-        def _(slot=slot):
-            place = rows_of(slot_group(slot), count)
-            begin(sources[slot], rows_ref.at[place, :], sems.at[slot])
-
-    for origin in range(origins):
-        for piece in range(pieces):
-            start = (origin * pieces + piece) * depth
-            full_ref[start : start + depth, :] = pieces_ref[piece, origin, 0:depth, :]
-    for slot in range(slots):
-
-        @pl.when(here(slot))
-        def _(slot=slot):
-            place = rows_of(slot_group(slot), count)
-            pltpu.make_async_copy(sources[slot], rows_ref.at[place, :], sems.at[slot]).wait()
-
-    for group in range(n_mem):
-        place = slice(group * count, (group + 1) * count)
-        made_ref[place, :] = jnp.dot(
-            rows_ref[place, :], full_ref[...], preferred_element_type=jnp.float32
-        ).astype(jnp.bfloat16)
-    stored = begin(made_ref, win_ref, out_sem)
-    tail_ref[...] = made_ref[total - WINDOW : total, HDIM:]
-    stored.wait()
-
-
-def window_attend_body(count, win_ref, halo_ref, out_ref, held_ref, keys_ref, sem):
-    load = begin(win_ref, held_ref, sem)
-    total = held_ref.shape[0]
+    tail_ref[...] = win_ref[total - WINDOW : total, HDIM:]
+
+
+def window_attend_body(count, win_ref, halo_ref, out_ref, keys_ref):
+    total = win_ref.shape[0]
     keys_ref[0:WINDOW, :] = halo_ref[...]
     span = count + WINDOW
     row = lax.broadcasted_iota(jnp.int32, (count, span), 0)
@@ -523,14 +434,13 @@
     distance = row + WINDOW - column
     within = (distance >= 0) & (distance < WINDOW)
     missing = jnp.where(lax.axis_index("ctx") == 0, WINDOW, 0)
-    load.wait()
-    keys_ref[WINDOW:, :] = held_ref[:, HDIM:]
+    keys_ref[WINDOW:, :] = win_ref[:, HDIM:]
     for block in range(total // count):
         start = block * count
         keys = keys_ref[start : start + span, :HDIM]
         values = keys_ref[start : start + span, HDIM:]
         scores = lax.dot_general(
-            held_ref[start : start + count, :HDIM],
+            win_ref[start : start + count, :HDIM],
             keys,
             (((1,), (1,)), ((), ())),
             preferred_element_type=jnp.float32,
@@ -545,62 +455,43 @@
         )
 
 
-def finish_body(n_mem, shift, *refs):
+def finish_body(n_mem, shift, bit, *refs):
     proj_ref, intra_ref, coef_ref, last_query_ref, last_coef_ref, extra_ref = refs[:6]
-    window_ref, prefix_ref, out_ref = refs[6:9]
-    query_s, intra_s, extra_s, coef_s, window_s, sems = refs[9:]
+    window_ref, prefix_ref, got_ref, out_ref, query_s, intra_s, coef_s = refs[6:]
     mine = lax.axis_index("mem")
     count, width = out_ref.shape
     group = lax.rem(mine + shift, n_mem)
     here = rows_of(group, count)
     is_last = ((mine == 0) & (group == n_mem - 1)) | ((mine == n_mem - 1) & (group == 0))
-    has_extra = (mine == n_mem - 1) | is_last
-    early = [
-        pltpu.make_async_copy(proj_ref.at[here, pl.ds(0, width)], query_s, sems.at[0]),
-        pltpu.make_async_copy(intra_ref.at[here, :], intra_s, sems.at[1]),
-        pltpu.make_async_copy(coef_ref.at[here, :], coef_s, sems.at[2]),
-    ]
-    late = [
-        pltpu.make_async_copy(last_query_ref, query_s, sems.at[3]),
-        pltpu.make_async_copy(last_coef_ref, coef_s, sems.at[4]),
-    ]
-    extra = pltpu.make_async_copy(extra_ref.at[here, :], extra_s, sems.at[5])
-    window = begin(window_ref.at[here, :], window_s, sems.at[6])
-
-    @pl.when(has_extra)
-    def _():
-        extra.start()
 
     @pl.when(is_last)
     def _():
-        for copy in late:
-            copy.start()
-        intra_s[...] = jnp.zeros_like(intra_s)
-        for copy in late:
-            copy.wait()
+        query_s[...] = last_query_ref[...]
+        coef_s[...] = last_coef_ref[...]
+        intra_s[...] = extra_ref[here, :]
 
     @pl.when(jnp.logical_not(is_last))
     def _():
-        for copy in early:
-            copy.start()
-        for copy in early:
-            copy.wait()
-
-    @pl.when(has_extra)
+        query_s[...] = proj_ref[here, 0:width]
+        coef_s[...] = coef_ref[here, :]
+        intra_s[...] = intra_ref[here, :]
+
+    @pl.when((mine == n_mem - 1) & jnp.logical_not(is_last))
     def _():
-        extra.wait()
-        intra_s[...] += extra_s[...]
-
-    window.wait()
+        intra_s[...] += extra_ref[here, :]
+
+    later = (lax.axis_index("ctx") & bit) != 0
+    got = jnp.where(later, got_ref[...].astype(jnp.float32), 0.0)
+    prefix = (prefix_ref[...] + got).astype(jnp.bfloat16)
     coef = coef_s[...]
     for head in range(HEADS):
-        columns = slice(head * HDIM, (head + 1) * HDIM)
+        columns = head_columns(head)
         summed = intra_s[:, columns] + jnp.dot(
-            query_s[:, columns], prefix_ref[columns, :], preferred_element_type=jnp.float32
+            query_s[:, columns], prefix[columns, :], preferred_element_type=jnp.float32
         )
         factor = lax.rsqrt(jnp.mean(summed * summed, axis=-1, keepdims=True) + norm_eps)
         memory_out = (summed * factor).astype(jnp.bfloat16).astype(jnp.float32)
-        window_part = jnp.where(mine == head, window_s[...], 0.0)
+        window_part = jnp.where(mine == head, window_ref[here, :], 0.0)
         out_ref[:, columns] = (coef * memory_out + window_part).astype(out_ref.dtype)
 
 
@@ -611,25 +502,37 @@
     refs[-1][...] = total.astype(jnp.bfloat16)
 
 
-def running_sums_body(pieces_ref, sums_ref):
-    total = jnp.zeros(pieces_ref.shape[1:], jnp.float32)
-    for index in range(pieces_ref.shape[0]):
-        sums_ref[index] = total.astype(jnp.bfloat16)
-        total += pieces_ref[index]
-
-
-def exclusive_prefix(state):
+def double_body(bit, got_ref, total_ref, *refs):
+    if len(refs) == 4:
+        before_ref, total_out, prefix_ref, sent_ref = refs
+        before = before_ref[...]
+    else:
+        total_out, prefix_ref, sent_ref = refs
+        before = 0.0
+    got = got_ref[...].astype(jnp.float32)
+    later = (lax.axis_index("ctx") & bit) != 0
+    prefix_ref[...] = before + jnp.where(later, got, 0.0)
+    total = total_ref[...] + got
+    total_out[...] = total
+    sent_ref[...] = total.astype(jnp.bfloat16)
+
+
+def exclusive_prefix(state, sent):
     devices = lax.axis_size("ctx")
-    pieces = state.reshape(devices, -1, state.shape[1])
-    pieces = lax.all_to_all(pieces, "ctx", split_axis=0, concat_axis=0, tiled=True)
-    sums = kernel_call(
-        running_sums_body,
-        "running_sums",
-        jax.ShapeDtypeStruct(pieces.shape, jnp.bfloat16),
-        pieces.size,
-        6 * pieces.size,
-    )(pieces)
-    return lax.all_to_all(sums, "ctx", split_axis=0, concat_axis=0, tiled=True).reshape(state.shape)
+    kinds = [
+        jax.ShapeDtypeStruct(state.shape, kind) for kind in (jnp.float32, jnp.float32, jnp.bfloat16)
+    ]
+    before = ()
+    bit = 1
+    while 2 * bit < devices:
+        got = lax.ppermute(sent, "ctx", [(i, i ^ bit) for i in range(devices)])
+        state, prefix, sent = kernel_call(
+            functools.partial(double_body, bit), f"double{bit}", kinds, 4 * state.size, 16 * state.size
+        )(got, state, *before)
+        before = (prefix,)
+        bit *= 2
+    got = lax.ppermute(sent, "ctx", [(i, i + bit) for i in range(devices) if not i & bit])
+    return prefix, got, bit
 
 
 def dense_shards(tokens, routes, router, mem_weight, win_weight):
@@ -661,9 +564,9 @@
         [shape(cut + ROUTE_ROWS, 3 * HDIM)] * n_mem,
         1 << 20,
         1 << 20,
-        in_specs=[HBM, WHOLE],
+        in_specs=[HBM, WHOLE, HBM],
         scratch_shapes=[pltpu.VMEM((cut, 3 * width), low), dma],
-    )(win_weight, routes.T)
+    )(win_weight, routes.T, below[1])
     packed = [packed[0]] + [
         lax.ppermute(packed[s], "mem", [(i, (i + s) % n_mem) for i in range(n_mem)])
         for s in range(1, n_mem)
@@ -675,7 +578,10 @@
         1 << 20,
         1 << 20,
     )(*packed)
-    pieces = lax.all_gather(packed, "ctx", axis=0, tiled=False)
+    pieces = [packed] + [
+        lax.ppermute(packed, "ctx", [(i, (i + s) % n_ctx) for i in range(n_ctx)])
+        for s in range(1, n_ctx)
+    ]
 
     weight = mem_weight[0]
     router_rows = router.T
@@ -692,49 +598,23 @@
         ),
         2 * total * depth * 3 * width,
         10 << 20,
-        in_specs=[HBM] * early + [WHOLE, WHOLE, HBM],
-        out_specs=[HBM, HBM, WHOLE, WHOLE],
-        scratch_shapes=[
-            pltpu.VMEM((early, count, depth), low),
-            pltpu.VMEM((depth, 3 * width), low),
-            pltpu.VMEM((total, 3 * width), low),
-            pltpu.VMEM((total, width), full),
-            dma((early,)),
-            dma,
-            dma((2,)),
-        ],
     )(*slots[:early], packed, router_rows, weight)
-    last_kv, state = kernel_call(
+    last_kv, state, sent = kernel_call(
         functools.partial(last_keys_body, n_mem),
         "last_keys",
-        (shape(count, 2 * width), shape(width, HDIM, full)),
+        (shape(count, 2 * width), shape(width, HDIM, full), shape(width, HDIM)),
         2 * count * depth * 2 * width,
         3 << 20,
-        in_specs=[HBM, HBM, WHOLE, HBM, WHOLE],
-        scratch_shapes=[
-            pltpu.VMEM((count, depth), low),
-            pltpu.VMEM((depth, 2 * width), low),
-            dma((3,)),
-        ],
     )(below[-1], above[-1], packed, weight, state)
-    prefix = exclusive_prefix(state)
-
-    win, tail = kernel_call(
-        functools.partial(window_project_body, n_mem),
+    prefix, got, bit = exclusive_prefix(state, sent)
+
+    win, tail, _ = kernel_call(
+        functools.partial(window_project_body, n_mem, n_ctx),
         "window_project",
-        (shape(total, 3 * HDIM), shape(WINDOW, 2 * HDIM)),
+        (shape(total, 3 * HDIM), shape(WINDOW, 2 * HDIM), shape(depth, 3 * HDIM)),
         2 * total * depth * 3 * HDIM,
         5 << 20,
-        in_specs=[HBM] * len(slots) + [WHOLE],
-        out_specs=[HBM, WHOLE],
-        scratch_shapes=[
-            pltpu.VMEM((total, depth), low),
-            pltpu.VMEM((depth, 3 * HDIM), low),
-            pltpu.VMEM((total, 3 * HDIM), low),
-            dma((len(slots),)),
-            dma,
-        ],
-    )(*slots, pieces)
+    )(*slots, *pieces)
     halo = passed_along(tail, "ctx", 1)
     last_query, last_coef, extra = kernel_call(
         functools.partial(last_queries_body, n_mem),
@@ -742,15 +622,6 @@
         (shape(count, width), shape(count, HDIM, full), shape(total, width, full)),
         8 * count * depth * width,
         8 << 20,
-        in_specs=[HBM, HBM, WHOLE, WHOLE, HBM, HBM, WHOLE],
-        out_specs=[WHOLE, WHOLE, HBM],
-        scratch_shapes=[
-            pltpu.VMEM((count, depth), low),
-            pltpu.VMEM((depth, width), low),
-            pltpu.VMEM((total, 3 * width), low),
-            pltpu.VMEM((total, width), full),
-            dma((6,)),
-        ],
     )(below[-1], above[-1], packed, router_rows, weight, proj, last_kv)
     window_part = kernel_call(
         functools.partial(window_attend_body, count),
@@ -758,31 +629,22 @@
         shape(total, HDIM, full),
         4 * total * (count + WINDOW) * HDIM,
         3 << 20,
-        in_specs=[HBM, WHOLE],
-        scratch_shapes=[
-            pltpu.VMEM((total, 3 * HDIM), low),
-            pltpu.VMEM((total + WINDOW, 2 * HDIM), low),
-            dma,
-        ],
+        scratch_shapes=[pltpu.VMEM((total + WINDOW, 2 * HDIM), low)],
     )(win, halo)
 
     def finish(shift):
         return kernel_call(
-            functools.partial(finish_body, n_mem, shift),
+            functools.partial(finish_body, n_mem, shift, bit),
             f"finish{shift}",
             shape(count, width, low if shift else full),
             2 * count * width * HDIM,
             2 << 20,
-            in_specs=[HBM] * 7 + [WHOLE],
             scratch_shapes=[
                 pltpu.VMEM((count, width), low),
                 pltpu.VMEM((count, width), full),
-                pltpu.VMEM((count, width), full),
                 pltpu.VMEM((count, HDIM), full),
-                pltpu.VMEM((count, HDIM), full),
-                dma((7,)),
             ],
-        )(proj, intra, coef, last_query, last_coef, extra, window_part, prefix)
+        )(proj, intra, coef, last_query, last_coef, extra, window_part, prefix, got)
 
     parts = []
     for shift in sorted(range(1, n_mem), key=lambda s: abs(2 * s - n_mem)):
@@ -801,6 +663,8 @@
         and router.shape[1] == n_mem
         and win_weight.shape[0] % (16 * n_ctx) == 0
         and tokens.shape[0] <= 3 * HDIM
+        and n_ctx >= 4
+        and n_ctx & (n_ctx - 1) == 0
         and n_mem * tokens.shape[0] >= WINDOW
     )
     body = dense_shards if dense else sparse_shards

time: 145 us -> 122 us (0.84)
  Pallas kernels: 50.2 us -> 20.8 us
  waiting for transfers between devices: 35.7 us -> 51.9 us
  between operations: 13.7 us -> 0.3 us
  local copies, waits for them, and re-layouts: 4.14 us -> 6.28 us
    ppermute x0 -> x10, starting transfers between devices: none -> 15.3 us  [the longest x7 12.1 us: dense_shards(): lax.ppermute(packed, 'ctx', [(i, (i + s) % n_ctx) for i in range(n_ctx)])]
    pallas_call x6 -> x7, Pallas kernels: 19.8 us -> 5.68 us  [the longest x1 2.97 us: dense_shards(): kernel_call(functools.partial(window_project_body, n_mem, n_ctx), 'window...]
    all_to_all x2 -> x0, starting transfers between devices: 10.4 us -> none  [the longest x1 7.11 us: exclusive_prefix(): lax.all_to_all(pieces, 'ctx', split_axis=0, concat_axis=0, tiled=True)]
    ppermute x0 -> x10, waiting for transfers between devices: none -> 8.79 us  [the longest x2 6.41 us: exclusive_prefix(): got = lax.ppermute(sent, 'ctx', [(i, i ^ bit) for i in range(devices)])]
    pallas_call x1, Pallas kernels: 17.5 us -> 11.8 us  [dense_shards(): kernel_call(functools.partial(early_body, n_mem, hops), 'early_rows', (sh...]
    ppermute x3, starting transfers between devices: 10.5 us -> 6.71 us  [dense_shards(): above.append(lax.ppermute(above[-1], 'mem', down))]
    pallas_call x1, Pallas kernels: 5.17 us -> 2.31 us  [dense_shards(): kernel_call(functools.partial(window_attend_body, count), 'window_attend'...]
    ppermute x3, waiting for transfers between devices: 17.7 us -> 20.5 us  [dense_shards(): parts.append(lax.ppermute(finish(shift), 'mem', pairs))]
  transfers between devices with their start and end apart: 16 -> 23, of which waited for: 7 -> 9; matrix products, arithmetic and copies ran while one was open for 0% -> 0% of each run, Pallas kernels for 25% -> 16%
where the time goes in v4:
time: 122 us; the launch traced here: 120 us
  waiting for transfers between devices  51.9 us (43%)
  starting transfers between devices  41.1 us (34%)
  Pallas kernels  20.8 us (17%)
  local copies, waits for them, and re-layouts  6.28 us (5%)
    ppermute x3, waiting for transfers between devices, dense_shards(): parts.append(lax.ppermute(finish(shift), 'mem', pairs))  20.5 us
    ppermute x3, waiting for transfers between devices, dense_shards(): above.append(lax.ppermute(above[-1], 'mem', down))  18 us
    ppermute x7, starting transfers between devices, dense_shards(): lax.ppermute(packed, 'ctx', [(i, (i + s) % n_ctx) for i in range(n_ctx)])  12.1 us
    pallas_call x1, Pallas kernels, dense_shards(): kernel_call(functools.partial(early_body, n_mem, hops), 'early_rows', (sh...  11.8 us
    ppermute x3, starting transfers between devices, dense_shards(): below.append(lax.ppermute(below[-1], 'mem', up))  7.16 us
    ppermute x3, starting transfers between devices, dense_shards(): above.append(lax.ppermute(above[-1], 'mem', down))  6.71 us
    ppermute x2, waiting for transfers between devices, exclusive_prefix(): got = lax.ppermute(sent, 'ctx', [(i, i ^ bit) for i in range(devices)])  6.41 us
    unnamed x16, local copies, waits for them, and re-layouts  6.28 us
  transfers between devices with their start and end apart: 23, of which 9 were waited for; matrix products, arithmetic and copies ran while one was open for 0% of the time, Pallas kernels for 16%

profile of v4, /device:TPU:9, one launch (start us, length us, event | category | flops | bytes accessed | tf_op | source)
XLA Modules:
  0.0 120.4 jit_solution(7483918848496962457)
XLA Ops:
  0.0 1.9 %collective-permute-start.1 = (bf16[256,1024]{1,0:T(8,128)(2,1)}, bf16[256,1024]{1,0:T(8,128)(2,1)S(1)}, u32[]{:S(2)}, u32[]{:S(2)}) collective-permute-start(bf16[256,1024]{1,0:T(8,128)(2,1)} %refs_0_.3), channel_id=1, source_target_pairs={{3,2},{2,1},{1,0},{7,6},{6,5},{5,4},{11,10},{10,9},{9,8},{15,14},{... | collective-permute-start | bytes 1572872 | tf_op jit(solution)/shard_map/ppermute | solution.py:556
  1.9 3.4 %collective-permute-start = (bf16[256,1024]{1,0:T(8,128)(2,1)}, bf16[256,1024]{1,0:T(8,128)(2,1)S(1)}, u32[]{:S(2)}, u32[]{:S(2)}) collective-permute-start(bf16[256,1024]{1,0:T(8,128)(2,1)} %refs_0_.3), channel_id=1, source_target_pairs={{0,1},{1,2},{2,3},{4,5},{5,6},{6,7},{8,9},{9,10},{10,11},{12,13},{... | collective-permute-start | bytes 1572872 | tf_op jit(solution)/shard_map/ppermute | solution.py:555
  5.3 9.6 %collective-permute-done.1.refs_2_ = bf16[256,1024]{1,0:T(8,128)(2,1)S(1)} collective-permute-done((bf16[256,1024]{1,0:T(8,128)(2,1)}, bf16[256,1024]{1,0:T(8,128)(2,1)S(1)}, u32[]{:S(2)}, u32[]{:S(2)}) %collective-permute-start.1) | collective-permute-done | bytes 524320 | tf_op jit(solution)/shard_map/ppermute | solution.py:556
  14.9 2.2 %collective-permute-start.3 = (bf16[256,1024]{1,0:T(8,128)(2,1)S(1)}, bf16[256,1024]{1,0:T(8,128)(2,1)S(1)}, u32[]{:S(2)}, u32[]{:S(2)}) collective-permute-start(bf16[256,1024]{1,0:T(8,128)(2,1)S(1)} %collective-permute-done.1.refs_2_), channel_id=1, source_target_pairs={{2,1},{1,0},{6,5},{5,4},{10,9},{9,8},{14,13},{13,12},{18,17},{17,1... | collective-permute-start | bytes 1572872 | tf_op jit(solution)/shard_map/ppermute | solution.py:556
  17.1 3.1 %collective-permute-start.2 = (bf16[256,1024]{1,0:T(8,128)(2,1)S(1)}, bf16[256,1024]{1,0:T(8,128)(2,1)S(1)}, u32[]{:S(2)}, u32[]{:S(2)}) collective-permute-start(bf16[256,1024]{1,0:T(8,128)(2,1)S(1)} %collective-permute-done._.refs_1_), channel_id=1, source_target_pairs={{1,2},{2,3},{5,6},{6,7},{9,10},{10,11},{13,14},{14,15},{17,18},{18... | collective-permute-start | bytes 1572872 | tf_op jit(solution)/shard_map/ppermute | solution.py:555
  20.2 8.4 %collective-permute-done.3.refs_4_ = bf16[256,1024]{1,0:T(8,128)(2,1)S(1)} collective-permute-done((bf16[256,1024]{1,0:T(8,128)(2,1)S(1)}, bf16[256,1024]{1,0:T(8,128)(2,1)S(1)}, u32[]{:S(2)}, u32[]{:S(2)}) %collective-permute-start.3) | collective-permute-done | bytes 524320 | tf_op jit(solution)/shard_map/ppermute | solution.py:556
  28.6 2.6 %collective-permute-start.8 = (bf16[256,1024]{1,0:T(8,128)(2,1)S(1)}, bf16[256,1024]{1,0:T(8,128)(2,1)S(1)}, u32[]{:S(2)}, u32[]{:S(2)}) collective-permute-start(bf16[256,1024]{1,0:T(8,128)(2,1)S(1)} %collective-permute-done.3.refs_4_), channel_id=1, source_target_pairs={{1,0},{5,4},{9,8},{13,12},{17,16},{21,20},{25,24},{29,28}} | collective-permute-start | bytes 1572872 | tf_op jit(solution)/shard_map/ppermute | solution.py:556
  33.9 2.8 %collective-permute-start.4 = (bf16[48,384]{1,0:T(8,128)(2,1)S(1)}, bf16[48,384]{1,0:T(8,128)(2,1)S(1)}, u32[]{:S(2)}, u32[]{:S(2)}) collective-permute-start(bf16[48,384]{1,0:T(8,128)(2,1)S(1)} %get-tuple-element.27), channel_id=1, source_target_pairs={{0,1},{1,2},{2,3},{3,0},{4,5},{5,6},{6,7},{7,4},{8,9},{9,10},{10,1... | collective-permute-start | bytes 110600 | tf_op jit(solution)/shard_map/ppermute | solution.py:571
  37.9 2.5 %collective-permute-done.5.refs_2_ = bf16[48,384]{1,0:T(8,128)(2,1)S(1)} collective-permute-done((bf16[48,384]{1,0:T(8,128)(2,1)S(1)}, bf16[48,384]{1,0:T(8,128)(2,1)S(1)}, u32[]{:S(2)}, u32[]{:S(2)}) %collective-permute-start.5) | collective-permute-done | bytes 36896 | tf_op jit(solution)/shard_map/ppermute | solution.py:571
  40.4 2.2 %collective-permute-done.6.refs_3_ = bf16[48,384]{1,0:T(8,128)(2,1)S(1)} collective-permute-done((bf16[48,384]{1,0:T(8,128)(2,1)S(1)}, bf16[48,384]{1,0:T(8,128)(2,1)S(1)}, u32[]{:S(2)}, u32[]{:S(2)}) %collective-permute-start.6) | collective-permute-done | bytes 36896 | tf_op jit(solution)/shard_map/ppermute | solution.py:571
  42.6 3.1 %collective-permute-start.15 = (bf16[4,48,384]{2,1,0:T(8,128)(2,1)S(1)}, bf16[4,48,384]{2,1,0:T(8,128)(2,1)S(1)}, u32[]{:S(2)}, u32[]{:S(2)}) collective-permute-start(bf16[4,48,384]{2,1,0:T(8,128)(2,1)S(1)} %arrange.1.refs_5_.packed_ref.refs_7_), channel_id=1, source_target_pairs={{0,28},{4,0},{8,4},{12,8},{16,12},{20,16},{24,20},{28,24},{1,29},{... | collective-permute-start | bytes 442376 | tf_op jit(solution)/shard_map/ppermute | solution.py:582
  45.8 1.7 %collective-permute-start.14 = (bf16[4,48,384]{2,1,0:T(8,128)(2,1)S(1)}, bf16[4,48,384]{2,1,0:T(8,128)(2,1)S(1)}, u32[]{:S(2)}, u32[]{:S(2)}) collective-permute-start(bf16[4,48,384]{2,1,0:T(8,128)(2,1)S(1)} %arrange.1.refs_5_.packed_ref.refs_7_), channel_id=1, source_target_pairs={{0,24},{4,28},{8,0},{12,4},{16,8},{20,12},{24,16},{28,20},{1,25},{... | collective-permute-start | bytes 442376 | tf_op jit(solution)/shard_map/ppermute | solution.py:582
  47.9 2.4 %collective-permute-done.15.refs_14_ = bf16[4,48,384]{2,1,0:T(8,128)(2,1)S(1)} collective-permute-done((bf16[4,48,384]{2,1,0:T(8,128)(2,1)S(1)}, bf16[4,48,384]{2,1,0:T(8,128)(2,1)S(1)}, u32[]{:S(2)}, u32[]{:S(2)}) %collective-permute-start.15) | collective-permute-done | bytes 147488 | tf_op jit(solution)/shard_map/ppermute | solution.py:582
  52.0 3.7 %collective-permute-start.11 = (bf16[4,48,384]{2,1,0:T(8,128)(2,1)S(1)}, bf16[4,48,384]{2,1,0:T(8,128)(2,1)S(1)}, u32[]{:S(2)}, u32[]{:S(2)}) collective-permute-start(bf16[4,48,384]{2,1,0:T(8,128)(2,1)S(1)} %arrange.1.refs_5_.packed_ref.refs_7_), channel_id=1, source_target_pairs={{0,12},{4,16},{8,20},{12,24},{16,28},{20,0},{24,4},{28,8},{1,13},{... | collective-permute-start | bytes 442376 | tf_op jit(solution)/shard_map/ppermute | solution.py:582
  57.2 1.9 %copy-done = bf16[1,1024,1536]{2,1,0:T(8,128)(2,1)S(1)} copy-done((bf16[1,1024,1536]{2,1,0:T(8,128)(2,1)S(1)}, bf16[1,1024,1536]{2,1,0:T(8,128)(2,1)}, u32[]{:S(2)}) %copy-start) | copy-done | bytes 3145752
  60.8 11.8 %early_rows.1 = (bf16[1024,1536]{1,0:T(8,128)(2,1)S(1)}, f32[1024,512]{1,0:T(8,128)S(1)}, f32[1024,128]{1,0:T(8,128)S(1)}, f32[512,128]{1,0:T(8,128)S(1)}) custom-call(bf16[256,1024]{1,0:T(8,128)(2,1)S(1)} %copy-done.3, bf16[256,1024]{1,0:T(8,128)(2,1)S(1)} %collective-permute-done._.refs_1_, bf16[256,1024]{1,0:T(8,128)(2,1)S(1)} %collective-permute-done.1.refs_2_, ...), custom_call_target="tpu_custom_call" | custom-call | flops 3221225472 | bytes 10485760 | tf_op jit(solution)/shard_map/early_rows/pallas_call | solution.py:590
  73.6 3.0 %window_project.1 = (bf16[1024,384]{1,0:T(8,128)(2,1)S(1)}, bf16[512,256]{1,0:T(8,128)(2,1)S(1)}, bf16[1024,384]{1,0:T(8,128)(2,1)}) custom-call(bf16[256,1024]{1,0:T(8,128)(2,1)S(1)} %copy-done.4, bf16[256,1024]{1,0:T(8,128)(2,1)S(1)} %collective-permute-done._.refs_1_, bf16[256,1024]{1,0:T(8,128)(2,1)S(1)} %collective-permute-done.1.refs_2_, ...), custom_call_target="tpu_custom_call" | custom-call | flops 805306368 | bytes 5242880 | tf_op jit(solution)/shard_map/window_project/pallas_call | solution.py:611
  76.6 1.9 %collective-permute-start.16 = (bf16[512,256]{1,0:T(8,128)(2,1)S(1)}, bf16[512,256]{1,0:T(8,128)(2,1)S(1)}, u32[]{:S(2)}, u32[]{:S(2)}) collective-permute-start(bf16[512,256]{1,0:T(8,128)(2,1)S(1)} %get-tuple-element.39), channel_id=1, source_target_pairs={{0,4},{4,8},{8,12},{12,16},{16,20},{20,24},{24,28},{1,5},{5,9},{9,... | collective-permute-start | bytes 786440 | tf_op jit(solution)/shard_map/ppermute | solution.py:21
  79.4 6.4 %collective-permute-done.18.got_ref = bf16[512,128]{1,0:T(8,128)(2,1)S(1)} collective-permute-done((bf16[512,128]{1,0:T(8,128)(2,1)S(1)}, bf16[512,128]{1,0:T(8,128)(2,1)S(1)}, u32[]{:S(2)}, u32[]{:S(2)}) %collective-permute-start.18) | collective-permute-done | bytes 131104 | tf_op jit(solution)/shard_map/ppermute | solution.py:528
  86.6 2.3 %collective-permute-start.19 = (bf16[512,128]{1,0:T(8,128)(2,1)S(1)}, bf16[512,128]{1,0:T(8,128)(2,1)S(1)}, u32[]{:S(2)}, u32[]{:S(2)}) collective-permute-start(bf16[512,128]{1,0:T(8,128)(2,1)S(1)} %get-tuple-element.46), channel_id=1, source_target_pairs={{0,16},{4,20},{8,24},{12,28},{1,17},{5,21},{9,25},{13,29},{2,18},{... | collective-permute-start | bytes 393224 | tf_op jit(solution)/shard_map/ppermute | solution.py:534
  88.9 2.3 %window_attend.1.refs_6_ = f32[1024,128]{1,0:T(8,128)S(1)} custom-call(bf16[1024,384]{1,0:T(8,128)(2,1)S(1)} %get-tuple-element.38.win_ref, bf16[512,256]{1,0:T(8,128)(2,1)S(1)} %collective-permute-done.16.halo_ref), custom_call_target="tpu_custom_call" | custom-call | flops 402653184 | bytes 3145728 | tf_op jit(solution)/shard_map/window_attend/pallas_call | solution.py:626
  91.8 4.4 %collective-permute-start.20 = (bf16[256,512]{1,0:T(8,128)(2,1)S(1)}, bf16[256,512]{1,0:T(8,128)(2,1)S(1)}, u32[]{:S(2)}, u32[]{:S(2)}) collective-permute-start(bf16[256,512]{1,0:T(8,128)(2,1)S(1)} %finish2.1), channel_id=1, source_target_pairs={{0,2},{1,3},{2,0},{3,1},{4,6},{5,7},{6,4},{7,5},{8,10},{9,11},{10,... | collective-permute-start | bytes 786440 | tf_op jit(solution)/shard_map/ppermute | solution.py:652
  99.1 8.8 %collective-permute-done.20.refs_1_ = bf16[256,512]{1,0:T(8,128)(2,1)S(1)} collective-permute-done((bf16[256,512]{1,0:T(8,128)(2,1)S(1)}, bf16[256,512]{1,0:T(8,128)(2,1)S(1)}, u32[]{:S(2)}, u32[]{:S(2)}) %collective-permute-start.20) | collective-permute-done | bytes 262176 | tf_op jit(solution)/shard_map/ppermute | solution.py:652
  107.9 11.2 %collective-permute-done.21.refs_2_ = bf16[256,512]{1,0:T(8,128)(2,1)S(1)} collective-permute-done((bf16[256,512]{1,0:T(8,128)(2,1)S(1)}, bf16[256,512]{1,0:T(8,128)(2,1)S(1)}, u32[]{:S(2)}, u32[]{:S(2)}) %collective-permute-start.21) | collective-permute-done | bytes 262176 | tf_op jit(solution)/shard_map/ppermute | solution.py:652
  (52 shorter events, 16.6 us)
Async XLA Ops:
  0.0 14.9 %collective-permute-start.1 = (bf16[256,1024]{1,0:T(8,128)(2,1)}, bf16[256,1024]{1,0:T(8,128)(2,1)S(1)}, u32[]{:S(2)}, u32[]{:S(2)}) collective-permute-start(bf16[256,1024]{1,0:T(8,128)(2,1)} %refs_0_.3), channel_id=1, source_target_pairs={{3,2},{2,1},{1,0},{7,6},{6,5},{5,4},{11,10},{10,9},{9,8},{15,14},{... | collective-permute-start | bytes 1572872 | tf_op jit(solution)/shard_map/ppermute | solution.py:556
  1.9 15.2 %collective-permute-start = (bf16[256,1024]{1,0:T(8,128)(2,1)}, bf16[256,1024]{1,0:T(8,128)(2,1)S(1)}, u32[]{:S(2)}, u32[]{:S(2)}) collective-permute-start(bf16[256,1024]{1,0:T(8,128)(2,1)} %refs_0_.3), channel_id=1, source_target_pairs={{0,1},{1,2},{2,3},{4,5},{5,6},{6,7},{8,9},{9,10},{10,11},{12,13},{... | collective-permute-start | bytes 1572872 | tf_op jit(solution)/shard_map/ppermute | solution.py:555
  14.9 13.8 %collective-permute-start.3 = (bf16[256,1024]{1,0:T(8,128)(2,1)S(1)}, bf16[256,1024]{1,0:T(8,128)(2,1)S(1)}, u32[]{:S(2)}, u32[]{:S(2)}) collective-permute-start(bf16[256,1024]{1,0:T(8,128)(2,1)S(1)} %collective-permute-done.1.refs_2_), channel_id=1, source_target_pairs={{2,1},{1,0},{6,5},{5,4},{10,9},{9,8},{14,13},{13,12},{18,17},{17,1... | collective-permute-start | bytes 1572872 | tf_op jit(solution)/shard_map/ppermute | solution.py:556
  17.1 14.1 %collective-permute-start.2 = (bf16[256,1024]{1,0:T(8,128)(2,1)S(1)}, bf16[256,1024]{1,0:T(8,128)(2,1)S(1)}, u32[]{:S(2)}, u32[]{:S(2)}) collective-permute-start(bf16[256,1024]{1,0:T(8,128)(2,1)S(1)} %collective-permute-done._.refs_1_), channel_id=1, source_target_pairs={{1,2},{2,3},{5,6},{6,7},{9,10},{10,11},{13,14},{14,15},{17,18},{18... | collective-permute-start | bytes 1572872 | tf_op jit(solution)/shard_map/ppermute | solution.py:555
  28.6 27.1 %collective-permute-start.8 = (bf16[256,1024]{1,0:T(8,128)(2,1)S(1)}, bf16[256,1024]{1,0:T(8,128)(2,1)S(1)}, u32[]{:S(2)}, u32[]{:S(2)}) collective-permute-start(bf16[256,1024]{1,0:T(8,128)(2,1)S(1)} %collective-permute-done.3.refs_4_), channel_id=1, source_target_pairs={{1,0},{5,4},{9,8},{13,12},{17,16},{21,20},{25,24},{29,28}} | collective-permute-start | bytes 1572872 | tf_op jit(solution)/shard_map/ppermute | solution.py:556
  31.2 24.5 %collective-permute-start.7 = (bf16[256,1024]{1,0:T(8,128)(2,1)S(1)}, bf16[256,1024]{1,0:T(8,128)(2,1)S(1)}, u32[]{:S(2)}, u32[]{:S(2)}) collective-permute-start(bf16[256,1024]{1,0:T(8,128)(2,1)S(1)} %collective-permute-done.2.refs_3_), channel_id=1, source_target_pairs={{2,3},{6,7},{10,11},{14,15},{18,19},{22,23},{26,27},{30,31}} | collective-permute-start | bytes 1572872 | tf_op jit(solution)/shard_map/ppermute | solution.py:555
  33.9 4.0 %collective-permute-start.4 = (bf16[48,384]{1,0:T(8,128)(2,1)S(1)}, bf16[48,384]{1,0:T(8,128)(2,1)S(1)}, u32[]{:S(2)}, u32[]{:S(2)}) collective-permute-start(bf16[48,384]{1,0:T(8,128)(2,1)S(1)} %get-tuple-element.27), channel_id=1, source_target_pairs={{0,1},{1,2},{2,3},{3,0},{4,5},{5,6},{6,7},{7,4},{8,9},{9,10},{10,1... | collective-permute-start | bytes 110600 | tf_op jit(solution)/shard_map/ppermute | solution.py:571
  36.7 3.8 %collective-permute-start.5 = (bf16[48,384]{1,0:T(8,128)(2,1)S(1)}, bf16[48,384]{1,0:T(8,128)(2,1)S(1)}, u32[]{:S(2)}, u32[]{:S(2)}) collective-permute-start(bf16[48,384]{1,0:T(8,128)(2,1)S(1)} %get-tuple-element.28), channel_id=1, source_target_pairs={{0,2},{1,3},{2,0},{3,1},{4,6},{5,7},{6,4},{7,5},{8,10},{9,11},{10,... | collective-permute-start | bytes 110600 | tf_op jit(solution)/shard_map/ppermute | solution.py:571
  36.7 5.9 %collective-permute-start.6 = (bf16[48,384]{1,0:T(8,128)(2,1)S(1)}, bf16[48,384]{1,0:T(8,128)(2,1)S(1)}, u32[]{:S(2)}, u32[]{:S(2)}) collective-permute-start(bf16[48,384]{1,0:T(8,128)(2,1)S(1)} %get-tuple-element.29), channel_id=1, source_target_pairs={{0,3},{1,0},{2,1},{3,2},{4,7},{5,4},{6,5},{7,6},{8,11},{9,8},{10,9... | collective-permute-start | bytes 110600 | tf_op jit(solution)/shard_map/ppermute | solution.py:571
  42.6 7.7 %collective-permute-start.15 = (bf16[4,48,384]{2,1,0:T(8,128)(2,1)S(1)}, bf16[4,48,384]{2,1,0:T(8,128)(2,1)S(1)}, u32[]{:S(2)}, u32[]{:S(2)}) collective-permute-start(bf16[4,48,384]{2,1,0:T(8,128)(2,1)S(1)} %arrange.1.refs_5_.packed_ref.refs_7_), channel_id=1, source_target_pairs={{0,28},{4,0},{8,4},{12,8},{16,12},{20,16},{24,20},{28,24},{1,29},{... | collective-permute-start | bytes 442376 | tf_op jit(solution)/shard_map/ppermute | solution.py:582
  45.8 6.2 %collective-permute-start.14 = (bf16[4,48,384]{2,1,0:T(8,128)(2,1)S(1)}, bf16[4,48,384]{2,1,0:T(8,128)(2,1)S(1)}, u32[]{:S(2)}, u32[]{:S(2)}) collective-permute-start(bf16[4,48,384]{2,1,0:T(8,128)(2,1)S(1)} %arrange.1.refs_5_.packed_ref.refs_7_), channel_id=1, source_target_pairs={{0,24},{4,28},{8,0},{12,4},{16,8},{20,12},{24,16},{28,20},{1,25},{... | collective-permute-start | bytes 442376 | tf_op jit(solution)/shard_map/ppermute | solution.py:582
  47.4 25.2 %collective-permute-start.13 = (bf16[4,48,384]{2,1,0:T(8,128)(2,1)S(1)}, bf16[4,48,384]{2,1,0:T(8,128)(2,1)S(1)}, u32[]{:S(2)}, u32[]{:S(2)}) collective-permute-start(bf16[4,48,384]{2,1,0:T(8,128)(2,1)S(1)} %arrange.1.refs_5_.packed_ref.refs_7_), channel_id=1, source_target_pairs={{0,20},{4,24},{8,28},{12,0},{16,4},{20,8},{24,12},{28,16},{1,21},{... | collective-permute-start | bytes 442376 | tf_op jit(solution)/shard_map/ppermute | solution.py:582
  50.3 22.5 %collective-permute-start.12 = (bf16[4,48,384]{2,1,0:T(8,128)(2,1)S(1)}, bf16[4,48,384]{2,1,0:T(8,128)(2,1)S(1)}, u32[]{:S(2)}, u32[]{:S(2)}) collective-permute-start(bf16[4,48,384]{2,1,0:T(8,128)(2,1)S(1)} %arrange.1.refs_5_.packed_ref.refs_7_), channel_id=1, source_target_pairs={{0,16},{4,20},{8,24},{12,28},{16,0},{20,4},{24,8},{28,12},{1,17},{... | collective-permute-start | bytes 442376 | tf_op jit(solution)/shard_map/ppermute | solution.py:582
  52.0 20.8 %collective-permute-start.11 = (bf16[4,48,384]{2,1,0:T(8,128)(2,1)S(1)}, bf16[4,48,384]{2,1,0:T(8,128)(2,1)S(1)}, u32[]{:S(2)}, u32[]{:S(2)}) collective-permute-start(bf16[4,48,384]{2,1,0:T(8,128)(2,1)S(1)} %arrange.1.refs_5_.packed_ref.refs_7_), channel_id=1, source_target_pairs={{0,12},{4,16},{8,20},{12,24},{16,28},{20,0},{24,4},{28,8},{1,13},{... | collective-permute-start | bytes 442376 | tf_op jit(solution)/shard_map/ppermute | solution.py:582
  55.7 17.1 %collective-permute-start.10 = (bf16[4,48,384]{2,1,0:T(8,128)(2,1)S(1)}, bf16[4,48,384]{2,1,0:T(8,128)(2,1)S(1)}, u32[]{:S(2)}, u32[]{:S(2)}) collective-permute-start(bf16[4,48,384]{2,1,0:T(8,128)(2,1)S(1)} %arrange.1.refs_5_.packed_ref.refs_7_), channel_id=1, source_target_pairs={{0,8},{4,12},{8,16},{12,20},{16,24},{20,28},{24,0},{28,4},{1,9},{5... | collective-permute-start | bytes 442376 | tf_op jit(solution)/shard_map/ppermute | solution.py:582
  55.7 17.1 %collective-permute-start.9 = (bf16[4,48,384]{2,1,0:T(8,128)(2,1)S(1)}, bf16[4,48,384]{2,1,0:T(8,128)(2,1)S(1)}, u32[]{:S(2)}, u32[]{:S(2)}) collective-permute-start(bf16[4,48,384]{2,1,0:T(8,128)(2,1)S(1)} %arrange.1.refs_5_.packed_ref.refs_7_), channel_id=1, source_target_pairs={{0,4},{4,8},{8,12},{12,16},{16,20},{20,24},{24,28},{28,0},{1,5},{5... | collective-permute-start | bytes 442376 | tf_op jit(solution)/shard_map/ppermute | solution.py:582
  72.7 16.2 %copy-start.6 = (bf16[1024,4]{0,1:T(4,128)(2,1)S(1)}, bf16[1024,4]{0,1:T(4,128)(2,1)}, u32[]{:S(2)}) copy-start(bf16[1024,4]{0,1:T(4,128)(2,1)} %param.7) | copy-start | bytes 24580
  72.7 5.9 %collective-permute-start.17 = (bf16[512,128]{1,0:T(8,128)(2,1)S(1)}, bf16[512,128]{1,0:T(8,128)(2,1)S(1)}, u32[]{:S(2)}, u32[]{:S(2)}) collective-permute-start(bf16[512,128]{1,0:T(8,128)(2,1)S(1)} %get-tuple-element.40), channel_id=1, source_target_pairs={{0,4},{4,0},{8,12},{12,8},{16,20},{20,16},{24,28},{28,24},{1,5},{5... | collective-permute-start | bytes 393224 | tf_op jit(solution)/shard_map/ppermute | solution.py:528
  76.6 12.3 %collective-permute-start.16 = (bf16[512,256]{1,0:T(8,128)(2,1)S(1)}, bf16[512,256]{1,0:T(8,128)(2,1)S(1)}, u32[]{:S(2)}, u32[]{:S(2)}) collective-permute-start(bf16[512,256]{1,0:T(8,128)(2,1)S(1)} %get-tuple-element.39), channel_id=1, source_target_pairs={{0,4},{4,8},{8,12},{12,16},{16,20},{20,24},{24,28},{1,5},{5,9},{9,... | collective-permute-start | bytes 786440 | tf_op jit(solution)/shard_map/ppermute | solution.py:21
  78.6 7.2 %collective-permute-start.18 = (bf16[512,128]{1,0:T(8,128)(2,1)S(1)}, bf16[512,128]{1,0:T(8,128)(2,1)S(1)}, u32[]{:S(2)}, u32[]{:S(2)}) collective-permute-start(bf16[512,128]{1,0:T(8,128)(2,1)S(1)} %get-tuple-element.42), channel_id=1, source_target_pairs={{0,8},{4,12},{8,0},{12,4},{16,24},{20,28},{24,16},{28,20},{1,9},{5... | collective-permute-start | bytes 393224 | tf_op jit(solution)/shard_map/ppermute | solution.py:528
  86.6 4.7 %collective-permute-start.19 = (bf16[512,128]{1,0:T(8,128)(2,1)S(1)}, bf16[512,128]{1,0:T(8,128)(2,1)S(1)}, u32[]{:S(2)}, u32[]{:S(2)}) collective-permute-start(bf16[512,128]{1,0:T(8,128)(2,1)S(1)} %get-tuple-element.46), channel_id=1, source_target_pairs={{0,16},{4,20},{8,24},{12,28},{1,17},{5,21},{9,25},{13,29},{2,18},{... | collective-permute-start | bytes 393224 | tf_op jit(solution)/shard_map/ppermute | solution.py:534
  91.8 16.2 %collective-permute-start.20 = (bf16[256,512]{1,0:T(8,128)(2,1)S(1)}, bf16[256,512]{1,0:T(8,128)(2,1)S(1)}, u32[]{:S(2)}, u32[]{:S(2)}) collective-permute-start(bf16[256,512]{1,0:T(8,128)(2,1)S(1)} %finish2.1), channel_id=1, source_target_pairs={{0,2},{1,3},{2,0},{3,1},{4,6},{5,7},{6,4},{7,5},{8,10},{9,11},{10,... | collective-permute-start | bytes 786440 | tf_op jit(solution)/shard_map/ppermute | solution.py:652
  96.6 22.5 %collective-permute-start.21 = (bf16[256,512]{1,0:T(8,128)(2,1)S(1)}, bf16[256,512]{1,0:T(8,128)(2,1)S(1)}, u32[]{:S(2)}, u32[]{:S(2)}) collective-permute-start(bf16[256,512]{1,0:T(8,128)(2,1)S(1)} %finish1.1), channel_id=1, source_target_pairs={{0,1},{1,2},{2,3},{3,0},{4,5},{5,6},{6,7},{7,4},{8,9},{9,10},{10,1... | collective-permute-start | bytes 786440 | tf_op jit(solution)/shard_map/ppermute | solution.py:652
  97.4 22.2 %collective-permute-start.22 = (bf16[256,512]{1,0:T(8,128)(2,1)S(1)}, bf16[256,512]{1,0:T(8,128)(2,1)S(1)}, u32[]{:S(2)}, u32[]{:S(2)}) collective-permute-start(bf16[256,512]{1,0:T(8,128)(2,1)S(1)} %finish3.1), channel_id=1, source_target_pairs={{0,3},{1,0},{2,1},{3,2},{4,7},{5,4},{6,5},{7,6},{8,11},{9,8},{10,9... | collective-permute-start | bytes 786440 | tf_op jit(solution)/shard_map/ppermute | solution.py:652
  (7 other events, 18.3 us)

commit v5 on v4

--- a/solution.py
+++ b/solution.py
@@ -177,7 +177,7 @@
     return copy
 
 
-def pack_body(weight_ref, routes_ref, _, *refs):
+def pack_body(weight_ref, routes_ref, *refs):
     outs, (rows_ref, sem) = refs[:-2], refs[-2:]
     cut, _ = rows_ref.shape
     width = HEADS * HDIM
@@ -548,25 +548,15 @@
     def shape(rows, columns, kind=low):
         return jax.ShapeDtypeStruct((rows, columns), kind)
 
-    below, above = [tokens], [tokens]
-    for hop in range(1, n_mem):
-        up = [(i, i + 1) for i in range(hop - 1, n_mem - 1)]
-        down = [(n_mem - 1 - i, n_mem - 1 - j) for i, j in up]
-        below.append(lax.ppermute(below[-1], "mem", up))
-        above.append(lax.ppermute(above[-1], "mem", down))
-    slots = [tokens]
-    for hop in range(1, n_mem):
-        slots += [below[hop], above[hop]]
-
     packed = kernel_call(
         pack_body,
         "pack",
         [shape(cut + ROUTE_ROWS, 3 * HDIM)] * n_mem,
         1 << 20,
         1 << 20,
-        in_specs=[HBM, WHOLE, HBM],
+        in_specs=[HBM, WHOLE],
         scratch_shapes=[pltpu.VMEM((cut, 3 * width), low), dma],
-    )(win_weight, routes.T, below[1])
+    )(win_weight, routes.T)
     packed = [packed[0]] + [
         lax.ppermute(packed[s], "mem", [(i, (i + s) % n_mem) for i in range(n_mem)])
         for s in range(1, n_mem)
@@ -582,6 +572,21 @@
         lax.ppermute(packed, "ctx", [(i, (i + s) % n_ctx) for i in range(n_ctx)])
         for s in range(1, n_ctx)
     ]
+
+    below, above = [tokens], [tokens]
+    for hop in range(1, n_mem):
+        up = [(i, i + 1) for i in range(hop - 1, n_mem - 1)]
+        down = [(n_mem - 1 - i, n_mem - 1 - j) for i, j in up]
+        from_below, from_above = below[-1], above[-1]
+        if hop == 2:
+            from_below, from_above, packed = lax.optimization_barrier((from_below, from_above, packed))
+        if hop == 3:
+            from_below, from_above, pieces = lax.optimization_barrier((from_below, from_above, pieces))
+        below.append(lax.ppermute(from_below, "mem", up))
+        above.append(lax.ppermute(from_above, "mem", down))
+    slots = [tokens]
+    for hop in range(1, n_mem):
+        slots += [below[hop], above[hop]]
 
     weight = mem_weight[0]
     router_rows = router.T

time: 122 us -> 111 us (0.910)
  waiting for transfers between devices: 51.9 us -> 40.6 us
    ppermute x6, waiting for transfers between devices: 18 us -> 0.02 us  [the longest x3 0.01 us: dense_shards(): below.append(lax.ppermute(from_below, 'mem', up))]
    ppermute x7, starting transfers between devices: 12.1 us -> 17.2 us  [dense_shards(): lax.ppermute(packed, 'ctx', [(i, (i + s) % n_ctx) for i in range(n_ctx)])]
    ppermute x3, waiting for transfers between devices: 4.68 us -> 7.72 us  [dense_shards(): lax.ppermute(packed[s], 'mem', [(i, (i + s) % n_mem) for i in range(n_mem)])]
    ppermute x3, starting transfers between devices: 5.97 us -> 3.13 us  [dense_shards(): parts.append(lax.ppermute(finish(shift), 'mem', pairs))]
    ppermute x7, waiting for transfers between devices: 2.38 us -> 5.18 us  [dense_shards(): lax.ppermute(packed, 'ctx', [(i, (i + s) % n_ctx) for i in range(n_ctx)])]
    ppermute x1, starting transfers between devices: 1.91 us -> 3.55 us  [passed_along(): return lax.ppermute(x, axis, pairs)]
    ppermute x3, starting transfers between devices: 4.02 us -> 2.64 us  [dense_shards(): lax.ppermute(packed[s], 'mem', [(i, (i + s) % n_mem) for i in range(n_mem)])]
    unnamed x16 -> x12, local copies, waits for them, and re-layouts: 6.28 us -> 5.43 us
  transfers between devices with their start and end apart: 23 -> 23, of which waited for: 9 -> 9; matrix products, arithmetic and copies ran while one was open for 0% -> 0% of each run, Pallas kernels for 16% -> 18%
where the time goes in v5:
time: 111 us; the launch traced here: 109 us
  starting transfers between devices  42.3 us (38%)
  waiting for transfers between devices  40.6 us (37%)
  Pallas kernels  20.8 us (19%)
  local copies, waits for them, and re-layouts  5.43 us (5%)
    ppermute x3, waiting for transfers between devices, dense_shards(): parts.append(lax.ppermute(finish(shift), 'mem', pairs))  20.4 us
    ppermute x7, starting transfers between devices, dense_shards(): lax.ppermute(packed, 'ctx', [(i, (i + s) % n_ctx) for i in range(n_ctx)])  17.2 us
    pallas_call x1, Pallas kernels, dense_shards(): kernel_call(functools.partial(early_body, n_mem, hops), 'early_rows', (sh...  11.8 us
    ppermute x3, waiting for transfers between devices, dense_shards(): lax.ppermute(packed[s], 'mem', [(i, (i + s) % n_mem) for i in range(n_mem)])  7.72 us
    ppermute x3, starting transfers between devices, dense_shards(): below.append(lax.ppermute(from_below, 'mem', up))  7.66 us
    ppermute x2, waiting for transfers between devices, exclusive_prefix(): got = lax.ppermute(sent, 'ctx', [(i, i ^ bit) for i in range(devices)])  6.41 us
    unnamed x12, local copies, waits for them, and re-layouts  5.43 us
    ppermute x7, waiting for transfers between devices, dense_shards(): lax.ppermute(packed, 'ctx', [(i, (i + s) % n_ctx) for i in range(n_ctx)])  5.18 us
  transfers between devices with their start and end apart: 23, of which 9 were waited for; matrix products, arithmetic and copies ran while one was open for 0% of the time, Pallas kernels for 18%

profile of v5, /device:TPU:9, one launch (start us, length us, event | category | flops | bytes accessed | tf_op | source)
XLA Modules:
  0.0 109.3 jit_solution(1437899417630650921)
XLA Ops:
  0.0 1.9 %collective-permute-start.1 = (bf16[256,1024]{1,0:T(8,128)(2,1)}, bf16[256,1024]{1,0:T(8,128)(2,1)S(1)}, u32[]{:S(2)}, u32[]{:S(2)}) collective-permute-start(bf16[256,1024]{1,0:T(8,128)(2,1)} %refs_0_.3), channel_id=1, source_target_pairs={{3,2},{2,1},{1,0},{7,6},{6,5},{5,4},{11,10},{10,9},{9,8},{15,14},{... | collective-permute-start | bytes 1572872 | tf_op jit(solution)/shard_map/ppermute | solution.py:586
  1.9 3.4 %collective-permute-start = (bf16[256,1024]{1,0:T(8,128)(2,1)}, bf16[256,1024]{1,0:T(8,128)(2,1)S(1)}, u32[]{:S(2)}, u32[]{:S(2)}) collective-permute-start(bf16[256,1024]{1,0:T(8,128)(2,1)} %refs_0_.3), channel_id=1, source_target_pairs={{0,1},{1,2},{2,3},{4,5},{5,6},{6,7},{8,9},{9,10},{10,11},{12,13},{... | collective-permute-start | bytes 1572872 | tf_op jit(solution)/shard_map/ppermute | solution.py:585
  7.3 1.4 %collective-permute-start.2 = (bf16[48,384]{1,0:T(8,128)(2,1)S(1)}, bf16[48,384]{1,0:T(8,128)(2,1)S(1)}, u32[]{:S(2)}, u32[]{:S(2)}) collective-permute-start(bf16[48,384]{1,0:T(8,128)(2,1)S(1)} %get-tuple-element.40), channel_id=1, source_target_pairs={{0,1},{1,2},{2,3},{3,0},{4,5},{5,6},{6,7},{7,4},{8,9},{9,10},{10,1... | collective-permute-start | bytes 110600 | tf_op jit(solution)/shard_map/ppermute | solution.py:561
  9.9 7.7 %collective-permute-done.2.refs_1_ = bf16[48,384]{1,0:T(8,128)(2,1)S(1)} collective-permute-done((bf16[48,384]{1,0:T(8,128)(2,1)S(1)}, bf16[48,384]{1,0:T(8,128)(2,1)S(1)}, u32[]{:S(2)}, u32[]{:S(2)}) %collective-permute-start.2) | collective-permute-done | bytes 36896 | tf_op jit(solution)/shard_map/ppermute | solution.py:561
  17.7 3.6 %collective-permute-start.5 = (bf16[256,1024]{1,0:T(8,128)(2,1)S(1)}, bf16[256,1024]{1,0:T(8,128)(2,1)S(1)}, u32[]{:S(2)}, u32[]{:S(2)}) collective-permute-start(bf16[256,1024]{1,0:T(8,128)(2,1)S(1)} %collective-permute-done.refs_1_), channel_id=1, source_target_pairs={{1,2},{2,3},{5,6},{6,7},{9,10},{10,11},{13,14},{14,15},{17,18},{18... | collective-permute-start | bytes 1572872 | tf_op jit(solution)/shard_map/ppermute | solution.py:585
  21.3 1.9 %collective-permute-start.6 = (bf16[256,1024]{1,0:T(8,128)(2,1)S(1)}, bf16[256,1024]{1,0:T(8,128)(2,1)S(1)}, u32[]{:S(2)}, u32[]{:S(2)}) collective-permute-start(bf16[256,1024]{1,0:T(8,128)(2,1)S(1)} %collective-permute-done.1.refs_2_), channel_id=1, source_target_pairs={{2,1},{1,0},{6,5},{5,4},{10,9},{9,8},{14,13},{13,12},{18,17},{17,1... | collective-permute-start | bytes 1572872 | tf_op jit(solution)/shard_map/ppermute | solution.py:586
  23.2 3.6 %collective-permute-start.13 = (bf16[4,48,384]{2,1,0:T(8,128)(2,1)S(1)}, bf16[4,48,384]{2,1,0:T(8,128)(2,1)S(1)}, u32[]{:S(2)}, u32[]{:S(2)}) collective-permute-start(bf16[4,48,384]{2,1,0:T(8,128)(2,1)S(1)} %arrange.1.refs_5_.packed_ref.refs_7_), channel_id=1, source_target_pairs={{0,28},{4,0},{8,4},{12,8},{16,12},{20,16},{24,20},{28,24},{1,29},{... | collective-permute-start | bytes 442376 | tf_op jit(solution)/shard_map/ppermute | solution.py:572
  26.8 2.2 %collective-permute-start.12 = (bf16[4,48,384]{2,1,0:T(8,128)(2,1)S(1)}, bf16[4,48,384]{2,1,0:T(8,128)(2,1)S(1)}, u32[]{:S(2)}, u32[]{:S(2)}) collective-permute-start(bf16[4,48,384]{2,1,0:T(8,128)(2,1)S(1)} %arrange.1.refs_5_.packed_ref.refs_7_), channel_id=1, source_target_pairs={{0,24},{4,28},{8,0},{12,4},{16,8},{20,12},{24,16},{28,20},{1,25},{... | collective-permute-start | bytes 442376 | tf_op jit(solution)/shard_map/ppermute | solution.py:572
  29.5 3.1 %collective-permute-done.13.refs_14_ = bf16[4,48,384]{2,1,0:T(8,128)(2,1)S(1)} collective-permute-done((bf16[4,48,384]{2,1,0:T(8,128)(2,1)S(1)}, bf16[4,48,384]{2,1,0:T(8,128)(2,1)S(1)}, u32[]{:S(2)}, u32[]{:S(2)}) %collective-permute-start.13) | collective-permute-done | bytes 147488 | tf_op jit(solution)/shard_map/ppermute | solution.py:572
  33.8 3.4 %collective-permute-start.9 = (bf16[4,48,384]{2,1,0:T(8,128)(2,1)S(1)}, bf16[4,48,384]{2,1,0:T(8,128)(2,1)S(1)}, u32[]{:S(2)}, u32[]{:S(2)}) collective-permute-start(bf16[4,48,384]{2,1,0:T(8,128)(2,1)S(1)} %arrange.1.refs_5_.packed_ref.refs_7_), channel_id=1, source_target_pairs={{0,12},{4,16},{8,20},{12,24},{16,28},{20,0},{24,4},{28,8},{1,13},{... | collective-permute-start | bytes 442376 | tf_op jit(solution)/shard_map/ppermute | solution.py:572
  37.3 2.5 %collective-permute-start.8 = (bf16[4,48,384]{2,1,0:T(8,128)(2,1)S(1)}, bf16[4,48,384]{2,1,0:T(8,128)(2,1)S(1)}, u32[]{:S(2)}, u32[]{:S(2)}) collective-permute-start(bf16[4,48,384]{2,1,0:T(8,128)(2,1)S(1)} %arrange.1.refs_5_.packed_ref.refs_7_), channel_id=1, source_target_pairs={{0,8},{4,12},{8,16},{12,20},{16,24},{20,28},{24,0},{28,4},{1,9},{5... | collective-permute-start | bytes 442376 | tf_op jit(solution)/shard_map/ppermute | solution.py:572
  39.8 3.7 %collective-permute-start.7 = (bf16[4,48,384]{2,1,0:T(8,128)(2,1)S(1)}, bf16[4,48,384]{2,1,0:T(8,128)(2,1)S(1)}, u32[]{:S(2)}, u32[]{:S(2)}) collective-permute-start(bf16[4,48,384]{2,1,0:T(8,128)(2,1)S(1)} %arrange.1.refs_5_.packed_ref.refs_7_), channel_id=1, source_target_pairs={{0,4},{4,8},{8,12},{12,16},{16,20},{20,24},{24,28},{28,0},{1,5},{5... | collective-permute-start | bytes 442376 | tf_op jit(solution)/shard_map/ppermute | solution.py:572
  43.5 1.3 %collective-permute-done.9.refs_10_ = bf16[4,48,384]{2,1,0:T(8,128)(2,1)S(1)} collective-permute-done((bf16[4,48,384]{2,1,0:T(8,128)(2,1)S(1)}, bf16[4,48,384]{2,1,0:T(8,128)(2,1)S(1)}, u32[]{:S(2)}, u32[]{:S(2)}) %collective-permute-start.9) | collective-permute-done | bytes 147488 | tf_op jit(solution)/shard_map/ppermute | solution.py:572
  47.7 1.9 %copy-done = bf16[1,1024,1536]{2,1,0:T(8,128)(2,1)S(1)} copy-done((bf16[1,1024,1536]{2,1,0:T(8,128)(2,1)S(1)}, bf16[1,1024,1536]{2,1,0:T(8,128)(2,1)}, u32[]{:S(2)}) %copy-start) | copy-done | bytes 3145752
  51.3 11.8 %early_rows.1 = (bf16[1024,1536]{1,0:T(8,128)(2,1)S(1)}, f32[1024,512]{1,0:T(8,128)S(1)}, f32[1024,128]{1,0:T(8,128)S(1)}, f32[512,128]{1,0:T(8,128)S(1)}) custom-call(bf16[256,1024]{1,0:T(8,128)(2,1)S(1)} %copy-done.3, bf16[256,1024]{1,0:T(8,128)(2,1)S(1)} %collective-permute-done.refs_1_, bf16[256,1024]{1,0:T(8,128)(2,1)S(1)} %collective-permute-done.1.refs_2_, ...), custom_call_target="tpu_custom_call" | custom-call | flops 3221225472 | bytes 10485760 | tf_op jit(solution)/shard_map/early_rows/pallas_call | solution.py:595
  64.1 3.0 %window_project.1 = (bf16[1024,384]{1,0:T(8,128)(2,1)S(1)}, bf16[512,256]{1,0:T(8,128)(2,1)S(1)}, bf16[1024,384]{1,0:T(8,128)(2,1)}) custom-call(bf16[256,1024]{1,0:T(8,128)(2,1)S(1)} %copy-done.3, bf16[256,1024]{1,0:T(8,128)(2,1)S(1)} %collective-permute-done.refs_1_, bf16[256,1024]{1,0:T(8,128)(2,1)S(1)} %collective-permute-done.1.refs_2_, ...), custom_call_target="tpu_custom_call" | custom-call | flops 805306368 | bytes 5242880 | tf_op jit(solution)/shard_map/window_project/pallas_call | solution.py:616
  67.0 3.5 %collective-permute-start.16 = (bf16[512,256]{1,0:T(8,128)(2,1)S(1)}, bf16[512,256]{1,0:T(8,128)(2,1)S(1)}, u32[]{:S(2)}, u32[]{:S(2)}) collective-permute-start(bf16[512,256]{1,0:T(8,128)(2,1)S(1)} %get-tuple-element.65), channel_id=1, source_target_pairs={{0,4},{4,8},{8,12},{12,16},{16,20},{20,24},{24,28},{1,5},{5,9},{9,... | collective-permute-start | bytes 786440 | tf_op jit(solution)/shard_map/ppermute | solution.py:21
  71.2 6.4 %collective-permute-done.18.got_ref = bf16[512,128]{1,0:T(8,128)(2,1)S(1)} collective-permute-done((bf16[512,128]{1,0:T(8,128)(2,1)S(1)}, bf16[512,128]{1,0:T(8,128)(2,1)S(1)}, u32[]{:S(2)}, u32[]{:S(2)}) %collective-permute-start.18) | collective-permute-done | bytes 131104 | tf_op jit(solution)/shard_map/ppermute | solution.py:528
  78.3 1.5 %collective-permute-start.19 = (bf16[512,128]{1,0:T(8,128)(2,1)S(1)}, bf16[512,128]{1,0:T(8,128)(2,1)S(1)}, u32[]{:S(2)}, u32[]{:S(2)}) collective-permute-start(bf16[512,128]{1,0:T(8,128)(2,1)S(1)} %get-tuple-element.72), channel_id=1, source_target_pairs={{0,16},{4,20},{8,24},{12,28},{1,17},{5,21},{9,25},{13,29},{2,18},{... | collective-permute-start | bytes 393224 | tf_op jit(solution)/shard_map/ppermute | solution.py:534
  79.9 2.3 %window_attend.1.refs_6_ = f32[1024,128]{1,0:T(8,128)S(1)} custom-call(bf16[1024,384]{1,0:T(8,128)(2,1)S(1)} %get-tuple-element.64.win_ref, bf16[512,256]{1,0:T(8,128)(2,1)S(1)} %collective-permute-done.16.halo_ref), custom_call_target="tpu_custom_call" | custom-call | flops 402653184 | bytes 3145728 | tf_op jit(solution)/shard_map/window_attend/pallas_call | solution.py:631
  84.5 1.4 %collective-permute-start.21 = (bf16[256,512]{1,0:T(8,128)(2,1)S(1)}, bf16[256,512]{1,0:T(8,128)(2,1)S(1)}, u32[]{:S(2)}, u32[]{:S(2)}) collective-permute-start(bf16[256,512]{1,0:T(8,128)(2,1)S(1)} %finish1.1), channel_id=1, source_target_pairs={{0,1},{1,2},{2,3},{3,0},{4,5},{5,6},{6,7},{7,4},{8,9},{9,10},{10,1... | collective-permute-start | bytes 786440 | tf_op jit(solution)/shard_map/ppermute | solution.py:657
  88.1 7.4 %collective-permute-done.20.refs_1_ = bf16[256,512]{1,0:T(8,128)(2,1)S(1)} collective-permute-done((bf16[256,512]{1,0:T(8,128)(2,1)S(1)}, bf16[256,512]{1,0:T(8,128)(2,1)S(1)}, u32[]{:S(2)}, u32[]{:S(2)}) %collective-permute-start.20) | collective-permute-done | bytes 262176 | tf_op jit(solution)/shard_map/ppermute | solution.py:657
  95.5 11.2 %collective-permute-done.21.refs_2_ = bf16[256,512]{1,0:T(8,128)(2,1)S(1)} collective-permute-done((bf16[256,512]{1,0:T(8,128)(2,1)S(1)}, bf16[256,512]{1,0:T(8,128)(2,1)S(1)}, u32[]{:S(2)}, u32[]{:S(2)}) %collective-permute-start.21) | collective-permute-done | bytes 262176 | tf_op jit(solution)/shard_map/ppermute | solution.py:657
  106.7 1.8 %collective-permute-done.22.refs_3_ = bf16[256,512]{1,0:T(8,128)(2,1)S(1)} collective-permute-done((bf16[256,512]{1,0:T(8,128)(2,1)S(1)}, bf16[256,512]{1,0:T(8,128)(2,1)S(1)}, u32[]{:S(2)}, u32[]{:S(2)}) %collective-permute-start.22) | collective-permute-done | bytes 262176 | tf_op jit(solution)/shard_map/ppermute | solution.py:657
  (48 shorter events, 17.1 us)
Async XLA Ops:
  0.0 17.6 %collective-permute-start.1 = (bf16[256,1024]{1,0:T(8,128)(2,1)}, bf16[256,1024]{1,0:T(8,128)(2,1)S(1)}, u32[]{:S(2)}, u32[]{:S(2)}) collective-permute-start(bf16[256,1024]{1,0:T(8,128)(2,1)} %refs_0_.3), channel_id=1, source_target_pairs={{3,2},{2,1},{1,0},{7,6},{6,5},{5,4},{11,10},{10,9},{9,8},{15,14},{... | collective-permute-start | bytes 1572872 | tf_op jit(solution)/shard_map/ppermute | solution.py:586
  1.9 15.7 %collective-permute-start = (bf16[256,1024]{1,0:T(8,128)(2,1)}, bf16[256,1024]{1,0:T(8,128)(2,1)S(1)}, u32[]{:S(2)}, u32[]{:S(2)}) collective-permute-start(bf16[256,1024]{1,0:T(8,128)(2,1)} %refs_0_.3), channel_id=1, source_target_pairs={{0,1},{1,2},{2,3},{4,5},{5,6},{6,7},{8,9},{9,10},{10,11},{12,13},{... | collective-permute-start | bytes 1572872 | tf_op jit(solution)/shard_map/ppermute | solution.py:585
  7.3 10.4 %collective-permute-start.2 = (bf16[48,384]{1,0:T(8,128)(2,1)S(1)}, bf16[48,384]{1,0:T(8,128)(2,1)S(1)}, u32[]{:S(2)}, u32[]{:S(2)}) collective-permute-start(bf16[48,384]{1,0:T(8,128)(2,1)S(1)} %get-tuple-element.40), channel_id=1, source_target_pairs={{0,1},{1,2},{2,3},{3,0},{4,5},{5,6},{6,7},{7,4},{8,9},{9,10},{10,1... | collective-permute-start | bytes 110600 | tf_op jit(solution)/shard_map/ppermute | solution.py:561
  8.6 9.0 %collective-permute-start.3 = (bf16[48,384]{1,0:T(8,128)(2,1)S(1)}, bf16[48,384]{1,0:T(8,128)(2,1)S(1)}, u32[]{:S(2)}, u32[]{:S(2)}) collective-permute-start(bf16[48,384]{1,0:T(8,128)(2,1)S(1)} %get-tuple-element.41), channel_id=1, source_target_pairs={{0,2},{1,3},{2,0},{3,1},{4,6},{5,7},{6,4},{7,5},{8,10},{9,11},{10,... | collective-permute-start | bytes 110600 | tf_op jit(solution)/shard_map/ppermute | solution.py:561
  9.4 8.2 %collective-permute-start.4 = (bf16[48,384]{1,0:T(8,128)(2,1)S(1)}, bf16[48,384]{1,0:T(8,128)(2,1)S(1)}, u32[]{:S(2)}, u32[]{:S(2)}) collective-permute-start(bf16[48,384]{1,0:T(8,128)(2,1)S(1)} %get-tuple-element.42), channel_id=1, source_target_pairs={{0,3},{1,0},{2,1},{3,2},{4,7},{5,4},{6,5},{7,6},{8,11},{9,8},{10,9... | collective-permute-start | bytes 110600 | tf_op jit(solution)/shard_map/ppermute | solution.py:561
  17.7 28.0 %collective-permute-start.5 = (bf16[256,1024]{1,0:T(8,128)(2,1)S(1)}, bf16[256,1024]{1,0:T(8,128)(2,1)S(1)}, u32[]{:S(2)}, u32[]{:S(2)}) collective-permute-start(bf16[256,1024]{1,0:T(8,128)(2,1)S(1)} %collective-permute-done.refs_1_), channel_id=1, source_target_pairs={{1,2},{2,3},{5,6},{6,7},{9,10},{10,11},{13,14},{14,15},{17,18},{18... | collective-permute-start | bytes 1572872 | tf_op jit(solution)/shard_map/ppermute | solution.py:585
  21.3 24.3 %collective-permute-start.6 = (bf16[256,1024]{1,0:T(8,128)(2,1)S(1)}, bf16[256,1024]{1,0:T(8,128)(2,1)S(1)}, u32[]{:S(2)}, u32[]{:S(2)}) collective-permute-start(bf16[256,1024]{1,0:T(8,128)(2,1)S(1)} %collective-permute-done.1.refs_2_), channel_id=1, source_target_pairs={{2,1},{1,0},{6,5},{5,4},{10,9},{9,8},{14,13},{13,12},{18,17},{17,1... | collective-permute-start | bytes 1572872 | tf_op jit(solution)/shard_map/ppermute | solution.py:586
  23.2 9.4 %collective-permute-start.13 = (bf16[4,48,384]{2,1,0:T(8,128)(2,1)S(1)}, bf16[4,48,384]{2,1,0:T(8,128)(2,1)S(1)}, u32[]{:S(2)}, u32[]{:S(2)}) collective-permute-start(bf16[4,48,384]{2,1,0:T(8,128)(2,1)S(1)} %arrange.1.refs_5_.packed_ref.refs_7_), channel_id=1, source_target_pairs={{0,28},{4,0},{8,4},{12,8},{16,12},{20,16},{24,20},{28,24},{1,29},{... | collective-permute-start | bytes 442376 | tf_op jit(solution)/shard_map/ppermute | solution.py:572
  26.8 7.0 %collective-permute-start.12 = (bf16[4,48,384]{2,1,0:T(8,128)(2,1)S(1)}, bf16[4,48,384]{2,1,0:T(8,128)(2,1)S(1)}, u32[]{:S(2)}, u32[]{:S(2)}) collective-permute-start(bf16[4,48,384]{2,1,0:T(8,128)(2,1)S(1)} %arrange.1.refs_5_.packed_ref.refs_7_), channel_id=1, source_target_pairs={{0,24},{4,28},{8,0},{12,4},{16,8},{20,12},{24,16},{28,20},{1,25},{... | collective-permute-start | bytes 442376 | tf_op jit(solution)/shard_map/ppermute | solution.py:572
  29.0 8.2 %collective-permute-start.11 = (bf16[4,48,384]{2,1,0:T(8,128)(2,1)S(1)}, bf16[4,48,384]{2,1,0:T(8,128)(2,1)S(1)}, u32[]{:S(2)}, u32[]{:S(2)}) collective-permute-start(bf16[4,48,384]{2,1,0:T(8,128)(2,1)S(1)} %arrange.1.refs_5_.packed_ref.refs_7_), channel_id=1, source_target_pairs={{0,20},{4,24},{8,28},{12,0},{16,4},{20,8},{24,12},{28,16},{1,21},{... | collective-permute-start | bytes 442376 | tf_op jit(solution)/shard_map/ppermute | solution.py:572
  32.6 7.2 %collective-permute-start.10 = (bf16[4,48,384]{2,1,0:T(8,128)(2,1)S(1)}, bf16[4,48,384]{2,1,0:T(8,128)(2,1)S(1)}, u32[]{:S(2)}, u32[]{:S(2)}) collective-permute-start(bf16[4,48,384]{2,1,0:T(8,128)(2,1)S(1)} %arrange.1.refs_5_.packed_ref.refs_7_), channel_id=1, source_target_pairs={{0,16},{4,20},{8,24},{12,28},{16,0},{20,4},{24,8},{28,12},{1,17},{... | collective-permute-start | bytes 442376 | tf_op jit(solution)/shard_map/ppermute | solution.py:572
  33.8 11.0 %collective-permute-start.9 = (bf16[4,48,384]{2,1,0:T(8,128)(2,1)S(1)}, bf16[4,48,384]{2,1,0:T(8,128)(2,1)S(1)}, u32[]{:S(2)}, u32[]{:S(2)}) collective-permute-start(bf16[4,48,384]{2,1,0:T(8,128)(2,1)S(1)} %arrange.1.refs_5_.packed_ref.refs_7_), channel_id=1, source_target_pairs={{0,12},{4,16},{8,20},{12,24},{16,28},{20,0},{24,4},{28,8},{1,13},{... | collective-permute-start | bytes 442376 | tf_op jit(solution)/shard_map/ppermute | solution.py:572
  37.3 7.6 %collective-permute-start.8 = (bf16[4,48,384]{2,1,0:T(8,128)(2,1)S(1)}, bf16[4,48,384]{2,1,0:T(8,128)(2,1)S(1)}, u32[]{:S(2)}, u32[]{:S(2)}) collective-permute-start(bf16[4,48,384]{2,1,0:T(8,128)(2,1)S(1)} %arrange.1.refs_5_.packed_ref.refs_7_), channel_id=1, source_target_pairs={{0,8},{4,12},{8,16},{12,20},{16,24},{20,28},{24,0},{28,4},{1,9},{5... | collective-permute-start | bytes 442376 | tf_op jit(solution)/shard_map/ppermute | solution.py:572
  39.8 5.8 %collective-permute-start.7 = (bf16[4,48,384]{2,1,0:T(8,128)(2,1)S(1)}, bf16[4,48,384]{2,1,0:T(8,128)(2,1)S(1)}, u32[]{:S(2)}, u32[]{:S(2)}) collective-permute-start(bf16[4,48,384]{2,1,0:T(8,128)(2,1)S(1)} %arrange.1.refs_5_.packed_ref.refs_7_), channel_id=1, source_target_pairs={{0,4},{4,8},{8,12},{12,16},{16,20},{20,24},{24,28},{28,0},{1,5},{5... | collective-permute-start | bytes 442376 | tf_op jit(solution)/shard_map/ppermute | solution.py:572
  45.6 17.4 %collective-permute-start.14 = (bf16[256,1024]{1,0:T(8,128)(2,1)S(1)}, bf16[256,1024]{1,0:T(8,128)(2,1)S(1)}, u32[]{:S(2)}, u32[]{:S(2)}) collective-permute-start(bf16[256,1024]{1,0:T(8,128)(2,1)S(1)} %collective-permute-done.5.refs_3_), channel_id=1, source_target_pairs={{2,3},{6,7},{10,11},{14,15},{18,19},{22,23},{26,27},{30,31}} | collective-permute-start | bytes 1572872 | tf_op jit(solution)/shard_map/ppermute | solution.py:585
  46.3 16.8 %collective-permute-start.15 = (bf16[256,1024]{1,0:T(8,128)(2,1)S(1)}, bf16[256,1024]{1,0:T(8,128)(2,1)S(1)}, u32[]{:S(2)}, u32[]{:S(2)}) collective-permute-start(bf16[256,1024]{1,0:T(8,128)(2,1)S(1)} %collective-permute-done.6.refs_4_), channel_id=1, source_target_pairs={{1,0},{5,4},{9,8},{13,12},{17,16},{21,20},{25,24},{29,28}} | collective-permute-start | bytes 1572872 | tf_op jit(solution)/shard_map/ppermute | solution.py:586
  51.3 11.8 %copy-start.1 = (bf16[1,1024,1536]{2,1,0:T(8,128)(2,1)S(1)}, bf16[1,1024,1536]{2,1,0:T(8,128)(2,1)}, u32[]{:S(2)}) copy-start(bf16[1,1024,1536]{2,1,0:T(8,128)(2,1)} %param.8) | copy-start | bytes 9437188
  63.1 7.4 %collective-permute-start.17 = (bf16[512,128]{1,0:T(8,128)(2,1)S(1)}, bf16[512,128]{1,0:T(8,128)(2,1)S(1)}, u32[]{:S(2)}, u32[]{:S(2)}) collective-permute-start(bf16[512,128]{1,0:T(8,128)(2,1)S(1)} %get-tuple-element.66), channel_id=1, source_target_pairs={{0,4},{4,0},{8,12},{12,8},{16,20},{20,16},{24,28},{28,24},{1,5},{5... | collective-permute-start | bytes 393224 | tf_op jit(solution)/shard_map/ppermute | solution.py:528
  67.0 12.8 %collective-permute-start.16 = (bf16[512,256]{1,0:T(8,128)(2,1)S(1)}, bf16[512,256]{1,0:T(8,128)(2,1)S(1)}, u32[]{:S(2)}, u32[]{:S(2)}) collective-permute-start(bf16[512,256]{1,0:T(8,128)(2,1)S(1)} %get-tuple-element.65), channel_id=1, source_target_pairs={{0,4},{4,8},{8,12},{12,16},{16,20},{20,24},{24,28},{1,5},{5,9},{9,... | collective-permute-start | bytes 786440 | tf_op jit(solution)/shard_map/ppermute | solution.py:21
  70.6 6.9 %collective-permute-start.18 = (bf16[512,128]{1,0:T(8,128)(2,1)S(1)}, bf16[512,128]{1,0:T(8,128)(2,1)S(1)}, u32[]{:S(2)}, u32[]{:S(2)}) collective-permute-start(bf16[512,128]{1,0:T(8,128)(2,1)S(1)} %get-tuple-element.68), channel_id=1, source_target_pairs={{0,8},{4,12},{8,0},{12,4},{16,24},{20,28},{24,16},{28,20},{1,9},{5... | collective-permute-start | bytes 393224 | tf_op jit(solution)/shard_map/ppermute | solution.py:528
  78.3 4.7 %collective-permute-start.19 = (bf16[512,128]{1,0:T(8,128)(2,1)S(1)}, bf16[512,128]{1,0:T(8,128)(2,1)S(1)}, u32[]{:S(2)}, u32[]{:S(2)}) collective-permute-start(bf16[512,128]{1,0:T(8,128)(2,1)S(1)} %get-tuple-element.72), channel_id=1, source_target_pairs={{0,16},{4,20},{8,24},{12,28},{1,17},{5,21},{9,25},{13,29},{2,18},{... | collective-permute-start | bytes 393224 | tf_op jit(solution)/shard_map/ppermute | solution.py:534
  83.5 12.0 %collective-permute-start.20 = (bf16[256,512]{1,0:T(8,128)(2,1)S(1)}, bf16[256,512]{1,0:T(8,128)(2,1)S(1)}, u32[]{:S(2)}, u32[]{:S(2)}) collective-permute-start(bf16[256,512]{1,0:T(8,128)(2,1)S(1)} %finish2.1), channel_id=1, source_target_pairs={{0,2},{1,3},{2,0},{3,1},{4,6},{5,7},{6,4},{7,5},{8,10},{9,11},{10,... | collective-permute-start | bytes 786440 | tf_op jit(solution)/shard_map/ppermute | solution.py:657
  84.5 22.2 %collective-permute-start.21 = (bf16[256,512]{1,0:T(8,128)(2,1)S(1)}, bf16[256,512]{1,0:T(8,128)(2,1)S(1)}, u32[]{:S(2)}, u32[]{:S(2)}) collective-permute-start(bf16[256,512]{1,0:T(8,128)(2,1)S(1)} %finish1.1), channel_id=1, source_target_pairs={{0,1},{1,2},{2,3},{3,0},{4,5},{5,6},{6,7},{7,4},{8,9},{9,10},{10,1... | collective-permute-start | bytes 786440 | tf_op jit(solution)/shard_map/ppermute | solution.py:657
  86.4 22.1 %collective-permute-start.22 = (bf16[256,512]{1,0:T(8,128)(2,1)S(1)}, bf16[256,512]{1,0:T(8,128)(2,1)S(1)}, u32[]{:S(2)}, u32[]{:S(2)}) collective-permute-start(bf16[256,512]{1,0:T(8,128)(2,1)S(1)} %finish3.1), channel_id=1, source_target_pairs={{0,3},{1,0},{2,1},{3,2},{4,7},{5,4},{6,5},{7,6},{8,11},{9,8},{10,9... | collective-permute-start | bytes 786440 | tf_op jit(solution)/shard_map/ppermute | solution.py:657
  (5 other events, 5.4 us)

commit v6 on v5

--- a/solution.py
+++ b/solution.py
@@ -203,10 +203,20 @@
 
 
 def arrange_body(*refs):
+    pieces, (routes_ref, rows_ref) = refs[:-2], refs[-2:]
+    mine = lax.axis_index("mem")
+    cut = rows_ref.shape[1]
+    for shift, piece_ref in enumerate(pieces):
+        origin = lax.rem(mine + len(pieces) - shift, len(pieces))
+        rows_ref[origin] = piece_ref[0:cut, :]
+        routes_ref[origin] = piece_ref[cut:, :]
+
+
+def combine_body(*refs):
     pieces, out_ref = refs[:-1], refs[-1]
-    mine = lax.axis_index("mem")
+    chip = lax.axis_index("ctx") // 2
     for shift, piece_ref in enumerate(pieces):
-        out_ref[lax.rem(mine + len(pieces) - shift, len(pieces))] = piece_ref[...]
+        out_ref[lax.rem(chip + len(pieces) - shift, len(pieces))] = piece_ref[...]
 
 
 def as_column(row, count):
@@ -217,9 +227,8 @@
 
 
 def members(group, packed_ref, count):
-    cut = packed_ref.shape[1] - ROUTE_ROWS
     mine = lax.axis_index("mem").astype(jnp.float32)
-    named = packed_ref[group, cut : cut + ROUTE_ROWS, 0:count].astype(jnp.float32)
+    named = packed_ref[group, :, 0:count].astype(jnp.float32)
     first = as_column(named[0:1, :], count)
     second = as_column(named[1:2, :], count)
     return first, second, first == mine, second == mine
@@ -274,23 +283,29 @@
     return slice((part * HEADS + head) * HDIM, (part * HEADS + head + 1) * HDIM)
 
 
-def early_body(n_mem, hops, *refs):
-    slots = 1 + 2 * hops
+def arrivals_body(n_mem, first_slot, last_slot, with_intra, *refs):
+    slots = last_slot - first_slot
     sources = refs[:slots]
-    packed_ref, router_ref, weight_ref = refs[slots : slots + 3]
-    proj_ref, intra_ref, coef_ref, state_ref = refs[slots + 3 :]
+    routes_ref, router_ref, weight_ref = refs[slots : slots + 3]
+    rest = refs[slots + 3 :]
+    outs = 4 if with_intra else 3
+    before, after = rest[:-outs], rest[-outs:]
+    proj_ref, coef_ref, state_ref = after[:3]
     count = sources[0].shape[0]
-    width = HEADS * HDIM
     mine = lax.axis_index("mem")
-    state_ref[...] = jnp.zeros_like(state_ref)
-    for slot in range(slots):
+    if before:
+        for old_ref, new_ref in zip(before, after):
+            new_ref[...] = old_ref[...]
+    else:
+        state_ref[...] = jnp.zeros_like(state_ref)
+    for slot in range(first_slot, last_slot):
         group = slot_group(slot)
 
         @pl.when(in_line(group, n_mem))
         def _(slot=slot, group=group):
             place = rows_of(group, count)
-            tokens = sources[slot][...]
-            first, second, is_first, is_second = members(group, packed_ref, count)
+            tokens = sources[slot - first_slot][...]
+            first, second, is_first, is_second = members(group, routes_ref, count)
             projected = jnp.dot(tokens, weight_ref[...], preferred_element_type=jnp.float32)
             projected = jnp.where(is_first | is_second, projected, 0.0).astype(jnp.bfloat16)
             proj_ref[place, :] = projected
@@ -301,6 +316,11 @@
                 state_ref[head_columns(head), :] += outer_sum(
                     projected[:, head_columns(head, 1)], projected[:, head_columns(head, 2)]
                 )
+
+    if not with_intra:
+        return
+    intra_ref = after[3]
+    hops = last_slot // 2
 
     def present(group):
         return jnp.abs(mine - group) <= hops
@@ -400,28 +420,35 @@
                 )
 
 
-def window_project_body(n_mem, n_ctx, *refs):
-    slots = 2 * n_mem - 1
-    sources, pieces = refs[:slots], refs[slots : slots + n_ctx]
-    win_ref, tail_ref, full_ref = refs[slots + n_ctx :]
-    origins, depth, _ = pieces[0].shape
-    depth = depth - ROUTE_ROWS
+def project_slots(n_mem, first_slot, sources, full_ref, win_ref):
     count = sources[0].shape[0]
-    my_ctx = lax.axis_index("ctx")
-    for shift, piece_ref in enumerate(pieces):
-        piece = lax.rem(my_ctx + n_ctx - shift, n_ctx)
+    for index, source_ref in enumerate(sources):
+        group = slot_group(first_slot + index)
+
+        @pl.when(in_line(group, n_mem))
+        def _(source_ref=source_ref, group=group):
+            win_ref[rows_of(group, count), :] = jnp.dot(
+                source_ref[...], full_ref[...], preferred_element_type=jnp.float32
+            ).astype(jnp.bfloat16)
+
+
+def window_early_body(n_mem, *refs):
+    sources, (mine_ref, other_ref, win_ref, full_ref) = refs[:-4], refs[-4:]
+    chips, origins, depth, _ = mine_ref.shape
+    core = lax.rem(lax.axis_index("ctx"), 2)
+    for pieces_ref, at in ((mine_ref, core), (other_ref, 1 - core)):
         for origin in range(origins):
-            full_ref[rows_of(origin * n_ctx + piece, depth), :] = piece_ref[origin, 0:depth, :]
-    for slot in range(slots):
-        group = slot_group(slot)
-
-        @pl.when(in_line(group, n_mem))
-        def _(slot=slot, group=group):
-            win_ref[rows_of(group, count), :] = jnp.dot(
-                sources[slot][...], full_ref[...], preferred_element_type=jnp.float32
-            ).astype(jnp.bfloat16)
-
-    total = n_mem * count
+            for chip in range(chips):
+                start = (origin * chips + chip) * 2 + at
+                full_ref[rows_of(start, depth), :] = pieces_ref[chip, origin]
+    project_slots(n_mem, 0, sources, full_ref, win_ref)
+
+
+def window_late_body(n_mem, first_slot, *refs):
+    sources, (full_ref, before_ref, win_ref, tail_ref) = refs[:-4], refs[-4:]
+    win_ref[...] = before_ref[...]
+    project_slots(n_mem, first_slot, sources, full_ref, win_ref)
+    total = win_ref.shape[0]
     tail_ref[...] = win_ref[total - WINDOW : total, HDIM:]
 
 
@@ -561,65 +588,91 @@
         lax.ppermute(packed[s], "mem", [(i, (i + s) % n_mem) for i in range(n_mem)])
         for s in range(1, n_mem)
     ]
-    packed = kernel_call(
+    all_routes, own_rows = kernel_call(
         arrange_body,
         "arrange",
-        jax.ShapeDtypeStruct((n_mem,) + packed[0].shape, low),
+        (
+            jax.ShapeDtypeStruct((n_mem, ROUTE_ROWS, 3 * HDIM), low),
+            jax.ShapeDtypeStruct((n_mem, cut, 3 * HDIM), low),
+        ),
         1 << 20,
         1 << 20,
     )(*packed)
-    pieces = [packed] + [
-        lax.ppermute(packed, "ctx", [(i, (i + s) % n_ctx) for i in range(n_ctx)])
-        for s in range(1, n_ctx)
-    ]
-
-    below, above = [tokens], [tokens]
-    for hop in range(1, n_mem):
+    chips = n_ctx // 2
+    of_core = kernel_call(
+        combine_body,
+        "combine",
+        jax.ShapeDtypeStruct((chips,) + own_rows.shape, low),
+        1 << 20,
+        1 << 20,
+    )(
+        own_rows,
+        *[
+            lax.ppermute(own_rows, "ctx", [(i, (i + 2 * s) % n_ctx) for i in range(n_ctx)])
+            for s in range(1, chips)
+        ],
+    )
+    weight = mem_weight[0]
+    router_rows = router.T
+    given = (all_routes, router_rows, weight)
+    project_flops = 2 * count * depth * 3 * width
+    kept = (shape(total, 3 * width), shape(total, HDIM, full), shape(width, HDIM, full))
+
+    def moved(hop, from_below, from_above):
         up = [(i, i + 1) for i in range(hop - 1, n_mem - 1)]
         down = [(n_mem - 1 - i, n_mem - 1 - j) for i, j in up]
-        from_below, from_above = below[-1], above[-1]
+        return lax.ppermute(from_below, "mem", up), lax.ppermute(from_above, "mem", down)
+
+    slots = [tokens]
+    below, above = moved(1, tokens, tokens)
+    slots += [below, above]
+    below, above, own_rows = lax.optimization_barrier((below, above, own_rows))
+    held = kernel_call(
+        functools.partial(arrivals_body, n_mem, 0, 3, False),
+        "near_rows",
+        kept,
+        3 * project_flops,
+        6 << 20,
+    )(*slots, *given)
+    for hop in range(2, n_mem):
+        below, above = moved(hop, below, above)
+        slots += [below, above]
         if hop == 2:
-            from_below, from_above, packed = lax.optimization_barrier((from_below, from_above, packed))
-        if hop == 3:
-            from_below, from_above, pieces = lax.optimization_barrier((from_below, from_above, pieces))
-        below.append(lax.ppermute(from_below, "mem", up))
-        above.append(lax.ppermute(from_above, "mem", down))
-    slots = [tokens]
-    for hop in range(1, n_mem):
-        slots += [below[hop], above[hop]]
-
-    weight = mem_weight[0]
-    router_rows = router.T
+            below, above, of_core, *held = lax.optimization_barrier((below, above, of_core, *held))
+    other_core = lax.ppermute(of_core, "ctx", [(i, i ^ 1) for i in range(n_ctx)])
     hops = n_mem - 2
     early = 1 + 2 * hops
-    proj, intra, coef, state = kernel_call(
-        functools.partial(early_body, n_mem, hops),
-        "early_rows",
-        (
-            shape(total, 3 * width),
-            shape(total, width, full),
-            shape(total, HDIM, full),
-            shape(width, HDIM, full),
-        ),
-        2 * total * depth * 3 * width,
-        10 << 20,
-    )(*slots[:early], packed, router_rows, weight)
+    proj, coef, state, intra = kernel_call(
+        functools.partial(arrivals_body, n_mem, 3, early, True),
+        "middle_rows",
+        kept + (shape(total, width, full),),
+        3 * project_flops,
+        6 << 20,
+    )(*slots[3:early], *given, *held)
+    win, win_weight_full = kernel_call(
+        functools.partial(window_early_body, n_mem),
+        "window_early",
+        (shape(total, 3 * HDIM), shape(depth, 3 * HDIM)),
+        2 * total * depth * 3 * HDIM,
+        5 << 20,
+    )(*slots[:early], of_core, other_core)
+    state, win = lax.optimization_barrier((state, win))
     last_kv, state, sent = kernel_call(
         functools.partial(last_keys_body, n_mem),
         "last_keys",
         (shape(count, 2 * width), shape(width, HDIM, full), shape(width, HDIM)),
         2 * count * depth * 2 * width,
         3 << 20,
-    )(below[-1], above[-1], packed, weight, state)
+    )(below, above, all_routes, weight, state)
     prefix, got, bit = exclusive_prefix(state, sent)
 
-    win, tail, _ = kernel_call(
-        functools.partial(window_project_body, n_mem, n_ctx),
-        "window_project",
-        (shape(total, 3 * HDIM), shape(WINDOW, 2 * HDIM), shape(depth, 3 * HDIM)),
-        2 * total * depth * 3 * HDIM,
-        5 << 20,
-    )(*slots, *pieces)
+    win, tail = kernel_call(
+        functools.partial(window_late_body, n_mem, early),
+        "window_late",
+        (shape(total, 3 * HDIM), shape(WINDOW, 2 * HDIM)),
+        2 * count * depth * 3 * HDIM,
+        3 << 20,
+    )(below, above, win_weight_full, win)
     halo = passed_along(tail, "ctx", 1)
     last_query, last_coef, extra = kernel_call(
         functools.partial(last_queries_body, n_mem),
@@ -627,7 +680,7 @@
         (shape(count, width), shape(count, HDIM, full), shape(total, width, full)),
         8 * count * depth * width,
         8 << 20,
-    )(below[-1], above[-1], packed, router_rows, weight, proj, last_kv)
+    )(below, above, *given, proj, last_kv)
     window_part = kernel_call(
         functools.partial(window_attend_body, count),
         "window_attend",

time: 111 us -> 102 us (0.919)
  starting transfers between devices: 42.3 us -> 36.2 us
  waiting for transfers between devices: 40.6 us -> 38 us
    ppermute x13 -> x10, starting transfers between devices: 30 us -> 20 us  [the longest x3 7.32 us: moved(): lax.ppermute(from_below, 'mem', up)]
    ppermute x3, starting transfers between devices: 3.13 us -> 6.2 us  [dense_shards(): parts.append(lax.ppermute(finish(shift), 'mem', pairs))]
    ppermute x13 -> x10, waiting for transfers between devices: 5.2 us -> 2.63 us  [the longest x3 2.61 us: dense_shards(): lax.ppermute(own_rows, 'ctx', [(i, (i + 2 * s) % n_ctx) for i in range(n_...]
    ppermute x3, waiting for transfers between devices: 7.72 us -> 8.97 us  [dense_shards(): lax.ppermute(packed[s], 'mem', [(i, (i + s) % n_mem) for i in range(n_mem)])]
    ppermute x3, starting transfers between devices: 2.64 us -> 3.83 us  [dense_shards(): lax.ppermute(packed[s], 'mem', [(i, (i + s) % n_mem) for i in range(n_mem)])]
    pallas_call x3 -> x6, Pallas kernels: 14.8 us -> 14.2 us  [the longest x1 8.16 us: dense_shards(): kernel_call(functools.partial(arrivals_body, n_mem, 3, early, True), 'mid...]
    unnamed x12 -> x14, local copies, waits for them, and re-layouts: 5.43 us -> 5.44 us
  transfers between devices with their start and end apart: 23 -> 20, of which waited for: 9 -> 9; matrix products, arithmetic and copies ran while one was open for 0% -> 0% of each run, Pallas kernels for 18% -> 19%
where the time goes in v6:
time: 102 us; the launch traced here: 100 us
  waiting for transfers between devices  38 us (37%)
  starting transfers between devices  36.2 us (35%)
  Pallas kernels  20.2 us (20%)
  local copies, waits for them, and re-layouts  5.44 us (5%)
    ppermute x3, waiting for transfers between devices, dense_shards(): parts.append(lax.ppermute(finish(shift), 'mem', pairs))  20 us
    ppermute x3, waiting for transfers between devices, dense_shards(): lax.ppermute(packed[s], 'mem', [(i, (i + s) % n_mem) for i in range(n_mem)])  8.97 us
    pallas_call x1, Pallas kernels, dense_shards(): kernel_call(functools.partial(arrivals_body, n_mem, 3, early, True), 'mid...  8.16 us
    ppermute x3, starting transfers between devices, moved(): lax.ppermute(from_below, 'mem', up)  7.32 us
    ppermute x2, waiting for transfers between devices, exclusive_prefix(): got = lax.ppermute(sent, 'ctx', [(i, i ^ bit) for i in range(devices)])  6.41 us
    ppermute x3, starting transfers between devices, dense_shards(): parts.append(lax.ppermute(finish(shift), 'mem', pairs))  6.2 us
    unnamed x14, local copies, waits for them, and re-layouts  5.44 us
    ppermute x3, starting transfers between devices, moved(): lax.ppermute(from_above, 'mem', down)  5.35 us
  transfers between devices with their start and end apart: 20, of which 9 were waited for; matrix products, arithmetic and copies ran while one was open for 0% of the time, Pallas kernels for 19%

profile of v6, /device:TPU:9, one launch (start us, length us, event | category | flops | bytes accessed | tf_op | source)
XLA Modules:
  0.0 100.2 jit_solution(18389268168838854959)
XLA Ops:
  0.0 3.2 %collective-permute-start = (bf16[256,1024]{1,0:T(8,128)(2,1)}, bf16[256,1024]{1,0:T(8,128)(2,1)S(1)}, u32[]{:S(2)}, u32[]{:S(2)}) collective-permute-start(bf16[256,1024]{1,0:T(8,128)(2,1)} %refs_0_.3), channel_id=1, source_target_pairs={{0,1},{1,2},{2,3},{4,5},{5,6},{6,7},{8,9},{9,10},{10,11},{12,13},{... | collective-permute-start | bytes 1572872 | tf_op jit(solution)/shard_map/ppermute | solution.py:624
  3.2 2.1 %collective-permute-start.1 = (bf16[256,1024]{1,0:T(8,128)(2,1)}, bf16[256,1024]{1,0:T(8,128)(2,1)S(1)}, u32[]{:S(2)}, u32[]{:S(2)}) collective-permute-start(bf16[256,1024]{1,0:T(8,128)(2,1)} %refs_0_.3), channel_id=1, source_target_pairs={{3,2},{2,1},{1,0},{7,6},{6,5},{5,4},{11,10},{10,9},{9,8},{15,14},{... | collective-permute-start | bytes 1572872 | tf_op jit(solution)/shard_map/ppermute | solution.py:624
  7.3 1.3 %collective-permute-start.2 = (bf16[48,384]{1,0:T(8,128)(2,1)S(1)}, bf16[48,384]{1,0:T(8,128)(2,1)S(1)}, u32[]{:S(2)}, u32[]{:S(2)}) collective-permute-start(bf16[48,384]{1,0:T(8,128)(2,1)S(1)} %get-tuple-element.44), channel_id=1, source_target_pairs={{0,1},{1,2},{2,3},{3,0},{4,5},{5,6},{6,7},{7,4},{8,9},{9,10},{10,1... | collective-permute-start | bytes 110600 | tf_op jit(solution)/shard_map/ppermute | solution.py:588
  9.7 1.4 %collective-permute-start.4 = (bf16[48,384]{1,0:T(8,128)(2,1)S(1)}, bf16[48,384]{1,0:T(8,128)(2,1)S(1)}, u32[]{:S(2)}, u32[]{:S(2)}) collective-permute-start(bf16[48,384]{1,0:T(8,128)(2,1)S(1)} %get-tuple-element.46), channel_id=1, source_target_pairs={{0,3},{1,0},{2,1},{3,2},{4,7},{5,4},{6,5},{7,6},{8,11},{9,8},{10,9... | collective-permute-start | bytes 110600 | tf_op jit(solution)/shard_map/ppermute | solution.py:588
  11.1 4.6 %collective-permute-done.2.refs_1_ = bf16[48,384]{1,0:T(8,128)(2,1)S(1)} collective-permute-done((bf16[48,384]{1,0:T(8,128)(2,1)S(1)}, bf16[48,384]{1,0:T(8,128)(2,1)S(1)}, u32[]{:S(2)}, u32[]{:S(2)}) %collective-permute-start.2) | collective-permute-done | bytes 36896 | tf_op jit(solution)/shard_map/ppermute | solution.py:588
  15.7 4.4 %collective-permute-done.3.refs_2_ = bf16[48,384]{1,0:T(8,128)(2,1)S(1)} collective-permute-done((bf16[48,384]{1,0:T(8,128)(2,1)S(1)}, bf16[48,384]{1,0:T(8,128)(2,1)S(1)}, u32[]{:S(2)}, u32[]{:S(2)}) %collective-permute-start.3) | collective-permute-done | bytes 36896 | tf_op jit(solution)/shard_map/ppermute | solution.py:588
  20.1 3.3 %collective-permute-start.5 = (bf16[256,1024]{1,0:T(8,128)(2,1)S(1)}, bf16[256,1024]{1,0:T(8,128)(2,1)S(1)}, u32[]{:S(2)}, u32[]{:S(2)}) collective-permute-start(bf16[256,1024]{1,0:T(8,128)(2,1)S(1)} %collective-permute-done.refs_1_), channel_id=1, source_target_pairs={{1,2},{2,3},{5,6},{6,7},{9,10},{10,11},{13,14},{14,15},{17,18},{18... | collective-permute-start | bytes 1572872 | tf_op jit(solution)/shard_map/ppermute | solution.py:624
  23.4 1.9 %collective-permute-start.6 = (bf16[256,1024]{1,0:T(8,128)(2,1)S(1)}, bf16[256,1024]{1,0:T(8,128)(2,1)S(1)}, u32[]{:S(2)}, u32[]{:S(2)}) collective-permute-start(bf16[256,1024]{1,0:T(8,128)(2,1)S(1)} %collective-permute-done.1.refs_2_), channel_id=1, source_target_pairs={{2,1},{1,0},{6,5},{5,4},{10,9},{9,8},{14,13},{13,12},{18,17},{17,1... | collective-permute-start | bytes 1572872 | tf_op jit(solution)/shard_map/ppermute | solution.py:624
  25.4 1.3 %collective-permute-start.7 = (bf16[4,32,384]{2,1,0:T(8,128)(2,1)S(1)}, bf16[4,32,384]{2,1,0:T(8,128)(2,1)S(1)}, u32[]{:S(2)}, u32[]{:S(2)}) collective-permute-start(bf16[4,32,384]{2,1,0:T(8,128)(2,1)S(1)} %get-tuple-element.47.refs_0_), channel_id=1, source_target_pairs={{0,8},{4,12},{8,16},{12,20},{16,24},{20,28},{24,0},{28,4},{1,9},{5... | collective-permute-start | bytes 294920 | tf_op jit(solution)/shard_map/ppermute | solution.py:611
  29.9 1.3 %collective-permute-done.8.refs_2_ = bf16[4,32,384]{2,1,0:T(8,128)(2,1)S(1)} collective-permute-done((bf16[4,32,384]{2,1,0:T(8,128)(2,1)S(1)}, bf16[4,32,384]{2,1,0:T(8,128)(2,1)S(1)}, u32[]{:S(2)}, u32[]{:S(2)}) %collective-permute-start.8) | collective-permute-done | bytes 98336 | tf_op jit(solution)/shard_map/ppermute | solution.py:611
  31.7 1.9 %copy-done = bf16[1,1024,1536]{2,1,0:T(8,128)(2,1)S(1)} copy-done((bf16[1,1024,1536]{2,1,0:T(8,128)(2,1)S(1)}, bf16[1,1024,1536]{2,1,0:T(8,128)(2,1)}, u32[]{:S(2)}) %copy-start) | copy-done | bytes 3145752
  35.3 3.9 %near_rows.1 = (bf16[1024,1536]{1,0:T(8,128)(2,1)S(1)}, f32[1024,128]{1,0:T(8,128)S(1)}, f32[512,128]{1,0:T(8,128)S(1)}) custom-call(bf16[256,1024]{1,0:T(8,128)(2,1)S(1)} %copy-done.3, bf16[256,1024]{1,0:T(8,128)(2,1)S(1)} %collective-permute-done.refs_1_, bf16[256,1024]{1,0:T(8,128)(2,1)S(1)} %collective-permute-done.1.refs_2_, ...), custom_call_target="tpu_custom_call" | custom-call | flops 2415919104 | bytes 6291456 | tf_op jit(solution)/shard_map/near_rows/pallas_call | solution.py:630
  40.1 1.3 %collective-permute-start.11 = (bf16[256,1024]{1,0:T(8,128)(2,1)S(1)}, bf16[256,1024]{1,0:T(8,128)(2,1)S(1)}, u32[]{:S(2)}, u32[]{:S(2)}) collective-permute-start(bf16[256,1024]{1,0:T(8,128)(2,1)S(1)} %collective-permute-done.6.refs_1_.refs_4_), channel_id=1, source_target_pairs={{1,0},{5,4},{9,8},{13,12},{17,16},{21,20},{25,24},{29,28}} | collective-permute-start | bytes 1572872 | tf_op jit(solution)/shard_map/ppermute | solution.py:624
  41.4 3.6 %collective-permute-start.12 = (bf16[4,4,32,384]{3,2,1,0:T(8,128)(2,1)S(1)}, bf16[4,4,32,384]{3,2,1,0:T(8,128)(2,1)S(1)}, u32[]{:S(2)}, u32[]{:S(2)}) collective-permute-start(bf16[4,4,32,384]{3,2,1,0:T(8,128)(2,1)S(1)} %combine.1.refs_5_), channel_id=1, source_target_pairs={{0,4},{4,0},{8,12},{12,8},{16,20},{20,16},{24,28},{28,24},{1,5},{5... | collective-permute-start | bytes 1179656 | tf_op jit(solution)/shard_map/ppermute | solution.py:642
  45.0 8.2 %middle_rows.1 = (bf16[1024,1536]{1,0:T(8,128)(2,1)S(1)}, f32[1024,128]{1,0:T(8,128)S(1)}, f32[512,128]{1,0:T(8,128)S(1)}, f32[1024,512]{1,0:T(8,128)S(1)}) custom-call(bf16[256,1024]{1,0:T(8,128)(2,1)S(1)} %collective-permute-done.5.refs_0_.refs_3_, bf16[256,1024]{1,0:T(8,128)(2,1)S(1)} %collective-permute-done.6.refs_1_.refs_4_, ...), custom_call_target="tpu_custom_call" | custom-call | flops 2415919104 | bytes 6291456 | tf_op jit(solution)/shard_map/middle_rows/pallas_call | solution.py:645
  53.2 1.8 %window_early.1 = (bf16[1024,384]{1,0:T(8,128)(2,1)S(1)}, bf16[1024,384]{1,0:T(8,128)(2,1)S(1)}) custom-call(bf16[256,1024]{1,0:T(8,128)(2,1)S(1)} %copy-done.4, bf16[256,1024]{1,0:T(8,128)(2,1)S(1)} %collective-permute-done.refs_1_, bf16[256,1024]{1,0:T(8,128)(2,1)S(1)} %collective-permute-done.1.refs_2_, ...), custom_call_target="tpu_custom_call" | custom-call | flops 805306368 | bytes 5242880 | tf_op jit(solution)/shard_map/window_early/pallas_call | solution.py:652
  55.5 3.4 %collective-permute-start.13 = (bf16[512,256]{1,0:T(8,128)(2,1)S(1)}, bf16[512,256]{1,0:T(8,128)(2,1)S(1)}, u32[]{:S(2)}, u32[]{:S(2)}) collective-permute-start(bf16[512,256]{1,0:T(8,128)(2,1)S(1)} %get-tuple-element.73), channel_id=1, source_target_pairs={{0,4},{4,8},{8,12},{12,16},{16,20},{20,24},{24,28},{1,5},{5,9},{9,... | collective-permute-start | bytes 786440 | tf_op jit(solution)/shard_map/ppermute | solution.py:21
  59.3 6.4 %collective-permute-done.15.got_ref = bf16[512,128]{1,0:T(8,128)(2,1)S(1)} collective-permute-done((bf16[512,128]{1,0:T(8,128)(2,1)S(1)}, bf16[512,128]{1,0:T(8,128)(2,1)S(1)}, u32[]{:S(2)}, u32[]{:S(2)}) %collective-permute-start.15) | collective-permute-done | bytes 131104 | tf_op jit(solution)/shard_map/ppermute | solution.py:555
  66.5 2.4 %collective-permute-start.16 = (bf16[512,128]{1,0:T(8,128)(2,1)S(1)}, bf16[512,128]{1,0:T(8,128)(2,1)S(1)}, u32[]{:S(2)}, u32[]{:S(2)}) collective-permute-start(bf16[512,128]{1,0:T(8,128)(2,1)S(1)} %get-tuple-element.80), channel_id=1, source_target_pairs={{0,16},{4,20},{8,24},{12,28},{1,17},{5,21},{9,25},{13,29},{2,18},{... | collective-permute-start | bytes 393224 | tf_op jit(solution)/shard_map/ppermute | solution.py:561
  68.9 2.3 %window_attend.1.refs_6_ = f32[1024,128]{1,0:T(8,128)S(1)} custom-call(bf16[1024,384]{1,0:T(8,128)(2,1)S(1)} %get-tuple-element.72.win_ref, bf16[512,256]{1,0:T(8,128)(2,1)S(1)} %collective-permute-done.13.halo_ref), custom_call_target="tpu_custom_call" | custom-call | flops 402653184 | bytes 3145728 | tf_op jit(solution)/shard_map/window_attend/pallas_call | solution.py:684
  71.8 4.6 %collective-permute-start.17 = (bf16[256,512]{1,0:T(8,128)(2,1)S(1)}, bf16[256,512]{1,0:T(8,128)(2,1)S(1)}, u32[]{:S(2)}, u32[]{:S(2)}) collective-permute-start(bf16[256,512]{1,0:T(8,128)(2,1)S(1)} %finish2.1), channel_id=1, source_target_pairs={{0,2},{1,3},{2,0},{3,1},{4,6},{5,7},{6,4},{7,5},{8,10},{9,11},{10,... | collective-permute-start | bytes 786440 | tf_op jit(solution)/shard_map/ppermute | solution.py:710
  79.4 7.9 %collective-permute-done.17.refs_1_ = bf16[256,512]{1,0:T(8,128)(2,1)S(1)} collective-permute-done((bf16[256,512]{1,0:T(8,128)(2,1)S(1)}, bf16[256,512]{1,0:T(8,128)(2,1)S(1)}, u32[]{:S(2)}, u32[]{:S(2)}) %collective-permute-start.17) | collective-permute-done | bytes 262176 | tf_op jit(solution)/shard_map/ppermute | solution.py:710
  87.3 10.8 %collective-permute-done.18.refs_2_ = bf16[256,512]{1,0:T(8,128)(2,1)S(1)} collective-permute-done((bf16[256,512]{1,0:T(8,128)(2,1)S(1)}, bf16[256,512]{1,0:T(8,128)(2,1)S(1)}, u32[]{:S(2)}, u32[]{:S(2)}) %collective-permute-start.18) | collective-permute-done | bytes 262176 | tf_op jit(solution)/shard_map/ppermute | solution.py:710
  98.0 1.4 %collective-permute-done.19.refs_3_ = bf16[256,512]{1,0:T(8,128)(2,1)S(1)} collective-permute-done((bf16[256,512]{1,0:T(8,128)(2,1)S(1)}, bf16[256,512]{1,0:T(8,128)(2,1)S(1)}, u32[]{:S(2)}, u32[]{:S(2)}) %collective-permute-start.19) | collective-permute-done | bytes 262176 | tf_op jit(solution)/shard_map/ppermute | solution.py:710
  (47 shorter events, 15.4 us)
Async XLA Ops:
  0.0 20.1 %collective-permute-start = (bf16[256,1024]{1,0:T(8,128)(2,1)}, bf16[256,1024]{1,0:T(8,128)(2,1)S(1)}, u32[]{:S(2)}, u32[]{:S(2)}) collective-permute-start(bf16[256,1024]{1,0:T(8,128)(2,1)} %refs_0_.3), channel_id=1, source_target_pairs={{0,1},{1,2},{2,3},{4,5},{5,6},{6,7},{8,9},{9,10},{10,11},{12,13},{... | collective-permute-start | bytes 1572872 | tf_op jit(solution)/shard_map/ppermute | solution.py:624
  3.2 16.9 %collective-permute-start.1 = (bf16[256,1024]{1,0:T(8,128)(2,1)}, bf16[256,1024]{1,0:T(8,128)(2,1)S(1)}, u32[]{:S(2)}, u32[]{:S(2)}) collective-permute-start(bf16[256,1024]{1,0:T(8,128)(2,1)} %refs_0_.3), channel_id=1, source_target_pairs={{3,2},{2,1},{1,0},{7,6},{6,5},{5,4},{11,10},{10,9},{9,8},{15,14},{... | collective-permute-start | bytes 1572872 | tf_op jit(solution)/shard_map/ppermute | solution.py:624
  5.3 1.1 %copy-start.2 = (bf16[256,1536]{1,0:T(8,128)(2,1)S(1)}, bf16[256,1536]{1,0:T(8,128)(2,1)}, u32[]{:S(2)}) copy-start(bf16[256,1536]{1,0:T(8,128)(2,1)} %weight_ref.1) | copy-start | bytes 2359300
  7.3 8.4 %collective-permute-start.2 = (bf16[48,384]{1,0:T(8,128)(2,1)S(1)}, bf16[48,384]{1,0:T(8,128)(2,1)S(1)}, u32[]{:S(2)}, u32[]{:S(2)}) collective-permute-start(bf16[48,384]{1,0:T(8,128)(2,1)S(1)} %get-tuple-element.44), channel_id=1, source_target_pairs={{0,1},{1,2},{2,3},{3,0},{4,5},{5,6},{6,7},{7,4},{8,9},{9,10},{10,1... | collective-permute-start | bytes 110600 | tf_op jit(solution)/shard_map/ppermute | solution.py:588
  8.6 11.5 %collective-permute-start.3 = (bf16[48,384]{1,0:T(8,128)(2,1)S(1)}, bf16[48,384]{1,0:T(8,128)(2,1)S(1)}, u32[]{:S(2)}, u32[]{:S(2)}) collective-permute-start(bf16[48,384]{1,0:T(8,128)(2,1)S(1)} %get-tuple-element.45), channel_id=1, source_target_pairs={{0,2},{1,3},{2,0},{3,1},{4,6},{5,7},{6,4},{7,5},{8,10},{9,11},{10,... | collective-permute-start | bytes 110600 | tf_op jit(solution)/shard_map/ppermute | solution.py:588
  9.7 10.4 %collective-permute-start.4 = (bf16[48,384]{1,0:T(8,128)(2,1)S(1)}, bf16[48,384]{1,0:T(8,128)(2,1)S(1)}, u32[]{:S(2)}, u32[]{:S(2)}) collective-permute-start(bf16[48,384]{1,0:T(8,128)(2,1)S(1)} %get-tuple-element.46), channel_id=1, source_target_pairs={{0,3},{1,0},{2,1},{3,2},{4,7},{5,4},{6,5},{7,6},{8,11},{9,8},{10,9... | collective-permute-start | bytes 110600 | tf_op jit(solution)/shard_map/ppermute | solution.py:588
  20.1 19.1 %collective-permute-start.5 = (bf16[256,1024]{1,0:T(8,128)(2,1)S(1)}, bf16[256,1024]{1,0:T(8,128)(2,1)S(1)}, u32[]{:S(2)}, u32[]{:S(2)}) collective-permute-start(bf16[256,1024]{1,0:T(8,128)(2,1)S(1)} %collective-permute-done.refs_1_), channel_id=1, source_target_pairs={{1,2},{2,3},{5,6},{6,7},{9,10},{10,11},{13,14},{14,15},{17,18},{18... | collective-permute-start | bytes 1572872 | tf_op jit(solution)/shard_map/ppermute | solution.py:624
  23.4 15.8 %collective-permute-start.6 = (bf16[256,1024]{1,0:T(8,128)(2,1)S(1)}, bf16[256,1024]{1,0:T(8,128)(2,1)S(1)}, u32[]{:S(2)}, u32[]{:S(2)}) collective-permute-start(bf16[256,1024]{1,0:T(8,128)(2,1)S(1)} %collective-permute-done.1.refs_2_), channel_id=1, source_target_pairs={{2,1},{1,0},{6,5},{5,4},{10,9},{9,8},{14,13},{13,12},{18,17},{17,1... | collective-permute-start | bytes 1572872 | tf_op jit(solution)/shard_map/ppermute | solution.py:624
  25.4 4.5 %collective-permute-start.7 = (bf16[4,32,384]{2,1,0:T(8,128)(2,1)S(1)}, bf16[4,32,384]{2,1,0:T(8,128)(2,1)S(1)}, u32[]{:S(2)}, u32[]{:S(2)}) collective-permute-start(bf16[4,32,384]{2,1,0:T(8,128)(2,1)S(1)} %get-tuple-element.47.refs_0_), channel_id=1, source_target_pairs={{0,8},{4,12},{8,16},{12,20},{16,24},{20,28},{24,0},{28,4},{1,9},{5... | collective-permute-start | bytes 294920 | tf_op jit(solution)/shard_map/ppermute | solution.py:611
  26.6 4.5 %collective-permute-start.8 = (bf16[4,32,384]{2,1,0:T(8,128)(2,1)S(1)}, bf16[4,32,384]{2,1,0:T(8,128)(2,1)S(1)}, u32[]{:S(2)}, u32[]{:S(2)}) collective-permute-start(bf16[4,32,384]{2,1,0:T(8,128)(2,1)S(1)} %get-tuple-element.47.refs_0_), channel_id=1, source_target_pairs={{0,16},{4,20},{8,24},{12,28},{16,0},{20,4},{24,8},{28,12},{1,17},{... | collective-permute-start | bytes 294920 | tf_op jit(solution)/shard_map/ppermute | solution.py:611
  27.9 3.8 %collective-permute-start.9 = (bf16[4,32,384]{2,1,0:T(8,128)(2,1)S(1)}, bf16[4,32,384]{2,1,0:T(8,128)(2,1)S(1)}, u32[]{:S(2)}, u32[]{:S(2)}) collective-permute-start(bf16[4,32,384]{2,1,0:T(8,128)(2,1)S(1)} %get-tuple-element.47.refs_0_), channel_id=1, source_target_pairs={{0,24},{4,28},{8,0},{12,4},{16,8},{20,12},{24,16},{28,20},{1,25},{... | collective-permute-start | bytes 294920 | tf_op jit(solution)/shard_map/ppermute | solution.py:611
  31.7 1.9 %copy-start = (bf16[1,1024,1536]{2,1,0:T(8,128)(2,1)S(1)}, bf16[1,1024,1536]{2,1,0:T(8,128)(2,1)}, u32[]{:S(2)}) copy-start(bf16[1,1024,1536]{2,1,0:T(8,128)(2,1)} %param.8) | copy-start | bytes 9437188
  35.3 9.7 %copy-start.1 = (bf16[1,1024,1536]{2,1,0:T(8,128)(2,1)S(1)}, bf16[1,1024,1536]{2,1,0:T(8,128)(2,1)}, u32[]{:S(2)}) copy-start(bf16[1,1024,1536]{2,1,0:T(8,128)(2,1)} %param.8) | copy-start | bytes 9437188
  39.2 14.0 %copy-start.4 = (bf16[256,1024]{1,0:T(8,128)(2,1)S(1)}, bf16[256,1024]{1,0:T(8,128)(2,1)}, u32[]{:S(2)}) copy-start(bf16[256,1024]{1,0:T(8,128)(2,1)} %refs_0_.3) | copy-start | bytes 1572868
  39.2 15.8 %collective-permute-start.10 = (bf16[256,1024]{1,0:T(8,128)(2,1)S(1)}, bf16[256,1024]{1,0:T(8,128)(2,1)S(1)}, u32[]{:S(2)}, u32[]{:S(2)}) collective-permute-start(bf16[256,1024]{1,0:T(8,128)(2,1)S(1)} %collective-permute-done.5.refs_0_.refs_3_), channel_id=1, source_target_pairs={{2,3},{6,7},{10,11},{14,15},{18,19},{22,23},{26,27},{30,31}} | collective-permute-start | bytes 1572872 | tf_op jit(solution)/shard_map/ppermute | solution.py:624
  40.1 15.0 %collective-permute-start.11 = (bf16[256,1024]{1,0:T(8,128)(2,1)S(1)}, bf16[256,1024]{1,0:T(8,128)(2,1)S(1)}, u32[]{:S(2)}, u32[]{:S(2)}) collective-permute-start(bf16[256,1024]{1,0:T(8,128)(2,1)S(1)} %collective-permute-done.6.refs_1_.refs_4_), channel_id=1, source_target_pairs={{1,0},{5,4},{9,8},{13,12},{17,16},{21,20},{25,24},{29,28}} | collective-permute-start | bytes 1572872 | tf_op jit(solution)/shard_map/ppermute | solution.py:624
  41.4 11.8 %collective-permute-start.12 = (bf16[4,4,32,384]{3,2,1,0:T(8,128)(2,1)S(1)}, bf16[4,4,32,384]{3,2,1,0:T(8,128)(2,1)S(1)}, u32[]{:S(2)}, u32[]{:S(2)}) collective-permute-start(bf16[4,4,32,384]{3,2,1,0:T(8,128)(2,1)S(1)} %combine.1.refs_5_), channel_id=1, source_target_pairs={{0,4},{4,0},{8,12},{12,8},{16,20},{20,16},{24,28},{28,24},{1,5},{5... | collective-permute-start | bytes 1179656 | tf_op jit(solution)/shard_map/ppermute | solution.py:642
  55.1 3.8 %collective-permute-start.14 = (bf16[512,128]{1,0:T(8,128)(2,1)S(1)}, bf16[512,128]{1,0:T(8,128)(2,1)S(1)}, u32[]{:S(2)}, u32[]{:S(2)}) collective-permute-start(bf16[512,128]{1,0:T(8,128)(2,1)S(1)} %get-tuple-element.74), channel_id=1, source_target_pairs={{0,4},{4,0},{8,12},{12,8},{16,20},{20,16},{24,28},{28,24},{1,5},{5... | collective-permute-start | bytes 393224 | tf_op jit(solution)/shard_map/ppermute | solution.py:555
  55.5 13.4 %collective-permute-start.13 = (bf16[512,256]{1,0:T(8,128)(2,1)S(1)}, bf16[512,256]{1,0:T(8,128)(2,1)S(1)}, u32[]{:S(2)}, u32[]{:S(2)}) collective-permute-start(bf16[512,256]{1,0:T(8,128)(2,1)S(1)} %get-tuple-element.73), channel_id=1, source_target_pairs={{0,4},{4,8},{8,12},{12,16},{16,20},{20,24},{24,28},{1,5},{5,9},{9,... | collective-permute-start | bytes 786440 | tf_op jit(solution)/shard_map/ppermute | solution.py:21
  59.0 6.8 %collective-permute-start.15 = (bf16[512,128]{1,0:T(8,128)(2,1)S(1)}, bf16[512,128]{1,0:T(8,128)(2,1)S(1)}, u32[]{:S(2)}, u32[]{:S(2)}) collective-permute-start(bf16[512,128]{1,0:T(8,128)(2,1)S(1)} %get-tuple-element.76), channel_id=1, source_target_pairs={{0,8},{4,12},{8,0},{12,4},{16,24},{20,28},{24,16},{28,20},{1,9},{5... | collective-permute-start | bytes 393224 | tf_op jit(solution)/shard_map/ppermute | solution.py:555
  66.5 4.8 %collective-permute-start.16 = (bf16[512,128]{1,0:T(8,128)(2,1)S(1)}, bf16[512,128]{1,0:T(8,128)(2,1)S(1)}, u32[]{:S(2)}, u32[]{:S(2)}) collective-permute-start(bf16[512,128]{1,0:T(8,128)(2,1)S(1)} %get-tuple-element.80), channel_id=1, source_target_pairs={{0,16},{4,20},{8,24},{12,28},{1,17},{5,21},{9,25},{13,29},{2,18},{... | collective-permute-start | bytes 393224 | tf_op jit(solution)/shard_map/ppermute | solution.py:561
  71.8 15.5 %collective-permute-start.17 = (bf16[256,512]{1,0:T(8,128)(2,1)S(1)}, bf16[256,512]{1,0:T(8,128)(2,1)S(1)}, u32[]{:S(2)}, u32[]{:S(2)}) collective-permute-start(bf16[256,512]{1,0:T(8,128)(2,1)S(1)} %finish2.1), channel_id=1, source_target_pairs={{0,2},{1,3},{2,0},{3,1},{4,6},{5,7},{6,4},{7,5},{8,10},{9,11},{10,... | collective-permute-start | bytes 786440 | tf_op jit(solution)/shard_map/ppermute | solution.py:710
  76.9 21.1 %collective-permute-start.18 = (bf16[256,512]{1,0:T(8,128)(2,1)S(1)}, bf16[256,512]{1,0:T(8,128)(2,1)S(1)}, u32[]{:S(2)}, u32[]{:S(2)}) collective-permute-start(bf16[256,512]{1,0:T(8,128)(2,1)S(1)} %finish1.1), channel_id=1, source_target_pairs={{0,1},{1,2},{2,3},{3,0},{4,5},{5,6},{6,7},{7,4},{8,9},{9,10},{10,1... | collective-permute-start | bytes 786440 | tf_op jit(solution)/shard_map/ppermute | solution.py:710
  78.1 21.3 %collective-permute-start.19 = (bf16[256,512]{1,0:T(8,128)(2,1)S(1)}, bf16[256,512]{1,0:T(8,128)(2,1)S(1)}, u32[]{:S(2)}, u32[]{:S(2)}) collective-permute-start(bf16[256,512]{1,0:T(8,128)(2,1)S(1)} %finish3.1), channel_id=1, source_target_pairs={{0,3},{1,0},{2,1},{3,2},{4,7},{5,4},{6,5},{7,6},{8,11},{9,8},{10,9... | collective-permute-start | bytes 786440 | tf_op jit(solution)/shard_map/ppermute | solution.py:710
  (3 other events, 2.4 us)

commit v7 on v6

--- a/solution.py
+++ b/solution.py
@@ -153,6 +153,8 @@
 
 HBM = pl.BlockSpec(memory_space=pltpu.HBM)
 WHOLE = pl.BlockSpec()
+
+
 ROUTE_ROWS = 16
 
 
@@ -202,6 +204,12 @@
             out_ref[0:cut, part * HDIM : (part + 1) * HDIM] = rows_ref[:, at]
 
 
+def stage_body(*refs):
+    half = len(refs) // 2
+    for source_ref, target_ref in zip(refs[:half], refs[half:]):
+        target_ref[...] = source_ref[...]
+
+
 def arrange_body(*refs):
     pieces, (routes_ref, rows_ref) = refs[:-2], refs[-2:]
     mine = lax.axis_index("mem")
@@ -226,9 +234,9 @@
     return jnp.sum(jnp.where(diagonal, row, 0.0), axis=1, keepdims=True)
 
 
-def members(group, packed_ref, count):
+def members(group, routes_ref, count):
     mine = lax.axis_index("mem").astype(jnp.float32)
-    named = packed_ref[group, :, 0:count].astype(jnp.float32)
+    named = routes_ref[group, :, 0:count].astype(jnp.float32)
     first = as_column(named[0:1, :], count)
     second = as_column(named[1:2, :], count)
     return first, second, first == mine, second == mine
@@ -352,7 +360,7 @@
                     )
 
 
-def last_keys_body(n_mem, below_ref, above_ref, packed_ref, weight_ref, before_ref, *refs):
+def last_keys_body(n_mem, below_ref, above_ref, routes_ref, weight_ref, before_ref, *refs):
     kv_ref, state_ref, sent_ref = refs
     count = below_ref.shape[0]
     width = HEADS * HDIM
@@ -361,7 +369,7 @@
 
     @pl.when((mine == 0) | (mine == n_mem - 1))
     def _():
-        _, _, is_first, is_second = members(n_mem - 1 - mine, packed_ref, count)
+        _, _, is_first, is_second = members(n_mem - 1 - mine, routes_ref, count)
         tokens = jnp.where(mine == 0, above_ref[...], below_ref[...])
         projected = jnp.dot(tokens, weight_ref[:, width:], preferred_element_type=jnp.float32)
         projected = jnp.where(is_first | is_second, projected, 0.0).astype(jnp.bfloat16)
@@ -374,7 +382,7 @@
     sent_ref[...] = state_ref[...].astype(jnp.bfloat16)
 
 
-def last_queries_body(n_mem, below_ref, above_ref, packed_ref, router_ref, weight_ref, proj_ref, kv_ref, *refs):
+def last_queries_body(n_mem, below_ref, above_ref, routes_ref, router_ref, weight_ref, proj_ref, kv_ref, *refs):
     query_ref, coef_ref, extra_ref = refs
     count = below_ref.shape[0]
     total = extra_ref.shape[0]
@@ -385,7 +393,7 @@
     @pl.when((mine == 0) | (mine == n_mem - 1))
     def _():
         tokens = jnp.where(mine == 0, above_ref[...], below_ref[...])
-        first, second, is_first, is_second = members(n_mem - 1 - mine, packed_ref, count)
+        first, second, is_first, is_second = members(n_mem - 1 - mine, routes_ref, count)
         coef_ref[...] = coefficients(tokens, router_ref[...], first, second, is_first, is_second)
         queries = jnp.dot(tokens, weight_ref[:, 0:width], preferred_element_type=jnp.float32)
         query_ref[...] = jnp.where(is_first | is_second, queries, 0.0).astype(jnp.bfloat16)
@@ -482,7 +490,7 @@
         )
 
 
-def finish_body(n_mem, shift, bit, *refs):
+def finish_body(n_mem, shift, *refs):
     proj_ref, intra_ref, coef_ref, last_query_ref, last_coef_ref, extra_ref = refs[:6]
     window_ref, prefix_ref, got_ref, out_ref, query_s, intra_s, coef_s = refs[6:]
     mine = lax.axis_index("mem")
@@ -507,9 +515,7 @@
     def _():
         intra_s[...] += extra_ref[here, :]
 
-    later = (lax.axis_index("ctx") & bit) != 0
-    got = jnp.where(later, got_ref[...].astype(jnp.float32), 0.0)
-    prefix = (prefix_ref[...] + got).astype(jnp.bfloat16)
+    prefix = (prefix_ref[...] + got_ref[...].astype(jnp.float32)).astype(jnp.bfloat16)
     coef = coef_s[...]
     for head in range(HEADS):
         columns = head_columns(head)
@@ -529,37 +535,30 @@
     refs[-1][...] = total.astype(jnp.bfloat16)
 
 
-def double_body(bit, got_ref, total_ref, *refs):
-    if len(refs) == 4:
-        before_ref, total_out, prefix_ref, sent_ref = refs
-        before = before_ref[...]
-    else:
-        total_out, prefix_ref, sent_ref = refs
-        before = 0.0
-    got = got_ref[...].astype(jnp.float32)
-    later = (lax.axis_index("ctx") & bit) != 0
-    prefix_ref[...] = before + jnp.where(later, got, 0.0)
-    total = total_ref[...] + got
-    total_out[...] = total
-    sent_ref[...] = total.astype(jnp.bfloat16)
+def fold_body(bit, *refs):
+    *before, got_ref, state_ref, prefix_ref, sent_ref = refs
+    prefix = got_ref[...].astype(jnp.float32)
+    for before_ref in before:
+        prefix += before_ref[...]
+    prefix_ref[...] = prefix
+    earlier = (lax.axis_index("ctx") & bit) == 0
+    sent_ref[...] = (prefix + jnp.where(earlier, state_ref[...], 0.0)).astype(jnp.bfloat16)
 
 
 def exclusive_prefix(state, sent):
     devices = lax.axis_size("ctx")
-    kinds = [
-        jax.ShapeDtypeStruct(state.shape, kind) for kind in (jnp.float32, jnp.float32, jnp.bfloat16)
-    ]
-    before = ()
-    bit = 1
-    while 2 * bit < devices:
+    bit = devices // 2
+    got = lax.ppermute(sent, "ctx", [(i, i + bit) for i in range(devices) if not i & bit])
+    prefix = ()
+    kinds = [jax.ShapeDtypeStruct(state.shape, kind) for kind in (jnp.float32, jnp.bfloat16)]
+    while bit > 1:
+        bit //= 2
+        held, sent = kernel_call(
+            functools.partial(fold_body, bit), f"fold{bit}", kinds, 4 * state.size, 16 * state.size
+        )(*prefix, got, state)
+        prefix = (held,)
         got = lax.ppermute(sent, "ctx", [(i, i ^ bit) for i in range(devices)])
-        state, prefix, sent = kernel_call(
-            functools.partial(double_body, bit), f"double{bit}", kinds, 4 * state.size, 16 * state.size
-        )(got, state, *before)
-        before = (prefix,)
-        bit *= 2
-    got = lax.ppermute(sent, "ctx", [(i, i + bit) for i in range(devices) if not i & bit])
-    return prefix, got, bit
+    return held, got
 
 
 def dense_shards(tokens, routes, router, mem_weight, win_weight):
@@ -574,6 +573,11 @@
 
     def shape(rows, columns, kind=low):
         return jax.ShapeDtypeStruct((rows, columns), kind)
+
+    def moved(hop, from_below, from_above):
+        up = [(i, i + 1) for i in range(hop - 1, n_mem - 1)]
+        down = [(n_mem - 1 - i, n_mem - 1 - j) for i, j in up]
+        return lax.ppermute(from_below, "mem", up), lax.ppermute(from_above, "mem", down)
 
     packed = kernel_call(
         pack_body,
@@ -588,6 +592,8 @@
         lax.ppermute(packed[s], "mem", [(i, (i + s) % n_mem) for i in range(n_mem)])
         for s in range(1, n_mem)
     ]
+    sent_tokens, packed = lax.optimization_barrier((tokens, packed))
+    slots = list(moved(1, sent_tokens, sent_tokens))
     all_routes, own_rows = kernel_call(
         arrange_body,
         "arrange",
@@ -599,47 +605,44 @@
         1 << 20,
     )(*packed)
     chips = n_ctx // 2
+    of_chips = [
+        lax.ppermute(own_rows, "ctx", [(i, (i + 2 * s) % n_ctx) for i in range(n_ctx)])
+        for s in range(1, chips)
+    ]
+    staged = kernel_call(
+        stage_body,
+        "stage",
+        [shape(count, depth), shape(n_mem, depth), shape(depth, 3 * width)],
+        4 << 20,
+        4 << 20,
+    )(tokens, router.T, mem_weight[0])
     of_core = kernel_call(
         combine_body,
         "combine",
         jax.ShapeDtypeStruct((chips,) + own_rows.shape, low),
         1 << 20,
         1 << 20,
-    )(
-        own_rows,
-        *[
-            lax.ppermute(own_rows, "ctx", [(i, (i + 2 * s) % n_ctx) for i in range(n_ctx)])
-            for s in range(1, chips)
-        ],
-    )
-    weight = mem_weight[0]
-    router_rows = router.T
+    )(own_rows, *of_chips)
+    below, above, staged, of_core = lax.optimization_barrier((*slots, staged, of_core))
+    own_tokens, router_rows, weight = staged
+    slots = [own_tokens] + slots
+    below, above = moved(2, below, above)
+    slots += [below, above]
+    other_core = lax.ppermute(of_core, "ctx", [(i, i ^ 1) for i in range(n_ctx)])
     given = (all_routes, router_rows, weight)
     project_flops = 2 * count * depth * 3 * width
     kept = (shape(total, 3 * width), shape(total, HDIM, full), shape(width, HDIM, full))
-
-    def moved(hop, from_below, from_above):
-        up = [(i, i + 1) for i in range(hop - 1, n_mem - 1)]
-        down = [(n_mem - 1 - i, n_mem - 1 - j) for i, j in up]
-        return lax.ppermute(from_below, "mem", up), lax.ppermute(from_above, "mem", down)
-
-    slots = [tokens]
-    below, above = moved(1, tokens, tokens)
-    slots += [below, above]
-    below, above, own_rows = lax.optimization_barrier((below, above, own_rows))
     held = kernel_call(
         functools.partial(arrivals_body, n_mem, 0, 3, False),
         "near_rows",
         kept,
         3 * project_flops,
         6 << 20,
-    )(*slots, *given)
-    for hop in range(2, n_mem):
+    )(*slots[:3], *given)
+    below, above, held, other_core = lax.optimization_barrier((below, above, held, other_core))
+    for hop in range(3, n_mem):
         below, above = moved(hop, below, above)
         slots += [below, above]
-        if hop == 2:
-            below, above, of_core, *held = lax.optimization_barrier((below, above, of_core, *held))
-    other_core = lax.ppermute(of_core, "ctx", [(i, i ^ 1) for i in range(n_ctx)])
     hops = n_mem - 2
     early = 1 + 2 * hops
     proj, coef, state, intra = kernel_call(
@@ -664,7 +667,7 @@
         2 * count * depth * 2 * width,
         3 << 20,
     )(below, above, all_routes, weight, state)
-    prefix, got, bit = exclusive_prefix(state, sent)
+    prefix, got = exclusive_prefix(state, sent)
 
     win, tail = kernel_call(
         functools.partial(window_late_body, n_mem, early),
@@ -692,7 +695,7 @@
 
     def finish(shift):
         return kernel_call(
-            functools.partial(finish_body, n_mem, shift, bit),
+            functools.partial(finish_body, n_mem, shift),
             f"finish{shift}",
             shape(count, width, low if shift else full),
             2 * count * width * HDIM,

time: 102 us -> 101 us (level)
  the two profiles are of different devices: /device:TPU:9 before, /device:TPU:0 now
where the time goes in v7:
time: 101 us
  waiting for transfers between devices  47.2 us (47%)
  starting transfers between devices  29 us (29%)
  Pallas kernels  18.9 us (19%)
  local copies, waits for them, and re-layouts  5.44 us (5%)
    ppermute x3, waiting for transfers between devices, dense_shards(): parts.append(lax.ppermute(finish(shift), 'mem', pairs))  19.7 us
    ppermute x3, waiting for transfers between devices, moved(): lax.ppermute(from_above, 'mem', down)  19.1 us
    ppermute x3, starting transfers between devices, dense_shards(): lax.ppermute(packed[s], 'mem', [(i, (i + s) % n_mem) for i in range(n_mem)])  7.01 us
    pallas_call x1, Pallas kernels, dense_shards(): kernel_call(functools.partial(arrivals_body, n_mem, 3, early, True), 'mid...  5.57 us
    unnamed x10, local copies, waits for them, and re-layouts  5.44 us
    ppermute x2, waiting for transfers between devices, exclusive_prefix(): got = lax.ppermute(sent, 'ctx', [(i, i ^ bit) for i in range(devices)])  4.79 us
    ppermute x3, starting transfers between devices, dense_shards(): lax.ppermute(own_rows, 'ctx', [(i, (i + 2 * s) % n_ctx) for i in range(n_...  4.5 us
    ppermute x3, starting transfers between devices, moved(): lax.ppermute(from_above, 'mem', down)  3.88 us
  transfers between devices with their start and end apart: 20, of which 10 were waited for; matrix products, arithmetic and copies ran while one was open for 0% of the time, Pallas kernels for 16%

profile of v7, /device:TPU:0, one launch (start us, length us, event | category | flops | bytes accessed | tf_op | source)
XLA Modules:
  0.0 100.9 jit_solution(11195408274552969639)
XLA Ops:
  2.0 3.1 %collective-permute-start = (bf16[48,384]{1,0:T(8,128)(2,1)S(1)}, bf16[48,384]{1,0:T(8,128)(2,1)S(1)}, u32[]{:S(2)}, u32[]{:S(2)}) collective-permute-start(bf16[48,384]{1,0:T(8,128)(2,1)S(1)} %get-tuple-element.55), channel_id=1, source_target_pairs={{0,1},{1,2},{2,3},{3,0},{4,5},{5,6},{6,7},{7,4},{8,9},{9,10},{10,1... | collective-permute-start | bytes 110600 | tf_op jit(solution)/shard_map/ppermute | solution.py:592
  5.0 2.6 %collective-permute-start.1 = (bf16[48,384]{1,0:T(8,128)(2,1)S(1)}, bf16[48,384]{1,0:T(8,128)(2,1)S(1)}, u32[]{:S(2)}, u32[]{:S(2)}) collective-permute-start(bf16[48,384]{1,0:T(8,128)(2,1)S(1)} %get-tuple-element.56), channel_id=1, source_target_pairs={{0,2},{1,3},{2,0},{3,1},{4,6},{5,7},{6,4},{7,5},{8,10},{9,11},{10,... | collective-permute-start | bytes 110600 | tf_op jit(solution)/shard_map/ppermute | solution.py:592
  7.6 1.3 %collective-permute-start.2 = (bf16[48,384]{1,0:T(8,128)(2,1)S(1)}, bf16[48,384]{1,0:T(8,128)(2,1)S(1)}, u32[]{:S(2)}, u32[]{:S(2)}) collective-permute-start(bf16[48,384]{1,0:T(8,128)(2,1)S(1)} %get-tuple-element.57), channel_id=1, source_target_pairs={{0,3},{1,0},{2,1},{3,2},{4,7},{5,4},{6,5},{7,6},{8,11},{9,8},{10,9... | collective-permute-start | bytes 110600 | tf_op jit(solution)/shard_map/ppermute | solution.py:592
  11.6 2.2 %collective-permute-start.3 = (bf16[256,1024]{1,0:T(8,128)(2,1)}, bf16[256,1024]{1,0:T(8,128)(2,1)S(1)}, u32[]{:S(2)}, u32[]{:S(2)}) collective-permute-start(bf16[256,1024]{1,0:T(8,128)(2,1)} %refs_0_.1), channel_id=1, source_target_pairs={{0,1},{1,2},{2,3},{4,5},{5,6},{6,7},{8,9},{9,10},{10,11},{12,13},{... | collective-permute-start | bytes 1572872 | tf_op jit(solution)/shard_map/ppermute | solution.py:580
  15.1 1.5 %collective-permute-start.5 = (bf16[4,32,384]{2,1,0:T(8,128)(2,1)S(1)}, bf16[4,32,384]{2,1,0:T(8,128)(2,1)S(1)}, u32[]{:S(2)}, u32[]{:S(2)}) collective-permute-start(bf16[4,32,384]{2,1,0:T(8,128)(2,1)S(1)} %get-tuple-element.66.refs_0_), channel_id=1, source_target_pairs={{0,8},{4,12},{8,16},{12,20},{16,24},{20,28},{24,0},{28,4},{1,9},{5... | collective-permute-start | bytes 294920 | tf_op jit(solution)/shard_map/ppermute | solution.py:609
  16.7 1.5 %collective-permute-start.6 = (bf16[4,32,384]{2,1,0:T(8,128)(2,1)S(1)}, bf16[4,32,384]{2,1,0:T(8,128)(2,1)S(1)}, u32[]{:S(2)}, u32[]{:S(2)}) collective-permute-start(bf16[4,32,384]{2,1,0:T(8,128)(2,1)S(1)} %get-tuple-element.66.refs_0_), channel_id=1, source_target_pairs={{0,16},{4,20},{8,24},{12,28},{16,0},{20,4},{24,8},{28,12},{1,17},{... | collective-permute-start | bytes 294920 | tf_op jit(solution)/shard_map/ppermute | solution.py:609
  18.2 1.4 %collective-permute-start.7 = (bf16[4,32,384]{2,1,0:T(8,128)(2,1)S(1)}, bf16[4,32,384]{2,1,0:T(8,128)(2,1)S(1)}, u32[]{:S(2)}, u32[]{:S(2)}) collective-permute-start(bf16[4,32,384]{2,1,0:T(8,128)(2,1)S(1)} %get-tuple-element.66.refs_0_), channel_id=1, source_target_pairs={{0,24},{4,28},{8,0},{12,4},{16,8},{20,12},{24,16},{28,20},{1,25},{... | collective-permute-start | bytes 294920 | tf_op jit(solution)/shard_map/ppermute | solution.py:609
  19.6 1.9 %copy-done = bf16[1,1024,1536]{2,1,0:T(8,128)(2,1)S(1)} copy-done((bf16[1,1024,1536]{2,1,0:T(8,128)(2,1)S(1)}, bf16[1,1024,1536]{2,1,0:T(8,128)(2,1)}, u32[]{:S(2)}) %copy-start) | copy-done | bytes 3145752
  24.2 4.0 %collective-permute-done.4.refs_2_ = bf16[256,1024]{1,0:T(8,128)(2,1)S(1)} collective-permute-done((bf16[256,1024]{1,0:T(8,128)(2,1)}, bf16[256,1024]{1,0:T(8,128)(2,1)S(1)}, u32[]{:S(2)}, u32[]{:S(2)}) %collective-permute-start.4) | collective-permute-done | bytes 524320 | tf_op jit(solution)/shard_map/ppermute | solution.py:580
  30.3 2.6 %near_rows.1 = (bf16[1024,1536]{1,0:T(8,128)(2,1)S(1)}, f32[1024,128]{1,0:T(8,128)S(1)}, f32[512,128]{1,0:T(8,128)S(1)}) custom-call(bf16[256,1024]{1,0:T(8,128)(2,1)S(1)} %get-tuple-element.72.refs_0_, bf16[256,1024]{1,0:T(8,128)(2,1)S(1)} %collective-permute-done.3.refs_1_, bf16[256,1024]{1,0:T(8,128)(2,1)S(1)} %collective-permute-done.4.refs_2_, ...), custom_call_target="tpu_custom_call" | custom-call | flops 2415919104 | bytes 6291456 | tf_op jit(solution)/shard_map/near_rows/pallas_call | solution.py:635
  32.9 11.5 %collective-permute-done.9.refs_1_.refs_4_ = bf16[256,1024]{1,0:T(8,128)(2,1)S(1)} collective-permute-done((bf16[256,1024]{1,0:T(8,128)(2,1)S(1)}, bf16[256,1024]{1,0:T(8,128)(2,1)S(1)}, u32[]{:S(2)}, u32[]{:S(2)}) %collective-permute-start.9) | collective-permute-done | bytes 524320 | tf_op jit(solution)/shard_map/ppermute | solution.py:580
  46.4 1.4 %window_early.1 = (bf16[1024,384]{1,0:T(8,128)(2,1)S(1)}, bf16[1024,384]{1,0:T(8,128)(2,1)S(1)}) custom-call(bf16[256,1024]{1,0:T(8,128)(2,1)S(1)} %get-tuple-element.72.refs_0_, bf16[256,1024]{1,0:T(8,128)(2,1)S(1)} %collective-permute-done.3.refs_1_, bf16[256,1024]{1,0:T(8,128)(2,1)S(1)} %collective-permute-done.4.refs_2_, ...), custom_call_target="tpu_custom_call" | custom-call | flops 805306368 | bytes 5242880 | tf_op jit(solution)/shard_map/window_early/pallas_call | solution.py:655
  47.8 5.6 %middle_rows.1 = (bf16[1024,1536]{1,0:T(8,128)(2,1)S(1)}, f32[1024,128]{1,0:T(8,128)S(1)}, f32[512,128]{1,0:T(8,128)S(1)}, f32[1024,512]{1,0:T(8,128)S(1)}) custom-call(bf16[256,1024]{1,0:T(8,128)(2,1)S(1)} %collective-permute-done.8.refs_0_.refs_3_, bf16[256,1024]{1,0:T(8,128)(2,1)S(1)} %collective-permute-done.9.refs_1_.refs_4_, ...), custom_call_target="tpu_custom_call" | custom-call | flops 2415919104 | bytes 6291456 | tf_op jit(solution)/shard_map/middle_rows/pallas_call | solution.py:648
  53.4 3.6 %collective-permute-done.12.above_ref.refs_1_ = bf16[256,1024]{1,0:T(8,128)(2,1)S(1)} collective-permute-done((bf16[256,1024]{1,0:T(8,128)(2,1)S(1)}, bf16[256,1024]{1,0:T(8,128)(2,1)S(1)}, u32[]{:S(2)}, u32[]{:S(2)}) %collective-permute-start.12) | collective-permute-done | bytes 524320 | tf_op jit(solution)/shard_map/ppermute | solution.py:580
  57.9 3.4 %collective-permute-start.14 = (bf16[512,128]{1,0:T(8,128)(2,1)S(1)}, bf16[512,128]{1,0:T(8,128)(2,1)S(1)}, u32[]{:S(2)}, u32[]{:S(2)}) collective-permute-start(bf16[512,128]{1,0:T(8,128)(2,1)S(1)} %get-tuple-element.97), channel_id=1, source_target_pairs={{0,16},{4,20},{8,24},{12,28},{1,17},{5,21},{9,25},{13,29},{2,18},{... | collective-permute-start | bytes 393224 | tf_op jit(solution)/shard_map/ppermute | solution.py:551
  62.1 1.3 %collective-permute-start.13 = (bf16[512,256]{1,0:T(8,128)(2,1)S(1)}, bf16[512,256]{1,0:T(8,128)(2,1)S(1)}, u32[]{:S(2)}, u32[]{:S(2)}) collective-permute-start(bf16[512,256]{1,0:T(8,128)(2,1)S(1)} %get-tuple-element.96), channel_id=1, source_target_pairs={{0,4},{4,8},{8,12},{12,16},{16,20},{20,24},{24,28},{1,5},{5,9},{9,... | collective-permute-start | bytes 786440 | tf_op jit(solution)/shard_map/ppermute | solution.py:21
  63.9 1.7 %collective-permute-start.15 = (bf16[512,128]{1,0:T(8,128)(2,1)S(1)}, bf16[512,128]{1,0:T(8,128)(2,1)S(1)}, u32[]{:S(2)}, u32[]{:S(2)}) collective-permute-start(bf16[512,128]{1,0:T(8,128)(2,1)S(1)} %get-tuple-element.100), channel_id=1, source_target_pairs={{0,8},{4,12},{8,0},{12,4},{16,24},{20,28},{24,16},{28,20},{1,9},{5... | collective-permute-start | bytes 393224 | tf_op jit(solution)/shard_map/ppermute | solution.py:560
  65.6 4.8 %collective-permute-done.15.refs_1_ = bf16[512,128]{1,0:T(8,128)(2,1)S(1)} collective-permute-done((bf16[512,128]{1,0:T(8,128)(2,1)S(1)}, bf16[512,128]{1,0:T(8,128)(2,1)S(1)}, u32[]{:S(2)}, u32[]{:S(2)}) %collective-permute-start.15) | collective-permute-done | bytes 131104 | tf_op jit(solution)/shard_map/ppermute | solution.py:560
  70.4 1.4 %collective-permute-start.16 = (bf16[512,128]{1,0:T(8,128)(2,1)S(1)}, bf16[512,128]{1,0:T(8,128)(2,1)S(1)}, u32[]{:S(2)}, u32[]{:S(2)}) collective-permute-start(bf16[512,128]{1,0:T(8,128)(2,1)S(1)} %get-tuple-element.102), channel_id=1, source_target_pairs={{0,4},{4,0},{8,12},{12,8},{16,20},{20,16},{24,28},{28,24},{1,5},{5... | collective-permute-start | bytes 393224 | tf_op jit(solution)/shard_map/ppermute | solution.py:560
  71.8 2.1 %last_queries.1 = (bf16[256,512]{1,0:T(8,128)(2,1)S(1)}, f32[256,128]{1,0:T(8,128)S(1)}, f32[1024,512]{1,0:T(8,128)S(1)}) custom-call(bf16[256,1024]{1,0:T(8,128)(2,1)S(1)} %collective-permute-done.11.below_ref.refs_0_, bf16[256,1024]{1,0:T(8,128)(2,1)S(1)} %collective-permute-done.12.above_ref.refs_1_, ...), custom_call_target="tpu_custom_call" | custom-call | flops 1073741824 | bytes 8388608 | tf_op jit(solution)/shard_map/last_queries/pallas_call | solution.py:680
  73.9 2.3 %window_attend.1.refs_6_ = f32[1024,128]{1,0:T(8,128)S(1)} custom-call(bf16[1024,384]{1,0:T(8,128)(2,1)S(1)} %get-tuple-element.95.win_ref, bf16[512,256]{1,0:T(8,128)(2,1)S(1)} %collective-permute-done.13.halo_ref), custom_call_target="tpu_custom_call" | custom-call | flops 402653184 | bytes 3145728 | tf_op jit(solution)/shard_map/window_attend/pallas_call | solution.py:687
  77.3 2.0 %collective-permute-start.18 = (bf16[256,512]{1,0:T(8,128)(2,1)S(1)}, bf16[256,512]{1,0:T(8,128)(2,1)S(1)}, u32[]{:S(2)}, u32[]{:S(2)}) collective-permute-start(bf16[256,512]{1,0:T(8,128)(2,1)S(1)} %finish1.1), channel_id=1, source_target_pairs={{0,1},{1,2},{2,3},{3,0},{4,5},{5,6},{6,7},{7,4},{8,9},{9,10},{10,1... | collective-permute-start | bytes 786440 | tf_op jit(solution)/shard_map/ppermute | solution.py:713
  80.4 10.4 %collective-permute-done.19.refs_3_ = bf16[256,512]{1,0:T(8,128)(2,1)S(1)} collective-permute-done((bf16[256,512]{1,0:T(8,128)(2,1)S(1)}, bf16[256,512]{1,0:T(8,128)(2,1)S(1)}, u32[]{:S(2)}, u32[]{:S(2)}) %collective-permute-start.19) | collective-permute-done | bytes 262176 | tf_op jit(solution)/shard_map/ppermute | solution.py:713
  90.8 9.2 %collective-permute-done.17.refs_1_ = bf16[256,512]{1,0:T(8,128)(2,1)S(1)} collective-permute-done((bf16[256,512]{1,0:T(8,128)(2,1)S(1)}, bf16[256,512]{1,0:T(8,128)(2,1)S(1)}, u32[]{:S(2)}, u32[]{:S(2)}) %collective-permute-start.17) | collective-permute-done | bytes 262176 | tf_op jit(solution)/shard_map/ppermute | solution.py:713
  (44 shorter events, 17.6 us)
Async XLA Ops:
  0.0 1.1 %copy-start.1 = (bf16[256,1536]{1,0:T(8,128)(2,1)S(1)}, bf16[256,1536]{1,0:T(8,128)(2,1)}, u32[]{:S(2)}) copy-start(bf16[256,1536]{1,0:T(8,128)(2,1)} %weight_ref.1) | copy-start | bytes 2359300
  2.0 7.0 %collective-permute-start = (bf16[48,384]{1,0:T(8,128)(2,1)S(1)}, bf16[48,384]{1,0:T(8,128)(2,1)S(1)}, u32[]{:S(2)}, u32[]{:S(2)}) collective-permute-start(bf16[48,384]{1,0:T(8,128)(2,1)S(1)} %get-tuple-element.55), channel_id=1, source_target_pairs={{0,1},{1,2},{2,3},{3,0},{4,5},{5,6},{6,7},{7,4},{8,9},{9,10},{10,1... | collective-permute-start | bytes 110600 | tf_op jit(solution)/shard_map/ppermute | solution.py:592
  5.0 5.2 %collective-permute-start.1 = (bf16[48,384]{1,0:T(8,128)(2,1)S(1)}, bf16[48,384]{1,0:T(8,128)(2,1)S(1)}, u32[]{:S(2)}, u32[]{:S(2)}) collective-permute-start(bf16[48,384]{1,0:T(8,128)(2,1)S(1)} %get-tuple-element.56), channel_id=1, source_target_pairs={{0,2},{1,3},{2,0},{3,1},{4,6},{5,7},{6,4},{7,5},{8,10},{9,11},{10,... | collective-permute-start | bytes 110600 | tf_op jit(solution)/shard_map/ppermute | solution.py:592
  7.6 4.0 %collective-permute-start.2 = (bf16[48,384]{1,0:T(8,128)(2,1)S(1)}, bf16[48,384]{1,0:T(8,128)(2,1)S(1)}, u32[]{:S(2)}, u32[]{:S(2)}) collective-permute-start(bf16[48,384]{1,0:T(8,128)(2,1)S(1)} %get-tuple-element.57), channel_id=1, source_target_pairs={{0,3},{1,0},{2,1},{3,2},{4,7},{5,4},{6,5},{7,6},{8,11},{9,8},{10,9... | collective-permute-start | bytes 110600 | tf_op jit(solution)/shard_map/ppermute | solution.py:592
  11.6 12.6 %collective-permute-start.3 = (bf16[256,1024]{1,0:T(8,128)(2,1)}, bf16[256,1024]{1,0:T(8,128)(2,1)S(1)}, u32[]{:S(2)}, u32[]{:S(2)}) collective-permute-start(bf16[256,1024]{1,0:T(8,128)(2,1)} %refs_0_.1), channel_id=1, source_target_pairs={{0,1},{1,2},{2,3},{4,5},{5,6},{6,7},{8,9},{9,10},{10,11},{12,13},{... | collective-permute-start | bytes 1572872 | tf_op jit(solution)/shard_map/ppermute | solution.py:580
  13.8 14.4 %collective-permute-start.4 = (bf16[256,1024]{1,0:T(8,128)(2,1)}, bf16[256,1024]{1,0:T(8,128)(2,1)S(1)}, u32[]{:S(2)}, u32[]{:S(2)}) collective-permute-start(bf16[256,1024]{1,0:T(8,128)(2,1)} %refs_0_.1), channel_id=1, source_target_pairs={{3,2},{2,1},{1,0},{7,6},{6,5},{5,4},{11,10},{10,9},{9,8},{15,14},{... | collective-permute-start | bytes 1572872 | tf_op jit(solution)/shard_map/ppermute | solution.py:580
  15.1 8.4 %collective-permute-start.5 = (bf16[4,32,384]{2,1,0:T(8,128)(2,1)S(1)}, bf16[4,32,384]{2,1,0:T(8,128)(2,1)S(1)}, u32[]{:S(2)}, u32[]{:S(2)}) collective-permute-start(bf16[4,32,384]{2,1,0:T(8,128)(2,1)S(1)} %get-tuple-element.66.refs_0_), channel_id=1, source_target_pairs={{0,8},{4,12},{8,16},{12,20},{16,24},{20,28},{24,0},{28,4},{1,9},{5... | collective-permute-start | bytes 294920 | tf_op jit(solution)/shard_map/ppermute | solution.py:609
  16.7 6.8 %collective-permute-start.6 = (bf16[4,32,384]{2,1,0:T(8,128)(2,1)S(1)}, bf16[4,32,384]{2,1,0:T(8,128)(2,1)S(1)}, u32[]{:S(2)}, u32[]{:S(2)}) collective-permute-start(bf16[4,32,384]{2,1,0:T(8,128)(2,1)S(1)} %get-tuple-element.66.refs_0_), channel_id=1, source_target_pairs={{0,16},{4,20},{8,24},{12,28},{16,0},{20,4},{24,8},{28,12},{1,17},{... | collective-permute-start | bytes 294920 | tf_op jit(solution)/shard_map/ppermute | solution.py:609
  18.2 5.3 %collective-permute-start.7 = (bf16[4,32,384]{2,1,0:T(8,128)(2,1)S(1)}, bf16[4,32,384]{2,1,0:T(8,128)(2,1)S(1)}, u32[]{:S(2)}, u32[]{:S(2)}) collective-permute-start(bf16[4,32,384]{2,1,0:T(8,128)(2,1)S(1)} %get-tuple-element.66.refs_0_), channel_id=1, source_target_pairs={{0,24},{4,28},{8,0},{12,4},{16,8},{20,12},{24,16},{28,20},{1,25},{... | collective-permute-start | bytes 294920 | tf_op jit(solution)/shard_map/ppermute | solution.py:609
  19.6 1.9 %copy-start = (bf16[1,1024,1536]{2,1,0:T(8,128)(2,1)S(1)}, bf16[1,1024,1536]{2,1,0:T(8,128)(2,1)}, u32[]{:S(2)}) copy-start(bf16[1,1024,1536]{2,1,0:T(8,128)(2,1)} %param.8) | copy-start | bytes 9437188
  21.5 1.0 %copy-start.2 = (bf16[256,1024]{1,0:T(8,128)(2,1)S(1)}, bf16[256,1024]{1,0:T(8,128)(2,1)}, u32[]{:S(2)}) copy-start(bf16[256,1024]{1,0:T(8,128)(2,1)} %refs_0_.1) | copy-start | bytes 1572868
  22.6 0.7 copy-start.3
  28.2 4.7 %collective-permute-start.8 = (bf16[256,1024]{1,0:T(8,128)(2,1)S(1)}, bf16[256,1024]{1,0:T(8,128)(2,1)S(1)}, u32[]{:S(2)}, u32[]{:S(2)}) collective-permute-start(bf16[256,1024]{1,0:T(8,128)(2,1)S(1)} %collective-permute-done.3.refs_1_), channel_id=1, source_target_pairs={{1,2},{2,3},{5,6},{6,7},{9,10},{10,11},{13,14},{14,15},{17,18},{18... | collective-permute-start | bytes 1572872 | tf_op jit(solution)/shard_map/ppermute | solution.py:580
  28.9 15.5 %collective-permute-start.9 = (bf16[256,1024]{1,0:T(8,128)(2,1)S(1)}, bf16[256,1024]{1,0:T(8,128)(2,1)S(1)}, u32[]{:S(2)}, u32[]{:S(2)}) collective-permute-start(bf16[256,1024]{1,0:T(8,128)(2,1)S(1)} %collective-permute-done.4.refs_2_), channel_id=1, source_target_pairs={{2,1},{1,0},{6,5},{5,4},{10,9},{9,8},{14,13},{13,12},{18,17},{17,1... | collective-permute-start | bytes 1572872 | tf_op jit(solution)/shard_map/ppermute | solution.py:580
  30.2 2.7 %collective-permute-start.10 = (bf16[4,4,32,384]{3,2,1,0:T(8,128)(2,1)S(1)}, bf16[4,4,32,384]{3,2,1,0:T(8,128)(2,1)S(1)}, u32[]{:S(2)}, u32[]{:S(2)}) collective-permute-start(bf16[4,4,32,384]{3,2,1,0:T(8,128)(2,1)S(1)} %combine.1.refs_5_), channel_id=1, source_target_pairs={{0,4},{4,0},{8,12},{12,8},{16,20},{20,16},{24,28},{28,24},{1,5},{5... | collective-permute-start | bytes 1179656 | tf_op jit(solution)/shard_map/ppermute | solution.py:631
  44.4 9.0 %collective-permute-start.11 = (bf16[256,1024]{1,0:T(8,128)(2,1)S(1)}, bf16[256,1024]{1,0:T(8,128)(2,1)S(1)}, u32[]{:S(2)}, u32[]{:S(2)}) collective-permute-start(bf16[256,1024]{1,0:T(8,128)(2,1)S(1)} %collective-permute-done.8.refs_0_.refs_3_), channel_id=1, source_target_pairs={{2,3},{6,7},{10,11},{14,15},{18,19},{22,23},{26,27},{30,31}} | collective-permute-start | bytes 1572872 | tf_op jit(solution)/shard_map/ppermute | solution.py:580
  45.1 11.9 %collective-permute-start.12 = (bf16[256,1024]{1,0:T(8,128)(2,1)S(1)}, bf16[256,1024]{1,0:T(8,128)(2,1)S(1)}, u32[]{:S(2)}, u32[]{:S(2)}) collective-permute-start(bf16[256,1024]{1,0:T(8,128)(2,1)S(1)} %collective-permute-done.9.refs_1_.refs_4_), channel_id=1, source_target_pairs={{1,0},{5,4},{9,8},{13,12},{17,16},{21,20},{25,24},{29,28}} | collective-permute-start | bytes 1572872 | tf_op jit(solution)/shard_map/ppermute | solution.py:580
  57.9 5.9 %collective-permute-start.14 = (bf16[512,128]{1,0:T(8,128)(2,1)S(1)}, bf16[512,128]{1,0:T(8,128)(2,1)S(1)}, u32[]{:S(2)}, u32[]{:S(2)}) collective-permute-start(bf16[512,128]{1,0:T(8,128)(2,1)S(1)} %get-tuple-element.97), channel_id=1, source_target_pairs={{0,16},{4,20},{8,24},{12,28},{1,17},{5,21},{9,25},{13,29},{2,18},{... | collective-permute-start | bytes 393224 | tf_op jit(solution)/shard_map/ppermute | solution.py:551
  62.1 11.9 %collective-permute-start.13 = (bf16[512,256]{1,0:T(8,128)(2,1)S(1)}, bf16[512,256]{1,0:T(8,128)(2,1)S(1)}, u32[]{:S(2)}, u32[]{:S(2)}) collective-permute-start(bf16[512,256]{1,0:T(8,128)(2,1)S(1)} %get-tuple-element.96), channel_id=1, source_target_pairs={{0,4},{4,8},{8,12},{12,16},{16,20},{20,24},{24,28},{1,5},{5,9},{9,... | collective-permute-start | bytes 786440 | tf_op jit(solution)/shard_map/ppermute | solution.py:21
  63.9 6.5 %collective-permute-start.15 = (bf16[512,128]{1,0:T(8,128)(2,1)S(1)}, bf16[512,128]{1,0:T(8,128)(2,1)S(1)}, u32[]{:S(2)}, u32[]{:S(2)}) collective-permute-start(bf16[512,128]{1,0:T(8,128)(2,1)S(1)} %get-tuple-element.100), channel_id=1, source_target_pairs={{0,8},{4,12},{8,0},{12,4},{16,24},{20,28},{24,16},{28,20},{1,9},{5... | collective-permute-start | bytes 393224 | tf_op jit(solution)/shard_map/ppermute | solution.py:560
  70.4 5.8 %collective-permute-start.16 = (bf16[512,128]{1,0:T(8,128)(2,1)S(1)}, bf16[512,128]{1,0:T(8,128)(2,1)S(1)}, u32[]{:S(2)}, u32[]{:S(2)}) collective-permute-start(bf16[512,128]{1,0:T(8,128)(2,1)S(1)} %get-tuple-element.102), channel_id=1, source_target_pairs={{0,4},{4,0},{8,12},{12,8},{16,20},{20,16},{24,28},{28,24},{1,5},{5... | collective-permute-start | bytes 393224 | tf_op jit(solution)/shard_map/ppermute | solution.py:560
  76.8 14.1 %collective-permute-start.19 = (bf16[256,512]{1,0:T(8,128)(2,1)S(1)}, bf16[256,512]{1,0:T(8,128)(2,1)S(1)}, u32[]{:S(2)}, u32[]{:S(2)}) collective-permute-start(bf16[256,512]{1,0:T(8,128)(2,1)S(1)} %finish3.1), channel_id=1, source_target_pairs={{0,3},{1,0},{2,1},{3,2},{4,7},{5,4},{6,5},{7,6},{8,11},{9,8},{10,9... | collective-permute-start | bytes 786440 | tf_op jit(solution)/shard_map/ppermute | solution.py:713
  77.3 13.5 %collective-permute-start.18 = (bf16[256,512]{1,0:T(8,128)(2,1)S(1)}, bf16[256,512]{1,0:T(8,128)(2,1)S(1)}, u32[]{:S(2)}, u32[]{:S(2)}) collective-permute-start(bf16[256,512]{1,0:T(8,128)(2,1)S(1)} %finish1.1), channel_id=1, source_target_pairs={{0,1},{1,2},{2,3},{3,0},{4,5},{5,6},{6,7},{7,4},{8,9},{9,10},{10,1... | collective-permute-start | bytes 786440 | tf_op jit(solution)/shard_map/ppermute | solution.py:713
  79.8 20.2 %collective-permute-start.17 = (bf16[256,512]{1,0:T(8,128)(2,1)S(1)}, bf16[256,512]{1,0:T(8,128)(2,1)S(1)}, u32[]{:S(2)}, u32[]{:S(2)}) collective-permute-start(bf16[256,512]{1,0:T(8,128)(2,1)S(1)} %finish2.1), channel_id=1, source_target_pairs={{0,2},{1,3},{2,0},{3,1},{4,6},{5,7},{6,4},{7,5},{8,10},{9,11},{10,... | collective-permute-start | bytes 786440 | tf_op jit(solution)/shard_map/ppermute | solution.py:713
  (1 other events, 0.7 us)

commit v8 on v7

--- a/solution.py
+++ b/solution.py
@@ -545,7 +545,7 @@
     sent_ref[...] = (prefix + jnp.where(earlier, state_ref[...], 0.0)).astype(jnp.bfloat16)
 
 
-def exclusive_prefix(state, sent):
+def exclusive_prefix(state, sent, beside):
     devices = lax.axis_size("ctx")
     bit = devices // 2
     got = lax.ppermute(sent, "ctx", [(i, i + bit) for i in range(devices) if not i & bit])
@@ -553,12 +553,14 @@
     kinds = [jax.ShapeDtypeStruct(state.shape, kind) for kind in (jnp.float32, jnp.bfloat16)]
     while bit > 1:
         bit //= 2
+        if bit == 1:
+            got, beside = lax.optimization_barrier((got, beside))
         held, sent = kernel_call(
             functools.partial(fold_body, bit), f"fold{bit}", kinds, 4 * state.size, 16 * state.size
         )(*prefix, got, state)
         prefix = (held,)
         got = lax.ppermute(sent, "ctx", [(i, i ^ bit) for i in range(devices)])
-    return held, got
+    return held, got, beside
 
 
 def dense_shards(tokens, routes, router, mem_weight, win_weight):
@@ -592,8 +594,7 @@
         lax.ppermute(packed[s], "mem", [(i, (i + s) % n_mem) for i in range(n_mem)])
         for s in range(1, n_mem)
     ]
-    sent_tokens, packed = lax.optimization_barrier((tokens, packed))
-    slots = list(moved(1, sent_tokens, sent_tokens))
+    slots = list(moved(1, tokens, tokens))
     all_routes, own_rows = kernel_call(
         arrange_body,
         "arrange",
@@ -604,11 +605,6 @@
         1 << 20,
         1 << 20,
     )(*packed)
-    chips = n_ctx // 2
-    of_chips = [
-        lax.ppermute(own_rows, "ctx", [(i, (i + 2 * s) % n_ctx) for i in range(n_ctx)])
-        for s in range(1, chips)
-    ]
     staged = kernel_call(
         stage_body,
         "stage",
@@ -616,19 +612,13 @@
         4 << 20,
         4 << 20,
     )(tokens, router.T, mem_weight[0])
-    of_core = kernel_call(
-        combine_body,
-        "combine",
-        jax.ShapeDtypeStruct((chips,) + own_rows.shape, low),
-        1 << 20,
-        1 << 20,
-    )(own_rows, *of_chips)
-    below, above, staged, of_core = lax.optimization_barrier((*slots, staged, of_core))
+    below, above, staged, all_routes, own_rows = lax.optimization_barrier(
+        (*slots, staged, all_routes, own_rows)
+    )
     own_tokens, router_rows, weight = staged
     slots = [own_tokens] + slots
     below, above = moved(2, below, above)
     slots += [below, above]
-    other_core = lax.ppermute(of_core, "ctx", [(i, i ^ 1) for i in range(n_ctx)])
     given = (all_routes, router_rows, weight)
     project_flops = 2 * count * depth * 3 * width
     kept = (shape(total, 3 * width), shape(total, HDIM, full), shape(width, HDIM, full))
@@ -639,7 +629,21 @@
         3 * project_flops,
         6 << 20,
     )(*slots[:3], *given)
-    below, above, held, other_core = lax.optimization_barrier((below, above, held, other_core))
+    chips = n_ctx // 2
+    of_chips = [
+        lax.ppermute(own_rows, "ctx", [(i, (i + 2 * s) % n_ctx) for i in range(n_ctx)])
+        for s in range(1, chips)
+    ]
+    held, of_chips = lax.optimization_barrier((held, of_chips))
+    of_core = kernel_call(
+        combine_body,
+        "combine",
+        jax.ShapeDtypeStruct((chips,) + own_rows.shape, low),
+        1 << 20,
+        1 << 20,
+    )(own_rows, *of_chips)
+    below, above, held, of_core = lax.optimization_barrier((below, above, held, of_core))
+    other_core = lax.ppermute(of_core, "ctx", [(i, i ^ 1) for i in range(n_ctx)])
     for hop in range(3, n_mem):
         below, above = moved(hop, below, above)
         slots += [below, above]
@@ -667,8 +671,7 @@
         2 * count * depth * 2 * width,
         3 << 20,
     )(below, above, all_routes, weight, state)
-    prefix, got = exclusive_prefix(state, sent)
-
+    win, last_kv = lax.optimization_barrier((win, last_kv))
     win, tail = kernel_call(
         functools.partial(window_late_body, n_mem, early),
         "window_late",
@@ -693,6 +696,9 @@
         scratch_shapes=[pltpu.VMEM((total + WINDOW, 2 * HDIM), low)],
     )(win, halo)
 
+    local = (last_query, last_coef, extra, window_part)
+    prefix, got, local = exclusive_prefix(state, sent, local)
+
     def finish(shift):
         return kernel_call(
             functools.partial(finish_body, n_mem, shift),
@@ -705,7 +711,7 @@
                 pltpu.VMEM((count, width), full),
                 pltpu.VMEM((count, HDIM), full),
             ],
-        )(proj, intra, coef, last_query, last_coef, extra, window_part, prefix, got)
+        )(proj, intra, coef, *local, prefix, got)
 
     parts = []
     for shift in sorted(range(1, n_mem), key=lambda s: abs(2 * s - n_mem)):

time: 101 us -> 99.4 us (0.984)
  waiting for transfers between devices: 47.2 us -> 45.3 us
    ppermute x3, waiting for transfers between devices: 19.1 us -> 11.4 us  [moved(): lax.ppermute(from_above, 'mem', down)]
    ppermute x1, waiting for transfers between devices: 0.46 us -> 5.01 us  [exclusive_prefix(): lax.ppermute(sent, 'ctx', [(i, i + bit) for i in range(devices) if not i...]
    ppermute x2, starting transfers between devices: 3.08 us -> 0.14 us  [exclusive_prefix(): got = lax.ppermute(sent, 'ctx', [(i, i ^ bit) for i in range(devices)])]
    ppermute x3, waiting for transfers between devices: 2.61 us -> 5.43 us  [dense_shards(): lax.ppermute(packed[s], 'mem', [(i, (i + s) % n_mem) for i in range(n_mem)])]
    ppermute x3, starting transfers between devices: 3.57 us -> 6.33 us  [moved(): lax.ppermute(from_below, 'mem', up)]
    ppermute x2, waiting for transfers between devices: 4.79 us -> 2.5 us  [exclusive_prefix(): got = lax.ppermute(sent, 'ctx', [(i, i ^ bit) for i in range(devices)])]
  transfers between devices with their start and end apart: 20 -> 20, of which waited for: 10 -> 9; matrix products, arithmetic and copies ran while one was open for 0% -> 0% of each run, Pallas kernels for 16% -> 16%
where the time goes in v8:
time: 99.4 us; the launch traced here: 99 us
  waiting for transfers between devices  45.3 us (46%)
  starting transfers between devices  29 us (29%)
  Pallas kernels  18.9 us (19%)
  local copies, waits for them, and re-layouts  5.43 us (5%)
    ppermute x3, waiting for transfers between devices, dense_shards(): parts.append(lax.ppermute(finish(shift), 'mem', pairs))  20.3 us
    ppermute x3, waiting for transfers between devices, moved(): lax.ppermute(from_above, 'mem', down)  11.4 us
    ppermute x3, starting transfers between devices, dense_shards(): lax.ppermute(packed[s], 'mem', [(i, (i + s) % n_mem) for i in range(n_mem)])  6.61 us
    ppermute x3, starting transfers between devices, moved(): lax.ppermute(from_below, 'mem', up)  6.33 us
    pallas_call x1, Pallas kernels, dense_shards(): kernel_call(functools.partial(arrivals_body, n_mem, 3, early, True), 'mid...  5.57 us
    unnamed x10, local copies, waits for them, and re-layouts  5.43 us
    ppermute x3, waiting for transfers between devices, dense_shards(): lax.ppermute(packed[s], 'mem', [(i, (i + s) % n_mem) for i in range(n_mem)])  5.43 us
    ppermute x1, waiting for transfers between devices, exclusive_prefix(): lax.ppermute(sent, 'ctx', [(i, i + bit) for i in range(devices) if not i...  5.01 us
  transfers between devices with their start and end apart: 20, of which 9 were waited for; matrix products, arithmetic and copies ran while one was open for 0% of the time, Pallas kernels for 16%

profile of v8, /device:TPU:0, one launch (start us, length us, event | category | flops | bytes accessed | tf_op | source)
XLA Modules:
  0.0 99.0 jit_solution(970945641002842466)
XLA Ops:
  0.0 5.0 %collective-permute-start = (bf16[256,1024]{1,0:T(8,128)(2,1)}, bf16[256,1024]{1,0:T(8,128)(2,1)S(1)}, u32[]{:S(2)}, u32[]{:S(2)}) collective-permute-start(bf16[256,1024]{1,0:T(8,128)(2,1)} %refs_0_.1), channel_id=1, source_target_pairs={{0,1},{1,2},{2,3},{4,5},{5,6},{6,7},{8,9},{9,10},{10,11},{12,13},{... | collective-permute-start | bytes 1572872 | tf_op jit(solution)/shard_map/ppermute | solution.py:582
  5.0 1.3 %collective-permute-start.1 = (bf16[256,1024]{1,0:T(8,128)(2,1)}, bf16[256,1024]{1,0:T(8,128)(2,1)S(1)}, u32[]{:S(2)}, u32[]{:S(2)}) collective-permute-start(bf16[256,1024]{1,0:T(8,128)(2,1)} %refs_0_.1), channel_id=1, source_target_pairs={{3,2},{2,1},{1,0},{7,6},{6,5},{5,4},{11,10},{10,9},{9,8},{15,14},{... | collective-permute-start | bytes 1572872 | tf_op jit(solution)/shard_map/ppermute | solution.py:582
  8.2 2.7 %collective-permute-start.2 = (bf16[48,384]{1,0:T(8,128)(2,1)S(1)}, bf16[48,384]{1,0:T(8,128)(2,1)S(1)}, u32[]{:S(2)}, u32[]{:S(2)}) collective-permute-start(bf16[48,384]{1,0:T(8,128)(2,1)S(1)} %get-tuple-element.67), channel_id=1, source_target_pairs={{0,1},{1,2},{2,3},{3,0},{4,5},{5,6},{6,7},{7,4},{8,9},{9,10},{10,1... | collective-permute-start | bytes 110600 | tf_op jit(solution)/shard_map/ppermute | solution.py:594
  10.9 2.6 %collective-permute-start.3 = (bf16[48,384]{1,0:T(8,128)(2,1)S(1)}, bf16[48,384]{1,0:T(8,128)(2,1)S(1)}, u32[]{:S(2)}, u32[]{:S(2)}) collective-permute-start(bf16[48,384]{1,0:T(8,128)(2,1)S(1)} %get-tuple-element.68), channel_id=1, source_target_pairs={{0,2},{1,3},{2,0},{3,1},{4,6},{5,7},{6,4},{7,5},{8,10},{9,11},{10,... | collective-permute-start | bytes 110600 | tf_op jit(solution)/shard_map/ppermute | solution.py:594
  13.5 1.3 %collective-permute-start.4 = (bf16[48,384]{1,0:T(8,128)(2,1)S(1)}, bf16[48,384]{1,0:T(8,128)(2,1)S(1)}, u32[]{:S(2)}, u32[]{:S(2)}) collective-permute-start(bf16[48,384]{1,0:T(8,128)(2,1)S(1)} %get-tuple-element.69), channel_id=1, source_target_pairs={{0,3},{1,0},{2,1},{3,2},{4,7},{5,4},{6,5},{7,6},{8,11},{9,8},{10,9... | collective-permute-start | bytes 110600 | tf_op jit(solution)/shard_map/ppermute | solution.py:594
  14.8 1.9 %copy-done = bf16[1,1024,1536]{2,1,0:T(8,128)(2,1)S(1)} copy-done((bf16[1,1024,1536]{2,1,0:T(8,128)(2,1)S(1)}, bf16[1,1024,1536]{2,1,0:T(8,128)(2,1)}, u32[]{:S(2)}) %copy-start) | copy-done | bytes 3145752
  18.7 5.4 %collective-permute-done.2.refs_1_ = bf16[48,384]{1,0:T(8,128)(2,1)S(1)} collective-permute-done((bf16[48,384]{1,0:T(8,128)(2,1)S(1)}, bf16[48,384]{1,0:T(8,128)(2,1)S(1)}, u32[]{:S(2)}, u32[]{:S(2)}) %collective-permute-start.2) | collective-permute-done | bytes 36896 | tf_op jit(solution)/shard_map/ppermute | solution.py:594
  26.2 1.5 %collective-permute-start.7 = (bf16[4,32,384]{2,1,0:T(8,128)(2,1)S(1)}, bf16[4,32,384]{2,1,0:T(8,128)(2,1)S(1)}, u32[]{:S(2)}, u32[]{:S(2)}) collective-permute-start(bf16[4,32,384]{2,1,0:T(8,128)(2,1)S(1)} %get-tuple-element.81.refs_0_), channel_id=1, source_target_pairs={{0,8},{4,12},{8,16},{12,20},{16,24},{20,28},{24,0},{28,4},{1,9},{5... | collective-permute-start | bytes 294920 | tf_op jit(solution)/shard_map/ppermute | solution.py:634
  27.7 1.5 %collective-permute-start.8 = (bf16[4,32,384]{2,1,0:T(8,128)(2,1)S(1)}, bf16[4,32,384]{2,1,0:T(8,128)(2,1)S(1)}, u32[]{:S(2)}, u32[]{:S(2)}) collective-permute-start(bf16[4,32,384]{2,1,0:T(8,128)(2,1)S(1)} %get-tuple-element.81.refs_0_), channel_id=1, source_target_pairs={{0,16},{4,20},{8,24},{12,28},{16,0},{20,4},{24,8},{28,12},{1,17},{... | collective-permute-start | bytes 294920 | tf_op jit(solution)/shard_map/ppermute | solution.py:634
  29.2 1.4 %collective-permute-start.9 = (bf16[4,32,384]{2,1,0:T(8,128)(2,1)S(1)}, bf16[4,32,384]{2,1,0:T(8,128)(2,1)S(1)}, u32[]{:S(2)}, u32[]{:S(2)}) collective-permute-start(bf16[4,32,384]{2,1,0:T(8,128)(2,1)S(1)} %get-tuple-element.81.refs_0_), channel_id=1, source_target_pairs={{0,24},{4,28},{8,0},{12,4},{16,8},{20,12},{24,16},{28,20},{1,25},{... | collective-permute-start | bytes 294920 | tf_op jit(solution)/shard_map/ppermute | solution.py:634
  30.7 2.6 %near_rows.1 = (bf16[1024,1536]{1,0:T(8,128)(2,1)S(1)}, f32[1024,128]{1,0:T(8,128)S(1)}, f32[512,128]{1,0:T(8,128)S(1)}) custom-call(bf16[256,1024]{1,0:T(8,128)(2,1)S(1)} %get-tuple-element.77.refs_0_, bf16[256,1024]{1,0:T(8,128)(2,1)S(1)} %collective-permute-done.refs_1_, bf16[256,1024]{1,0:T(8,128)(2,1)S(1)} %collective-permute-done.1.refs_2_, ...), custom_call_target="tpu_custom_call" | custom-call | flops 2415919104 | bytes 6291456 | tf_op jit(solution)/shard_map/near_rows/pallas_call | solution.py:625
  33.9 6.4 %collective-permute-done.6.refs_1_.refs_4_ = bf16[256,1024]{1,0:T(8,128)(2,1)S(1)} collective-permute-done((bf16[256,1024]{1,0:T(8,128)(2,1)S(1)}, bf16[256,1024]{1,0:T(8,128)(2,1)S(1)}, u32[]{:S(2)}, u32[]{:S(2)}) %collective-permute-start.6) | collective-permute-done | bytes 524320 | tf_op jit(solution)/shard_map/ppermute | solution.py:582
  42.4 5.6 %middle_rows.1 = (bf16[1024,1536]{1,0:T(8,128)(2,1)S(1)}, f32[1024,128]{1,0:T(8,128)S(1)}, f32[512,128]{1,0:T(8,128)S(1)}, f32[1024,512]{1,0:T(8,128)S(1)}) custom-call(bf16[256,1024]{1,0:T(8,128)(2,1)S(1)} %collective-permute-done.5.refs_0_.refs_3_, bf16[256,1024]{1,0:T(8,128)(2,1)S(1)} %collective-permute-done.6.refs_1_.refs_4_, ...), custom_call_target="tpu_custom_call" | custom-call | flops 2415919104 | bytes 6291456 | tf_op jit(solution)/shard_map/middle_rows/pallas_call | solution.py:652
  47.9 1.4 %window_early.1 = (bf16[1024,384]{1,0:T(8,128)(2,1)S(1)}, bf16[1024,384]{1,0:T(8,128)(2,1)S(1)}) custom-call(bf16[256,1024]{1,0:T(8,128)(2,1)S(1)} %get-tuple-element.77.refs_0_, bf16[256,1024]{1,0:T(8,128)(2,1)S(1)} %collective-permute-done.refs_1_, bf16[256,1024]{1,0:T(8,128)(2,1)S(1)} %collective-permute-done.1.refs_2_, ...), custom_call_target="tpu_custom_call" | custom-call | flops 805306368 | bytes 5242880 | tf_op jit(solution)/shard_map/window_early/pallas_call | solution.py:659
  49.4 5.1 %collective-permute-done.11.above_ref.refs_1_ = bf16[256,1024]{1,0:T(8,128)(2,1)S(1)} collective-permute-done((bf16[256,1024]{1,0:T(8,128)(2,1)S(1)}, bf16[256,1024]{1,0:T(8,128)(2,1)S(1)}, u32[]{:S(2)}, u32[]{:S(2)}) %collective-permute-start.11) | collective-permute-done | bytes 524320 | tf_op jit(solution)/shard_map/ppermute | solution.py:582
  56.1 1.3 %collective-permute-start.15 = (bf16[512,256]{1,0:T(8,128)(2,1)S(1)}, bf16[512,256]{1,0:T(8,128)(2,1)S(1)}, u32[]{:S(2)}, u32[]{:S(2)}) collective-permute-start(bf16[512,256]{1,0:T(8,128)(2,1)S(1)} %get-tuple-element.112), channel_id=1, source_target_pairs={{0,4},{4,8},{8,12},{12,16},{16,20},{20,24},{24,28},{1,5},{5,9},{9,... | collective-permute-start | bytes 786440 | tf_op jit(solution)/shard_map/ppermute | solution.py:21
  57.4 4.0 %collective-permute-start.13 = (bf16[512,128]{1,0:T(8,128)(2,1)S(1)}, bf16[512,128]{1,0:T(8,128)(2,1)S(1)}, u32[]{:S(2)}, u32[]{:S(2)}) collective-permute-start(bf16[512,128]{1,0:T(8,128)(2,1)S(1)} %get-tuple-element.100), channel_id=1, source_target_pairs={{0,16},{4,20},{8,24},{12,28},{1,17},{5,21},{9,25},{13,29},{2,18},{... | collective-permute-start | bytes 393224 | tf_op jit(solution)/shard_map/ppermute | solution.py:551
  61.5 5.0 %collective-permute-done.13.refs_0_ = bf16[512,128]{1,0:T(8,128)(2,1)S(1)} collective-permute-done((bf16[512,128]{1,0:T(8,128)(2,1)S(1)}, bf16[512,128]{1,0:T(8,128)(2,1)S(1)}, u32[]{:S(2)}, u32[]{:S(2)}) %collective-permute-start.13) | collective-permute-done | bytes 131104 | tf_op jit(solution)/shard_map/ppermute | solution.py:551
  66.6 2.1 %last_queries.1 = (bf16[256,512]{1,0:T(8,128)(2,1)S(1)}, f32[256,128]{1,0:T(8,128)S(1)}, f32[1024,512]{1,0:T(8,128)S(1)}) custom-call(bf16[256,1024]{1,0:T(8,128)(2,1)S(1)} %collective-permute-done.10.below_ref.refs_0_, bf16[256,1024]{1,0:T(8,128)(2,1)S(1)} %collective-permute-done.11.above_ref.refs_1_, ...), custom_call_target="tpu_custom_call" | custom-call | flops 1073741824 | bytes 8388608 | tf_op jit(solution)/shard_map/last_queries/pallas_call | solution.py:683
  68.7 2.3 %window_attend.1.refs_6_ = f32[1024,128]{1,0:T(8,128)S(1)} custom-call(bf16[1024,384]{1,0:T(8,128)(2,1)S(1)} %get-tuple-element.111.win_ref, bf16[512,256]{1,0:T(8,128)(2,1)S(1)} %collective-permute-done.15.halo_ref), custom_call_target="tpu_custom_call" | custom-call | flops 402653184 | bytes 3145728 | tf_op jit(solution)/shard_map/window_attend/pallas_call | solution.py:690
  72.4 1.3 %collective-permute-done.16.refs_8_ = bf16[512,128]{1,0:T(8,128)(2,1)S(1)} collective-permute-done((bf16[512,128]{1,0:T(8,128)(2,1)S(1)}, bf16[512,128]{1,0:T(8,128)(2,1)S(1)}, u32[]{:S(2)}, u32[]{:S(2)}) %collective-permute-start.16) | collective-permute-done | bytes 131104 | tf_op jit(solution)/shard_map/ppermute | solution.py:562
  74.7 2.0 %collective-permute-start.18 = (bf16[256,512]{1,0:T(8,128)(2,1)S(1)}, bf16[256,512]{1,0:T(8,128)(2,1)S(1)}, u32[]{:S(2)}, u32[]{:S(2)}) collective-permute-start(bf16[256,512]{1,0:T(8,128)(2,1)S(1)} %finish1.1), channel_id=1, source_target_pairs={{0,1},{1,2},{2,3},{3,0},{4,5},{5,6},{6,7},{7,4},{8,9},{9,10},{10,1... | collective-permute-start | bytes 786440 | tf_op jit(solution)/shard_map/ppermute | solution.py:719
  77.8 10.4 %collective-permute-done.19.refs_3_ = bf16[256,512]{1,0:T(8,128)(2,1)S(1)} collective-permute-done((bf16[256,512]{1,0:T(8,128)(2,1)S(1)}, bf16[256,512]{1,0:T(8,128)(2,1)S(1)}, u32[]{:S(2)}, u32[]{:S(2)}) %collective-permute-start.19) | collective-permute-done | bytes 262176 | tf_op jit(solution)/shard_map/ppermute | solution.py:719
  88.2 9.9 %collective-permute-done.17.refs_1_ = bf16[256,512]{1,0:T(8,128)(2,1)S(1)} collective-permute-done((bf16[256,512]{1,0:T(8,128)(2,1)S(1)}, bf16[256,512]{1,0:T(8,128)(2,1)S(1)}, u32[]{:S(2)}, u32[]{:S(2)}) %collective-permute-start.17) | collective-permute-done | bytes 262176 | tf_op jit(solution)/shard_map/ppermute | solution.py:719
  (44 shorter events, 14.5 us)
Async XLA Ops:
  0.0 24.2 %collective-permute-start = (bf16[256,1024]{1,0:T(8,128)(2,1)}, bf16[256,1024]{1,0:T(8,128)(2,1)S(1)}, u32[]{:S(2)}, u32[]{:S(2)}) collective-permute-start(bf16[256,1024]{1,0:T(8,128)(2,1)} %refs_0_.1), channel_id=1, source_target_pairs={{0,1},{1,2},{2,3},{4,5},{5,6},{6,7},{8,9},{9,10},{10,11},{12,13},{... | collective-permute-start | bytes 1572872 | tf_op jit(solution)/shard_map/ppermute | solution.py:582
  5.0 19.2 %collective-permute-start.1 = (bf16[256,1024]{1,0:T(8,128)(2,1)}, bf16[256,1024]{1,0:T(8,128)(2,1)S(1)}, u32[]{:S(2)}, u32[]{:S(2)}) collective-permute-start(bf16[256,1024]{1,0:T(8,128)(2,1)} %refs_0_.1), channel_id=1, source_target_pairs={{3,2},{2,1},{1,0},{7,6},{6,5},{5,4},{11,10},{10,9},{9,8},{15,14},{... | collective-permute-start | bytes 1572872 | tf_op jit(solution)/shard_map/ppermute | solution.py:582
  6.3 1.1 %copy-start.1 = (bf16[256,1536]{1,0:T(8,128)(2,1)S(1)}, bf16[256,1536]{1,0:T(8,128)(2,1)}, u32[]{:S(2)}) copy-start(bf16[256,1536]{1,0:T(8,128)(2,1)} %weight_ref.1) | copy-start | bytes 2359300
  8.2 15.9 %collective-permute-start.2 = (bf16[48,384]{1,0:T(8,128)(2,1)S(1)}, bf16[48,384]{1,0:T(8,128)(2,1)S(1)}, u32[]{:S(2)}, u32[]{:S(2)}) collective-permute-start(bf16[48,384]{1,0:T(8,128)(2,1)S(1)} %get-tuple-element.67), channel_id=1, source_target_pairs={{0,1},{1,2},{2,3},{3,0},{4,5},{5,6},{6,7},{7,4},{8,9},{9,10},{10,1... | collective-permute-start | bytes 110600 | tf_op jit(solution)/shard_map/ppermute | solution.py:594
  10.9 13.2 %collective-permute-start.3 = (bf16[48,384]{1,0:T(8,128)(2,1)S(1)}, bf16[48,384]{1,0:T(8,128)(2,1)S(1)}, u32[]{:S(2)}, u32[]{:S(2)}) collective-permute-start(bf16[48,384]{1,0:T(8,128)(2,1)S(1)} %get-tuple-element.68), channel_id=1, source_target_pairs={{0,2},{1,3},{2,0},{3,1},{4,6},{5,7},{6,4},{7,5},{8,10},{9,11},{10,... | collective-permute-start | bytes 110600 | tf_op jit(solution)/shard_map/ppermute | solution.py:594
  13.5 10.6 %collective-permute-start.4 = (bf16[48,384]{1,0:T(8,128)(2,1)S(1)}, bf16[48,384]{1,0:T(8,128)(2,1)S(1)}, u32[]{:S(2)}, u32[]{:S(2)}) collective-permute-start(bf16[48,384]{1,0:T(8,128)(2,1)S(1)} %get-tuple-element.69), channel_id=1, source_target_pairs={{0,3},{1,0},{2,1},{3,2},{4,7},{5,4},{6,5},{7,6},{8,11},{9,8},{10,9... | collective-permute-start | bytes 110600 | tf_op jit(solution)/shard_map/ppermute | solution.py:594
  14.8 1.9 %copy-start = (bf16[1,1024,1536]{2,1,0:T(8,128)(2,1)S(1)}, bf16[1,1024,1536]{2,1,0:T(8,128)(2,1)}, u32[]{:S(2)}) copy-start(bf16[1,1024,1536]{2,1,0:T(8,128)(2,1)} %param.8) | copy-start | bytes 9437188
  16.7 1.0 %copy-start.2 = (bf16[256,1024]{1,0:T(8,128)(2,1)S(1)}, bf16[256,1024]{1,0:T(8,128)(2,1)}, u32[]{:S(2)}) copy-start(bf16[256,1024]{1,0:T(8,128)(2,1)} %refs_0_.1) | copy-start | bytes 1572868
  17.8 0.7 copy-start.3
  24.2 9.7 %collective-permute-start.5 = (bf16[256,1024]{1,0:T(8,128)(2,1)S(1)}, bf16[256,1024]{1,0:T(8,128)(2,1)S(1)}, u32[]{:S(2)}, u32[]{:S(2)}) collective-permute-start(bf16[256,1024]{1,0:T(8,128)(2,1)S(1)} %collective-permute-done.refs_1_), channel_id=1, source_target_pairs={{1,2},{2,3},{5,6},{6,7},{9,10},{10,11},{13,14},{14,15},{17,18},{18... | collective-permute-start | bytes 1572872 | tf_op jit(solution)/shard_map/ppermute | solution.py:582
  24.9 15.4 %collective-permute-start.6 = (bf16[256,1024]{1,0:T(8,128)(2,1)S(1)}, bf16[256,1024]{1,0:T(8,128)(2,1)S(1)}, u32[]{:S(2)}, u32[]{:S(2)}) collective-permute-start(bf16[256,1024]{1,0:T(8,128)(2,1)S(1)} %collective-permute-done.1.refs_2_), channel_id=1, source_target_pairs={{2,1},{1,0},{6,5},{5,4},{10,9},{9,8},{14,13},{13,12},{18,17},{17,1... | collective-permute-start | bytes 1572872 | tf_op jit(solution)/shard_map/ppermute | solution.py:582
  26.2 7.1 %collective-permute-start.7 = (bf16[4,32,384]{2,1,0:T(8,128)(2,1)S(1)}, bf16[4,32,384]{2,1,0:T(8,128)(2,1)S(1)}, u32[]{:S(2)}, u32[]{:S(2)}) collective-permute-start(bf16[4,32,384]{2,1,0:T(8,128)(2,1)S(1)} %get-tuple-element.81.refs_0_), channel_id=1, source_target_pairs={{0,8},{4,12},{8,16},{12,20},{16,24},{20,28},{24,0},{28,4},{1,9},{5... | collective-permute-start | bytes 294920 | tf_op jit(solution)/shard_map/ppermute | solution.py:634
  27.7 5.6 %collective-permute-start.8 = (bf16[4,32,384]{2,1,0:T(8,128)(2,1)S(1)}, bf16[4,32,384]{2,1,0:T(8,128)(2,1)S(1)}, u32[]{:S(2)}, u32[]{:S(2)}) collective-permute-start(bf16[4,32,384]{2,1,0:T(8,128)(2,1)S(1)} %get-tuple-element.81.refs_0_), channel_id=1, source_target_pairs={{0,16},{4,20},{8,24},{12,28},{16,0},{20,4},{24,8},{28,12},{1,17},{... | collective-permute-start | bytes 294920 | tf_op jit(solution)/shard_map/ppermute | solution.py:634
  29.2 4.6 %collective-permute-start.9 = (bf16[4,32,384]{2,1,0:T(8,128)(2,1)S(1)}, bf16[4,32,384]{2,1,0:T(8,128)(2,1)S(1)}, u32[]{:S(2)}, u32[]{:S(2)}) collective-permute-start(bf16[4,32,384]{2,1,0:T(8,128)(2,1)S(1)} %get-tuple-element.81.refs_0_), channel_id=1, source_target_pairs={{0,24},{4,28},{8,0},{12,4},{16,8},{20,12},{24,16},{28,20},{1,25},{... | collective-permute-start | bytes 294920 | tf_op jit(solution)/shard_map/ppermute | solution.py:634
  40.3 9.1 %collective-permute-start.10 = (bf16[256,1024]{1,0:T(8,128)(2,1)S(1)}, bf16[256,1024]{1,0:T(8,128)(2,1)S(1)}, u32[]{:S(2)}, u32[]{:S(2)}) collective-permute-start(bf16[256,1024]{1,0:T(8,128)(2,1)S(1)} %collective-permute-done.5.refs_0_.refs_3_), channel_id=1, source_target_pairs={{2,3},{6,7},{10,11},{14,15},{18,19},{22,23},{26,27},{30,31}} | collective-permute-start | bytes 1572872 | tf_op jit(solution)/shard_map/ppermute | solution.py:582
  41.0 13.4 %collective-permute-start.11 = (bf16[256,1024]{1,0:T(8,128)(2,1)S(1)}, bf16[256,1024]{1,0:T(8,128)(2,1)S(1)}, u32[]{:S(2)}, u32[]{:S(2)}) collective-permute-start(bf16[256,1024]{1,0:T(8,128)(2,1)S(1)} %collective-permute-done.6.refs_1_.refs_4_), channel_id=1, source_target_pairs={{1,0},{5,4},{9,8},{13,12},{17,16},{21,20},{25,24},{29,28}} | collective-permute-start | bytes 1572872 | tf_op jit(solution)/shard_map/ppermute | solution.py:582
  42.3 5.7 %collective-permute-start.12 = (bf16[4,4,32,384]{3,2,1,0:T(8,128)(2,1)S(1)}, bf16[4,4,32,384]{3,2,1,0:T(8,128)(2,1)S(1)}, u32[]{:S(2)}, u32[]{:S(2)}) collective-permute-start(bf16[4,4,32,384]{3,2,1,0:T(8,128)(2,1)S(1)} %combine.1.refs_5_), channel_id=1, source_target_pairs={{0,4},{4,0},{8,12},{12,8},{16,20},{20,16},{24,28},{28,24},{1,5},{5... | collective-permute-start | bytes 1179656 | tf_op jit(solution)/shard_map/ppermute | solution.py:646
  56.1 12.6 %collective-permute-start.15 = (bf16[512,256]{1,0:T(8,128)(2,1)S(1)}, bf16[512,256]{1,0:T(8,128)(2,1)S(1)}, u32[]{:S(2)}, u32[]{:S(2)}) collective-permute-start(bf16[512,256]{1,0:T(8,128)(2,1)S(1)} %get-tuple-element.112), channel_id=1, source_target_pairs={{0,4},{4,8},{8,12},{12,16},{16,20},{20,24},{24,28},{1,5},{5,9},{9,... | collective-permute-start | bytes 786440 | tf_op jit(solution)/shard_map/ppermute | solution.py:21
  57.4 9.1 %collective-permute-start.13 = (bf16[512,128]{1,0:T(8,128)(2,1)S(1)}, bf16[512,128]{1,0:T(8,128)(2,1)S(1)}, u32[]{:S(2)}, u32[]{:S(2)}) collective-permute-start(bf16[512,128]{1,0:T(8,128)(2,1)S(1)} %get-tuple-element.100), channel_id=1, source_target_pairs={{0,16},{4,20},{8,24},{12,28},{1,17},{5,21},{9,25},{13,29},{2,18},{... | collective-permute-start | bytes 393224 | tf_op jit(solution)/shard_map/ppermute | solution.py:551
  66.5 5.7 %collective-permute-start.14 = (bf16[512,128]{1,0:T(8,128)(2,1)S(1)}, bf16[512,128]{1,0:T(8,128)(2,1)S(1)}, u32[]{:S(2)}, u32[]{:S(2)}) collective-permute-start(bf16[512,128]{1,0:T(8,128)(2,1)S(1)} %get-tuple-element.102), channel_id=1, source_target_pairs={{0,8},{4,12},{8,0},{12,4},{16,24},{20,28},{24,16},{28,20},{1,9},{5... | collective-permute-start | bytes 393224 | tf_op jit(solution)/shard_map/ppermute | solution.py:562
  72.3 1.4 %collective-permute-start.16 = (bf16[512,128]{1,0:T(8,128)(2,1)S(1)}, bf16[512,128]{1,0:T(8,128)(2,1)S(1)}, u32[]{:S(2)}, u32[]{:S(2)}) collective-permute-start(bf16[512,128]{1,0:T(8,128)(2,1)S(1)} %get-tuple-element.120), channel_id=1, source_target_pairs={{0,4},{4,0},{8,12},{12,8},{16,20},{20,16},{24,28},{28,24},{1,5},{5... | collective-permute-start | bytes 393224 | tf_op jit(solution)/shard_map/ppermute | solution.py:562
  74.2 14.0 %collective-permute-start.19 = (bf16[256,512]{1,0:T(8,128)(2,1)S(1)}, bf16[256,512]{1,0:T(8,128)(2,1)S(1)}, u32[]{:S(2)}, u32[]{:S(2)}) collective-permute-start(bf16[256,512]{1,0:T(8,128)(2,1)S(1)} %finish3.1), channel_id=1, source_target_pairs={{0,3},{1,0},{2,1},{3,2},{4,7},{5,4},{6,5},{7,6},{8,11},{9,8},{10,9... | collective-permute-start | bytes 786440 | tf_op jit(solution)/shard_map/ppermute | solution.py:719
  74.7 13.5 %collective-permute-start.18 = (bf16[256,512]{1,0:T(8,128)(2,1)S(1)}, bf16[256,512]{1,0:T(8,128)(2,1)S(1)}, u32[]{:S(2)}, u32[]{:S(2)}) collective-permute-start(bf16[256,512]{1,0:T(8,128)(2,1)S(1)} %finish1.1), channel_id=1, source_target_pairs={{0,1},{1,2},{2,3},{3,0},{4,5},{5,6},{6,7},{7,4},{8,9},{9,10},{10,1... | collective-permute-start | bytes 786440 | tf_op jit(solution)/shard_map/ppermute | solution.py:719
  77.2 20.9 %collective-permute-start.17 = (bf16[256,512]{1,0:T(8,128)(2,1)S(1)}, bf16[256,512]{1,0:T(8,128)(2,1)S(1)}, u32[]{:S(2)}, u32[]{:S(2)}) collective-permute-start(bf16[256,512]{1,0:T(8,128)(2,1)S(1)} %finish2.1), channel_id=1, source_target_pairs={{0,2},{1,3},{2,0},{3,1},{4,6},{5,7},{6,4},{7,5},{8,10},{9,11},{10,... | collective-permute-start | bytes 786440 | tf_op jit(solution)/shard_map/ppermute | solution.py:719
  (1 other events, 0.7 us)

commit v9 on v8

--- a/solution.py
+++ b/solution.py
@@ -441,7 +441,7 @@
 
 
 def window_early_body(n_mem, *refs):
-    sources, (mine_ref, other_ref, win_ref, full_ref) = refs[:-4], refs[-4:]
+    sources, (mine_ref, other_ref, win_ref, full_ref, tail_ref) = refs[:-5], refs[-5:]
     chips, origins, depth, _ = mine_ref.shape
     core = lax.rem(lax.axis_index("ctx"), 2)
     for pieces_ref, at in ((mine_ref, core), (other_ref, 1 - core)):
@@ -450,19 +450,26 @@
                 start = (origin * chips + chip) * 2 + at
                 full_ref[rows_of(start, depth), :] = pieces_ref[chip, origin]
     project_slots(n_mem, 0, sources, full_ref, win_ref)
+    total = win_ref.shape[0]
+    tail_ref[...] = win_ref[total - WINDOW : total, HDIM:]
 
 
 def window_late_body(n_mem, first_slot, *refs):
     sources, (full_ref, before_ref, win_ref, tail_ref) = refs[:-4], refs[-4:]
     win_ref[...] = before_ref[...]
     project_slots(n_mem, first_slot, sources, full_ref, win_ref)
-    total = win_ref.shape[0]
-    tail_ref[...] = win_ref[total - WINDOW : total, HDIM:]
-
-
-def window_attend_body(count, win_ref, halo_ref, out_ref, keys_ref):
+    total, count = win_ref.shape[0], tail_ref.shape[0]
+    tail_ref[...] = win_ref[total - count : total, HDIM:]
+
+
+def window_attend_body(count, win_ref, halo_ref, late_ref, out_ref, keys_ref):
     total = win_ref.shape[0]
     keys_ref[0:WINDOW, :] = halo_ref[...]
+
+    @pl.when(lax.axis_index("mem") == 0)
+    def _():
+        keys_ref[WINDOW - count : WINDOW, :] = late_ref[...]
+
     span = count + WINDOW
     row = lax.broadcasted_iota(jnp.int32, (count, span), 0)
     column = lax.broadcasted_iota(jnp.int32, (count, span), 1)
@@ -543,24 +550,6 @@
     prefix_ref[...] = prefix
     earlier = (lax.axis_index("ctx") & bit) == 0
     sent_ref[...] = (prefix + jnp.where(earlier, state_ref[...], 0.0)).astype(jnp.bfloat16)
-
-
-def exclusive_prefix(state, sent, beside):
-    devices = lax.axis_size("ctx")
-    bit = devices // 2
-    got = lax.ppermute(sent, "ctx", [(i, i + bit) for i in range(devices) if not i & bit])
-    prefix = ()
-    kinds = [jax.ShapeDtypeStruct(state.shape, kind) for kind in (jnp.float32, jnp.bfloat16)]
-    while bit > 1:
-        bit //= 2
-        if bit == 1:
-            got, beside = lax.optimization_barrier((got, beside))
-        held, sent = kernel_call(
-            functools.partial(fold_body, bit), f"fold{bit}", kinds, 4 * state.size, 16 * state.size
-        )(*prefix, got, state)
-        prefix = (held,)
-        got = lax.ppermute(sent, "ctx", [(i, i ^ bit) for i in range(devices)])
-    return held, got, beside
 
 
 def dense_shards(tokens, routes, router, mem_weight, win_weight):
@@ -656,13 +645,14 @@
         3 * project_flops,
         6 << 20,
     )(*slots[3:early], *given, *held)
-    win, win_weight_full = kernel_call(
+    win, win_weight_full, tail = kernel_call(
         functools.partial(window_early_body, n_mem),
         "window_early",
-        (shape(total, 3 * HDIM), shape(depth, 3 * HDIM)),
+        (shape(total, 3 * HDIM), shape(depth, 3 * HDIM), shape(WINDOW, 2 * HDIM)),
         2 * total * depth * 3 * HDIM,
         5 << 20,
     )(*slots[:early], of_core, other_core)
+    halo = passed_along(tail, "ctx", 1)
     state, win = lax.optimization_barrier((state, win))
     last_kv, state, sent = kernel_call(
         functools.partial(last_keys_body, n_mem),
@@ -671,15 +661,6 @@
         2 * count * depth * 2 * width,
         3 << 20,
     )(below, above, all_routes, weight, state)
-    win, last_kv = lax.optimization_barrier((win, last_kv))
-    win, tail = kernel_call(
-        functools.partial(window_late_body, n_mem, early),
-        "window_late",
-        (shape(total, 3 * HDIM), shape(WINDOW, 2 * HDIM)),
-        2 * count * depth * 3 * HDIM,
-        3 << 20,
-    )(below, above, win_weight_full, win)
-    halo = passed_along(tail, "ctx", 1)
     last_query, last_coef, extra = kernel_call(
         functools.partial(last_queries_body, n_mem),
         "last_queries",
@@ -687,6 +668,35 @@
         8 * count * depth * width,
         8 << 20,
     )(below, above, *given, proj, last_kv)
+    local = (last_query, last_coef, extra)
+    bit = n_ctx // 2
+    got = lax.ppermute(sent, "ctx", [(i, i + bit) for i in range(n_ctx) if not i & bit])
+    prefix, late = (), None
+    while bit > 1:
+        bit //= 2
+        if bit == 1:
+            got, local = lax.optimization_barrier((got, local))
+        held, sent = kernel_call(
+            functools.partial(fold_body, bit),
+            f"fold{bit}",
+            (shape(width, HDIM, full), shape(width, HDIM)),
+            4 * width * HDIM,
+            16 * width * HDIM,
+        )(*prefix, got, state)
+        prefix = (held,)
+        got = lax.ppermute(sent, "ctx", [(i, i ^ bit) for i in range(n_ctx)])
+        if late is None:
+            win, held = lax.optimization_barrier((win, held))
+            win, tail = kernel_call(
+                functools.partial(window_late_body, n_mem, early),
+                "window_late",
+                (shape(total, 3 * HDIM), shape(count, 2 * HDIM)),
+                2 * count * depth * 3 * HDIM,
+                3 << 20,
+            )(below, above, win_weight_full, win)
+            ends = [(c * n_mem, (c + 1) * n_mem) for c in range(n_ctx - 1)]
+            late = lax.ppermute(tail, ("ctx", "mem"), ends)
+    prefix = held
     window_part = kernel_call(
         functools.partial(window_attend_body, count),
         "window_attend",
@@ -694,10 +704,8 @@
         4 * total * (count + WINDOW) * HDIM,
         3 << 20,
         scratch_shapes=[pltpu.VMEM((total + WINDOW, 2 * HDIM), low)],
-    )(win, halo)
-
-    local = (last_query, last_coef, extra, window_part)
-    prefix, got, local = exclusive_prefix(state, sent, local)
+    )(win, halo, late)
+    local += (window_part,)
 
     def finish(shift):
         return kernel_call(
@@ -732,7 +740,7 @@
         and tokens.shape[0] <= 3 * HDIM
         and n_ctx >= 4
         and n_ctx & (n_ctx - 1) == 0
-        and n_mem * tokens.shape[0] >= WINDOW
+        and (n_mem - 1) * tokens.shape[0] >= WINDOW
     )
     body = dense_shards if dense else sparse_shards
     return body(tokens, routes, router, mem_weight, win_weight)

time: 99.4 us -> 97.9 us (0.985)
  waiting for transfers between devices: 45.3 us -> 40.7 us
  starting transfers between devices: 29 us -> 32 us
    ppermute x3 -> x4, waiting for transfers between devices: 7.51 us -> 1.8 us  [the longest x1 1.18 us: dense_shards(): lax.ppermute(sent, 'ctx', [(i, i + bit) for i in range(n_ctx) if not i &...]
    ppermute x3 -> x4, starting transfers between devices: 4.19 us -> 7.11 us  [the longest x1 3.43 us: dense_shards(): lax.ppermute(sent, 'ctx', [(i, i + bit) for i in range(n_ctx) if not i &...]
    ppermute x3, waiting for transfers between devices: 20.3 us -> 21.5 us  [dense_shards(): parts.append(lax.ppermute(finish(shift), 'mem', pairs))]
  transfers between devices with their start and end apart: 20 -> 21, of which waited for: 9 -> 8; matrix products, arithmetic and copies ran while one was open for 0% -> 0% of each run, Pallas kernels for 16% -> 17%
where the time goes in v9:
time: 97.9 us; the launch traced here: 97.4 us
  waiting for transfers between devices  40.7 us (42%)
  starting transfers between devices  32 us (33%)
  Pallas kernels  19 us (19%)
  local copies, waits for them, and re-layouts  5.43 us (6%)
    ppermute x3, waiting for transfers between devices, dense_shards(): parts.append(lax.ppermute(finish(shift), 'mem', pairs))  21.5 us
    ppermute x3, waiting for transfers between devices, moved(): lax.ppermute(from_above, 'mem', down)  11.4 us
    ppermute x3, starting transfers between devices, dense_shards(): lax.ppermute(packed[s], 'mem', [(i, (i + s) % n_mem) for i in range(n_mem)])  6.61 us
    ppermute x3, starting transfers between devices, moved(): lax.ppermute(from_below, 'mem', up)  6.33 us
    pallas_call x1, Pallas kernels, dense_shards(): kernel_call(functools.partial(arrivals_body, n_mem, 3, early, True), 'mid...  5.58 us
    unnamed x10, local copies, waits for them, and re-layouts  5.43 us
    ppermute x3, waiting for transfers between devices, dense_shards(): lax.ppermute(packed[s], 'mem', [(i, (i + s) % n_mem) for i in range(n_mem)])  5.43 us
    ppermute x3, starting transfers between devices, dense_shards(): lax.ppermute(own_rows, 'ctx', [(i, (i + 2 * s) % n_ctx) for i in range(n_...  4.5 us
  transfers between devices with their start and end apart: 21, of which 8 were waited for; matrix products, arithmetic and copies ran while one was open for 0% of the time, Pallas kernels for 17%

profile of v9, /device:TPU:0, one launch (start us, length us, event | category | flops | bytes accessed | tf_op | source)
XLA Modules:
  0.0 97.4 jit_solution(4027250110402804577)
XLA Ops:
  0.0 5.0 %collective-permute-start = (bf16[256,1024]{1,0:T(8,128)(2,1)}, bf16[256,1024]{1,0:T(8,128)(2,1)S(1)}, u32[]{:S(2)}, u32[]{:S(2)}) collective-permute-start(bf16[256,1024]{1,0:T(8,128)(2,1)} %refs_0_.1), channel_id=1, source_target_pairs={{0,1},{1,2},{2,3},{4,5},{5,6},{6,7},{8,9},{9,10},{10,11},{12,13},{... | collective-permute-start | bytes 1572872 | tf_op jit(solution)/shard_map/ppermute | solution.py:571
  5.0 1.3 %collective-permute-start.1 = (bf16[256,1024]{1,0:T(8,128)(2,1)}, bf16[256,1024]{1,0:T(8,128)(2,1)S(1)}, u32[]{:S(2)}, u32[]{:S(2)}) collective-permute-start(bf16[256,1024]{1,0:T(8,128)(2,1)} %refs_0_.1), channel_id=1, source_target_pairs={{3,2},{2,1},{1,0},{7,6},{6,5},{5,4},{11,10},{10,9},{9,8},{15,14},{... | collective-permute-start | bytes 1572872 | tf_op jit(solution)/shard_map/ppermute | solution.py:571
  8.2 2.7 %collective-permute-start.2 = (bf16[48,384]{1,0:T(8,128)(2,1)S(1)}, bf16[48,384]{1,0:T(8,128)(2,1)S(1)}, u32[]{:S(2)}, u32[]{:S(2)}) collective-permute-start(bf16[48,384]{1,0:T(8,128)(2,1)S(1)} %get-tuple-element.66), channel_id=1, source_target_pairs={{0,1},{1,2},{2,3},{3,0},{4,5},{5,6},{6,7},{7,4},{8,9},{9,10},{10,1... | collective-permute-start | bytes 110600 | tf_op jit(solution)/shard_map/ppermute | solution.py:583
  10.9 2.6 %collective-permute-start.3 = (bf16[48,384]{1,0:T(8,128)(2,1)S(1)}, bf16[48,384]{1,0:T(8,128)(2,1)S(1)}, u32[]{:S(2)}, u32[]{:S(2)}) collective-permute-start(bf16[48,384]{1,0:T(8,128)(2,1)S(1)} %get-tuple-element.67), channel_id=1, source_target_pairs={{0,2},{1,3},{2,0},{3,1},{4,6},{5,7},{6,4},{7,5},{8,10},{9,11},{10,... | collective-permute-start | bytes 110600 | tf_op jit(solution)/shard_map/ppermute | solution.py:583
  13.5 1.3 %collective-permute-start.4 = (bf16[48,384]{1,0:T(8,128)(2,1)S(1)}, bf16[48,384]{1,0:T(8,128)(2,1)S(1)}, u32[]{:S(2)}, u32[]{:S(2)}) collective-permute-start(bf16[48,384]{1,0:T(8,128)(2,1)S(1)} %get-tuple-element.68), channel_id=1, source_target_pairs={{0,3},{1,0},{2,1},{3,2},{4,7},{5,4},{6,5},{7,6},{8,11},{9,8},{10,9... | collective-permute-start | bytes 110600 | tf_op jit(solution)/shard_map/ppermute | solution.py:583
  14.8 1.9 %copy-done = bf16[1,1024,1536]{2,1,0:T(8,128)(2,1)S(1)} copy-done((bf16[1,1024,1536]{2,1,0:T(8,128)(2,1)S(1)}, bf16[1,1024,1536]{2,1,0:T(8,128)(2,1)}, u32[]{:S(2)}) %copy-start) | copy-done | bytes 3145752
  18.7 5.4 %collective-permute-done.2.refs_1_ = bf16[48,384]{1,0:T(8,128)(2,1)S(1)} collective-permute-done((bf16[48,384]{1,0:T(8,128)(2,1)S(1)}, bf16[48,384]{1,0:T(8,128)(2,1)S(1)}, u32[]{:S(2)}, u32[]{:S(2)}) %collective-permute-start.2) | collective-permute-done | bytes 36896 | tf_op jit(solution)/shard_map/ppermute | solution.py:583
  26.2 1.5 %collective-permute-start.7 = (bf16[4,32,384]{2,1,0:T(8,128)(2,1)S(1)}, bf16[4,32,384]{2,1,0:T(8,128)(2,1)S(1)}, u32[]{:S(2)}, u32[]{:S(2)}) collective-permute-start(bf16[4,32,384]{2,1,0:T(8,128)(2,1)S(1)} %get-tuple-element.80.refs_0_), channel_id=1, source_target_pairs={{0,8},{4,12},{8,16},{12,20},{16,24},{20,28},{24,0},{28,4},{1,9},{5... | collective-permute-start | bytes 294920 | tf_op jit(solution)/shard_map/ppermute | solution.py:623
  27.7 1.5 %collective-permute-start.8 = (bf16[4,32,384]{2,1,0:T(8,128)(2,1)S(1)}, bf16[4,32,384]{2,1,0:T(8,128)(2,1)S(1)}, u32[]{:S(2)}, u32[]{:S(2)}) collective-permute-start(bf16[4,32,384]{2,1,0:T(8,128)(2,1)S(1)} %get-tuple-element.80.refs_0_), channel_id=1, source_target_pairs={{0,16},{4,20},{8,24},{12,28},{16,0},{20,4},{24,8},{28,12},{1,17},{... | collective-permute-start | bytes 294920 | tf_op jit(solution)/shard_map/ppermute | solution.py:623
  29.2 1.4 %collective-permute-start.9 = (bf16[4,32,384]{2,1,0:T(8,128)(2,1)S(1)}, bf16[4,32,384]{2,1,0:T(8,128)(2,1)S(1)}, u32[]{:S(2)}, u32[]{:S(2)}) collective-permute-start(bf16[4,32,384]{2,1,0:T(8,128)(2,1)S(1)} %get-tuple-element.80.refs_0_), channel_id=1, source_target_pairs={{0,24},{4,28},{8,0},{12,4},{16,8},{20,12},{24,16},{28,20},{1,25},{... | collective-permute-start | bytes 294920 | tf_op jit(solution)/shard_map/ppermute | solution.py:623
  30.7 2.6 %near_rows.1 = (bf16[1024,1536]{1,0:T(8,128)(2,1)S(1)}, f32[1024,128]{1,0:T(8,128)S(1)}, f32[512,128]{1,0:T(8,128)S(1)}) custom-call(bf16[256,1024]{1,0:T(8,128)(2,1)S(1)} %get-tuple-element.76.refs_0_, bf16[256,1024]{1,0:T(8,128)(2,1)S(1)} %collective-permute-done.refs_1_, bf16[256,1024]{1,0:T(8,128)(2,1)S(1)} %collective-permute-done.1.refs_2_, ...), custom_call_target="tpu_custom_call" | custom-call | flops 2415919104 | bytes 6291456 | tf_op jit(solution)/shard_map/near_rows/pallas_call | solution.py:614
  33.9 6.4 %collective-permute-done.6.refs_1_.refs_4_ = bf16[256,1024]{1,0:T(8,128)(2,1)S(1)} collective-permute-done((bf16[256,1024]{1,0:T(8,128)(2,1)S(1)}, bf16[256,1024]{1,0:T(8,128)(2,1)S(1)}, u32[]{:S(2)}, u32[]{:S(2)}) %collective-permute-start.6) | collective-permute-done | bytes 524320 | tf_op jit(solution)/shard_map/ppermute | solution.py:571
  42.4 5.6 %middle_rows.1 = (bf16[1024,1536]{1,0:T(8,128)(2,1)S(1)}, f32[1024,128]{1,0:T(8,128)S(1)}, f32[512,128]{1,0:T(8,128)S(1)}, f32[1024,512]{1,0:T(8,128)S(1)}) custom-call(bf16[256,1024]{1,0:T(8,128)(2,1)S(1)} %collective-permute-done.5.refs_0_.refs_3_, bf16[256,1024]{1,0:T(8,128)(2,1)S(1)} %collective-permute-done.6.refs_1_.refs_4_, ...), custom_call_target="tpu_custom_call" | custom-call | flops 2415919104 | bytes 6291456 | tf_op jit(solution)/shard_map/middle_rows/pallas_call | solution.py:641
  48.0 1.4 %window_early.1 = (bf16[1024,384]{1,0:T(8,128)(2,1)S(1)}, bf16[1024,384]{1,0:T(8,128)(2,1)S(1)}, bf16[512,256]{1,0:T(8,128)(2,1)S(1)}) custom-call(bf16[256,1024]{1,0:T(8,128)(2,1)S(1)} %get-tuple-element.76.refs_0_, bf16[256,1024]{1,0:T(8,128)(2,1)S(1)} %collective-permute-done.refs_1_, bf16[256,1024]{1,0:T(8,128)(2,1)S(1)} %collective-permute-done.1.refs_2_, ...), custom_call_target="tpu_custom_call" | custom-call | flops 805306368 | bytes 5242880 | tf_op jit(solution)/shard_map/window_early/pallas_call | solution.py:648
  49.4 5.0 %collective-permute-done.11.above_ref.refs_1_ = bf16[256,1024]{1,0:T(8,128)(2,1)S(1)} collective-permute-done((bf16[256,1024]{1,0:T(8,128)(2,1)S(1)}, bf16[256,1024]{1,0:T(8,128)(2,1)S(1)}, u32[]{:S(2)}, u32[]{:S(2)}) %collective-permute-start.11) | collective-permute-done | bytes 524320 | tf_op jit(solution)/shard_map/ppermute | solution.py:571
  55.4 3.4 %collective-permute-start.13 = (bf16[512,128]{1,0:T(8,128)(2,1)S(1)}, bf16[512,128]{1,0:T(8,128)(2,1)S(1)}, u32[]{:S(2)}, u32[]{:S(2)}) collective-permute-start(bf16[512,128]{1,0:T(8,128)(2,1)S(1)} %get-tuple-element.99), channel_id=1, source_target_pairs={{0,16},{4,20},{8,24},{12,28},{1,17},{5,21},{9,25},{13,29},{2,18},{... | collective-permute-start | bytes 393224 | tf_op jit(solution)/shard_map/ppermute | solution.py:673
  58.8 1.3 %collective-permute-start.15 = (bf16[512,256]{1,0:T(8,128)(2,1)S(1)}, bf16[512,256]{1,0:T(8,128)(2,1)S(1)}, u32[]{:S(2)}, u32[]{:S(2)}) collective-permute-start(bf16[512,256]{1,0:T(8,128)(2,1)S(1)} %get-tuple-element.114), channel_id=1, source_target_pairs={{0,4},{4,8},{8,12},{12,16},{16,20},{20,24},{24,28},{1,5},{5,9},{9,... | collective-permute-start | bytes 786440 | tf_op jit(solution)/shard_map/ppermute | solution.py:21
  61.4 1.6 %collective-permute-start.14 = (bf16[512,128]{1,0:T(8,128)(2,1)S(1)}, bf16[512,128]{1,0:T(8,128)(2,1)S(1)}, u32[]{:S(2)}, u32[]{:S(2)}) collective-permute-start(bf16[512,128]{1,0:T(8,128)(2,1)S(1)} %get-tuple-element.101), channel_id=1, source_target_pairs={{0,8},{4,12},{8,0},{12,4},{16,24},{20,28},{24,16},{28,20},{1,9},{5... | collective-permute-start | bytes 393224 | tf_op jit(solution)/shard_map/ppermute | solution.py:687
  63.6 1.5 %collective-permute-start.16 = (bf16[256,256]{1,0:T(8,128)(2,1)S(1)}, bf16[256,256]{1,0:T(8,128)(2,1)S(1)}, u32[]{:S(2)}, u32[]{:S(2)}) collective-permute-start(bf16[256,256]{1,0:T(8,128)(2,1)S(1)} %get-tuple-element.115), channel_id=1, source_target_pairs={{0,4},{4,8},{8,12},{12,16},{16,20},{20,24},{24,28}} | collective-permute-start | bytes 393224 | tf_op jit(solution)/shard_map/ppermute | solution.py:698
  65.1 2.1 %last_queries.1 = (bf16[256,512]{1,0:T(8,128)(2,1)S(1)}, f32[256,128]{1,0:T(8,128)S(1)}, f32[1024,512]{1,0:T(8,128)S(1)}) custom-call(bf16[256,1024]{1,0:T(8,128)(2,1)S(1)} %collective-permute-done.10.below_ref.refs_0_, bf16[256,1024]{1,0:T(8,128)(2,1)S(1)} %collective-permute-done.11.above_ref.refs_1_, ...), custom_call_target="tpu_custom_call" | custom-call | flops 1073741824 | bytes 8388608 | tf_op jit(solution)/shard_map/last_queries/pallas_call | solution.py:664
  68.6 2.3 %window_attend.1.refs_6_ = f32[1024,128]{1,0:T(8,128)S(1)} custom-call(bf16[1024,384]{1,0:T(8,128)(2,1)S(1)} %get-tuple-element.113.win_ref, bf16[512,256]{1,0:T(8,128)(2,1)S(1)} %collective-permute-done.15.halo_ref, bf16[256,256]{1,0:T(8,128)(2,1)S(1)} %collective-permute-done.16.late_ref), custom_call_target="tpu_custom_call" | custom-call | flops 402653184 | bytes 3145728 | tf_op jit(solution)/shard_map/window_attend/pallas_call | solution.py:700
  72.0 2.0 %collective-permute-start.19 = (bf16[256,512]{1,0:T(8,128)(2,1)S(1)}, bf16[256,512]{1,0:T(8,128)(2,1)S(1)}, u32[]{:S(2)}, u32[]{:S(2)}) collective-permute-start(bf16[256,512]{1,0:T(8,128)(2,1)S(1)} %finish1.1), channel_id=1, source_target_pairs={{0,1},{1,2},{2,3},{3,0},{4,5},{5,6},{6,7},{7,4},{8,9},{9,10},{10,1... | collective-permute-start | bytes 786440 | tf_op jit(solution)/shard_map/ppermute | solution.py:727
  75.1 10.9 %collective-permute-done.20.refs_3_ = bf16[256,512]{1,0:T(8,128)(2,1)S(1)} collective-permute-done((bf16[256,512]{1,0:T(8,128)(2,1)S(1)}, bf16[256,512]{1,0:T(8,128)(2,1)S(1)}, u32[]{:S(2)}, u32[]{:S(2)}) %collective-permute-start.20) | collective-permute-done | bytes 262176 | tf_op jit(solution)/shard_map/ppermute | solution.py:727
  86.0 10.6 %collective-permute-done.18.refs_1_ = bf16[256,512]{1,0:T(8,128)(2,1)S(1)} collective-permute-done((bf16[256,512]{1,0:T(8,128)(2,1)S(1)}, bf16[256,512]{1,0:T(8,128)(2,1)S(1)}, u32[]{:S(2)}, u32[]{:S(2)}) %collective-permute-start.18) | collective-permute-done | bytes 262176 | tf_op jit(solution)/shard_map/ppermute | solution.py:727
  (46 shorter events, 15.7 us)
Async XLA Ops:
  0.0 24.2 %collective-permute-start = (bf16[256,1024]{1,0:T(8,128)(2,1)}, bf16[256,1024]{1,0:T(8,128)(2,1)S(1)}, u32[]{:S(2)}, u32[]{:S(2)}) collective-permute-start(bf16[256,1024]{1,0:T(8,128)(2,1)} %refs_0_.1), channel_id=1, source_target_pairs={{0,1},{1,2},{2,3},{4,5},{5,6},{6,7},{8,9},{9,10},{10,11},{12,13},{... | collective-permute-start | bytes 1572872 | tf_op jit(solution)/shard_map/ppermute | solution.py:571
  5.0 19.2 %collective-permute-start.1 = (bf16[256,1024]{1,0:T(8,128)(2,1)}, bf16[256,1024]{1,0:T(8,128)(2,1)S(1)}, u32[]{:S(2)}, u32[]{:S(2)}) collective-permute-start(bf16[256,1024]{1,0:T(8,128)(2,1)} %refs_0_.1), channel_id=1, source_target_pairs={{3,2},{2,1},{1,0},{7,6},{6,5},{5,4},{11,10},{10,9},{9,8},{15,14},{... | collective-permute-start | bytes 1572872 | tf_op jit(solution)/shard_map/ppermute | solution.py:571
  6.3 1.1 %copy-start.1 = (bf16[256,1536]{1,0:T(8,128)(2,1)S(1)}, bf16[256,1536]{1,0:T(8,128)(2,1)}, u32[]{:S(2)}) copy-start(bf16[256,1536]{1,0:T(8,128)(2,1)} %weight_ref.1) | copy-start | bytes 2359300
  8.2 15.9 %collective-permute-start.2 = (bf16[48,384]{1,0:T(8,128)(2,1)S(1)}, bf16[48,384]{1,0:T(8,128)(2,1)S(1)}, u32[]{:S(2)}, u32[]{:S(2)}) collective-permute-start(bf16[48,384]{1,0:T(8,128)(2,1)S(1)} %get-tuple-element.66), channel_id=1, source_target_pairs={{0,1},{1,2},{2,3},{3,0},{4,5},{5,6},{6,7},{7,4},{8,9},{9,10},{10,1... | collective-permute-start | bytes 110600 | tf_op jit(solution)/shard_map/ppermute | solution.py:583
  10.9 13.2 %collective-permute-start.3 = (bf16[48,384]{1,0:T(8,128)(2,1)S(1)}, bf16[48,384]{1,0:T(8,128)(2,1)S(1)}, u32[]{:S(2)}, u32[]{:S(2)}) collective-permute-start(bf16[48,384]{1,0:T(8,128)(2,1)S(1)} %get-tuple-element.67), channel_id=1, source_target_pairs={{0,2},{1,3},{2,0},{3,1},{4,6},{5,7},{6,4},{7,5},{8,10},{9,11},{10,... | collective-permute-start | bytes 110600 | tf_op jit(solution)/shard_map/ppermute | solution.py:583
  13.5 10.6 %collective-permute-start.4 = (bf16[48,384]{1,0:T(8,128)(2,1)S(1)}, bf16[48,384]{1,0:T(8,128)(2,1)S(1)}, u32[]{:S(2)}, u32[]{:S(2)}) collective-permute-start(bf16[48,384]{1,0:T(8,128)(2,1)S(1)} %get-tuple-element.68), channel_id=1, source_target_pairs={{0,3},{1,0},{2,1},{3,2},{4,7},{5,4},{6,5},{7,6},{8,11},{9,8},{10,9... | collective-permute-start | bytes 110600 | tf_op jit(solution)/shard_map/ppermute | solution.py:583
  14.8 1.9 %copy-start = (bf16[1,1024,1536]{2,1,0:T(8,128)(2,1)S(1)}, bf16[1,1024,1536]{2,1,0:T(8,128)(2,1)}, u32[]{:S(2)}) copy-start(bf16[1,1024,1536]{2,1,0:T(8,128)(2,1)} %param.8) | copy-start | bytes 9437188
  16.7 1.0 %copy-start.2 = (bf16[256,1024]{1,0:T(8,128)(2,1)S(1)}, bf16[256,1024]{1,0:T(8,128)(2,1)}, u32[]{:S(2)}) copy-start(bf16[256,1024]{1,0:T(8,128)(2,1)} %refs_0_.1) | copy-start | bytes 1572868
  24.2 9.7 %collective-permute-start.5 = (bf16[256,1024]{1,0:T(8,128)(2,1)S(1)}, bf16[256,1024]{1,0:T(8,128)(2,1)S(1)}, u32[]{:S(2)}, u32[]{:S(2)}) collective-permute-start(bf16[256,1024]{1,0:T(8,128)(2,1)S(1)} %collective-permute-done.refs_1_), channel_id=1, source_target_pairs={{1,2},{2,3},{5,6},{6,7},{9,10},{10,11},{13,14},{14,15},{17,18},{18... | collective-permute-start | bytes 1572872 | tf_op jit(solution)/shard_map/ppermute | solution.py:571
  24.9 15.4 %collective-permute-start.6 = (bf16[256,1024]{1,0:T(8,128)(2,1)S(1)}, bf16[256,1024]{1,0:T(8,128)(2,1)S(1)}, u32[]{:S(2)}, u32[]{:S(2)}) collective-permute-start(bf16[256,1024]{1,0:T(8,128)(2,1)S(1)} %collective-permute-done.1.refs_2_), channel_id=1, source_target_pairs={{2,1},{1,0},{6,5},{5,4},{10,9},{9,8},{14,13},{13,12},{18,17},{17,1... | collective-permute-start | bytes 1572872 | tf_op jit(solution)/shard_map/ppermute | solution.py:571
  26.2 7.1 %collective-permute-start.7 = (bf16[4,32,384]{2,1,0:T(8,128)(2,1)S(1)}, bf16[4,32,384]{2,1,0:T(8,128)(2,1)S(1)}, u32[]{:S(2)}, u32[]{:S(2)}) collective-permute-start(bf16[4,32,384]{2,1,0:T(8,128)(2,1)S(1)} %get-tuple-element.80.refs_0_), channel_id=1, source_target_pairs={{0,8},{4,12},{8,16},{12,20},{16,24},{20,28},{24,0},{28,4},{1,9},{5... | collective-permute-start | bytes 294920 | tf_op jit(solution)/shard_map/ppermute | solution.py:623
  27.7 5.6 %collective-permute-start.8 = (bf16[4,32,384]{2,1,0:T(8,128)(2,1)S(1)}, bf16[4,32,384]{2,1,0:T(8,128)(2,1)S(1)}, u32[]{:S(2)}, u32[]{:S(2)}) collective-permute-start(bf16[4,32,384]{2,1,0:T(8,128)(2,1)S(1)} %get-tuple-element.80.refs_0_), channel_id=1, source_target_pairs={{0,16},{4,20},{8,24},{12,28},{16,0},{20,4},{24,8},{28,12},{1,17},{... | collective-permute-start | bytes 294920 | tf_op jit(solution)/shard_map/ppermute | solution.py:623
  29.2 4.6 %collective-permute-start.9 = (bf16[4,32,384]{2,1,0:T(8,128)(2,1)S(1)}, bf16[4,32,384]{2,1,0:T(8,128)(2,1)S(1)}, u32[]{:S(2)}, u32[]{:S(2)}) collective-permute-start(bf16[4,32,384]{2,1,0:T(8,128)(2,1)S(1)} %get-tuple-element.80.refs_0_), channel_id=1, source_target_pairs={{0,24},{4,28},{8,0},{12,4},{16,8},{20,12},{24,16},{28,20},{1,25},{... | collective-permute-start | bytes 294920 | tf_op jit(solution)/shard_map/ppermute | solution.py:623
  40.3 9.1 %collective-permute-start.10 = (bf16[256,1024]{1,0:T(8,128)(2,1)S(1)}, bf16[256,1024]{1,0:T(8,128)(2,1)S(1)}, u32[]{:S(2)}, u32[]{:S(2)}) collective-permute-start(bf16[256,1024]{1,0:T(8,128)(2,1)S(1)} %collective-permute-done.5.refs_0_.refs_3_), channel_id=1, source_target_pairs={{2,3},{6,7},{10,11},{14,15},{18,19},{22,23},{26,27},{30,31}} | collective-permute-start | bytes 1572872 | tf_op jit(solution)/shard_map/ppermute | solution.py:571
  41.0 13.4 %collective-permute-start.11 = (bf16[256,1024]{1,0:T(8,128)(2,1)S(1)}, bf16[256,1024]{1,0:T(8,128)(2,1)S(1)}, u32[]{:S(2)}, u32[]{:S(2)}) collective-permute-start(bf16[256,1024]{1,0:T(8,128)(2,1)S(1)} %collective-permute-done.6.refs_1_.refs_4_), channel_id=1, source_target_pairs={{1,0},{5,4},{9,8},{13,12},{17,16},{21,20},{25,24},{29,28}} | collective-permute-start | bytes 1572872 | tf_op jit(solution)/shard_map/ppermute | solution.py:571
  42.3 5.7 %collective-permute-start.12 = (bf16[4,4,32,384]{3,2,1,0:T(8,128)(2,1)S(1)}, bf16[4,4,32,384]{3,2,1,0:T(8,128)(2,1)S(1)}, u32[]{:S(2)}, u32[]{:S(2)}) collective-permute-start(bf16[4,4,32,384]{3,2,1,0:T(8,128)(2,1)S(1)} %combine.1.refs_5_), channel_id=1, source_target_pairs={{0,4},{4,0},{8,12},{12,8},{16,20},{20,16},{24,28},{28,24},{1,5},{5... | collective-permute-start | bytes 1179656 | tf_op jit(solution)/shard_map/ppermute | solution.py:635
  55.4 5.9 %collective-permute-start.13 = (bf16[512,128]{1,0:T(8,128)(2,1)S(1)}, bf16[512,128]{1,0:T(8,128)(2,1)S(1)}, u32[]{:S(2)}, u32[]{:S(2)}) collective-permute-start(bf16[512,128]{1,0:T(8,128)(2,1)S(1)} %get-tuple-element.99), channel_id=1, source_target_pairs={{0,16},{4,20},{8,24},{12,28},{1,17},{5,21},{9,25},{13,29},{2,18},{... | collective-permute-start | bytes 393224 | tf_op jit(solution)/shard_map/ppermute | solution.py:673
  58.8 9.7 %collective-permute-start.15 = (bf16[512,256]{1,0:T(8,128)(2,1)S(1)}, bf16[512,256]{1,0:T(8,128)(2,1)S(1)}, u32[]{:S(2)}, u32[]{:S(2)}) collective-permute-start(bf16[512,256]{1,0:T(8,128)(2,1)S(1)} %get-tuple-element.114), channel_id=1, source_target_pairs={{0,4},{4,8},{8,12},{12,16},{16,20},{20,24},{24,28},{1,5},{5,9},{9,... | collective-permute-start | bytes 786440 | tf_op jit(solution)/shard_map/ppermute | solution.py:21
  61.4 6.5 %collective-permute-start.14 = (bf16[512,128]{1,0:T(8,128)(2,1)S(1)}, bf16[512,128]{1,0:T(8,128)(2,1)S(1)}, u32[]{:S(2)}, u32[]{:S(2)}) collective-permute-start(bf16[512,128]{1,0:T(8,128)(2,1)S(1)} %get-tuple-element.101), channel_id=1, source_target_pairs={{0,8},{4,12},{8,0},{12,4},{16,24},{20,28},{24,16},{28,20},{1,9},{5... | collective-permute-start | bytes 393224 | tf_op jit(solution)/shard_map/ppermute | solution.py:687
  63.6 4.9 %collective-permute-start.16 = (bf16[256,256]{1,0:T(8,128)(2,1)S(1)}, bf16[256,256]{1,0:T(8,128)(2,1)S(1)}, u32[]{:S(2)}, u32[]{:S(2)}) collective-permute-start(bf16[256,256]{1,0:T(8,128)(2,1)S(1)} %get-tuple-element.115), channel_id=1, source_target_pairs={{0,4},{4,8},{8,12},{12,16},{16,20},{20,24},{24,28}} | collective-permute-start | bytes 393224 | tf_op jit(solution)/shard_map/ppermute | solution.py:698
  67.9 3.0 %collective-permute-start.17 = (bf16[512,128]{1,0:T(8,128)(2,1)S(1)}, bf16[512,128]{1,0:T(8,128)(2,1)S(1)}, u32[]{:S(2)}, u32[]{:S(2)}) collective-permute-start(bf16[512,128]{1,0:T(8,128)(2,1)S(1)} %get-tuple-element.118), channel_id=1, source_target_pairs={{0,4},{4,0},{8,12},{12,8},{16,20},{20,16},{24,28},{28,24},{1,5},{5... | collective-permute-start | bytes 393224 | tf_op jit(solution)/shard_map/ppermute | solution.py:687
  71.4 14.5 %collective-permute-start.20 = (bf16[256,512]{1,0:T(8,128)(2,1)S(1)}, bf16[256,512]{1,0:T(8,128)(2,1)S(1)}, u32[]{:S(2)}, u32[]{:S(2)}) collective-permute-start(bf16[256,512]{1,0:T(8,128)(2,1)S(1)} %finish3.1), channel_id=1, source_target_pairs={{0,3},{1,0},{2,1},{3,2},{4,7},{5,4},{6,5},{7,6},{8,11},{9,8},{10,9... | collective-permute-start | bytes 786440 | tf_op jit(solution)/shard_map/ppermute | solution.py:727
  72.0 14.0 %collective-permute-start.19 = (bf16[256,512]{1,0:T(8,128)(2,1)S(1)}, bf16[256,512]{1,0:T(8,128)(2,1)S(1)}, u32[]{:S(2)}, u32[]{:S(2)}) collective-permute-start(bf16[256,512]{1,0:T(8,128)(2,1)S(1)} %finish1.1), channel_id=1, source_target_pairs={{0,1},{1,2},{2,3},{3,0},{4,5},{5,6},{6,7},{7,4},{8,9},{9,10},{10,1... | collective-permute-start | bytes 786440 | tf_op jit(solution)/shard_map/ppermute | solution.py:727
  74.5 22.1 %collective-permute-start.18 = (bf16[256,512]{1,0:T(8,128)(2,1)S(1)}, bf16[256,512]{1,0:T(8,128)(2,1)S(1)}, u32[]{:S(2)}, u32[]{:S(2)}) collective-permute-start(bf16[256,512]{1,0:T(8,128)(2,1)S(1)} %finish2.1), channel_id=1, source_target_pairs={{0,2},{1,3},{2,0},{3,1},{4,6},{5,7},{6,4},{7,5},{8,10},{9,11},{10,... | collective-permute-start | bytes 786440 | tf_op jit(solution)/shard_map/ppermute | solution.py:727
  (2 other events, 1.4 us)

commit v10 on v9

--- a/solution.py
+++ b/solution.py
@@ -280,7 +280,8 @@
 
 def slot_group(slot):
     hop = (slot + 1) // 2
-    return lax.axis_index("mem") + (-hop if slot % 2 else hop)
+    from_below = (slot % 2 == 1) == (hop == 1)
+    return lax.axis_index("mem") + (-hop if from_below else hop)
 
 
 def in_line(group, n_mem):
@@ -360,7 +361,7 @@
                     )
 
 
-def last_keys_body(n_mem, below_ref, above_ref, routes_ref, weight_ref, before_ref, *refs):
+def last_keys_body(n_mem, above_ref, below_ref, routes_ref, weight_ref, before_ref, *refs):
     kv_ref, state_ref, sent_ref = refs
     count = below_ref.shape[0]
     width = HEADS * HDIM
@@ -382,7 +383,7 @@
     sent_ref[...] = state_ref[...].astype(jnp.bfloat16)
 
 
-def last_queries_body(n_mem, below_ref, above_ref, routes_ref, router_ref, weight_ref, proj_ref, kv_ref, *refs):
+def last_queries_body(n_mem, above_ref, below_ref, routes_ref, router_ref, weight_ref, proj_ref, kv_ref, *refs):
     query_ref, coef_ref, extra_ref = refs
     count = below_ref.shape[0]
     total = extra_ref.shape[0]
@@ -568,7 +569,11 @@
     def moved(hop, from_below, from_above):
         up = [(i, i + 1) for i in range(hop - 1, n_mem - 1)]
         down = [(n_mem - 1 - i, n_mem - 1 - j) for i, j in up]
-        return lax.ppermute(from_below, "mem", up), lax.ppermute(from_above, "mem", down)
+        if hop == 1:
+            from_below = lax.ppermute(from_below, "mem", up)
+            return from_below, lax.ppermute(from_above, "mem", down)
+        from_above = lax.ppermute(from_above, "mem", down)
+        return lax.ppermute(from_below, "mem", up), from_above
 
     packed = kernel_call(
         pack_body,
@@ -607,7 +612,7 @@
     own_tokens, router_rows, weight = staged
     slots = [own_tokens] + slots
     below, above = moved(2, below, above)
-    slots += [below, above]
+    slots += [above, below]
     given = (all_routes, router_rows, weight)
     project_flops = 2 * count * depth * 3 * width
     kept = (shape(total, 3 * width), shape(total, HDIM, full), shape(width, HDIM, full))
@@ -631,11 +636,11 @@
         1 << 20,
         1 << 20,
     )(own_rows, *of_chips)
-    below, above, held, of_core = lax.optimization_barrier((below, above, held, of_core))
+    above, below, held, of_core = lax.optimization_barrier((above, below, held, of_core))
     other_core = lax.ppermute(of_core, "ctx", [(i, i ^ 1) for i in range(n_ctx)])
     for hop in range(3, n_mem):
         below, above = moved(hop, below, above)
-        slots += [below, above]
+        slots += [above, below]
     hops = n_mem - 2
     early = 1 + 2 * hops
     proj, coef, state, intra = kernel_call(
@@ -660,14 +665,14 @@
         (shape(count, 2 * width), shape(width, HDIM, full), shape(width, HDIM)),
         2 * count * depth * 2 * width,
         3 << 20,
-    )(below, above, all_routes, weight, state)
+    )(above, below, all_routes, weight, state)
     last_query, last_coef, extra = kernel_call(
         functools.partial(last_queries_body, n_mem),
         "last_queries",
         (shape(count, width), shape(count, HDIM, full), shape(total, width, full)),
         8 * count * depth * width,
         8 << 20,
-    )(below, above, *given, proj, last_kv)
+    )(above, below, *given, proj, last_kv)
     local = (last_query, last_coef, extra)
     bit = n_ctx // 2
     got = lax.ppermute(sent, "ctx", [(i, i + bit) for i in range(n_ctx) if not i & bit])
@@ -693,7 +698,7 @@
                 (shape(total, 3 * HDIM), shape(count, 2 * HDIM)),
                 2 * count * depth * 3 * HDIM,
                 3 << 20,
-            )(below, above, win_weight_full, win)
+            )(above, below, win_weight_full, win)
             ends = [(c * n_mem, (c + 1) * n_mem) for c in range(n_ctx - 1)]
             late = lax.ppermute(tail, ("ctx", "mem"), ends)
     prefix = held
@@ -707,7 +712,7 @@
     )(win, halo, late)
     local += (window_part,)
 
-    def finish(shift):
+    def finish(shift, prefix):
         return kernel_call(
             functools.partial(finish_body, n_mem, shift),
             f"finish{shift}",
@@ -723,11 +728,11 @@
 
     parts = []
     for shift in sorted(range(1, n_mem), key=lambda s: abs(2 * s - n_mem)):
-        pairs = [(i, (i + shift) % n_mem) for i in range(n_mem)]
-        parts.append(lax.ppermute(finish(shift), "mem", pairs))
+        part = finish(shift, prefix)
+        parts.append(lax.ppermute(part, "mem", [(i, (i + shift) % n_mem) for i in range(n_mem)]))
     return kernel_call(
         add_body, "add_parts", shape(count, width), n_mem * count * width, 2 << 20
-    )(finish(0), *parts)
+    )(finish(0, prefix), *parts)
 
 
 def shards(tokens, routes, router, mem_weight, win_weight):

time: 97.9 us -> 96.5 us (0.986)
  waiting for transfers between devices: 40.7 us -> 34.8 us
  starting transfers between devices: 32 us -> 36.5 us
    ppermute x9, waiting for transfers between devices: 32.9 us -> 27 us  [the longest x3 20.2 us: dense_shards(): lax.ppermute(part, 'mem', [(i, (i + shift) % n_mem) for i in range(n_mem)])]
    ppermute x9, starting transfers between devices: 12.4 us -> 16.9 us  [the longest x3 6.74 us: dense_shards(): lax.ppermute(part, 'mem', [(i, (i + shift) % n_mem) for i in range(n_mem)])]
  transfers between devices with their start and end apart: 21 -> 21, of which waited for: 8 -> 9; matrix products, arithmetic and copies ran while one was open for 0% -> 0% of each run, Pallas kernels for 17% -> 17%
where the time goes in v10:
time: 96.5 us; the launch traced here: 96 us
  starting transfers between devices  36.5 us (38%)
  waiting for transfers between devices  34.8 us (36%)
  Pallas kernels  19 us (20%)
  local copies, waits for them, and re-layouts  5.43 us (6%)
    ppermute x3, waiting for transfers between devices, dense_shards(): lax.ppermute(part, 'mem', [(i, (i + shift) % n_mem) for i in range(n_mem)])  20.2 us
    ppermute x2, waiting for transfers between devices, moved(): from_above = lax.ppermute(from_above, 'mem', down)  6.85 us
    ppermute x3, starting transfers between devices, dense_shards(): lax.ppermute(part, 'mem', [(i, (i + shift) % n_mem) for i in range(n_mem)])  6.74 us
    ppermute x3, starting transfers between devices, dense_shards(): lax.ppermute(packed[s], 'mem', [(i, (i + s) % n_mem) for i in range(n_mem)])  6.61 us
    pallas_call x1, Pallas kernels, dense_shards(): kernel_call(functools.partial(arrivals_body, n_mem, 3, early, True), 'mid...  5.57 us
    unnamed x10, local copies, waits for them, and re-layouts  5.43 us
    ppermute x3, waiting for transfers between devices, dense_shards(): lax.ppermute(packed[s], 'mem', [(i, (i + s) % n_mem) for i in range(n_mem)])  5.43 us
    ppermute x1, starting transfers between devices, moved(): from_below = lax.ppermute(from_below, 'mem', up)  4.95 us
  transfers between devices with their start and end apart: 21, of which 9 were waited for; matrix products, arithmetic and copies ran while one was open for 0% of the time, Pallas kernels for 17%

profile of v10, /device:TPU:0, one launch (start us, length us, event | category | flops | bytes accessed | tf_op | source)
XLA Modules:
  0.0 96.0 jit_solution(2090103514223493671)
XLA Ops:
  0.0 5.0 %collective-permute-start = (bf16[256,1024]{1,0:T(8,128)(2,1)}, bf16[256,1024]{1,0:T(8,128)(2,1)S(1)}, u32[]{:S(2)}, u32[]{:S(2)}) collective-permute-start(bf16[256,1024]{1,0:T(8,128)(2,1)} %refs_0_.1), channel_id=1, source_target_pairs={{0,1},{1,2},{2,3},{4,5},{5,6},{6,7},{8,9},{9,10},{10,11},{12,13},{... | collective-permute-start | bytes 1572872 | tf_op jit(solution)/shard_map/ppermute | solution.py:573
  8.2 2.7 %collective-permute-start.2 = (bf16[48,384]{1,0:T(8,128)(2,1)S(1)}, bf16[48,384]{1,0:T(8,128)(2,1)S(1)}, u32[]{:S(2)}, u32[]{:S(2)}) collective-permute-start(bf16[48,384]{1,0:T(8,128)(2,1)S(1)} %get-tuple-element.66), channel_id=1, source_target_pairs={{0,1},{1,2},{2,3},{3,0},{4,5},{5,6},{6,7},{7,4},{8,9},{9,10},{10,1... | collective-permute-start | bytes 110600 | tf_op jit(solution)/shard_map/ppermute | solution.py:588
  10.9 2.6 %collective-permute-start.3 = (bf16[48,384]{1,0:T(8,128)(2,1)S(1)}, bf16[48,384]{1,0:T(8,128)(2,1)S(1)}, u32[]{:S(2)}, u32[]{:S(2)}) collective-permute-start(bf16[48,384]{1,0:T(8,128)(2,1)S(1)} %get-tuple-element.67), channel_id=1, source_target_pairs={{0,2},{1,3},{2,0},{3,1},{4,6},{5,7},{6,4},{7,5},{8,10},{9,11},{10,... | collective-permute-start | bytes 110600 | tf_op jit(solution)/shard_map/ppermute | solution.py:588
  13.5 1.3 %collective-permute-start.4 = (bf16[48,384]{1,0:T(8,128)(2,1)S(1)}, bf16[48,384]{1,0:T(8,128)(2,1)S(1)}, u32[]{:S(2)}, u32[]{:S(2)}) collective-permute-start(bf16[48,384]{1,0:T(8,128)(2,1)S(1)} %get-tuple-element.68), channel_id=1, source_target_pairs={{0,3},{1,0},{2,1},{3,2},{4,7},{5,4},{6,5},{7,6},{8,11},{9,8},{10,9... | collective-permute-start | bytes 110600 | tf_op jit(solution)/shard_map/ppermute | solution.py:588
  14.8 1.9 %copy-done = bf16[1,1024,1536]{2,1,0:T(8,128)(2,1)S(1)} copy-done((bf16[1,1024,1536]{2,1,0:T(8,128)(2,1)S(1)}, bf16[1,1024,1536]{2,1,0:T(8,128)(2,1)}, u32[]{:S(2)}) %copy-start) | copy-done | bytes 3145752
  18.7 5.4 %collective-permute-done.2.refs_1_ = bf16[48,384]{1,0:T(8,128)(2,1)S(1)} collective-permute-done((bf16[48,384]{1,0:T(8,128)(2,1)S(1)}, bf16[48,384]{1,0:T(8,128)(2,1)S(1)}, u32[]{:S(2)}, u32[]{:S(2)}) %collective-permute-start.2) | collective-permute-done | bytes 36896 | tf_op jit(solution)/shard_map/ppermute | solution.py:588
  26.2 1.5 %collective-permute-start.7 = (bf16[4,32,384]{2,1,0:T(8,128)(2,1)S(1)}, bf16[4,32,384]{2,1,0:T(8,128)(2,1)S(1)}, u32[]{:S(2)}, u32[]{:S(2)}) collective-permute-start(bf16[4,32,384]{2,1,0:T(8,128)(2,1)S(1)} %get-tuple-element.80.refs_0_), channel_id=1, source_target_pairs={{0,8},{4,12},{8,16},{12,20},{16,24},{20,28},{24,0},{28,4},{1,9},{5... | collective-permute-start | bytes 294920 | tf_op jit(solution)/shard_map/ppermute | solution.py:628
  27.7 1.5 %collective-permute-start.8 = (bf16[4,32,384]{2,1,0:T(8,128)(2,1)S(1)}, bf16[4,32,384]{2,1,0:T(8,128)(2,1)S(1)}, u32[]{:S(2)}, u32[]{:S(2)}) collective-permute-start(bf16[4,32,384]{2,1,0:T(8,128)(2,1)S(1)} %get-tuple-element.80.refs_0_), channel_id=1, source_target_pairs={{0,16},{4,20},{8,24},{12,28},{16,0},{20,4},{24,8},{28,12},{1,17},{... | collective-permute-start | bytes 294920 | tf_op jit(solution)/shard_map/ppermute | solution.py:628
  29.2 1.4 %collective-permute-start.9 = (bf16[4,32,384]{2,1,0:T(8,128)(2,1)S(1)}, bf16[4,32,384]{2,1,0:T(8,128)(2,1)S(1)}, u32[]{:S(2)}, u32[]{:S(2)}) collective-permute-start(bf16[4,32,384]{2,1,0:T(8,128)(2,1)S(1)} %get-tuple-element.80.refs_0_), channel_id=1, source_target_pairs={{0,24},{4,28},{8,0},{12,4},{16,8},{20,12},{24,16},{28,20},{1,25},{... | collective-permute-start | bytes 294920 | tf_op jit(solution)/shard_map/ppermute | solution.py:628
  30.7 2.6 %near_rows.1 = (bf16[1024,1536]{1,0:T(8,128)(2,1)S(1)}, f32[1024,128]{1,0:T(8,128)S(1)}, f32[512,128]{1,0:T(8,128)S(1)}) custom-call(bf16[256,1024]{1,0:T(8,128)(2,1)S(1)} %get-tuple-element.76.refs_0_, bf16[256,1024]{1,0:T(8,128)(2,1)S(1)} %collective-permute-done.refs_1_, bf16[256,1024]{1,0:T(8,128)(2,1)S(1)} %collective-permute-done.1.refs_2_, ...), custom_call_target="tpu_custom_call" | custom-call | flops 2415919104 | bytes 6291456 | tf_op jit(solution)/shard_map/near_rows/pallas_call | solution.py:619
  33.9 3.4 %collective-permute-done.5.refs_0_.refs_3_ = bf16[256,1024]{1,0:T(8,128)(2,1)S(1)} collective-permute-done((bf16[256,1024]{1,0:T(8,128)(2,1)S(1)}, bf16[256,1024]{1,0:T(8,128)(2,1)S(1)}, u32[]{:S(2)}, u32[]{:S(2)}) %collective-permute-start.5) | collective-permute-done | bytes 524320 | tf_op jit(solution)/shard_map/ppermute | solution.py:575
  39.4 5.6 %middle_rows.1 = (bf16[1024,1536]{1,0:T(8,128)(2,1)S(1)}, f32[1024,128]{1,0:T(8,128)S(1)}, f32[512,128]{1,0:T(8,128)S(1)}, f32[1024,512]{1,0:T(8,128)S(1)}) custom-call(bf16[256,1024]{1,0:T(8,128)(2,1)S(1)} %collective-permute-done.5.refs_0_.refs_3_, bf16[256,1024]{1,0:T(8,128)(2,1)S(1)} %collective-permute-done.6.refs_1_.refs_4_, ...), custom_call_target="tpu_custom_call" | custom-call | flops 2415919104 | bytes 6291456 | tf_op jit(solution)/shard_map/middle_rows/pallas_call | solution.py:646
  45.0 1.4 %window_early.1 = (bf16[1024,384]{1,0:T(8,128)(2,1)S(1)}, bf16[1024,384]{1,0:T(8,128)(2,1)S(1)}, bf16[512,256]{1,0:T(8,128)(2,1)S(1)}) custom-call(bf16[256,1024]{1,0:T(8,128)(2,1)S(1)} %get-tuple-element.76.refs_0_, bf16[256,1024]{1,0:T(8,128)(2,1)S(1)} %collective-permute-done.refs_1_, bf16[256,1024]{1,0:T(8,128)(2,1)S(1)} %collective-permute-done.1.refs_2_, ...), custom_call_target="tpu_custom_call" | custom-call | flops 805306368 | bytes 5242880 | tf_op jit(solution)/shard_map/window_early/pallas_call | solution.py:653
  46.5 3.4 %collective-permute-done.10.above_ref.refs_0_ = bf16[256,1024]{1,0:T(8,128)(2,1)S(1)} collective-permute-done((bf16[256,1024]{1,0:T(8,128)(2,1)S(1)}, bf16[256,1024]{1,0:T(8,128)(2,1)S(1)}, u32[]{:S(2)}, u32[]{:S(2)}) %collective-permute-start.10) | collective-permute-done | bytes 524320 | tf_op jit(solution)/shard_map/ppermute | solution.py:575
  50.8 3.4 %collective-permute-start.13 = (bf16[512,128]{1,0:T(8,128)(2,1)S(1)}, bf16[512,128]{1,0:T(8,128)(2,1)S(1)}, u32[]{:S(2)}, u32[]{:S(2)}) collective-permute-start(bf16[512,128]{1,0:T(8,128)(2,1)S(1)} %get-tuple-element.99), channel_id=1, source_target_pairs={{0,16},{4,20},{8,24},{12,28},{1,17},{5,21},{9,25},{13,29},{2,18},{... | collective-permute-start | bytes 393224 | tf_op jit(solution)/shard_map/ppermute | solution.py:678
  56.8 1.6 %collective-permute-start.14 = (bf16[512,128]{1,0:T(8,128)(2,1)S(1)}, bf16[512,128]{1,0:T(8,128)(2,1)S(1)}, u32[]{:S(2)}, u32[]{:S(2)}) collective-permute-start(bf16[512,128]{1,0:T(8,128)(2,1)S(1)} %get-tuple-element.101), channel_id=1, source_target_pairs={{0,8},{4,12},{8,0},{12,4},{16,24},{20,28},{24,16},{28,20},{1,9},{5... | collective-permute-start | bytes 393224 | tf_op jit(solution)/shard_map/ppermute | solution.py:692
  59.1 1.5 %collective-permute-start.16 = (bf16[256,256]{1,0:T(8,128)(2,1)S(1)}, bf16[256,256]{1,0:T(8,128)(2,1)S(1)}, u32[]{:S(2)}, u32[]{:S(2)}) collective-permute-start(bf16[256,256]{1,0:T(8,128)(2,1)S(1)} %get-tuple-element.115), channel_id=1, source_target_pairs={{0,4},{4,8},{8,12},{12,16},{16,20},{20,24},{24,28}} | collective-permute-start | bytes 393224 | tf_op jit(solution)/shard_map/ppermute | solution.py:703
  60.6 2.1 %last_queries.1 = (bf16[256,512]{1,0:T(8,128)(2,1)S(1)}, f32[256,128]{1,0:T(8,128)S(1)}, f32[1024,512]{1,0:T(8,128)S(1)}) custom-call(bf16[256,1024]{1,0:T(8,128)(2,1)S(1)} %collective-permute-done.10.above_ref.refs_0_, bf16[256,1024]{1,0:T(8,128)(2,1)S(1)} %collective-permute-done.11.below_ref.refs_1_, ...), custom_call_target="tpu_custom_call" | custom-call | flops 1073741824 | bytes 8388608 | tf_op jit(solution)/shard_map/last_queries/pallas_call | solution.py:669
  64.0 2.3 %window_attend.1.refs_6_ = f32[1024,128]{1,0:T(8,128)S(1)} custom-call(bf16[1024,384]{1,0:T(8,128)(2,1)S(1)} %get-tuple-element.113.win_ref, bf16[512,256]{1,0:T(8,128)(2,1)S(1)} %collective-permute-done.15.halo_ref, bf16[256,256]{1,0:T(8,128)(2,1)S(1)} %collective-permute-done.16.late_ref), custom_call_target="tpu_custom_call" | custom-call | flops 402653184 | bytes 3145728 | tf_op jit(solution)/shard_map/window_attend/pallas_call | solution.py:705
  66.9 5.1 %collective-permute-start.20 = (bf16[256,512]{1,0:T(8,128)(2,1)S(1)}, bf16[256,512]{1,0:T(8,128)(2,1)S(1)}, u32[]{:S(2)}, u32[]{:S(2)}) collective-permute-start(bf16[256,512]{1,0:T(8,128)(2,1)S(1)} %finish3.1), channel_id=1, source_target_pairs={{0,3},{1,0},{2,1},{3,2},{4,7},{5,4},{6,5},{7,6},{8,11},{9,8},{10,9... | collective-permute-start | bytes 786440 | tf_op jit(solution)/shard_map/ppermute | solution.py:732
  73.0 1.6 %collective-permute-start.18 = (bf16[256,512]{1,0:T(8,128)(2,1)S(1)}, bf16[256,512]{1,0:T(8,128)(2,1)S(1)}, u32[]{:S(2)}, u32[]{:S(2)}) collective-permute-start(bf16[256,512]{1,0:T(8,128)(2,1)S(1)} %finish2.1), channel_id=1, source_target_pairs={{0,2},{1,3},{2,0},{3,1},{4,6},{5,7},{6,4},{7,5},{8,10},{9,11},{10,... | collective-permute-start | bytes 786440 | tf_op jit(solution)/shard_map/ppermute | solution.py:732
  75.0 3.6 %collective-permute-done.20.refs_3_ = bf16[256,512]{1,0:T(8,128)(2,1)S(1)} collective-permute-done((bf16[256,512]{1,0:T(8,128)(2,1)S(1)}, bf16[256,512]{1,0:T(8,128)(2,1)S(1)}, u32[]{:S(2)}, u32[]{:S(2)}) %collective-permute-start.20) | collective-permute-done | bytes 262176 | tf_op jit(solution)/shard_map/ppermute | solution.py:732
  78.7 7.1 %collective-permute-done.19.refs_2_ = bf16[256,512]{1,0:T(8,128)(2,1)S(1)} collective-permute-done((bf16[256,512]{1,0:T(8,128)(2,1)S(1)}, bf16[256,512]{1,0:T(8,128)(2,1)S(1)}, u32[]{:S(2)}, u32[]{:S(2)}) %collective-permute-start.19) | collective-permute-done | bytes 262176 | tf_op jit(solution)/shard_map/ppermute | solution.py:732
  85.8 9.5 %collective-permute-done.18.refs_1_ = bf16[256,512]{1,0:T(8,128)(2,1)S(1)} collective-permute-done((bf16[256,512]{1,0:T(8,128)(2,1)S(1)}, bf16[256,512]{1,0:T(8,128)(2,1)S(1)}, u32[]{:S(2)}, u32[]{:S(2)}) %collective-permute-start.18) | collective-permute-done | bytes 262176 | tf_op jit(solution)/shard_map/ppermute | solution.py:732
  (46 shorter events, 18.2 us)
Async XLA Ops:
  0.0 24.2 %collective-permute-start = (bf16[256,1024]{1,0:T(8,128)(2,1)}, bf16[256,1024]{1,0:T(8,128)(2,1)S(1)}, u32[]{:S(2)}, u32[]{:S(2)}) collective-permute-start(bf16[256,1024]{1,0:T(8,128)(2,1)} %refs_0_.1), channel_id=1, source_target_pairs={{0,1},{1,2},{2,3},{4,5},{5,6},{6,7},{8,9},{9,10},{10,11},{12,13},{... | collective-permute-start | bytes 1572872 | tf_op jit(solution)/shard_map/ppermute | solution.py:573
  5.0 19.2 %collective-permute-start.1 = (bf16[256,1024]{1,0:T(8,128)(2,1)}, bf16[256,1024]{1,0:T(8,128)(2,1)S(1)}, u32[]{:S(2)}, u32[]{:S(2)}) collective-permute-start(bf16[256,1024]{1,0:T(8,128)(2,1)} %refs_0_.1), channel_id=1, source_target_pairs={{3,2},{2,1},{1,0},{7,6},{6,5},{5,4},{11,10},{10,9},{9,8},{15,14},{... | collective-permute-start | bytes 1572872 | tf_op jit(solution)/shard_map/ppermute | solution.py:574
  6.3 1.1 %copy-start.1 = (bf16[256,1536]{1,0:T(8,128)(2,1)S(1)}, bf16[256,1536]{1,0:T(8,128)(2,1)}, u32[]{:S(2)}) copy-start(bf16[256,1536]{1,0:T(8,128)(2,1)} %weight_ref.1) | copy-start | bytes 2359300
  8.2 15.9 %collective-permute-start.2 = (bf16[48,384]{1,0:T(8,128)(2,1)S(1)}, bf16[48,384]{1,0:T(8,128)(2,1)S(1)}, u32[]{:S(2)}, u32[]{:S(2)}) collective-permute-start(bf16[48,384]{1,0:T(8,128)(2,1)S(1)} %get-tuple-element.66), channel_id=1, source_target_pairs={{0,1},{1,2},{2,3},{3,0},{4,5},{5,6},{6,7},{7,4},{8,9},{9,10},{10,1... | collective-permute-start | bytes 110600 | tf_op jit(solution)/shard_map/ppermute | solution.py:588
  10.9 13.2 %collective-permute-start.3 = (bf16[48,384]{1,0:T(8,128)(2,1)S(1)}, bf16[48,384]{1,0:T(8,128)(2,1)S(1)}, u32[]{:S(2)}, u32[]{:S(2)}) collective-permute-start(bf16[48,384]{1,0:T(8,128)(2,1)S(1)} %get-tuple-element.67), channel_id=1, source_target_pairs={{0,2},{1,3},{2,0},{3,1},{4,6},{5,7},{6,4},{7,5},{8,10},{9,11},{10,... | collective-permute-start | bytes 110600 | tf_op jit(solution)/shard_map/ppermute | solution.py:588
  13.5 10.6 %collective-permute-start.4 = (bf16[48,384]{1,0:T(8,128)(2,1)S(1)}, bf16[48,384]{1,0:T(8,128)(2,1)S(1)}, u32[]{:S(2)}, u32[]{:S(2)}) collective-permute-start(bf16[48,384]{1,0:T(8,128)(2,1)S(1)} %get-tuple-element.68), channel_id=1, source_target_pairs={{0,3},{1,0},{2,1},{3,2},{4,7},{5,4},{6,5},{7,6},{8,11},{9,8},{10,9... | collective-permute-start | bytes 110600 | tf_op jit(solution)/shard_map/ppermute | solution.py:588
  14.8 1.9 %copy-start = (bf16[1,1024,1536]{2,1,0:T(8,128)(2,1)S(1)}, bf16[1,1024,1536]{2,1,0:T(8,128)(2,1)}, u32[]{:S(2)}) copy-start(bf16[1,1024,1536]{2,1,0:T(8,128)(2,1)} %param.8) | copy-start | bytes 9437188
  16.7 1.0 %copy-start.2 = (bf16[256,1024]{1,0:T(8,128)(2,1)S(1)}, bf16[256,1024]{1,0:T(8,128)(2,1)}, u32[]{:S(2)}) copy-start(bf16[256,1024]{1,0:T(8,128)(2,1)} %refs_0_.1) | copy-start | bytes 1572868
  24.2 13.2 %collective-permute-start.5 = (bf16[256,1024]{1,0:T(8,128)(2,1)S(1)}, bf16[256,1024]{1,0:T(8,128)(2,1)S(1)}, u32[]{:S(2)}, u32[]{:S(2)}) collective-permute-start(bf16[256,1024]{1,0:T(8,128)(2,1)S(1)} %collective-permute-done.1.refs_2_), channel_id=1, source_target_pairs={{2,1},{1,0},{6,5},{5,4},{10,9},{9,8},{14,13},{13,12},{18,17},{17,1... | collective-permute-start | bytes 1572872 | tf_op jit(solution)/shard_map/ppermute | solution.py:575
  25.5 11.9 %collective-permute-start.6 = (bf16[256,1024]{1,0:T(8,128)(2,1)S(1)}, bf16[256,1024]{1,0:T(8,128)(2,1)S(1)}, u32[]{:S(2)}, u32[]{:S(2)}) collective-permute-start(bf16[256,1024]{1,0:T(8,128)(2,1)S(1)} %collective-permute-done.refs_1_), channel_id=1, source_target_pairs={{1,2},{2,3},{5,6},{6,7},{9,10},{10,11},{13,14},{14,15},{17,18},{18... | collective-permute-start | bytes 1572872 | tf_op jit(solution)/shard_map/ppermute | solution.py:576
  26.2 7.1 %collective-permute-start.7 = (bf16[4,32,384]{2,1,0:T(8,128)(2,1)S(1)}, bf16[4,32,384]{2,1,0:T(8,128)(2,1)S(1)}, u32[]{:S(2)}, u32[]{:S(2)}) collective-permute-start(bf16[4,32,384]{2,1,0:T(8,128)(2,1)S(1)} %get-tuple-element.80.refs_0_), channel_id=1, source_target_pairs={{0,8},{4,12},{8,16},{12,20},{16,24},{20,28},{24,0},{28,4},{1,9},{5... | collective-permute-start | bytes 294920 | tf_op jit(solution)/shard_map/ppermute | solution.py:628
  27.7 5.6 %collective-permute-start.8 = (bf16[4,32,384]{2,1,0:T(8,128)(2,1)S(1)}, bf16[4,32,384]{2,1,0:T(8,128)(2,1)S(1)}, u32[]{:S(2)}, u32[]{:S(2)}) collective-permute-start(bf16[4,32,384]{2,1,0:T(8,128)(2,1)S(1)} %get-tuple-element.80.refs_0_), channel_id=1, source_target_pairs={{0,16},{4,20},{8,24},{12,28},{16,0},{20,4},{24,8},{28,12},{1,17},{... | collective-permute-start | bytes 294920 | tf_op jit(solution)/shard_map/ppermute | solution.py:628
  29.2 4.6 %collective-permute-start.9 = (bf16[4,32,384]{2,1,0:T(8,128)(2,1)S(1)}, bf16[4,32,384]{2,1,0:T(8,128)(2,1)S(1)}, u32[]{:S(2)}, u32[]{:S(2)}) collective-permute-start(bf16[4,32,384]{2,1,0:T(8,128)(2,1)S(1)} %get-tuple-element.80.refs_0_), channel_id=1, source_target_pairs={{0,24},{4,28},{8,0},{12,4},{16,8},{20,12},{24,16},{28,20},{1,25},{... | collective-permute-start | bytes 294920 | tf_op jit(solution)/shard_map/ppermute | solution.py:628
  37.4 12.5 %collective-permute-start.10 = (bf16[256,1024]{1,0:T(8,128)(2,1)S(1)}, bf16[256,1024]{1,0:T(8,128)(2,1)S(1)}, u32[]{:S(2)}, u32[]{:S(2)}) collective-permute-start(bf16[256,1024]{1,0:T(8,128)(2,1)S(1)} %collective-permute-done.5.refs_0_.refs_3_), channel_id=1, source_target_pairs={{1,0},{5,4},{9,8},{13,12},{17,16},{21,20},{25,24},{29,28}} | collective-permute-start | bytes 1572872 | tf_op jit(solution)/shard_map/ppermute | solution.py:575
  38.7 11.2 %collective-permute-start.11 = (bf16[256,1024]{1,0:T(8,128)(2,1)S(1)}, bf16[256,1024]{1,0:T(8,128)(2,1)S(1)}, u32[]{:S(2)}, u32[]{:S(2)}) collective-permute-start(bf16[256,1024]{1,0:T(8,128)(2,1)S(1)} %collective-permute-done.6.refs_1_.refs_4_), channel_id=1, source_target_pairs={{2,3},{6,7},{10,11},{14,15},{18,19},{22,23},{26,27},{30,31}} | collective-permute-start | bytes 1572872 | tf_op jit(solution)/shard_map/ppermute | solution.py:576
  39.4 5.7 %collective-permute-start.12 = (bf16[4,4,32,384]{3,2,1,0:T(8,128)(2,1)S(1)}, bf16[4,4,32,384]{3,2,1,0:T(8,128)(2,1)S(1)}, u32[]{:S(2)}, u32[]{:S(2)}) collective-permute-start(bf16[4,4,32,384]{3,2,1,0:T(8,128)(2,1)S(1)} %combine.1.refs_5_), channel_id=1, source_target_pairs={{0,4},{4,0},{8,12},{12,8},{16,20},{20,16},{24,28},{28,24},{1,5},{5... | collective-permute-start | bytes 1179656 | tf_op jit(solution)/shard_map/ppermute | solution.py:640
  50.8 5.9 %collective-permute-start.13 = (bf16[512,128]{1,0:T(8,128)(2,1)S(1)}, bf16[512,128]{1,0:T(8,128)(2,1)S(1)}, u32[]{:S(2)}, u32[]{:S(2)}) collective-permute-start(bf16[512,128]{1,0:T(8,128)(2,1)S(1)} %get-tuple-element.99), channel_id=1, source_target_pairs={{0,16},{4,20},{8,24},{12,28},{1,17},{5,21},{9,25},{13,29},{2,18},{... | collective-permute-start | bytes 393224 | tf_op jit(solution)/shard_map/ppermute | solution.py:678
  54.3 9.7 %collective-permute-start.15 = (bf16[512,256]{1,0:T(8,128)(2,1)S(1)}, bf16[512,256]{1,0:T(8,128)(2,1)S(1)}, u32[]{:S(2)}, u32[]{:S(2)}) collective-permute-start(bf16[512,256]{1,0:T(8,128)(2,1)S(1)} %get-tuple-element.114), channel_id=1, source_target_pairs={{0,4},{4,8},{8,12},{12,16},{16,20},{20,24},{24,28},{1,5},{5,9},{9,... | collective-permute-start | bytes 786440 | tf_op jit(solution)/shard_map/ppermute | solution.py:21
  56.8 6.5 %collective-permute-start.14 = (bf16[512,128]{1,0:T(8,128)(2,1)S(1)}, bf16[512,128]{1,0:T(8,128)(2,1)S(1)}, u32[]{:S(2)}, u32[]{:S(2)}) collective-permute-start(bf16[512,128]{1,0:T(8,128)(2,1)S(1)} %get-tuple-element.101), channel_id=1, source_target_pairs={{0,8},{4,12},{8,0},{12,4},{16,24},{20,28},{24,16},{28,20},{1,9},{5... | collective-permute-start | bytes 393224 | tf_op jit(solution)/shard_map/ppermute | solution.py:692
  59.1 5.0 %collective-permute-start.16 = (bf16[256,256]{1,0:T(8,128)(2,1)S(1)}, bf16[256,256]{1,0:T(8,128)(2,1)S(1)}, u32[]{:S(2)}, u32[]{:S(2)}) collective-permute-start(bf16[256,256]{1,0:T(8,128)(2,1)S(1)} %get-tuple-element.115), channel_id=1, source_target_pairs={{0,4},{4,8},{8,12},{12,16},{16,20},{20,24},{24,28}} | collective-permute-start | bytes 393224 | tf_op jit(solution)/shard_map/ppermute | solution.py:703
  63.4 3.0 %collective-permute-start.17 = (bf16[512,128]{1,0:T(8,128)(2,1)S(1)}, bf16[512,128]{1,0:T(8,128)(2,1)S(1)}, u32[]{:S(2)}, u32[]{:S(2)}) collective-permute-start(bf16[512,128]{1,0:T(8,128)(2,1)S(1)} %get-tuple-element.118), channel_id=1, source_target_pairs={{0,4},{4,0},{8,12},{12,8},{16,20},{20,16},{24,28},{28,24},{1,5},{5... | collective-permute-start | bytes 393224 | tf_op jit(solution)/shard_map/ppermute | solution.py:692
  66.9 11.8 %collective-permute-start.20 = (bf16[256,512]{1,0:T(8,128)(2,1)S(1)}, bf16[256,512]{1,0:T(8,128)(2,1)S(1)}, u32[]{:S(2)}, u32[]{:S(2)}) collective-permute-start(bf16[256,512]{1,0:T(8,128)(2,1)S(1)} %finish3.1), channel_id=1, source_target_pairs={{0,3},{1,0},{2,1},{3,2},{4,7},{5,4},{6,5},{7,6},{8,11},{9,8},{10,9... | collective-permute-start | bytes 786440 | tf_op jit(solution)/shard_map/ppermute | solution.py:732
  72.4 13.3 %collective-permute-start.19 = (bf16[256,512]{1,0:T(8,128)(2,1)S(1)}, bf16[256,512]{1,0:T(8,128)(2,1)S(1)}, u32[]{:S(2)}, u32[]{:S(2)}) collective-permute-start(bf16[256,512]{1,0:T(8,128)(2,1)S(1)} %finish1.1), channel_id=1, source_target_pairs={{0,1},{1,2},{2,3},{3,0},{4,5},{5,6},{6,7},{7,4},{8,9},{9,10},{10,1... | collective-permute-start | bytes 786440 | tf_op jit(solution)/shard_map/ppermute | solution.py:732
  73.0 22.2 %collective-permute-start.18 = (bf16[256,512]{1,0:T(8,128)(2,1)S(1)}, bf16[256,512]{1,0:T(8,128)(2,1)S(1)}, u32[]{:S(2)}, u32[]{:S(2)}) collective-permute-start(bf16[256,512]{1,0:T(8,128)(2,1)S(1)} %finish2.1), channel_id=1, source_target_pairs={{0,2},{1,3},{2,0},{3,1},{4,6},{5,7},{6,4},{7,5},{8,10},{9,11},{10,... | collective-permute-start | bytes 786440 | tf_op jit(solution)/shard_map/ppermute | solution.py:732
  (2 other events, 1.4 us)

commit v11 on v10

--- a/solution.py
+++ b/solution.py
@@ -727,7 +727,7 @@
         )(proj, intra, coef, *local, prefix, got)
 
     parts = []
-    for shift in sorted(range(1, n_mem), key=lambda s: abs(2 * s - n_mem)):
+    for shift in sorted(range(1, n_mem), key=lambda s: -abs(2 * s - n_mem)):
         part = finish(shift, prefix)
         parts.append(lax.ppermute(part, "mem", [(i, (i + shift) % n_mem) for i in range(n_mem)]))
     return kernel_call(

time: 96.5 us -> 95.1 us (0.985)
  the two profiles are of different devices: /device:TPU:0 before, /device:TPU:9 now
where the time goes in v11:
time: 95.1 us; the launch traced here: 93.7 us
  starting transfers between devices  37.4 us (39%)
  waiting for transfers between devices  30.8 us (32%)
  Pallas kernels  19.8 us (21%)
  local copies, waits for them, and re-layouts  5.43 us (6%)
    ppermute x3, waiting for transfers between devices, dense_shards(): lax.ppermute(part, 'mem', [(i, (i + shift) % n_mem) for i in range(n_mem)])  20.5 us
    pallas_call x1, Pallas kernels, dense_shards(): kernel_call(functools.partial(arrivals_body, n_mem, 3, early, True), 'mid...  8.17 us
    unnamed x10, local copies, waits for them, and re-layouts  5.43 us
    ppermute x3, waiting for transfers between devices, dense_shards(): lax.ppermute(packed[s], 'mem', [(i, (i + s) % n_mem) for i in range(n_mem)])  5.1 us
    ppermute x3, starting transfers between devices, dense_shards(): lax.ppermute(part, 'mem', [(i, (i + shift) % n_mem) for i in range(n_mem)])  4.74 us
    ppermute x2, waiting for transfers between devices, dense_shards(): got = lax.ppermute(sent, 'ctx', [(i, i ^ bit) for i in range(n_ctx)])  4.65 us
    ppermute x1, starting transfers between devices, dense_shards(): lax.ppermute(of_core, 'ctx', [(i, i ^ 1) for i in range(n_ctx)])  4.08 us
    pallas_call x1, Pallas kernels, dense_shards(): kernel_call(functools.partial(arrivals_body, n_mem, 0, 3, False), 'near_r...  3.87 us
  transfers between devices with their start and end apart: 21, of which 6 were waited for; matrix products, arithmetic and copies ran while one was open for 0% of the time, Pallas kernels for 20%

profile of v11, /device:TPU:9, one launch (start us, length us, event | category | flops | bytes accessed | tf_op | source)
XLA Modules:
  0.0 93.7 jit_solution(14856921823443994451)
XLA Ops:
  0.0 3.2 %collective-permute-start = (bf16[256,1024]{1,0:T(8,128)(2,1)}, bf16[256,1024]{1,0:T(8,128)(2,1)S(1)}, u32[]{:S(2)}, u32[]{:S(2)}) collective-permute-start(bf16[256,1024]{1,0:T(8,128)(2,1)} %refs_0_.1), channel_id=1, source_target_pairs={{0,1},{1,2},{2,3},{4,5},{5,6},{6,7},{8,9},{9,10},{10,11},{12,13},{... | collective-permute-start | bytes 1572872 | tf_op jit(solution)/shard_map/ppermute | solution.py:573
  3.2 2.1 %collective-permute-start.1 = (bf16[256,1024]{1,0:T(8,128)(2,1)}, bf16[256,1024]{1,0:T(8,128)(2,1)S(1)}, u32[]{:S(2)}, u32[]{:S(2)}) collective-permute-start(bf16[256,1024]{1,0:T(8,128)(2,1)} %refs_0_.1), channel_id=1, source_target_pairs={{3,2},{2,1},{1,0},{7,6},{6,5},{5,4},{11,10},{10,9},{9,8},{15,14},{... | collective-permute-start | bytes 1572872 | tf_op jit(solution)/shard_map/ppermute | solution.py:574
  7.3 1.3 %collective-permute-start.2 = (bf16[48,384]{1,0:T(8,128)(2,1)S(1)}, bf16[48,384]{1,0:T(8,128)(2,1)S(1)}, u32[]{:S(2)}, u32[]{:S(2)}) collective-permute-start(bf16[48,384]{1,0:T(8,128)(2,1)S(1)} %get-tuple-element.66), channel_id=1, source_target_pairs={{0,1},{1,2},{2,3},{3,0},{4,5},{5,6},{6,7},{7,4},{8,9},{9,10},{10,1... | collective-permute-start | bytes 110600 | tf_op jit(solution)/shard_map/ppermute | solution.py:588
  9.7 1.4 %collective-permute-start.4 = (bf16[48,384]{1,0:T(8,128)(2,1)S(1)}, bf16[48,384]{1,0:T(8,128)(2,1)S(1)}, u32[]{:S(2)}, u32[]{:S(2)}) collective-permute-start(bf16[48,384]{1,0:T(8,128)(2,1)S(1)} %get-tuple-element.68), channel_id=1, source_target_pairs={{0,3},{1,0},{2,1},{3,2},{4,7},{5,4},{6,5},{7,6},{8,11},{9,8},{10,9... | collective-permute-start | bytes 110600 | tf_op jit(solution)/shard_map/ppermute | solution.py:588
  11.1 1.9 %copy-done = bf16[1,1024,1536]{2,1,0:T(8,128)(2,1)S(1)} copy-done((bf16[1,1024,1536]{2,1,0:T(8,128)(2,1)S(1)}, bf16[1,1024,1536]{2,1,0:T(8,128)(2,1)}, u32[]{:S(2)}) %copy-start) | copy-done | bytes 3145752
  15.7 4.4 %collective-permute-done.3.refs_2_ = bf16[48,384]{1,0:T(8,128)(2,1)S(1)} collective-permute-done((bf16[48,384]{1,0:T(8,128)(2,1)S(1)}, bf16[48,384]{1,0:T(8,128)(2,1)S(1)}, u32[]{:S(2)}, u32[]{:S(2)}) %collective-permute-start.3) | collective-permute-done | bytes 36896 | tf_op jit(solution)/shard_map/ppermute | solution.py:588
  20.1 2.3 %collective-permute-start.5 = (bf16[256,1024]{1,0:T(8,128)(2,1)S(1)}, bf16[256,1024]{1,0:T(8,128)(2,1)S(1)}, u32[]{:S(2)}, u32[]{:S(2)}) collective-permute-start(bf16[256,1024]{1,0:T(8,128)(2,1)S(1)} %collective-permute-done.1.refs_2_), channel_id=1, source_target_pairs={{2,1},{1,0},{6,5},{5,4},{10,9},{9,8},{14,13},{13,12},{18,17},{17,1... | collective-permute-start | bytes 1572872 | tf_op jit(solution)/shard_map/ppermute | solution.py:575
  22.5 3.0 %collective-permute-start.6 = (bf16[256,1024]{1,0:T(8,128)(2,1)S(1)}, bf16[256,1024]{1,0:T(8,128)(2,1)S(1)}, u32[]{:S(2)}, u32[]{:S(2)}) collective-permute-start(bf16[256,1024]{1,0:T(8,128)(2,1)S(1)} %collective-permute-done.refs_1_), channel_id=1, source_target_pairs={{1,2},{2,3},{5,6},{6,7},{9,10},{10,11},{13,14},{14,15},{17,18},{18... | collective-permute-start | bytes 1572872 | tf_op jit(solution)/shard_map/ppermute | solution.py:576
  25.5 1.3 %collective-permute-start.7 = (bf16[4,32,384]{2,1,0:T(8,128)(2,1)S(1)}, bf16[4,32,384]{2,1,0:T(8,128)(2,1)S(1)}, u32[]{:S(2)}, u32[]{:S(2)}) collective-permute-start(bf16[4,32,384]{2,1,0:T(8,128)(2,1)S(1)} %get-tuple-element.80.refs_0_), channel_id=1, source_target_pairs={{0,8},{4,12},{8,16},{12,20},{16,24},{20,28},{24,0},{28,4},{1,9},{5... | collective-permute-start | bytes 294920 | tf_op jit(solution)/shard_map/ppermute | solution.py:628
  26.8 1.2 %collective-permute-start.8 = (bf16[4,32,384]{2,1,0:T(8,128)(2,1)S(1)}, bf16[4,32,384]{2,1,0:T(8,128)(2,1)S(1)}, u32[]{:S(2)}, u32[]{:S(2)}) collective-permute-start(bf16[4,32,384]{2,1,0:T(8,128)(2,1)S(1)} %get-tuple-element.80.refs_0_), channel_id=1, source_target_pairs={{0,16},{4,20},{8,24},{12,28},{16,0},{20,4},{24,8},{28,12},{1,17},{... | collective-permute-start | bytes 294920 | tf_op jit(solution)/shard_map/ppermute | solution.py:628
  28.0 1.2 %collective-permute-start.9 = (bf16[4,32,384]{2,1,0:T(8,128)(2,1)S(1)}, bf16[4,32,384]{2,1,0:T(8,128)(2,1)S(1)}, u32[]{:S(2)}, u32[]{:S(2)}) collective-permute-start(bf16[4,32,384]{2,1,0:T(8,128)(2,1)S(1)} %get-tuple-element.80.refs_0_), channel_id=1, source_target_pairs={{0,24},{4,28},{8,0},{12,4},{16,8},{20,12},{24,16},{28,20},{1,25},{... | collective-permute-start | bytes 294920 | tf_op jit(solution)/shard_map/ppermute | solution.py:628
  29.1 3.9 %near_rows.1 = (bf16[1024,1536]{1,0:T(8,128)(2,1)S(1)}, f32[1024,128]{1,0:T(8,128)S(1)}, f32[512,128]{1,0:T(8,128)S(1)}) custom-call(bf16[256,1024]{1,0:T(8,128)(2,1)S(1)} %get-tuple-element.76.refs_0_, bf16[256,1024]{1,0:T(8,128)(2,1)S(1)} %collective-permute-done.refs_1_, bf16[256,1024]{1,0:T(8,128)(2,1)S(1)} %collective-permute-done.1.refs_2_, ...), custom_call_target="tpu_custom_call" | custom-call | flops 2415919104 | bytes 6291456 | tf_op jit(solution)/shard_map/near_rows/pallas_call | solution.py:619
  33.7 1.3 %collective-permute-start.10 = (bf16[256,1024]{1,0:T(8,128)(2,1)S(1)}, bf16[256,1024]{1,0:T(8,128)(2,1)S(1)}, u32[]{:S(2)}, u32[]{:S(2)}) collective-permute-start(bf16[256,1024]{1,0:T(8,128)(2,1)S(1)} %collective-permute-done.5.refs_0_.refs_3_), channel_id=1, source_target_pairs={{1,0},{5,4},{9,8},{13,12},{17,16},{21,20},{25,24},{29,28}} | collective-permute-start | bytes 1572872 | tf_op jit(solution)/shard_map/ppermute | solution.py:575
  35.7 4.1 %collective-permute-start.12 = (bf16[4,4,32,384]{3,2,1,0:T(8,128)(2,1)S(1)}, bf16[4,4,32,384]{3,2,1,0:T(8,128)(2,1)S(1)}, u32[]{:S(2)}, u32[]{:S(2)}) collective-permute-start(bf16[4,4,32,384]{3,2,1,0:T(8,128)(2,1)S(1)} %combine.1.refs_5_), channel_id=1, source_target_pairs={{0,4},{4,0},{8,12},{12,8},{16,20},{20,16},{24,28},{28,24},{1,5},{5... | collective-permute-start | bytes 1179656 | tf_op jit(solution)/shard_map/ppermute | solution.py:640
  39.8 8.2 %middle_rows.1 = (bf16[1024,1536]{1,0:T(8,128)(2,1)S(1)}, f32[1024,128]{1,0:T(8,128)S(1)}, f32[512,128]{1,0:T(8,128)S(1)}, f32[1024,512]{1,0:T(8,128)S(1)}) custom-call(bf16[256,1024]{1,0:T(8,128)(2,1)S(1)} %collective-permute-done.5.refs_0_.refs_3_, bf16[256,1024]{1,0:T(8,128)(2,1)S(1)} %collective-permute-done.6.refs_1_.refs_4_, ...), custom_call_target="tpu_custom_call" | custom-call | flops 2415919104 | bytes 6291456 | tf_op jit(solution)/shard_map/middle_rows/pallas_call | solution.py:646
  47.9 1.9 %window_early.1 = (bf16[1024,384]{1,0:T(8,128)(2,1)S(1)}, bf16[1024,384]{1,0:T(8,128)(2,1)S(1)}, bf16[512,256]{1,0:T(8,128)(2,1)S(1)}) custom-call(bf16[256,1024]{1,0:T(8,128)(2,1)S(1)} %get-tuple-element.76.refs_0_, bf16[256,1024]{1,0:T(8,128)(2,1)S(1)} %collective-permute-done.refs_1_, bf16[256,1024]{1,0:T(8,128)(2,1)S(1)} %collective-permute-done.1.refs_2_, ...), custom_call_target="tpu_custom_call" | custom-call | flops 805306368 | bytes 5242880 | tf_op jit(solution)/shard_map/window_early/pallas_call | solution.py:653
  49.9 3.1 %collective-permute-start.13 = (bf16[512,128]{1,0:T(8,128)(2,1)S(1)}, bf16[512,128]{1,0:T(8,128)(2,1)S(1)}, u32[]{:S(2)}, u32[]{:S(2)}) collective-permute-start(bf16[512,128]{1,0:T(8,128)(2,1)S(1)} %get-tuple-element.99), channel_id=1, source_target_pairs={{0,16},{4,20},{8,24},{12,28},{1,17},{5,21},{9,25},{13,29},{2,18},{... | collective-permute-start | bytes 393224 | tf_op jit(solution)/shard_map/ppermute | solution.py:678
  53.0 3.3 %collective-permute-start.15 = (bf16[512,256]{1,0:T(8,128)(2,1)S(1)}, bf16[512,256]{1,0:T(8,128)(2,1)S(1)}, u32[]{:S(2)}, u32[]{:S(2)}) collective-permute-start(bf16[512,256]{1,0:T(8,128)(2,1)S(1)} %get-tuple-element.114), channel_id=1, source_target_pairs={{0,4},{4,8},{8,12},{12,16},{16,20},{20,24},{24,28},{1,5},{5,9},{9,... | collective-permute-start | bytes 786440 | tf_op jit(solution)/shard_map/ppermute | solution.py:21
  58.2 4.6 %collective-permute-done.14.refs_1_ = bf16[512,128]{1,0:T(8,128)(2,1)S(1)} collective-permute-done((bf16[512,128]{1,0:T(8,128)(2,1)S(1)}, bf16[512,128]{1,0:T(8,128)(2,1)S(1)}, u32[]{:S(2)}, u32[]{:S(2)}) %collective-permute-start.14) | collective-permute-done | bytes 131104 | tf_op jit(solution)/shard_map/ppermute | solution.py:692
  63.4 2.3 %window_attend.1.refs_6_ = f32[1024,128]{1,0:T(8,128)S(1)} custom-call(bf16[1024,384]{1,0:T(8,128)(2,1)S(1)} %get-tuple-element.113.win_ref, bf16[512,256]{1,0:T(8,128)(2,1)S(1)} %collective-permute-done.15.halo_ref, bf16[256,256]{1,0:T(8,128)(2,1)S(1)} %collective-permute-done.16.late_ref), custom_call_target="tpu_custom_call" | custom-call | flops 402653184 | bytes 3145728 | tf_op jit(solution)/shard_map/window_attend/pallas_call | solution.py:705
  66.2 3.2 %collective-permute-start.20 = (bf16[256,512]{1,0:T(8,128)(2,1)S(1)}, bf16[256,512]{1,0:T(8,128)(2,1)S(1)}, u32[]{:S(2)}, u32[]{:S(2)}) collective-permute-start(bf16[256,512]{1,0:T(8,128)(2,1)S(1)} %finish2.1), channel_id=1, source_target_pairs={{0,2},{1,3},{2,0},{3,1},{4,6},{5,7},{6,4},{7,5},{8,10},{9,11},{10,... | collective-permute-start | bytes 786440 | tf_op jit(solution)/shard_map/ppermute | solution.py:732
  69.9 1.2 %collective-permute-start.19 = (bf16[256,512]{1,0:T(8,128)(2,1)S(1)}, bf16[256,512]{1,0:T(8,128)(2,1)S(1)}, u32[]{:S(2)}, u32[]{:S(2)}) collective-permute-start(bf16[256,512]{1,0:T(8,128)(2,1)S(1)} %finish3.1), channel_id=1, source_target_pairs={{0,3},{1,0},{2,1},{3,2},{4,7},{5,4},{6,5},{7,6},{8,11},{9,8},{10,9... | collective-permute-start | bytes 786440 | tf_op jit(solution)/shard_map/ppermute | solution.py:732
  72.4 13.5 %collective-permute-done.20.refs_3_ = bf16[256,512]{1,0:T(8,128)(2,1)S(1)} collective-permute-done((bf16[256,512]{1,0:T(8,128)(2,1)S(1)}, bf16[256,512]{1,0:T(8,128)(2,1)S(1)}, u32[]{:S(2)}, u32[]{:S(2)}) %collective-permute-start.20) | collective-permute-done | bytes 262176 | tf_op jit(solution)/shard_map/ppermute | solution.py:732
  85.9 7.0 %collective-permute-done.19.refs_2_ = bf16[256,512]{1,0:T(8,128)(2,1)S(1)} collective-permute-done((bf16[256,512]{1,0:T(8,128)(2,1)S(1)}, bf16[256,512]{1,0:T(8,128)(2,1)S(1)}, u32[]{:S(2)}, u32[]{:S(2)}) %collective-permute-start.19) | collective-permute-done | bytes 262176 | tf_op jit(solution)/shard_map/ppermute | solution.py:732
  (46 shorter events, 12.6 us)
Async XLA Ops:
  0.0 20.1 %collective-permute-start = (bf16[256,1024]{1,0:T(8,128)(2,1)}, bf16[256,1024]{1,0:T(8,128)(2,1)S(1)}, u32[]{:S(2)}, u32[]{:S(2)}) collective-permute-start(bf16[256,1024]{1,0:T(8,128)(2,1)} %refs_0_.1), channel_id=1, source_target_pairs={{0,1},{1,2},{2,3},{4,5},{5,6},{6,7},{8,9},{9,10},{10,11},{12,13},{... | collective-permute-start | bytes 1572872 | tf_op jit(solution)/shard_map/ppermute | solution.py:573
  3.2 16.9 %collective-permute-start.1 = (bf16[256,1024]{1,0:T(8,128)(2,1)}, bf16[256,1024]{1,0:T(8,128)(2,1)S(1)}, u32[]{:S(2)}, u32[]{:S(2)}) collective-permute-start(bf16[256,1024]{1,0:T(8,128)(2,1)} %refs_0_.1), channel_id=1, source_target_pairs={{3,2},{2,1},{1,0},{7,6},{6,5},{5,4},{11,10},{10,9},{9,8},{15,14},{... | collective-permute-start | bytes 1572872 | tf_op jit(solution)/shard_map/ppermute | solution.py:574
  5.3 1.1 %copy-start.1 = (bf16[256,1536]{1,0:T(8,128)(2,1)S(1)}, bf16[256,1536]{1,0:T(8,128)(2,1)}, u32[]{:S(2)}) copy-start(bf16[256,1536]{1,0:T(8,128)(2,1)} %weight_ref.1) | copy-start | bytes 2359300
  7.3 8.4 %collective-permute-start.2 = (bf16[48,384]{1,0:T(8,128)(2,1)S(1)}, bf16[48,384]{1,0:T(8,128)(2,1)S(1)}, u32[]{:S(2)}, u32[]{:S(2)}) collective-permute-start(bf16[48,384]{1,0:T(8,128)(2,1)S(1)} %get-tuple-element.66), channel_id=1, source_target_pairs={{0,1},{1,2},{2,3},{3,0},{4,5},{5,6},{6,7},{7,4},{8,9},{9,10},{10,1... | collective-permute-start | bytes 110600 | tf_op jit(solution)/shard_map/ppermute | solution.py:588
  8.6 11.5 %collective-permute-start.3 = (bf16[48,384]{1,0:T(8,128)(2,1)S(1)}, bf16[48,384]{1,0:T(8,128)(2,1)S(1)}, u32[]{:S(2)}, u32[]{:S(2)}) collective-permute-start(bf16[48,384]{1,0:T(8,128)(2,1)S(1)} %get-tuple-element.67), channel_id=1, source_target_pairs={{0,2},{1,3},{2,0},{3,1},{4,6},{5,7},{6,4},{7,5},{8,10},{9,11},{10,... | collective-permute-start | bytes 110600 | tf_op jit(solution)/shard_map/ppermute | solution.py:588
  9.7 10.4 %collective-permute-start.4 = (bf16[48,384]{1,0:T(8,128)(2,1)S(1)}, bf16[48,384]{1,0:T(8,128)(2,1)S(1)}, u32[]{:S(2)}, u32[]{:S(2)}) collective-permute-start(bf16[48,384]{1,0:T(8,128)(2,1)S(1)} %get-tuple-element.68), channel_id=1, source_target_pairs={{0,3},{1,0},{2,1},{3,2},{4,7},{5,4},{6,5},{7,6},{8,11},{9,8},{10,9... | collective-permute-start | bytes 110600 | tf_op jit(solution)/shard_map/ppermute | solution.py:588
  11.1 1.9 %copy-start = (bf16[1,1024,1536]{2,1,0:T(8,128)(2,1)S(1)}, bf16[1,1024,1536]{2,1,0:T(8,128)(2,1)}, u32[]{:S(2)}) copy-start(bf16[1,1024,1536]{2,1,0:T(8,128)(2,1)} %param.8) | copy-start | bytes 9437188
  13.0 1.0 %copy-start.2 = (bf16[256,1024]{1,0:T(8,128)(2,1)S(1)}, bf16[256,1024]{1,0:T(8,128)(2,1)}, u32[]{:S(2)}) copy-start(bf16[256,1024]{1,0:T(8,128)(2,1)} %refs_0_.1) | copy-start | bytes 1572868
  20.1 13.0 %collective-permute-start.5 = (bf16[256,1024]{1,0:T(8,128)(2,1)S(1)}, bf16[256,1024]{1,0:T(8,128)(2,1)S(1)}, u32[]{:S(2)}, u32[]{:S(2)}) collective-permute-start(bf16[256,1024]{1,0:T(8,128)(2,1)S(1)} %collective-permute-done.1.refs_2_), channel_id=1, source_target_pairs={{2,1},{1,0},{6,5},{5,4},{10,9},{9,8},{14,13},{13,12},{18,17},{17,1... | collective-permute-start | bytes 1572872 | tf_op jit(solution)/shard_map/ppermute | solution.py:575
  22.5 11.2 %collective-permute-start.6 = (bf16[256,1024]{1,0:T(8,128)(2,1)S(1)}, bf16[256,1024]{1,0:T(8,128)(2,1)S(1)}, u32[]{:S(2)}, u32[]{:S(2)}) collective-permute-start(bf16[256,1024]{1,0:T(8,128)(2,1)S(1)} %collective-permute-done.refs_1_), channel_id=1, source_target_pairs={{1,2},{2,3},{5,6},{6,7},{9,10},{10,11},{13,14},{14,15},{17,18},{18... | collective-permute-start | bytes 1572872 | tf_op jit(solution)/shard_map/ppermute | solution.py:576
  25.5 7.5 %collective-permute-start.7 = (bf16[4,32,384]{2,1,0:T(8,128)(2,1)S(1)}, bf16[4,32,384]{2,1,0:T(8,128)(2,1)S(1)}, u32[]{:S(2)}, u32[]{:S(2)}) collective-permute-start(bf16[4,32,384]{2,1,0:T(8,128)(2,1)S(1)} %get-tuple-element.80.refs_0_), channel_id=1, source_target_pairs={{0,8},{4,12},{8,16},{12,20},{16,24},{20,28},{24,0},{28,4},{1,9},{5... | collective-permute-start | bytes 294920 | tf_op jit(solution)/shard_map/ppermute | solution.py:628
  26.8 6.3 %collective-permute-start.8 = (bf16[4,32,384]{2,1,0:T(8,128)(2,1)S(1)}, bf16[4,32,384]{2,1,0:T(8,128)(2,1)S(1)}, u32[]{:S(2)}, u32[]{:S(2)}) collective-permute-start(bf16[4,32,384]{2,1,0:T(8,128)(2,1)S(1)} %get-tuple-element.80.refs_0_), channel_id=1, source_target_pairs={{0,16},{4,20},{8,24},{12,28},{16,0},{20,4},{24,8},{28,12},{1,17},{... | collective-permute-start | bytes 294920 | tf_op jit(solution)/shard_map/ppermute | solution.py:628
  28.0 5.1 %collective-permute-start.9 = (bf16[4,32,384]{2,1,0:T(8,128)(2,1)S(1)}, bf16[4,32,384]{2,1,0:T(8,128)(2,1)S(1)}, u32[]{:S(2)}, u32[]{:S(2)}) collective-permute-start(bf16[4,32,384]{2,1,0:T(8,128)(2,1)S(1)} %get-tuple-element.80.refs_0_), channel_id=1, source_target_pairs={{0,24},{4,28},{8,0},{12,4},{16,8},{20,12},{24,16},{28,20},{1,25},{... | collective-permute-start | bytes 294920 | tf_op jit(solution)/shard_map/ppermute | solution.py:628
  33.7 16.2 %collective-permute-start.10 = (bf16[256,1024]{1,0:T(8,128)(2,1)S(1)}, bf16[256,1024]{1,0:T(8,128)(2,1)S(1)}, u32[]{:S(2)}, u32[]{:S(2)}) collective-permute-start(bf16[256,1024]{1,0:T(8,128)(2,1)S(1)} %collective-permute-done.5.refs_0_.refs_3_), channel_id=1, source_target_pairs={{1,0},{5,4},{9,8},{13,12},{17,16},{21,20},{25,24},{29,28}} | collective-permute-start | bytes 1572872 | tf_op jit(solution)/shard_map/ppermute | solution.py:575
  35.0 14.8 %collective-permute-start.11 = (bf16[256,1024]{1,0:T(8,128)(2,1)S(1)}, bf16[256,1024]{1,0:T(8,128)(2,1)S(1)}, u32[]{:S(2)}, u32[]{:S(2)}) collective-permute-start(bf16[256,1024]{1,0:T(8,128)(2,1)S(1)} %collective-permute-done.6.refs_1_.refs_4_), channel_id=1, source_target_pairs={{2,3},{6,7},{10,11},{14,15},{18,19},{22,23},{26,27},{30,31}} | collective-permute-start | bytes 1572872 | tf_op jit(solution)/shard_map/ppermute | solution.py:576
  35.7 12.3 %collective-permute-start.12 = (bf16[4,4,32,384]{3,2,1,0:T(8,128)(2,1)S(1)}, bf16[4,4,32,384]{3,2,1,0:T(8,128)(2,1)S(1)}, u32[]{:S(2)}, u32[]{:S(2)}) collective-permute-start(bf16[4,4,32,384]{3,2,1,0:T(8,128)(2,1)S(1)} %combine.1.refs_5_), channel_id=1, source_target_pairs={{0,4},{4,0},{8,12},{12,8},{16,20},{20,16},{24,28},{28,24},{1,5},{5... | collective-permute-start | bytes 1179656 | tf_op jit(solution)/shard_map/ppermute | solution.py:640
  49.9 6.5 %collective-permute-start.13 = (bf16[512,128]{1,0:T(8,128)(2,1)S(1)}, bf16[512,128]{1,0:T(8,128)(2,1)S(1)}, u32[]{:S(2)}, u32[]{:S(2)}) collective-permute-start(bf16[512,128]{1,0:T(8,128)(2,1)S(1)} %get-tuple-element.99), channel_id=1, source_target_pairs={{0,16},{4,20},{8,24},{12,28},{1,17},{5,21},{9,25},{13,29},{2,18},{... | collective-permute-start | bytes 393224 | tf_op jit(solution)/shard_map/ppermute | solution.py:678
  53.0 10.4 %collective-permute-start.15 = (bf16[512,256]{1,0:T(8,128)(2,1)S(1)}, bf16[512,256]{1,0:T(8,128)(2,1)S(1)}, u32[]{:S(2)}, u32[]{:S(2)}) collective-permute-start(bf16[512,256]{1,0:T(8,128)(2,1)S(1)} %get-tuple-element.114), channel_id=1, source_target_pairs={{0,4},{4,8},{8,12},{12,16},{16,20},{20,24},{24,28},{1,5},{5,9},{9,... | collective-permute-start | bytes 786440 | tf_op jit(solution)/shard_map/ppermute | solution.py:21
  56.4 6.5 %collective-permute-start.14 = (bf16[512,128]{1,0:T(8,128)(2,1)S(1)}, bf16[512,128]{1,0:T(8,128)(2,1)S(1)}, u32[]{:S(2)}, u32[]{:S(2)}) collective-permute-start(bf16[512,128]{1,0:T(8,128)(2,1)S(1)} %get-tuple-element.101), channel_id=1, source_target_pairs={{0,8},{4,12},{8,0},{12,4},{16,24},{20,28},{24,16},{28,20},{1,9},{5... | collective-permute-start | bytes 393224 | tf_op jit(solution)/shard_map/ppermute | solution.py:692
  57.5 5.9 %collective-permute-start.16 = (bf16[256,256]{1,0:T(8,128)(2,1)S(1)}, bf16[256,256]{1,0:T(8,128)(2,1)S(1)}, u32[]{:S(2)}, u32[]{:S(2)}) collective-permute-start(bf16[256,256]{1,0:T(8,128)(2,1)S(1)} %get-tuple-element.115), channel_id=1, source_target_pairs={{0,4},{4,8},{8,12},{12,16},{16,20},{20,24},{24,28}} | collective-permute-start | bytes 393224 | tf_op jit(solution)/shard_map/ppermute | solution.py:703
  62.9 2.8 %collective-permute-start.17 = (bf16[512,128]{1,0:T(8,128)(2,1)S(1)}, bf16[512,128]{1,0:T(8,128)(2,1)S(1)}, u32[]{:S(2)}, u32[]{:S(2)}) collective-permute-start(bf16[512,128]{1,0:T(8,128)(2,1)S(1)} %get-tuple-element.118), channel_id=1, source_target_pairs={{0,4},{4,0},{8,12},{12,8},{16,20},{20,16},{24,28},{28,24},{1,5},{5... | collective-permute-start | bytes 393224 | tf_op jit(solution)/shard_map/ppermute | solution.py:692
  66.2 19.7 %collective-permute-start.20 = (bf16[256,512]{1,0:T(8,128)(2,1)S(1)}, bf16[256,512]{1,0:T(8,128)(2,1)S(1)}, u32[]{:S(2)}, u32[]{:S(2)}) collective-permute-start(bf16[256,512]{1,0:T(8,128)(2,1)S(1)} %finish2.1), channel_id=1, source_target_pairs={{0,2},{1,3},{2,0},{3,1},{4,6},{5,7},{6,4},{7,5},{8,10},{9,11},{10,... | collective-permute-start | bytes 786440 | tf_op jit(solution)/shard_map/ppermute | solution.py:732
  69.9 23.0 %collective-permute-start.19 = (bf16[256,512]{1,0:T(8,128)(2,1)S(1)}, bf16[256,512]{1,0:T(8,128)(2,1)S(1)}, u32[]{:S(2)}, u32[]{:S(2)}) collective-permute-start(bf16[256,512]{1,0:T(8,128)(2,1)S(1)} %finish3.1), channel_id=1, source_target_pairs={{0,3},{1,0},{2,1},{3,2},{4,7},{5,4},{6,5},{7,6},{8,11},{9,8},{10,9... | collective-permute-start | bytes 786440 | tf_op jit(solution)/shard_map/ppermute | solution.py:732
  71.6 21.4 %collective-permute-start.18 = (bf16[256,512]{1,0:T(8,128)(2,1)S(1)}, bf16[256,512]{1,0:T(8,128)(2,1)S(1)}, u32[]{:S(2)}, u32[]{:S(2)}) collective-permute-start(bf16[256,512]{1,0:T(8,128)(2,1)S(1)} %finish1.1), channel_id=1, source_target_pairs={{0,1},{1,2},{2,3},{3,0},{4,5},{5,6},{6,7},{7,4},{8,9},{9,10},{10,1... | collective-permute-start | bytes 786440 | tf_op jit(solution)/shard_map/ppermute | solution.py:732
  (2 other events, 1.4 us)

commit v12 on v11

--- a/solution.py
+++ b/solution.py
@@ -543,14 +543,14 @@
     refs[-1][...] = total.astype(jnp.bfloat16)
 
 
-def fold_body(bit, *refs):
-    *before, got_ref, state_ref, prefix_ref, sent_ref = refs
-    prefix = got_ref[...].astype(jnp.float32)
-    for before_ref in before:
-        prefix += before_ref[...]
+def fold_body(*refs):
+    gots, (state_ref, prefix_ref, sent_ref) = refs[:-3], refs[-3:]
+    prefix = gots[0][...].astype(jnp.float32)
+    for got_ref in gots[1:]:
+        prefix += got_ref[...].astype(jnp.float32)
     prefix_ref[...] = prefix
-    earlier = (lax.axis_index("ctx") & bit) == 0
-    sent_ref[...] = (prefix + jnp.where(earlier, state_ref[...], 0.0)).astype(jnp.bfloat16)
+    first_core = lax.rem(lax.axis_index("ctx"), 2) == 0
+    sent_ref[...] = (prefix + jnp.where(first_core, state_ref[...], 0.0)).astype(jnp.bfloat16)
 
 
 def dense_shards(tokens, routes, router, mem_weight, win_weight):
@@ -674,34 +674,29 @@
         8 << 20,
     )(above, below, *given, proj, last_kv)
     local = (last_query, last_coef, extra)
-    bit = n_ctx // 2
-    got = lax.ppermute(sent, "ctx", [(i, i + bit) for i in range(n_ctx) if not i & bit])
-    prefix, late = (), None
-    while bit > 1:
-        bit //= 2
-        if bit == 1:
-            got, local = lax.optimization_barrier((got, local))
-        held, sent = kernel_call(
-            functools.partial(fold_body, bit),
-            f"fold{bit}",
-            (shape(width, HDIM, full), shape(width, HDIM)),
-            4 * width * HDIM,
-            16 * width * HDIM,
-        )(*prefix, got, state)
-        prefix = (held,)
-        got = lax.ppermute(sent, "ctx", [(i, i ^ bit) for i in range(n_ctx)])
-        if late is None:
-            win, held = lax.optimization_barrier((win, held))
-            win, tail = kernel_call(
-                functools.partial(window_late_body, n_mem, early),
-                "window_late",
-                (shape(total, 3 * HDIM), shape(count, 2 * HDIM)),
-                2 * count * depth * 3 * HDIM,
-                3 << 20,
-            )(above, below, win_weight_full, win)
-            ends = [(c * n_mem, (c + 1) * n_mem) for c in range(n_ctx - 1)]
-            late = lax.ppermute(tail, ("ctx", "mem"), ends)
-    prefix = held
+    gots = [
+        lax.ppermute(sent, "ctx", [(i, i + 2 * s) for i in range(n_ctx - 2 * s)])
+        for s in range(1, chips)
+    ]
+    win, gots[0] = lax.optimization_barrier((win, gots[0]))
+    win, tail = kernel_call(
+        functools.partial(window_late_body, n_mem, early),
+        "window_late",
+        (shape(total, 3 * HDIM), shape(count, 2 * HDIM)),
+        2 * count * depth * 3 * HDIM,
+        3 << 20,
+    )(above, below, win_weight_full, win)
+    ends = [(c * n_mem, (c + 1) * n_mem) for c in range(n_ctx - 1)]
+    late = lax.ppermute(tail, ("ctx", "mem"), ends)
+    gots, local = lax.optimization_barrier((gots, local))
+    prefix, sent = kernel_call(
+        fold_body,
+        "fold",
+        (shape(width, HDIM, full), shape(width, HDIM)),
+        4 * width * HDIM,
+        16 * width * HDIM,
+    )(*gots, state)
+    got = lax.ppermute(sent, "ctx", [(i, i ^ 1) for i in range(n_ctx)])
     window_part = kernel_call(
         functools.partial(window_attend_body, count),
         "window_attend",
@@ -744,7 +739,7 @@
         and win_weight.shape[0] % (16 * n_ctx) == 0
         and tokens.shape[0] <= 3 * HDIM
         and n_ctx >= 4
-        and n_ctx & (n_ctx - 1) == 0
+        and n_ctx % 2 == 0
         and (n_mem - 1) * tokens.shape[0] >= WINDOW
     )
     body = dense_shards if dense else sparse_shards

time: 95.1 us -> 96.8 us (1.018)
  the two profiles are of different devices: /device:TPU:9 before, /device:TPU:21 now
where the time goes in v12:
time: 96.8 us; the launch traced here: 96.3 us
  waiting for transfers between devices  38.6 us (40%)
  starting transfers between devices  32.1 us (33%)
  Pallas kernels  19.8 us (20%)
  local copies, waits for them, and re-layouts  5.43 us (6%)
    ppermute x3, waiting for transfers between devices, dense_shards(): lax.ppermute(part, 'mem', [(i, (i + shift) % n_mem) for i in range(n_mem)])  22.1 us
    pallas_call x1, Pallas kernels, dense_shards(): kernel_call(functools.partial(arrivals_body, n_mem, 3, early, True), 'mid...  8.16 us
    ppermute x3, waiting for transfers between devices, dense_shards(): lax.ppermute(packed[s], 'mem', [(i, (i + s) % n_mem) for i in range(n_mem)])  6.39 us
    ppermute x3, waiting for transfers between devices, dense_shards(): lax.ppermute(sent, 'ctx', [(i, i + 2 * s) for i in range(n_ctx - 2 * s)])  6.34 us
    unnamed x10, local copies, waits for them, and re-layouts  5.43 us
    ppermute x3, starting transfers between devices, dense_shards(): lax.ppermute(sent, 'ctx', [(i, i + 2 * s) for i in range(n_ctx - 2 * s)])  5.08 us
    ppermute x2, starting transfers between devices, moved(): return (lax.ppermute(from_below, 'mem', up), from_above)  4.15 us
    ppermute x1, starting transfers between devices, dense_shards(): lax.ppermute(of_core, 'ctx', [(i, i ^ 1) for i in range(n_ctx)])  3.99 us
  transfers between devices with their start and end apart: 22, of which 9 were waited for; matrix products, arithmetic and copies ran while one was open for 0% of the time, Pallas kernels for 19%

profile of v12, /device:TPU:21, one launch (start us, length us, event | category | flops | bytes accessed | tf_op | source)
XLA Modules:
  0.0 96.3 jit_solution(1189117231960180104)
XLA Ops:
  0.0 3.2 %collective-permute-start = (bf16[256,1024]{1,0:T(8,128)(2,1)}, bf16[256,1024]{1,0:T(8,128)(2,1)S(1)}, u32[]{:S(2)}, u32[]{:S(2)}) collective-permute-start(bf16[256,1024]{1,0:T(8,128)(2,1)} %refs_0_.1), channel_id=1, source_target_pairs={{0,1},{1,2},{2,3},{4,5},{5,6},{6,7},{8,9},{9,10},{10,11},{12,13},{... | collective-permute-start | bytes 1572872 | tf_op jit(solution)/shard_map/ppermute | solution.py:573
  3.2 2.1 %collective-permute-start.1 = (bf16[256,1024]{1,0:T(8,128)(2,1)}, bf16[256,1024]{1,0:T(8,128)(2,1)S(1)}, u32[]{:S(2)}, u32[]{:S(2)}) collective-permute-start(bf16[256,1024]{1,0:T(8,128)(2,1)} %refs_0_.1), channel_id=1, source_target_pairs={{3,2},{2,1},{1,0},{7,6},{6,5},{5,4},{11,10},{10,9},{9,8},{15,14},{... | collective-permute-start | bytes 1572872 | tf_op jit(solution)/shard_map/ppermute | solution.py:574
  7.3 1.4 %collective-permute-start.2 = (bf16[48,384]{1,0:T(8,128)(2,1)S(1)}, bf16[48,384]{1,0:T(8,128)(2,1)S(1)}, u32[]{:S(2)}, u32[]{:S(2)}) collective-permute-start(bf16[48,384]{1,0:T(8,128)(2,1)S(1)} %get-tuple-element.67), channel_id=1, source_target_pairs={{0,1},{1,2},{2,3},{3,0},{4,5},{5,6},{6,7},{7,4},{8,9},{9,10},{10,1... | collective-permute-start | bytes 110600 | tf_op jit(solution)/shard_map/ppermute | solution.py:588
  9.9 1.9 %copy-done = bf16[1,1024,1536]{2,1,0:T(8,128)(2,1)S(1)} copy-done((bf16[1,1024,1536]{2,1,0:T(8,128)(2,1)S(1)}, bf16[1,1024,1536]{2,1,0:T(8,128)(2,1)}, u32[]{:S(2)}) %copy-start) | copy-done | bytes 3145752
  13.8 2.0 %collective-permute-done.2.refs_1_ = bf16[48,384]{1,0:T(8,128)(2,1)S(1)} collective-permute-done((bf16[48,384]{1,0:T(8,128)(2,1)S(1)}, bf16[48,384]{1,0:T(8,128)(2,1)S(1)}, u32[]{:S(2)}, u32[]{:S(2)}) %collective-permute-start.2) | collective-permute-done | bytes 36896 | tf_op jit(solution)/shard_map/ppermute | solution.py:588
  16.5 3.6 %collective-permute-done.4.refs_3_ = bf16[48,384]{1,0:T(8,128)(2,1)S(1)} collective-permute-done((bf16[48,384]{1,0:T(8,128)(2,1)S(1)}, bf16[48,384]{1,0:T(8,128)(2,1)S(1)}, u32[]{:S(2)}, u32[]{:S(2)}) %collective-permute-start.4) | collective-permute-done | bytes 36896 | tf_op jit(solution)/shard_map/ppermute | solution.py:588
  20.2 2.0 %collective-permute-start.5 = (bf16[256,1024]{1,0:T(8,128)(2,1)S(1)}, bf16[256,1024]{1,0:T(8,128)(2,1)S(1)}, u32[]{:S(2)}, u32[]{:S(2)}) collective-permute-start(bf16[256,1024]{1,0:T(8,128)(2,1)S(1)} %collective-permute-done.1.refs_2_), channel_id=1, source_target_pairs={{2,1},{1,0},{6,5},{5,4},{10,9},{9,8},{14,13},{13,12},{18,17},{17,1... | collective-permute-start | bytes 1572872 | tf_op jit(solution)/shard_map/ppermute | solution.py:575
  22.3 1.9 %collective-permute-start.6 = (bf16[256,1024]{1,0:T(8,128)(2,1)S(1)}, bf16[256,1024]{1,0:T(8,128)(2,1)S(1)}, u32[]{:S(2)}, u32[]{:S(2)}) collective-permute-start(bf16[256,1024]{1,0:T(8,128)(2,1)S(1)} %collective-permute-done.refs_1_), channel_id=1, source_target_pairs={{1,2},{2,3},{5,6},{6,7},{9,10},{10,11},{13,14},{14,15},{17,18},{18... | collective-permute-start | bytes 1572872 | tf_op jit(solution)/shard_map/ppermute | solution.py:576
  24.2 1.3 %collective-permute-start.7 = (bf16[4,32,384]{2,1,0:T(8,128)(2,1)S(1)}, bf16[4,32,384]{2,1,0:T(8,128)(2,1)S(1)}, u32[]{:S(2)}, u32[]{:S(2)}) collective-permute-start(bf16[4,32,384]{2,1,0:T(8,128)(2,1)S(1)} %get-tuple-element.81.refs_0_), channel_id=1, source_target_pairs={{0,8},{4,12},{8,16},{12,20},{16,24},{20,28},{24,0},{28,4},{1,9},{5... | collective-permute-start | bytes 294920 | tf_op jit(solution)/shard_map/ppermute | solution.py:628
  26.8 3.9 %near_rows.1 = (bf16[1024,1536]{1,0:T(8,128)(2,1)S(1)}, f32[1024,128]{1,0:T(8,128)S(1)}, f32[512,128]{1,0:T(8,128)S(1)}) custom-call(bf16[256,1024]{1,0:T(8,128)(2,1)S(1)} %get-tuple-element.77.refs_0_, bf16[256,1024]{1,0:T(8,128)(2,1)S(1)} %collective-permute-done.refs_1_, bf16[256,1024]{1,0:T(8,128)(2,1)S(1)} %collective-permute-done.1.refs_2_, ...), custom_call_target="tpu_custom_call" | custom-call | flops 2415919104 | bytes 6291456 | tf_op jit(solution)/shard_map/near_rows/pallas_call | solution.py:619
  30.8 3.8 %collective-permute-done.6.refs_1_.refs_4_ = bf16[256,1024]{1,0:T(8,128)(2,1)S(1)} collective-permute-done((bf16[256,1024]{1,0:T(8,128)(2,1)S(1)}, bf16[256,1024]{1,0:T(8,128)(2,1)S(1)}, u32[]{:S(2)}, u32[]{:S(2)}) %collective-permute-start.6) | collective-permute-done | bytes 524320 | tf_op jit(solution)/shard_map/ppermute | solution.py:576
  35.3 2.2 %collective-permute-start.12 = (bf16[256,1024]{1,0:T(8,128)(2,1)S(1)}, bf16[256,1024]{1,0:T(8,128)(2,1)S(1)}, u32[]{:S(2)}, u32[]{:S(2)}) collective-permute-start(bf16[256,1024]{1,0:T(8,128)(2,1)S(1)} %collective-permute-done.6.refs_1_.refs_4_), channel_id=1, source_target_pairs={{2,3},{6,7},{10,11},{14,15},{18,19},{22,23},{26,27},{30,31}} | collective-permute-start | bytes 1572872 | tf_op jit(solution)/shard_map/ppermute | solution.py:576
  37.5 4.0 %collective-permute-start.10 = (bf16[4,4,32,384]{3,2,1,0:T(8,128)(2,1)S(1)}, bf16[4,4,32,384]{3,2,1,0:T(8,128)(2,1)S(1)}, u32[]{:S(2)}, u32[]{:S(2)}) collective-permute-start(bf16[4,4,32,384]{3,2,1,0:T(8,128)(2,1)S(1)} %combine.1.refs_5_), channel_id=1, source_target_pairs={{0,4},{4,0},{8,12},{12,8},{16,20},{20,16},{24,28},{28,24},{1,5},{5... | collective-permute-start | bytes 1179656 | tf_op jit(solution)/shard_map/ppermute | solution.py:640
  41.5 8.2 %middle_rows.1 = (bf16[1024,1536]{1,0:T(8,128)(2,1)S(1)}, f32[1024,128]{1,0:T(8,128)S(1)}, f32[512,128]{1,0:T(8,128)S(1)}, f32[1024,512]{1,0:T(8,128)S(1)}) custom-call(bf16[256,1024]{1,0:T(8,128)(2,1)S(1)} %collective-permute-done.5.refs_0_.refs_3_, bf16[256,1024]{1,0:T(8,128)(2,1)S(1)} %collective-permute-done.6.refs_1_.refs_4_, ...), custom_call_target="tpu_custom_call" | custom-call | flops 2415919104 | bytes 6291456 | tf_op jit(solution)/shard_map/middle_rows/pallas_call | solution.py:646
  49.7 1.9 %window_early.1 = (bf16[1024,384]{1,0:T(8,128)(2,1)S(1)}, bf16[1024,384]{1,0:T(8,128)(2,1)S(1)}, bf16[512,256]{1,0:T(8,128)(2,1)S(1)}) custom-call(bf16[256,1024]{1,0:T(8,128)(2,1)S(1)} %get-tuple-element.77.refs_0_, bf16[256,1024]{1,0:T(8,128)(2,1)S(1)} %collective-permute-done.refs_1_, bf16[256,1024]{1,0:T(8,128)(2,1)S(1)} %collective-permute-done.1.refs_2_, ...), custom_call_target="tpu_custom_call" | custom-call | flops 805306368 | bytes 5242880 | tf_op jit(solution)/shard_map/window_early/pallas_call | solution.py:653
  51.6 3.1 %collective-permute-start.13 = (bf16[512,128]{1,0:T(8,128)(2,1)S(1)}, bf16[512,128]{1,0:T(8,128)(2,1)S(1)}, u32[]{:S(2)}, u32[]{:S(2)}) collective-permute-start(bf16[512,128]{1,0:T(8,128)(2,1)S(1)} %get-tuple-element.101), channel_id=1, source_target_pairs={{0,8},{4,12},{8,16},{12,20},{16,24},{20,28},{1,9},{5,13},{9,17},{1... | collective-permute-start | bytes 393224 | tf_op jit(solution)/shard_map/ppermute | solution.py:678
  54.7 1.9 %collective-permute-start.16 = (bf16[512,256]{1,0:T(8,128)(2,1)S(1)}, bf16[512,256]{1,0:T(8,128)(2,1)S(1)}, u32[]{:S(2)}, u32[]{:S(2)}) collective-permute-start(bf16[512,256]{1,0:T(8,128)(2,1)S(1)} %get-tuple-element.113), channel_id=1, source_target_pairs={{0,4},{4,8},{8,12},{12,16},{16,20},{20,24},{24,28},{1,5},{5,9},{9,... | collective-permute-start | bytes 786440 | tf_op jit(solution)/shard_map/ppermute | solution.py:21
  56.6 1.3 %collective-permute-start.14 = (bf16[512,128]{1,0:T(8,128)(2,1)S(1)}, bf16[512,128]{1,0:T(8,128)(2,1)S(1)}, u32[]{:S(2)}, u32[]{:S(2)}) collective-permute-start(bf16[512,128]{1,0:T(8,128)(2,1)S(1)} %get-tuple-element.101), channel_id=1, source_target_pairs={{0,16},{4,20},{8,24},{12,28},{1,17},{5,21},{9,25},{13,29},{2,18},{... | collective-permute-start | bytes 393224 | tf_op jit(solution)/shard_map/ppermute | solution.py:678
  60.5 5.5 %collective-permute-done.14.refs_1_ = bf16[512,128]{1,0:T(8,128)(2,1)S(1)} collective-permute-done((bf16[512,128]{1,0:T(8,128)(2,1)S(1)}, bf16[512,128]{1,0:T(8,128)(2,1)S(1)}, u32[]{:S(2)}, u32[]{:S(2)}) %collective-permute-start.14) | collective-permute-done | bytes 131104 | tf_op jit(solution)/shard_map/ppermute | solution.py:678
  66.6 2.3 %window_attend.1.refs_6_ = f32[1024,128]{1,0:T(8,128)S(1)} custom-call(bf16[1024,384]{1,0:T(8,128)(2,1)S(1)} %get-tuple-element.112.win_ref, bf16[512,256]{1,0:T(8,128)(2,1)S(1)} %collective-permute-done.16.halo_ref, bf16[256,256]{1,0:T(8,128)(2,1)S(1)} %collective-permute-done.17.late_ref), custom_call_target="tpu_custom_call" | custom-call | flops 402653184 | bytes 3145728 | tf_op jit(solution)/shard_map/window_attend/pallas_call | solution.py:700
  70.0 2.4 %collective-permute-start.20 = (bf16[256,512]{1,0:T(8,128)(2,1)S(1)}, bf16[256,512]{1,0:T(8,128)(2,1)S(1)}, u32[]{:S(2)}, u32[]{:S(2)}) collective-permute-start(bf16[256,512]{1,0:T(8,128)(2,1)S(1)} %finish3.1), channel_id=1, source_target_pairs={{0,3},{1,0},{2,1},{3,2},{4,7},{5,4},{6,5},{7,6},{8,11},{9,8},{10,9... | collective-permute-start | bytes 786440 | tf_op jit(solution)/shard_map/ppermute | solution.py:727
  73.4 7.6 %collective-permute-done.21.refs_3_ = bf16[256,512]{1,0:T(8,128)(2,1)S(1)} collective-permute-done((bf16[256,512]{1,0:T(8,128)(2,1)S(1)}, bf16[256,512]{1,0:T(8,128)(2,1)S(1)}, u32[]{:S(2)}, u32[]{:S(2)}) %collective-permute-start.21) | collective-permute-done | bytes 262176 | tf_op jit(solution)/shard_map/ppermute | solution.py:727
  81.0 11.2 %collective-permute-done.20.refs_2_ = bf16[256,512]{1,0:T(8,128)(2,1)S(1)} collective-permute-done((bf16[256,512]{1,0:T(8,128)(2,1)S(1)}, bf16[256,512]{1,0:T(8,128)(2,1)S(1)}, u32[]{:S(2)}, u32[]{:S(2)}) %collective-permute-start.20) | collective-permute-done | bytes 262176 | tf_op jit(solution)/shard_map/ppermute | solution.py:727
  92.2 3.3 %collective-permute-done.19.refs_1_ = bf16[256,512]{1,0:T(8,128)(2,1)S(1)} collective-permute-done((bf16[256,512]{1,0:T(8,128)(2,1)S(1)}, bf16[256,512]{1,0:T(8,128)(2,1)S(1)}, u32[]{:S(2)}, u32[]{:S(2)}) %collective-permute-start.19) | collective-permute-done | bytes 262176 | tf_op jit(solution)/shard_map/ppermute | solution.py:727
  (47 shorter events, 14.2 us)
Async XLA Ops:
  0.0 20.2 %collective-permute-start = (bf16[256,1024]{1,0:T(8,128)(2,1)}, bf16[256,1024]{1,0:T(8,128)(2,1)S(1)}, u32[]{:S(2)}, u32[]{:S(2)}) collective-permute-start(bf16[256,1024]{1,0:T(8,128)(2,1)} %refs_0_.1), channel_id=1, source_target_pairs={{0,1},{1,2},{2,3},{4,5},{5,6},{6,7},{8,9},{9,10},{10,11},{12,13},{... | collective-permute-start | bytes 1572872 | tf_op jit(solution)/shard_map/ppermute | solution.py:573
  3.2 17.0 %collective-permute-start.1 = (bf16[256,1024]{1,0:T(8,128)(2,1)}, bf16[256,1024]{1,0:T(8,128)(2,1)S(1)}, u32[]{:S(2)}, u32[]{:S(2)}) collective-permute-start(bf16[256,1024]{1,0:T(8,128)(2,1)} %refs_0_.1), channel_id=1, source_target_pairs={{3,2},{2,1},{1,0},{7,6},{6,5},{5,4},{11,10},{10,9},{9,8},{15,14},{... | collective-permute-start | bytes 1572872 | tf_op jit(solution)/shard_map/ppermute | solution.py:574
  5.3 1.1 %copy-start.1 = (bf16[256,1536]{1,0:T(8,128)(2,1)S(1)}, bf16[256,1536]{1,0:T(8,128)(2,1)}, u32[]{:S(2)}) copy-start(bf16[256,1536]{1,0:T(8,128)(2,1)} %weight_ref.1) | copy-start | bytes 2359300
  7.3 8.5 %collective-permute-start.2 = (bf16[48,384]{1,0:T(8,128)(2,1)S(1)}, bf16[48,384]{1,0:T(8,128)(2,1)S(1)}, u32[]{:S(2)}, u32[]{:S(2)}) collective-permute-start(bf16[48,384]{1,0:T(8,128)(2,1)S(1)} %get-tuple-element.67), channel_id=1, source_target_pairs={{0,1},{1,2},{2,3},{3,0},{4,5},{5,6},{6,7},{7,4},{8,9},{9,10},{10,1... | collective-permute-start | bytes 110600 | tf_op jit(solution)/shard_map/ppermute | solution.py:588
  8.6 7.9 %collective-permute-start.3 = (bf16[48,384]{1,0:T(8,128)(2,1)S(1)}, bf16[48,384]{1,0:T(8,128)(2,1)S(1)}, u32[]{:S(2)}, u32[]{:S(2)}) collective-permute-start(bf16[48,384]{1,0:T(8,128)(2,1)S(1)} %get-tuple-element.68), channel_id=1, source_target_pairs={{0,2},{1,3},{2,0},{3,1},{4,6},{5,7},{6,4},{7,5},{8,10},{9,11},{10,... | collective-permute-start | bytes 110600 | tf_op jit(solution)/shard_map/ppermute | solution.py:588
  8.7 11.5 %collective-permute-start.4 = (bf16[48,384]{1,0:T(8,128)(2,1)S(1)}, bf16[48,384]{1,0:T(8,128)(2,1)S(1)}, u32[]{:S(2)}, u32[]{:S(2)}) collective-permute-start(bf16[48,384]{1,0:T(8,128)(2,1)S(1)} %get-tuple-element.69), channel_id=1, source_target_pairs={{0,3},{1,0},{2,1},{3,2},{4,7},{5,4},{6,5},{7,6},{8,11},{9,8},{10,9... | collective-permute-start | bytes 110600 | tf_op jit(solution)/shard_map/ppermute | solution.py:588
  9.9 1.9 %copy-start = (bf16[1,1024,1536]{2,1,0:T(8,128)(2,1)S(1)}, bf16[1,1024,1536]{2,1,0:T(8,128)(2,1)}, u32[]{:S(2)}) copy-start(bf16[1,1024,1536]{2,1,0:T(8,128)(2,1)} %param.8) | copy-start | bytes 9437188
  20.2 10.6 %collective-permute-start.5 = (bf16[256,1024]{1,0:T(8,128)(2,1)S(1)}, bf16[256,1024]{1,0:T(8,128)(2,1)S(1)}, u32[]{:S(2)}, u32[]{:S(2)}) collective-permute-start(bf16[256,1024]{1,0:T(8,128)(2,1)S(1)} %collective-permute-done.1.refs_2_), channel_id=1, source_target_pairs={{2,1},{1,0},{6,5},{5,4},{10,9},{9,8},{14,13},{13,12},{18,17},{17,1... | collective-permute-start | bytes 1572872 | tf_op jit(solution)/shard_map/ppermute | solution.py:575
  22.3 12.3 %collective-permute-start.6 = (bf16[256,1024]{1,0:T(8,128)(2,1)S(1)}, bf16[256,1024]{1,0:T(8,128)(2,1)S(1)}, u32[]{:S(2)}, u32[]{:S(2)}) collective-permute-start(bf16[256,1024]{1,0:T(8,128)(2,1)S(1)} %collective-permute-done.refs_1_), channel_id=1, source_target_pairs={{1,2},{2,3},{5,6},{6,7},{9,10},{10,11},{13,14},{14,15},{17,18},{18... | collective-permute-start | bytes 1572872 | tf_op jit(solution)/shard_map/ppermute | solution.py:576
  24.2 6.5 %collective-permute-start.7 = (bf16[4,32,384]{2,1,0:T(8,128)(2,1)S(1)}, bf16[4,32,384]{2,1,0:T(8,128)(2,1)S(1)}, u32[]{:S(2)}, u32[]{:S(2)}) collective-permute-start(bf16[4,32,384]{2,1,0:T(8,128)(2,1)S(1)} %get-tuple-element.81.refs_0_), channel_id=1, source_target_pairs={{0,8},{4,12},{8,16},{12,20},{16,24},{20,28},{24,0},{28,4},{1,9},{5... | collective-permute-start | bytes 294920 | tf_op jit(solution)/shard_map/ppermute | solution.py:628
  25.4 5.3 %collective-permute-start.8 = (bf16[4,32,384]{2,1,0:T(8,128)(2,1)S(1)}, bf16[4,32,384]{2,1,0:T(8,128)(2,1)S(1)}, u32[]{:S(2)}, u32[]{:S(2)}) collective-permute-start(bf16[4,32,384]{2,1,0:T(8,128)(2,1)S(1)} %get-tuple-element.81.refs_0_), channel_id=1, source_target_pairs={{0,16},{4,20},{8,24},{12,28},{16,0},{20,4},{24,8},{28,12},{1,17},{... | collective-permute-start | bytes 294920 | tf_op jit(solution)/shard_map/ppermute | solution.py:628
  25.7 5.0 %collective-permute-start.9 = (bf16[4,32,384]{2,1,0:T(8,128)(2,1)S(1)}, bf16[4,32,384]{2,1,0:T(8,128)(2,1)S(1)}, u32[]{:S(2)}, u32[]{:S(2)}) collective-permute-start(bf16[4,32,384]{2,1,0:T(8,128)(2,1)S(1)} %get-tuple-element.81.refs_0_), channel_id=1, source_target_pairs={{0,24},{4,28},{8,0},{12,4},{16,8},{20,12},{24,16},{28,20},{1,25},{... | collective-permute-start | bytes 294920 | tf_op jit(solution)/shard_map/ppermute | solution.py:628
  34.6 17.0 %collective-permute-start.11 = (bf16[256,1024]{1,0:T(8,128)(2,1)S(1)}, bf16[256,1024]{1,0:T(8,128)(2,1)S(1)}, u32[]{:S(2)}, u32[]{:S(2)}) collective-permute-start(bf16[256,1024]{1,0:T(8,128)(2,1)S(1)} %collective-permute-done.5.refs_0_.refs_3_), channel_id=1, source_target_pairs={{1,0},{5,4},{9,8},{13,12},{17,16},{21,20},{25,24},{29,28}} | collective-permute-start | bytes 1572872 | tf_op jit(solution)/shard_map/ppermute | solution.py:575
  35.3 16.3 %collective-permute-start.12 = (bf16[256,1024]{1,0:T(8,128)(2,1)S(1)}, bf16[256,1024]{1,0:T(8,128)(2,1)S(1)}, u32[]{:S(2)}, u32[]{:S(2)}) collective-permute-start(bf16[256,1024]{1,0:T(8,128)(2,1)S(1)} %collective-permute-done.6.refs_1_.refs_4_), channel_id=1, source_target_pairs={{2,3},{6,7},{10,11},{14,15},{18,19},{22,23},{26,27},{30,31}} | collective-permute-start | bytes 1572872 | tf_op jit(solution)/shard_map/ppermute | solution.py:576
  37.5 12.2 %collective-permute-start.10 = (bf16[4,4,32,384]{3,2,1,0:T(8,128)(2,1)S(1)}, bf16[4,4,32,384]{3,2,1,0:T(8,128)(2,1)S(1)}, u32[]{:S(2)}, u32[]{:S(2)}) collective-permute-start(bf16[4,4,32,384]{3,2,1,0:T(8,128)(2,1)S(1)} %combine.1.refs_5_), channel_id=1, source_target_pairs={{0,4},{4,0},{8,12},{12,8},{16,20},{20,16},{24,28},{28,24},{1,5},{5... | collective-permute-start | bytes 1179656 | tf_op jit(solution)/shard_map/ppermute | solution.py:640
  51.6 7.9 %collective-permute-start.13 = (bf16[512,128]{1,0:T(8,128)(2,1)S(1)}, bf16[512,128]{1,0:T(8,128)(2,1)S(1)}, u32[]{:S(2)}, u32[]{:S(2)}) collective-permute-start(bf16[512,128]{1,0:T(8,128)(2,1)S(1)} %get-tuple-element.101), channel_id=1, source_target_pairs={{0,8},{4,12},{8,16},{12,20},{16,24},{20,28},{1,9},{5,13},{9,17},{1... | collective-permute-start | bytes 393224 | tf_op jit(solution)/shard_map/ppermute | solution.py:678
  54.7 11.9 %collective-permute-start.16 = (bf16[512,256]{1,0:T(8,128)(2,1)S(1)}, bf16[512,256]{1,0:T(8,128)(2,1)S(1)}, u32[]{:S(2)}, u32[]{:S(2)}) collective-permute-start(bf16[512,256]{1,0:T(8,128)(2,1)S(1)} %get-tuple-element.113), channel_id=1, source_target_pairs={{0,4},{4,8},{8,12},{12,16},{16,20},{20,24},{24,28},{1,5},{5,9},{9,... | collective-permute-start | bytes 786440 | tf_op jit(solution)/shard_map/ppermute | solution.py:21
  56.6 9.3 %collective-permute-start.14 = (bf16[512,128]{1,0:T(8,128)(2,1)S(1)}, bf16[512,128]{1,0:T(8,128)(2,1)S(1)}, u32[]{:S(2)}, u32[]{:S(2)}) collective-permute-start(bf16[512,128]{1,0:T(8,128)(2,1)S(1)} %get-tuple-element.101), channel_id=1, source_target_pairs={{0,16},{4,20},{8,24},{12,28},{1,17},{5,21},{9,25},{13,29},{2,18},{... | collective-permute-start | bytes 393224 | tf_op jit(solution)/shard_map/ppermute | solution.py:678
  57.9 8.0 %collective-permute-start.15 = (bf16[512,128]{1,0:T(8,128)(2,1)S(1)}, bf16[512,128]{1,0:T(8,128)(2,1)S(1)}, u32[]{:S(2)}, u32[]{:S(2)}) collective-permute-start(bf16[512,128]{1,0:T(8,128)(2,1)S(1)} %get-tuple-element.101), channel_id=1, source_target_pairs={{0,24},{4,28},{1,25},{5,29},{2,26},{6,30},{3,27},{7,31}} | collective-permute-start | bytes 393224 | tf_op jit(solution)/shard_map/ppermute | solution.py:678
  59.8 6.8 %collective-permute-start.17 = (bf16[256,256]{1,0:T(8,128)(2,1)S(1)}, bf16[256,256]{1,0:T(8,128)(2,1)S(1)}, u32[]{:S(2)}, u32[]{:S(2)}) collective-permute-start(bf16[256,256]{1,0:T(8,128)(2,1)S(1)} %get-tuple-element.114), channel_id=1, source_target_pairs={{0,4},{4,8},{8,12},{12,16},{16,20},{20,24},{24,28}} | collective-permute-start | bytes 393224 | tf_op jit(solution)/shard_map/ppermute | solution.py:690
  66.0 2.9 %collective-permute-start.18 = (bf16[512,128]{1,0:T(8,128)(2,1)S(1)}, bf16[512,128]{1,0:T(8,128)(2,1)S(1)}, u32[]{:S(2)}, u32[]{:S(2)}) collective-permute-start(bf16[512,128]{1,0:T(8,128)(2,1)S(1)} %get-tuple-element.120), channel_id=1, source_target_pairs={{0,4},{4,0},{8,12},{12,8},{16,20},{20,16},{24,28},{28,24},{1,5},{5... | collective-permute-start | bytes 393224 | tf_op jit(solution)/shard_map/ppermute | solution.py:699
  69.4 11.6 %collective-permute-start.21 = (bf16[256,512]{1,0:T(8,128)(2,1)S(1)}, bf16[256,512]{1,0:T(8,128)(2,1)S(1)}, u32[]{:S(2)}, u32[]{:S(2)}) collective-permute-start(bf16[256,512]{1,0:T(8,128)(2,1)S(1)} %finish2.1), channel_id=1, source_target_pairs={{0,2},{1,3},{2,0},{3,1},{4,6},{5,7},{6,4},{7,5},{8,10},{9,11},{10,... | collective-permute-start | bytes 786440 | tf_op jit(solution)/shard_map/ppermute | solution.py:727
  70.0 22.2 %collective-permute-start.20 = (bf16[256,512]{1,0:T(8,128)(2,1)S(1)}, bf16[256,512]{1,0:T(8,128)(2,1)S(1)}, u32[]{:S(2)}, u32[]{:S(2)}) collective-permute-start(bf16[256,512]{1,0:T(8,128)(2,1)S(1)} %finish3.1), channel_id=1, source_target_pairs={{0,3},{1,0},{2,1},{3,2},{4,7},{5,4},{6,5},{7,6},{8,11},{9,8},{10,9... | collective-permute-start | bytes 786440 | tf_op jit(solution)/shard_map/ppermute | solution.py:727
  72.8 22.6 %collective-permute-start.19 = (bf16[256,512]{1,0:T(8,128)(2,1)S(1)}, bf16[256,512]{1,0:T(8,128)(2,1)S(1)}, u32[]{:S(2)}, u32[]{:S(2)}) collective-permute-start(bf16[256,512]{1,0:T(8,128)(2,1)S(1)} %finish1.1), channel_id=1, source_target_pairs={{0,1},{1,2},{2,3},{3,0},{4,5},{5,6},{6,7},{7,4},{8,9},{9,10},{10,1... | collective-permute-start | bytes 786440 | tf_op jit(solution)/shard_map/ppermute | solution.py:727
  (3 other events, 2.4 us)

commit v13 on v11

--- a/solution.py
+++ b/solution.py
@@ -636,8 +636,8 @@
         1 << 20,
         1 << 20,
     )(own_rows, *of_chips)
+    other_core = lax.ppermute(of_core, "ctx", [(i, i ^ 1) for i in range(n_ctx)])
     above, below, held, of_core = lax.optimization_barrier((above, below, held, of_core))
-    other_core = lax.ppermute(of_core, "ctx", [(i, i ^ 1) for i in range(n_ctx)])
     for hop in range(3, n_mem):
         below, above = moved(hop, below, above)
         slots += [above, below]
@@ -676,6 +676,7 @@
     local = (last_query, last_coef, extra)
     bit = n_ctx // 2
     got = lax.ppermute(sent, "ctx", [(i, i + bit) for i in range(n_ctx) if not i & bit])
+    got, halo = lax.optimization_barrier((got, halo))
     prefix, late = (), None
     while bit > 1:
         bit //= 2

time: 95.1 us -> 95.7 us (level)
  waiting for transfers between devices: 30.8 us -> 32.4 us
    ppermute x1, waiting for transfers between devices: 0.01 us -> 2.66 us  [dense_shards(): lax.ppermute(sent, 'ctx', [(i, i + bit) for i in range(n_ctx) if not i &...]
where the time goes in v13:
time: 95.7 us; the launch traced here: 94.7 us
  starting transfers between devices  36.7 us (38%)
  waiting for transfers between devices  32.4 us (34%)
  Pallas kernels  19.8 us (21%)
  local copies, waits for them, and re-layouts  5.43 us (6%)
    ppermute x3, waiting for transfers between devices, dense_shards(): lax.ppermute(part, 'mem', [(i, (i + shift) % n_mem) for i in range(n_mem)])  20.4 us
    pallas_call x1, Pallas kernels, dense_shards(): kernel_call(functools.partial(arrivals_body, n_mem, 3, early, True), 'mid...  8.17 us
    unnamed x10, local copies, waits for them, and re-layouts  5.43 us
    ppermute x3, waiting for transfers between devices, dense_shards(): lax.ppermute(packed[s], 'mem', [(i, (i + s) % n_mem) for i in range(n_mem)])  5.1 us
    ppermute x3, starting transfers between devices, dense_shards(): lax.ppermute(part, 'mem', [(i, (i + shift) % n_mem) for i in range(n_mem)])  4.38 us
    ppermute x2, waiting for transfers between devices, dense_shards(): got = lax.ppermute(sent, 'ctx', [(i, i ^ bit) for i in range(n_ctx)])  4.23 us
    ppermute x1, starting transfers between devices, dense_shards(): lax.ppermute(of_core, 'ctx', [(i, i ^ 1) for i in range(n_ctx)])  4.19 us
    pallas_call x1, Pallas kernels, dense_shards(): kernel_call(functools.partial(arrivals_body, n_mem, 0, 3, False), 'near_r...  3.86 us
  transfers between devices with their start and end apart: 21, of which 6 were waited for; matrix products, arithmetic and copies ran while one was open for 0% of the time, Pallas kernels for 20%

profile of v13, /device:TPU:9, one launch (start us, length us, event | category | flops | bytes accessed | tf_op | source)
XLA Modules:
  0.0 94.7 jit_solution(4495455073680362136)
XLA Ops:
  0.0 3.2 %collective-permute-start = (bf16[256,1024]{1,0:T(8,128)(2,1)}, bf16[256,1024]{1,0:T(8,128)(2,1)S(1)}, u32[]{:S(2)}, u32[]{:S(2)}) collective-permute-start(bf16[256,1024]{1,0:T(8,128)(2,1)} %refs_0_.1), channel_id=1, source_target_pairs={{0,1},{1,2},{2,3},{4,5},{5,6},{6,7},{8,9},{9,10},{10,11},{12,13},{... | collective-permute-start | bytes 1572872 | tf_op jit(solution)/shard_map/ppermute | solution.py:573
  3.2 2.1 %collective-permute-start.1 = (bf16[256,1024]{1,0:T(8,128)(2,1)}, bf16[256,1024]{1,0:T(8,128)(2,1)S(1)}, u32[]{:S(2)}, u32[]{:S(2)}) collective-permute-start(bf16[256,1024]{1,0:T(8,128)(2,1)} %refs_0_.1), channel_id=1, source_target_pairs={{3,2},{2,1},{1,0},{7,6},{6,5},{5,4},{11,10},{10,9},{9,8},{15,14},{... | collective-permute-start | bytes 1572872 | tf_op jit(solution)/shard_map/ppermute | solution.py:574
  7.3 1.3 %collective-permute-start.2 = (bf16[48,384]{1,0:T(8,128)(2,1)S(1)}, bf16[48,384]{1,0:T(8,128)(2,1)S(1)}, u32[]{:S(2)}, u32[]{:S(2)}) collective-permute-start(bf16[48,384]{1,0:T(8,128)(2,1)S(1)} %get-tuple-element.68), channel_id=1, source_target_pairs={{0,1},{1,2},{2,3},{3,0},{4,5},{5,6},{6,7},{7,4},{8,9},{9,10},{10,1... | collective-permute-start | bytes 110600 | tf_op jit(solution)/shard_map/ppermute | solution.py:588
  9.7 1.4 %collective-permute-start.4 = (bf16[48,384]{1,0:T(8,128)(2,1)S(1)}, bf16[48,384]{1,0:T(8,128)(2,1)S(1)}, u32[]{:S(2)}, u32[]{:S(2)}) collective-permute-start(bf16[48,384]{1,0:T(8,128)(2,1)S(1)} %get-tuple-element.70), channel_id=1, source_target_pairs={{0,3},{1,0},{2,1},{3,2},{4,7},{5,4},{6,5},{7,6},{8,11},{9,8},{10,9... | collective-permute-start | bytes 110600 | tf_op jit(solution)/shard_map/ppermute | solution.py:588
  11.1 1.9 %copy-done = bf16[1,1024,1536]{2,1,0:T(8,128)(2,1)S(1)} copy-done((bf16[1,1024,1536]{2,1,0:T(8,128)(2,1)S(1)}, bf16[1,1024,1536]{2,1,0:T(8,128)(2,1)}, u32[]{:S(2)}) %copy-start) | copy-done | bytes 3145752
  15.7 4.4 %collective-permute-done.3.refs_2_ = bf16[48,384]{1,0:T(8,128)(2,1)S(1)} collective-permute-done((bf16[48,384]{1,0:T(8,128)(2,1)S(1)}, bf16[48,384]{1,0:T(8,128)(2,1)S(1)}, u32[]{:S(2)}, u32[]{:S(2)}) %collective-permute-start.3) | collective-permute-done | bytes 36896 | tf_op jit(solution)/shard_map/ppermute | solution.py:588
  20.1 2.3 %collective-permute-start.5 = (bf16[256,1024]{1,0:T(8,128)(2,1)S(1)}, bf16[256,1024]{1,0:T(8,128)(2,1)S(1)}, u32[]{:S(2)}, u32[]{:S(2)}) collective-permute-start(bf16[256,1024]{1,0:T(8,128)(2,1)S(1)} %collective-permute-done.1.refs_2_), channel_id=1, source_target_pairs={{2,1},{1,0},{6,5},{5,4},{10,9},{9,8},{14,13},{13,12},{18,17},{17,1... | collective-permute-start | bytes 1572872 | tf_op jit(solution)/shard_map/ppermute | solution.py:575
  22.5 3.0 %collective-permute-start.6 = (bf16[256,1024]{1,0:T(8,128)(2,1)S(1)}, bf16[256,1024]{1,0:T(8,128)(2,1)S(1)}, u32[]{:S(2)}, u32[]{:S(2)}) collective-permute-start(bf16[256,1024]{1,0:T(8,128)(2,1)S(1)} %collective-permute-done.refs_1_), channel_id=1, source_target_pairs={{1,2},{2,3},{5,6},{6,7},{9,10},{10,11},{13,14},{14,15},{17,18},{18... | collective-permute-start | bytes 1572872 | tf_op jit(solution)/shard_map/ppermute | solution.py:576
  25.5 1.3 %collective-permute-start.7 = (bf16[4,32,384]{2,1,0:T(8,128)(2,1)S(1)}, bf16[4,32,384]{2,1,0:T(8,128)(2,1)S(1)}, u32[]{:S(2)}, u32[]{:S(2)}) collective-permute-start(bf16[4,32,384]{2,1,0:T(8,128)(2,1)S(1)} %get-tuple-element.82.refs_0_), channel_id=1, source_target_pairs={{0,8},{4,12},{8,16},{12,20},{16,24},{20,28},{24,0},{28,4},{1,9},{5... | collective-permute-start | bytes 294920 | tf_op jit(solution)/shard_map/ppermute | solution.py:628
  26.8 1.2 %collective-permute-start.8 = (bf16[4,32,384]{2,1,0:T(8,128)(2,1)S(1)}, bf16[4,32,384]{2,1,0:T(8,128)(2,1)S(1)}, u32[]{:S(2)}, u32[]{:S(2)}) collective-permute-start(bf16[4,32,384]{2,1,0:T(8,128)(2,1)S(1)} %get-tuple-element.82.refs_0_), channel_id=1, source_target_pairs={{0,16},{4,20},{8,24},{12,28},{16,0},{20,4},{24,8},{28,12},{1,17},{... | collective-permute-start | bytes 294920 | tf_op jit(solution)/shard_map/ppermute | solution.py:628
  28.0 1.2 %collective-permute-start.9 = (bf16[4,32,384]{2,1,0:T(8,128)(2,1)S(1)}, bf16[4,32,384]{2,1,0:T(8,128)(2,1)S(1)}, u32[]{:S(2)}, u32[]{:S(2)}) collective-permute-start(bf16[4,32,384]{2,1,0:T(8,128)(2,1)S(1)} %get-tuple-element.82.refs_0_), channel_id=1, source_target_pairs={{0,24},{4,28},{8,0},{12,4},{16,8},{20,12},{24,16},{28,20},{1,25},{... | collective-permute-start | bytes 294920 | tf_op jit(solution)/shard_map/ppermute | solution.py:628
  29.1 3.9 %near_rows.1 = (bf16[1024,1536]{1,0:T(8,128)(2,1)S(1)}, f32[1024,128]{1,0:T(8,128)S(1)}, f32[512,128]{1,0:T(8,128)S(1)}) custom-call(bf16[256,1024]{1,0:T(8,128)(2,1)S(1)} %get-tuple-element.78.refs_0_, bf16[256,1024]{1,0:T(8,128)(2,1)S(1)} %collective-permute-done.refs_1_, bf16[256,1024]{1,0:T(8,128)(2,1)S(1)} %collective-permute-done.1.refs_2_, ...), custom_call_target="tpu_custom_call" | custom-call | flops 2415919104 | bytes 6291456 | tf_op jit(solution)/shard_map/near_rows/pallas_call | solution.py:619
  33.1 4.2 %collective-permute-start.12 = (bf16[4,4,32,384]{3,2,1,0:T(8,128)(2,1)S(1)}, bf16[4,4,32,384]{3,2,1,0:T(8,128)(2,1)S(1)}, u32[]{:S(2)}, u32[]{:S(2)}) collective-permute-start(bf16[4,4,32,384]{3,2,1,0:T(8,128)(2,1)S(1)} %combine.1.refs_5_), channel_id=1, source_target_pairs={{0,4},{4,0},{8,12},{12,8},{16,20},{20,16},{24,28},{28,24},{1,5},{5... | collective-permute-start | bytes 1179656 | tf_op jit(solution)/shard_map/ppermute | solution.py:639
  37.3 1.3 %collective-permute-start.10 = (bf16[256,1024]{1,0:T(8,128)(2,1)S(1)}, bf16[256,1024]{1,0:T(8,128)(2,1)S(1)}, u32[]{:S(2)}, u32[]{:S(2)}) collective-permute-start(bf16[256,1024]{1,0:T(8,128)(2,1)S(1)} %collective-permute-done.5.refs_0_.refs_3_), channel_id=1, source_target_pairs={{1,0},{5,4},{9,8},{13,12},{17,16},{21,20},{25,24},{29,28}} | collective-permute-start | bytes 1572872 | tf_op jit(solution)/shard_map/ppermute | solution.py:575
  39.4 1.9 %window_early.1 = (bf16[1024,384]{1,0:T(8,128)(2,1)S(1)}, bf16[1024,384]{1,0:T(8,128)(2,1)S(1)}, bf16[512,256]{1,0:T(8,128)(2,1)S(1)}) custom-call(bf16[256,1024]{1,0:T(8,128)(2,1)S(1)} %get-tuple-element.78.refs_0_, bf16[256,1024]{1,0:T(8,128)(2,1)S(1)} %collective-permute-done.refs_1_, bf16[256,1024]{1,0:T(8,128)(2,1)S(1)} %collective-permute-done.1.refs_2_, ...), custom_call_target="tpu_custom_call" | custom-call | flops 805306368 | bytes 5242880 | tf_op jit(solution)/shard_map/window_early/pallas_call | solution.py:653
  41.2 3.4 %collective-permute-start.14 = (bf16[512,256]{1,0:T(8,128)(2,1)S(1)}, bf16[512,256]{1,0:T(8,128)(2,1)S(1)}, u32[]{:S(2)}, u32[]{:S(2)}) collective-permute-start(bf16[512,256]{1,0:T(8,128)(2,1)S(1)} %get-tuple-element.102), channel_id=1, source_target_pairs={{0,4},{4,8},{8,12},{12,16},{16,20},{20,24},{24,28},{1,5},{5,9},{9,... | collective-permute-start | bytes 786440 | tf_op jit(solution)/shard_map/ppermute | solution.py:21
  44.6 8.2 %middle_rows.1 = (bf16[1024,1536]{1,0:T(8,128)(2,1)S(1)}, f32[1024,128]{1,0:T(8,128)S(1)}, f32[512,128]{1,0:T(8,128)S(1)}, f32[1024,512]{1,0:T(8,128)S(1)}) custom-call(bf16[256,1024]{1,0:T(8,128)(2,1)S(1)} %collective-permute-done.5.refs_0_.refs_3_, bf16[256,1024]{1,0:T(8,128)(2,1)S(1)} %collective-permute-done.6.refs_1_.refs_4_, ...), custom_call_target="tpu_custom_call" | custom-call | flops 2415919104 | bytes 6291456 | tf_op jit(solution)/shard_map/middle_rows/pallas_call | solution.py:646
  52.8 3.1 %collective-permute-start.13 = (bf16[512,128]{1,0:T(8,128)(2,1)S(1)}, bf16[512,128]{1,0:T(8,128)(2,1)S(1)}, u32[]{:S(2)}, u32[]{:S(2)}) collective-permute-start(bf16[512,128]{1,0:T(8,128)(2,1)S(1)} %get-tuple-element.101), channel_id=1, source_target_pairs={{0,16},{4,20},{8,24},{12,28},{1,17},{5,21},{9,25},{13,29},{2,18},{... | collective-permute-start | bytes 393224 | tf_op jit(solution)/shard_map/ppermute | solution.py:678
  56.0 2.7 %collective-permute-done.13.refs_0_ = bf16[512,128]{1,0:T(8,128)(2,1)S(1)} collective-permute-done((bf16[512,128]{1,0:T(8,128)(2,1)S(1)}, bf16[512,128]{1,0:T(8,128)(2,1)S(1)}, u32[]{:S(2)}, u32[]{:S(2)}) %collective-permute-start.13) | collective-permute-done | bytes 131104 | tf_op jit(solution)/shard_map/ppermute | solution.py:678
  59.8 4.2 %collective-permute-done.15.refs_1_ = bf16[512,128]{1,0:T(8,128)(2,1)S(1)} collective-permute-done((bf16[512,128]{1,0:T(8,128)(2,1)S(1)}, bf16[512,128]{1,0:T(8,128)(2,1)S(1)}, u32[]{:S(2)}, u32[]{:S(2)}) %collective-permute-start.15) | collective-permute-done | bytes 131104 | tf_op jit(solution)/shard_map/ppermute | solution.py:693
  64.8 2.3 %window_attend.1.refs_6_ = f32[1024,128]{1,0:T(8,128)S(1)} custom-call(bf16[1024,384]{1,0:T(8,128)(2,1)S(1)} %get-tuple-element.117.win_ref, bf16[512,256]{1,0:T(8,128)(2,1)S(1)} %collective-permute-done.14.halo_ref, bf16[256,256]{1,0:T(8,128)(2,1)S(1)} %collective-permute-done.16.late_ref), custom_call_target="tpu_custom_call" | custom-call | flops 402653184 | bytes 3145728 | tf_op jit(solution)/shard_map/window_attend/pallas_call | solution.py:706
  68.5 3.9 %collective-permute-start.19 = (bf16[256,512]{1,0:T(8,128)(2,1)S(1)}, bf16[256,512]{1,0:T(8,128)(2,1)S(1)}, u32[]{:S(2)}, u32[]{:S(2)}) collective-permute-start(bf16[256,512]{1,0:T(8,128)(2,1)S(1)} %finish3.1), channel_id=1, source_target_pairs={{0,3},{1,0},{2,1},{3,2},{4,7},{5,4},{6,5},{7,6},{8,11},{9,8},{10,9... | collective-permute-start | bytes 786440 | tf_op jit(solution)/shard_map/ppermute | solution.py:733
  73.5 11.5 %collective-permute-done.20.refs_3_ = bf16[256,512]{1,0:T(8,128)(2,1)S(1)} collective-permute-done((bf16[256,512]{1,0:T(8,128)(2,1)S(1)}, bf16[256,512]{1,0:T(8,128)(2,1)S(1)}, u32[]{:S(2)}, u32[]{:S(2)}) %collective-permute-start.20) | collective-permute-done | bytes 262176 | tf_op jit(solution)/shard_map/ppermute | solution.py:733
  85.0 8.8 %collective-permute-done.19.refs_2_ = bf16[256,512]{1,0:T(8,128)(2,1)S(1)} collective-permute-done((bf16[256,512]{1,0:T(8,128)(2,1)S(1)}, bf16[256,512]{1,0:T(8,128)(2,1)S(1)}, u32[]{:S(2)}, u32[]{:S(2)}) %collective-permute-start.19) | collective-permute-done | bytes 262176 | tf_op jit(solution)/shard_map/ppermute | solution.py:733
  (46 shorter events, 11.6 us)
Async XLA Ops:
  0.0 20.1 %collective-permute-start = (bf16[256,1024]{1,0:T(8,128)(2,1)}, bf16[256,1024]{1,0:T(8,128)(2,1)S(1)}, u32[]{:S(2)}, u32[]{:S(2)}) collective-permute-start(bf16[256,1024]{1,0:T(8,128)(2,1)} %refs_0_.1), channel_id=1, source_target_pairs={{0,1},{1,2},{2,3},{4,5},{5,6},{6,7},{8,9},{9,10},{10,11},{12,13},{... | collective-permute-start | bytes 1572872 | tf_op jit(solution)/shard_map/ppermute | solution.py:573
  3.2 16.9 %collective-permute-start.1 = (bf16[256,1024]{1,0:T(8,128)(2,1)}, bf16[256,1024]{1,0:T(8,128)(2,1)S(1)}, u32[]{:S(2)}, u32[]{:S(2)}) collective-permute-start(bf16[256,1024]{1,0:T(8,128)(2,1)} %refs_0_.1), channel_id=1, source_target_pairs={{3,2},{2,1},{1,0},{7,6},{6,5},{5,4},{11,10},{10,9},{9,8},{15,14},{... | collective-permute-start | bytes 1572872 | tf_op jit(solution)/shard_map/ppermute | solution.py:574
  5.3 1.1 %copy-start.1 = (bf16[256,1536]{1,0:T(8,128)(2,1)S(1)}, bf16[256,1536]{1,0:T(8,128)(2,1)}, u32[]{:S(2)}) copy-start(bf16[256,1536]{1,0:T(8,128)(2,1)} %weight_ref.1) | copy-start | bytes 2359300
  7.3 8.4 %collective-permute-start.2 = (bf16[48,384]{1,0:T(8,128)(2,1)S(1)}, bf16[48,384]{1,0:T(8,128)(2,1)S(1)}, u32[]{:S(2)}, u32[]{:S(2)}) collective-permute-start(bf16[48,384]{1,0:T(8,128)(2,1)S(1)} %get-tuple-element.68), channel_id=1, source_target_pairs={{0,1},{1,2},{2,3},{3,0},{4,5},{5,6},{6,7},{7,4},{8,9},{9,10},{10,1... | collective-permute-start | bytes 110600 | tf_op jit(solution)/shard_map/ppermute | solution.py:588
  8.6 11.5 %collective-permute-start.3 = (bf16[48,384]{1,0:T(8,128)(2,1)S(1)}, bf16[48,384]{1,0:T(8,128)(2,1)S(1)}, u32[]{:S(2)}, u32[]{:S(2)}) collective-permute-start(bf16[48,384]{1,0:T(8,128)(2,1)S(1)} %get-tuple-element.69), channel_id=1, source_target_pairs={{0,2},{1,3},{2,0},{3,1},{4,6},{5,7},{6,4},{7,5},{8,10},{9,11},{10,... | collective-permute-start | bytes 110600 | tf_op jit(solution)/shard_map/ppermute | solution.py:588
  9.7 10.4 %collective-permute-start.4 = (bf16[48,384]{1,0:T(8,128)(2,1)S(1)}, bf16[48,384]{1,0:T(8,128)(2,1)S(1)}, u32[]{:S(2)}, u32[]{:S(2)}) collective-permute-start(bf16[48,384]{1,0:T(8,128)(2,1)S(1)} %get-tuple-element.70), channel_id=1, source_target_pairs={{0,3},{1,0},{2,1},{3,2},{4,7},{5,4},{6,5},{7,6},{8,11},{9,8},{10,9... | collective-permute-start | bytes 110600 | tf_op jit(solution)/shard_map/ppermute | solution.py:588
  11.1 1.9 %copy-start = (bf16[1,1024,1536]{2,1,0:T(8,128)(2,1)S(1)}, bf16[1,1024,1536]{2,1,0:T(8,128)(2,1)}, u32[]{:S(2)}) copy-start(bf16[1,1024,1536]{2,1,0:T(8,128)(2,1)} %param.8) | copy-start | bytes 9437188
  13.0 1.0 %copy-start.2 = (bf16[256,1024]{1,0:T(8,128)(2,1)S(1)}, bf16[256,1024]{1,0:T(8,128)(2,1)}, u32[]{:S(2)}) copy-start(bf16[256,1024]{1,0:T(8,128)(2,1)} %refs_0_.1) | copy-start | bytes 1572868
  20.1 17.2 %collective-permute-start.5 = (bf16[256,1024]{1,0:T(8,128)(2,1)S(1)}, bf16[256,1024]{1,0:T(8,128)(2,1)S(1)}, u32[]{:S(2)}, u32[]{:S(2)}) collective-permute-start(bf16[256,1024]{1,0:T(8,128)(2,1)S(1)} %collective-permute-done.1.refs_2_), channel_id=1, source_target_pairs={{2,1},{1,0},{6,5},{5,4},{10,9},{9,8},{14,13},{13,12},{18,17},{17,1... | collective-permute-start | bytes 1572872 | tf_op jit(solution)/shard_map/ppermute | solution.py:575
  22.5 14.9 %collective-permute-start.6 = (bf16[256,1024]{1,0:T(8,128)(2,1)S(1)}, bf16[256,1024]{1,0:T(8,128)(2,1)S(1)}, u32[]{:S(2)}, u32[]{:S(2)}) collective-permute-start(bf16[256,1024]{1,0:T(8,128)(2,1)S(1)} %collective-permute-done.refs_1_), channel_id=1, source_target_pairs={{1,2},{2,3},{5,6},{6,7},{9,10},{10,11},{13,14},{14,15},{17,18},{18... | collective-permute-start | bytes 1572872 | tf_op jit(solution)/shard_map/ppermute | solution.py:576
  25.5 7.5 %collective-permute-start.7 = (bf16[4,32,384]{2,1,0:T(8,128)(2,1)S(1)}, bf16[4,32,384]{2,1,0:T(8,128)(2,1)S(1)}, u32[]{:S(2)}, u32[]{:S(2)}) collective-permute-start(bf16[4,32,384]{2,1,0:T(8,128)(2,1)S(1)} %get-tuple-element.82.refs_0_), channel_id=1, source_target_pairs={{0,8},{4,12},{8,16},{12,20},{16,24},{20,28},{24,0},{28,4},{1,9},{5... | collective-permute-start | bytes 294920 | tf_op jit(solution)/shard_map/ppermute | solution.py:628
  26.8 6.3 %collective-permute-start.8 = (bf16[4,32,384]{2,1,0:T(8,128)(2,1)S(1)}, bf16[4,32,384]{2,1,0:T(8,128)(2,1)S(1)}, u32[]{:S(2)}, u32[]{:S(2)}) collective-permute-start(bf16[4,32,384]{2,1,0:T(8,128)(2,1)S(1)} %get-tuple-element.82.refs_0_), channel_id=1, source_target_pairs={{0,16},{4,20},{8,24},{12,28},{16,0},{20,4},{24,8},{28,12},{1,17},{... | collective-permute-start | bytes 294920 | tf_op jit(solution)/shard_map/ppermute | solution.py:628
  28.0 5.0 %collective-permute-start.9 = (bf16[4,32,384]{2,1,0:T(8,128)(2,1)S(1)}, bf16[4,32,384]{2,1,0:T(8,128)(2,1)S(1)}, u32[]{:S(2)}, u32[]{:S(2)}) collective-permute-start(bf16[4,32,384]{2,1,0:T(8,128)(2,1)S(1)} %get-tuple-element.82.refs_0_), channel_id=1, source_target_pairs={{0,24},{4,28},{8,0},{12,4},{16,8},{20,12},{24,16},{28,20},{1,25},{... | collective-permute-start | bytes 294920 | tf_op jit(solution)/shard_map/ppermute | solution.py:628
  33.1 6.2 %collective-permute-start.12 = (bf16[4,4,32,384]{3,2,1,0:T(8,128)(2,1)S(1)}, bf16[4,4,32,384]{3,2,1,0:T(8,128)(2,1)S(1)}, u32[]{:S(2)}, u32[]{:S(2)}) collective-permute-start(bf16[4,4,32,384]{3,2,1,0:T(8,128)(2,1)S(1)} %combine.1.refs_5_), channel_id=1, source_target_pairs={{0,4},{4,0},{8,12},{12,8},{16,20},{20,16},{24,28},{28,24},{1,5},{5... | collective-permute-start | bytes 1179656 | tf_op jit(solution)/shard_map/ppermute | solution.py:639
  37.3 15.4 %collective-permute-start.10 = (bf16[256,1024]{1,0:T(8,128)(2,1)S(1)}, bf16[256,1024]{1,0:T(8,128)(2,1)S(1)}, u32[]{:S(2)}, u32[]{:S(2)}) collective-permute-start(bf16[256,1024]{1,0:T(8,128)(2,1)S(1)} %collective-permute-done.5.refs_0_.refs_3_), channel_id=1, source_target_pairs={{1,0},{5,4},{9,8},{13,12},{17,16},{21,20},{25,24},{29,28}} | collective-permute-start | bytes 1572872 | tf_op jit(solution)/shard_map/ppermute | solution.py:575
  38.6 14.1 %collective-permute-start.11 = (bf16[256,1024]{1,0:T(8,128)(2,1)S(1)}, bf16[256,1024]{1,0:T(8,128)(2,1)S(1)}, u32[]{:S(2)}, u32[]{:S(2)}) collective-permute-start(bf16[256,1024]{1,0:T(8,128)(2,1)S(1)} %collective-permute-done.6.refs_1_.refs_4_), channel_id=1, source_target_pairs={{2,3},{6,7},{10,11},{14,15},{18,19},{22,23},{26,27},{30,31}} | collective-permute-start | bytes 1572872 | tf_op jit(solution)/shard_map/ppermute | solution.py:576
  41.2 14.8 %collective-permute-start.14 = (bf16[512,256]{1,0:T(8,128)(2,1)S(1)}, bf16[512,256]{1,0:T(8,128)(2,1)S(1)}, u32[]{:S(2)}, u32[]{:S(2)}) collective-permute-start(bf16[512,256]{1,0:T(8,128)(2,1)S(1)} %get-tuple-element.102), channel_id=1, source_target_pairs={{0,4},{4,8},{8,12},{12,16},{16,20},{20,24},{24,28},{1,5},{5,9},{9,... | collective-permute-start | bytes 786440 | tf_op jit(solution)/shard_map/ppermute | solution.py:21
  52.8 5.8 %collective-permute-start.13 = (bf16[512,128]{1,0:T(8,128)(2,1)S(1)}, bf16[512,128]{1,0:T(8,128)(2,1)S(1)}, u32[]{:S(2)}, u32[]{:S(2)}) collective-permute-start(bf16[512,128]{1,0:T(8,128)(2,1)S(1)} %get-tuple-element.101), channel_id=1, source_target_pairs={{0,16},{4,20},{8,24},{12,28},{1,17},{5,21},{9,25},{13,29},{2,18},{... | collective-permute-start | bytes 393224 | tf_op jit(solution)/shard_map/ppermute | solution.py:678
  58.7 5.3 %collective-permute-start.15 = (bf16[512,128]{1,0:T(8,128)(2,1)S(1)}, bf16[512,128]{1,0:T(8,128)(2,1)S(1)}, u32[]{:S(2)}, u32[]{:S(2)}) collective-permute-start(bf16[512,128]{1,0:T(8,128)(2,1)S(1)} %get-tuple-element.105), channel_id=1, source_target_pairs={{0,8},{4,12},{8,0},{12,4},{16,24},{20,28},{24,16},{28,20},{1,9},{5... | collective-permute-start | bytes 393224 | tf_op jit(solution)/shard_map/ppermute | solution.py:693
  59.1 5.7 %collective-permute-start.16 = (bf16[256,256]{1,0:T(8,128)(2,1)S(1)}, bf16[256,256]{1,0:T(8,128)(2,1)S(1)}, u32[]{:S(2)}, u32[]{:S(2)}) collective-permute-start(bf16[256,256]{1,0:T(8,128)(2,1)S(1)} %get-tuple-element.119), channel_id=1, source_target_pairs={{0,4},{4,8},{8,12},{12,16},{16,20},{20,24},{24,28}} | collective-permute-start | bytes 393224 | tf_op jit(solution)/shard_map/ppermute | solution.py:704
  64.0 3.1 %collective-permute-start.17 = (bf16[512,128]{1,0:T(8,128)(2,1)S(1)}, bf16[512,128]{1,0:T(8,128)(2,1)S(1)}, u32[]{:S(2)}, u32[]{:S(2)}) collective-permute-start(bf16[512,128]{1,0:T(8,128)(2,1)S(1)} %get-tuple-element.122), channel_id=1, source_target_pairs={{0,4},{4,0},{8,12},{12,8},{16,20},{20,16},{24,28},{28,24},{1,5},{5... | collective-permute-start | bytes 393224 | tf_op jit(solution)/shard_map/ppermute | solution.py:693
  67.7 17.4 %collective-permute-start.20 = (bf16[256,512]{1,0:T(8,128)(2,1)S(1)}, bf16[256,512]{1,0:T(8,128)(2,1)S(1)}, u32[]{:S(2)}, u32[]{:S(2)}) collective-permute-start(bf16[256,512]{1,0:T(8,128)(2,1)S(1)} %finish2.1), channel_id=1, source_target_pairs={{0,2},{1,3},{2,0},{3,1},{4,6},{5,7},{6,4},{7,5},{8,10},{9,11},{10,... | collective-permute-start | bytes 786440 | tf_op jit(solution)/shard_map/ppermute | solution.py:733
  68.5 25.3 %collective-permute-start.19 = (bf16[256,512]{1,0:T(8,128)(2,1)S(1)}, bf16[256,512]{1,0:T(8,128)(2,1)S(1)}, u32[]{:S(2)}, u32[]{:S(2)}) collective-permute-start(bf16[256,512]{1,0:T(8,128)(2,1)S(1)} %finish3.1), channel_id=1, source_target_pairs={{0,3},{1,0},{2,1},{3,2},{4,7},{5,4},{6,5},{7,6},{8,11},{9,8},{10,9... | collective-permute-start | bytes 786440 | tf_op jit(solution)/shard_map/ppermute | solution.py:733
  72.9 20.9 %collective-permute-start.18 = (bf16[256,512]{1,0:T(8,128)(2,1)S(1)}, bf16[256,512]{1,0:T(8,128)(2,1)S(1)}, u32[]{:S(2)}, u32[]{:S(2)}) collective-permute-start(bf16[256,512]{1,0:T(8,128)(2,1)S(1)} %finish1.1), channel_id=1, source_target_pairs={{0,1},{1,2},{2,3},{3,0},{4,5},{5,6},{6,7},{7,4},{8,9},{9,10},{10,1... | collective-permute-start | bytes 786440 | tf_op jit(solution)/shard_map/ppermute | solution.py:733
  (2 other events, 1.4 us)

commit v14 on v11

--- a/solution.py
+++ b/solution.py
@@ -663,7 +663,7 @@
         functools.partial(last_keys_body, n_mem),
         "last_keys",
         (shape(count, 2 * width), shape(width, HDIM, full), shape(width, HDIM)),
-        2 * count * depth * 2 * width,
+        16 * count * depth * 2 * width,
         3 << 20,
     )(above, below, all_routes, weight, state)
     last_query, last_coef, extra = kernel_call(
@@ -676,6 +676,7 @@
     local = (last_query, last_coef, extra)
     bit = n_ctx // 2
     got = lax.ppermute(sent, "ctx", [(i, i + bit) for i in range(n_ctx) if not i & bit])
+    got, halo = lax.optimization_barrier((got, halo))
     prefix, late = (), None
     while bit > 1:
         bit //= 2

time: 95.1 us -> 97.3 us (1.023)
  waiting for transfers between devices: 30.8 us -> 33.5 us
    ppermute x1, waiting for transfers between devices: 0.01 us -> 3.82 us  [dense_shards(): lax.ppermute(sent, 'ctx', [(i, i + bit) for i in range(n_ctx) if not i &...]
  transfers between devices with their start and end apart: 21 -> 21, of which waited for: 6 -> 7; matrix products, arithmetic and copies ran while one was open for 0% -> 0% of each run, Pallas kernels for 20% -> 19%
where the time goes in v14:
time: 97.3 us; the launch traced here: 95.9 us
  starting transfers between devices  36.7 us (38%)
  waiting for transfers between devices  33.5 us (34%)
  Pallas kernels  19.8 us (20%)
  local copies, waits for them, and re-layouts  5.43 us (6%)
    ppermute x3, waiting for transfers between devices, dense_shards(): lax.ppermute(part, 'mem', [(i, (i + shift) % n_mem) for i in range(n_mem)])  20.4 us
    pallas_call x1, Pallas kernels, dense_shards(): kernel_call(functools.partial(arrivals_body, n_mem, 3, early, True), 'mid...  8.17 us
    unnamed x10, local copies, waits for them, and re-layouts  5.43 us
    ppermute x3, waiting for transfers between devices, dense_shards(): lax.ppermute(packed[s], 'mem', [(i, (i + s) % n_mem) for i in range(n_mem)])  5.1 us
    ppermute x3, starting transfers between devices, dense_shards(): lax.ppermute(part, 'mem', [(i, (i + shift) % n_mem) for i in range(n_mem)])  4.36 us
    ppermute x1, starting transfers between devices, dense_shards(): lax.ppermute(of_core, 'ctx', [(i, i ^ 1) for i in range(n_ctx)])  4.08 us
    pallas_call x1, Pallas kernels, dense_shards(): kernel_call(functools.partial(arrivals_body, n_mem, 0, 3, False), 'near_r...  3.86 us
    ppermute x3, starting transfers between devices, dense_shards(): lax.ppermute(packed[s], 'mem', [(i, (i + s) % n_mem) for i in range(n_mem)])  3.83 us
  transfers between devices with their start and end apart: 21, of which 7 were waited for; matrix products, arithmetic and copies ran while one was open for 0% of the time, Pallas kernels for 19%

profile of v14, /device:TPU:9, one launch (start us, length us, event | category | flops | bytes accessed | tf_op | source)
XLA Modules:
  0.0 95.9 jit_solution(3832668919318639634)
XLA Ops:
  0.0 3.2 %collective-permute-start = (bf16[256,1024]{1,0:T(8,128)(2,1)}, bf16[256,1024]{1,0:T(8,128)(2,1)S(1)}, u32[]{:S(2)}, u32[]{:S(2)}) collective-permute-start(bf16[256,1024]{1,0:T(8,128)(2,1)} %refs_0_.1), channel_id=1, source_target_pairs={{0,1},{1,2},{2,3},{4,5},{5,6},{6,7},{8,9},{9,10},{10,11},{12,13},{... | collective-permute-start | bytes 1572872 | tf_op jit(solution)/shard_map/ppermute | solution.py:573
  3.2 2.1 %collective-permute-start.1 = (bf16[256,1024]{1,0:T(8,128)(2,1)}, bf16[256,1024]{1,0:T(8,128)(2,1)S(1)}, u32[]{:S(2)}, u32[]{:S(2)}) collective-permute-start(bf16[256,1024]{1,0:T(8,128)(2,1)} %refs_0_.1), channel_id=1, source_target_pairs={{3,2},{2,1},{1,0},{7,6},{6,5},{5,4},{11,10},{10,9},{9,8},{15,14},{... | collective-permute-start | bytes 1572872 | tf_op jit(solution)/shard_map/ppermute | solution.py:574
  7.3 1.3 %collective-permute-start.2 = (bf16[48,384]{1,0:T(8,128)(2,1)S(1)}, bf16[48,384]{1,0:T(8,128)(2,1)S(1)}, u32[]{:S(2)}, u32[]{:S(2)}) collective-permute-start(bf16[48,384]{1,0:T(8,128)(2,1)S(1)} %get-tuple-element.68), channel_id=1, source_target_pairs={{0,1},{1,2},{2,3},{3,0},{4,5},{5,6},{6,7},{7,4},{8,9},{9,10},{10,1... | collective-permute-start | bytes 110600 | tf_op jit(solution)/shard_map/ppermute | solution.py:588
  9.7 1.4 %collective-permute-start.4 = (bf16[48,384]{1,0:T(8,128)(2,1)S(1)}, bf16[48,384]{1,0:T(8,128)(2,1)S(1)}, u32[]{:S(2)}, u32[]{:S(2)}) collective-permute-start(bf16[48,384]{1,0:T(8,128)(2,1)S(1)} %get-tuple-element.70), channel_id=1, source_target_pairs={{0,3},{1,0},{2,1},{3,2},{4,7},{5,4},{6,5},{7,6},{8,11},{9,8},{10,9... | collective-permute-start | bytes 110600 | tf_op jit(solution)/shard_map/ppermute | solution.py:588
  11.1 1.9 %copy-done = bf16[1,1024,1536]{2,1,0:T(8,128)(2,1)S(1)} copy-done((bf16[1,1024,1536]{2,1,0:T(8,128)(2,1)S(1)}, bf16[1,1024,1536]{2,1,0:T(8,128)(2,1)}, u32[]{:S(2)}) %copy-start) | copy-done | bytes 3145752
  15.7 4.4 %collective-permute-done.3.refs_2_ = bf16[48,384]{1,0:T(8,128)(2,1)S(1)} collective-permute-done((bf16[48,384]{1,0:T(8,128)(2,1)S(1)}, bf16[48,384]{1,0:T(8,128)(2,1)S(1)}, u32[]{:S(2)}, u32[]{:S(2)}) %collective-permute-start.3) | collective-permute-done | bytes 36896 | tf_op jit(solution)/shard_map/ppermute | solution.py:588
  20.1 2.3 %collective-permute-start.5 = (bf16[256,1024]{1,0:T(8,128)(2,1)S(1)}, bf16[256,1024]{1,0:T(8,128)(2,1)S(1)}, u32[]{:S(2)}, u32[]{:S(2)}) collective-permute-start(bf16[256,1024]{1,0:T(8,128)(2,1)S(1)} %collective-permute-done.1.refs_2_), channel_id=1, source_target_pairs={{2,1},{1,0},{6,5},{5,4},{10,9},{9,8},{14,13},{13,12},{18,17},{17,1... | collective-permute-start | bytes 1572872 | tf_op jit(solution)/shard_map/ppermute | solution.py:575
  22.5 3.0 %collective-permute-start.6 = (bf16[256,1024]{1,0:T(8,128)(2,1)S(1)}, bf16[256,1024]{1,0:T(8,128)(2,1)S(1)}, u32[]{:S(2)}, u32[]{:S(2)}) collective-permute-start(bf16[256,1024]{1,0:T(8,128)(2,1)S(1)} %collective-permute-done.refs_1_), channel_id=1, source_target_pairs={{1,2},{2,3},{5,6},{6,7},{9,10},{10,11},{13,14},{14,15},{17,18},{18... | collective-permute-start | bytes 1572872 | tf_op jit(solution)/shard_map/ppermute | solution.py:576
  25.5 1.3 %collective-permute-start.7 = (bf16[4,32,384]{2,1,0:T(8,128)(2,1)S(1)}, bf16[4,32,384]{2,1,0:T(8,128)(2,1)S(1)}, u32[]{:S(2)}, u32[]{:S(2)}) collective-permute-start(bf16[4,32,384]{2,1,0:T(8,128)(2,1)S(1)} %get-tuple-element.82.refs_0_), channel_id=1, source_target_pairs={{0,8},{4,12},{8,16},{12,20},{16,24},{20,28},{24,0},{28,4},{1,9},{5... | collective-permute-start | bytes 294920 | tf_op jit(solution)/shard_map/ppermute | solution.py:628
  26.8 1.2 %collective-permute-start.8 = (bf16[4,32,384]{2,1,0:T(8,128)(2,1)S(1)}, bf16[4,32,384]{2,1,0:T(8,128)(2,1)S(1)}, u32[]{:S(2)}, u32[]{:S(2)}) collective-permute-start(bf16[4,32,384]{2,1,0:T(8,128)(2,1)S(1)} %get-tuple-element.82.refs_0_), channel_id=1, source_target_pairs={{0,16},{4,20},{8,24},{12,28},{16,0},{20,4},{24,8},{28,12},{1,17},{... | collective-permute-start | bytes 294920 | tf_op jit(solution)/shard_map/ppermute | solution.py:628
  29.1 3.9 %near_rows.1 = (bf16[1024,1536]{1,0:T(8,128)(2,1)S(1)}, f32[1024,128]{1,0:T(8,128)S(1)}, f32[512,128]{1,0:T(8,128)S(1)}) custom-call(bf16[256,1024]{1,0:T(8,128)(2,1)S(1)} %get-tuple-element.78.refs_0_, bf16[256,1024]{1,0:T(8,128)(2,1)S(1)} %collective-permute-done.refs_1_, bf16[256,1024]{1,0:T(8,128)(2,1)S(1)} %collective-permute-done.1.refs_2_, ...), custom_call_target="tpu_custom_call" | custom-call | flops 2415919104 | bytes 6291456 | tf_op jit(solution)/shard_map/near_rows/pallas_call | solution.py:619
  33.7 1.3 %collective-permute-start.10 = (bf16[256,1024]{1,0:T(8,128)(2,1)S(1)}, bf16[256,1024]{1,0:T(8,128)(2,1)S(1)}, u32[]{:S(2)}, u32[]{:S(2)}) collective-permute-start(bf16[256,1024]{1,0:T(8,128)(2,1)S(1)} %collective-permute-done.5.refs_0_.refs_3_), channel_id=1, source_target_pairs={{1,0},{5,4},{9,8},{13,12},{17,16},{21,20},{25,24},{29,28}} | collective-permute-start | bytes 1572872 | tf_op jit(solution)/shard_map/ppermute | solution.py:575
  35.7 4.1 %collective-permute-start.12 = (bf16[4,4,32,384]{3,2,1,0:T(8,128)(2,1)S(1)}, bf16[4,4,32,384]{3,2,1,0:T(8,128)(2,1)S(1)}, u32[]{:S(2)}, u32[]{:S(2)}) collective-permute-start(bf16[4,4,32,384]{3,2,1,0:T(8,128)(2,1)S(1)} %combine.1.refs_5_), channel_id=1, source_target_pairs={{0,4},{4,0},{8,12},{12,8},{16,20},{20,16},{24,28},{28,24},{1,5},{5... | collective-permute-start | bytes 1179656 | tf_op jit(solution)/shard_map/ppermute | solution.py:640
  39.8 8.2 %middle_rows.1 = (bf16[1024,1536]{1,0:T(8,128)(2,1)S(1)}, f32[1024,128]{1,0:T(8,128)S(1)}, f32[512,128]{1,0:T(8,128)S(1)}, f32[1024,512]{1,0:T(8,128)S(1)}) custom-call(bf16[256,1024]{1,0:T(8,128)(2,1)S(1)} %collective-permute-done.5.refs_0_.refs_3_, bf16[256,1024]{1,0:T(8,128)(2,1)S(1)} %collective-permute-done.6.refs_1_.refs_4_, ...), custom_call_target="tpu_custom_call" | custom-call | flops 2415919104 | bytes 6291456 | tf_op jit(solution)/shard_map/middle_rows/pallas_call | solution.py:646
  47.9 1.9 %window_early.1 = (bf16[1024,384]{1,0:T(8,128)(2,1)S(1)}, bf16[1024,384]{1,0:T(8,128)(2,1)S(1)}, bf16[512,256]{1,0:T(8,128)(2,1)S(1)}) custom-call(bf16[256,1024]{1,0:T(8,128)(2,1)S(1)} %get-tuple-element.78.refs_0_, bf16[256,1024]{1,0:T(8,128)(2,1)S(1)} %collective-permute-done.refs_1_, bf16[256,1024]{1,0:T(8,128)(2,1)S(1)} %collective-permute-done.1.refs_2_, ...), custom_call_target="tpu_custom_call" | custom-call | flops 805306368 | bytes 5242880 | tf_op jit(solution)/shard_map/window_early/pallas_call | solution.py:653
  49.8 3.0 %collective-permute-start.14 = (bf16[512,256]{1,0:T(8,128)(2,1)S(1)}, bf16[512,256]{1,0:T(8,128)(2,1)S(1)}, u32[]{:S(2)}, u32[]{:S(2)}) collective-permute-start(bf16[512,256]{1,0:T(8,128)(2,1)S(1)} %get-tuple-element.102), channel_id=1, source_target_pairs={{0,4},{4,8},{8,12},{12,16},{16,20},{20,24},{24,28},{1,5},{5,9},{9,... | collective-permute-start | bytes 786440 | tf_op jit(solution)/shard_map/ppermute | solution.py:21
  52.9 3.1 %collective-permute-start.13 = (bf16[512,128]{1,0:T(8,128)(2,1)S(1)}, bf16[512,128]{1,0:T(8,128)(2,1)S(1)}, u32[]{:S(2)}, u32[]{:S(2)}) collective-permute-start(bf16[512,128]{1,0:T(8,128)(2,1)S(1)} %get-tuple-element.101), channel_id=1, source_target_pairs={{0,16},{4,20},{8,24},{12,28},{1,17},{5,21},{9,25},{13,29},{2,18},{... | collective-permute-start | bytes 393224 | tf_op jit(solution)/shard_map/ppermute | solution.py:678
  56.1 3.8 %collective-permute-done.13.refs_0_ = bf16[512,128]{1,0:T(8,128)(2,1)S(1)} collective-permute-done((bf16[512,128]{1,0:T(8,128)(2,1)S(1)}, bf16[512,128]{1,0:T(8,128)(2,1)S(1)}, u32[]{:S(2)}, u32[]{:S(2)}) %collective-permute-start.13) | collective-permute-done | bytes 131104 | tf_op jit(solution)/shard_map/ppermute | solution.py:678
  61.0 3.7 %collective-permute-done.15.refs_1_ = bf16[512,128]{1,0:T(8,128)(2,1)S(1)} collective-permute-done((bf16[512,128]{1,0:T(8,128)(2,1)S(1)}, bf16[512,128]{1,0:T(8,128)(2,1)S(1)}, u32[]{:S(2)}, u32[]{:S(2)}) %collective-permute-start.15) | collective-permute-done | bytes 131104 | tf_op jit(solution)/shard_map/ppermute | solution.py:693
  64.8 1.3 %collective-permute-start.17 = (bf16[512,128]{1,0:T(8,128)(2,1)S(1)}, bf16[512,128]{1,0:T(8,128)(2,1)S(1)}, u32[]{:S(2)}, u32[]{:S(2)}) collective-permute-start(bf16[512,128]{1,0:T(8,128)(2,1)S(1)} %get-tuple-element.122), channel_id=1, source_target_pairs={{0,4},{4,0},{8,12},{12,8},{16,20},{20,16},{24,28},{28,24},{1,5},{5... | collective-permute-start | bytes 393224 | tf_op jit(solution)/shard_map/ppermute | solution.py:693
  66.0 2.3 %window_attend.1.refs_6_ = f32[1024,128]{1,0:T(8,128)S(1)} custom-call(bf16[1024,384]{1,0:T(8,128)(2,1)S(1)} %get-tuple-element.117.win_ref, bf16[512,256]{1,0:T(8,128)(2,1)S(1)} %collective-permute-done.14.halo_ref, bf16[256,256]{1,0:T(8,128)(2,1)S(1)} %collective-permute-done.16.late_ref), custom_call_target="tpu_custom_call" | custom-call | flops 402653184 | bytes 3145728 | tf_op jit(solution)/shard_map/window_attend/pallas_call | solution.py:706
  69.4 4.2 %collective-permute-start.19 = (bf16[256,512]{1,0:T(8,128)(2,1)S(1)}, bf16[256,512]{1,0:T(8,128)(2,1)S(1)}, u32[]{:S(2)}, u32[]{:S(2)}) collective-permute-start(bf16[256,512]{1,0:T(8,128)(2,1)S(1)} %finish3.1), channel_id=1, source_target_pairs={{0,3},{1,0},{2,1},{3,2},{4,7},{5,4},{6,5},{7,6},{8,11},{9,8},{10,9... | collective-permute-start | bytes 786440 | tf_op jit(solution)/shard_map/ppermute | solution.py:733
  74.7 11.4 %collective-permute-done.20.refs_3_ = bf16[256,512]{1,0:T(8,128)(2,1)S(1)} collective-permute-done((bf16[256,512]{1,0:T(8,128)(2,1)S(1)}, bf16[256,512]{1,0:T(8,128)(2,1)S(1)}, u32[]{:S(2)}, u32[]{:S(2)}) %collective-permute-start.20) | collective-permute-done | bytes 262176 | tf_op jit(solution)/shard_map/ppermute | solution.py:733
  86.1 8.9 %collective-permute-done.19.refs_2_ = bf16[256,512]{1,0:T(8,128)(2,1)S(1)} collective-permute-done((bf16[256,512]{1,0:T(8,128)(2,1)S(1)}, bf16[256,512]{1,0:T(8,128)(2,1)S(1)}, u32[]{:S(2)}, u32[]{:S(2)}) %collective-permute-start.19) | collective-permute-done | bytes 262176 | tf_op jit(solution)/shard_map/ppermute | solution.py:733
  (46 shorter events, 12.3 us)
Async XLA Ops:
  0.0 20.1 %collective-permute-start = (bf16[256,1024]{1,0:T(8,128)(2,1)}, bf16[256,1024]{1,0:T(8,128)(2,1)S(1)}, u32[]{:S(2)}, u32[]{:S(2)}) collective-permute-start(bf16[256,1024]{1,0:T(8,128)(2,1)} %refs_0_.1), channel_id=1, source_target_pairs={{0,1},{1,2},{2,3},{4,5},{5,6},{6,7},{8,9},{9,10},{10,11},{12,13},{... | collective-permute-start | bytes 1572872 | tf_op jit(solution)/shard_map/ppermute | solution.py:573
  3.2 16.9 %collective-permute-start.1 = (bf16[256,1024]{1,0:T(8,128)(2,1)}, bf16[256,1024]{1,0:T(8,128)(2,1)S(1)}, u32[]{:S(2)}, u32[]{:S(2)}) collective-permute-start(bf16[256,1024]{1,0:T(8,128)(2,1)} %refs_0_.1), channel_id=1, source_target_pairs={{3,2},{2,1},{1,0},{7,6},{6,5},{5,4},{11,10},{10,9},{9,8},{15,14},{... | collective-permute-start | bytes 1572872 | tf_op jit(solution)/shard_map/ppermute | solution.py:574
  5.3 1.1 %copy-start.1 = (bf16[256,1536]{1,0:T(8,128)(2,1)S(1)}, bf16[256,1536]{1,0:T(8,128)(2,1)}, u32[]{:S(2)}) copy-start(bf16[256,1536]{1,0:T(8,128)(2,1)} %weight_ref.1) | copy-start | bytes 2359300
  7.3 8.4 %collective-permute-start.2 = (bf16[48,384]{1,0:T(8,128)(2,1)S(1)}, bf16[48,384]{1,0:T(8,128)(2,1)S(1)}, u32[]{:S(2)}, u32[]{:S(2)}) collective-permute-start(bf16[48,384]{1,0:T(8,128)(2,1)S(1)} %get-tuple-element.68), channel_id=1, source_target_pairs={{0,1},{1,2},{2,3},{3,0},{4,5},{5,6},{6,7},{7,4},{8,9},{9,10},{10,1... | collective-permute-start | bytes 110600 | tf_op jit(solution)/shard_map/ppermute | solution.py:588
  8.6 11.5 %collective-permute-start.3 = (bf16[48,384]{1,0:T(8,128)(2,1)S(1)}, bf16[48,384]{1,0:T(8,128)(2,1)S(1)}, u32[]{:S(2)}, u32[]{:S(2)}) collective-permute-start(bf16[48,384]{1,0:T(8,128)(2,1)S(1)} %get-tuple-element.69), channel_id=1, source_target_pairs={{0,2},{1,3},{2,0},{3,1},{4,6},{5,7},{6,4},{7,5},{8,10},{9,11},{10,... | collective-permute-start | bytes 110600 | tf_op jit(solution)/shard_map/ppermute | solution.py:588
  9.7 10.4 %collective-permute-start.4 = (bf16[48,384]{1,0:T(8,128)(2,1)S(1)}, bf16[48,384]{1,0:T(8,128)(2,1)S(1)}, u32[]{:S(2)}, u32[]{:S(2)}) collective-permute-start(bf16[48,384]{1,0:T(8,128)(2,1)S(1)} %get-tuple-element.70), channel_id=1, source_target_pairs={{0,3},{1,0},{2,1},{3,2},{4,7},{5,4},{6,5},{7,6},{8,11},{9,8},{10,9... | collective-permute-start | bytes 110600 | tf_op jit(solution)/shard_map/ppermute | solution.py:588
  11.1 1.9 %copy-start = (bf16[1,1024,1536]{2,1,0:T(8,128)(2,1)S(1)}, bf16[1,1024,1536]{2,1,0:T(8,128)(2,1)}, u32[]{:S(2)}) copy-start(bf16[1,1024,1536]{2,1,0:T(8,128)(2,1)} %param.8) | copy-start | bytes 9437188
  13.0 1.0 %copy-start.2 = (bf16[256,1024]{1,0:T(8,128)(2,1)S(1)}, bf16[256,1024]{1,0:T(8,128)(2,1)}, u32[]{:S(2)}) copy-start(bf16[256,1024]{1,0:T(8,128)(2,1)} %refs_0_.1) | copy-start | bytes 1572868
  20.1 13.0 %collective-permute-start.5 = (bf16[256,1024]{1,0:T(8,128)(2,1)S(1)}, bf16[256,1024]{1,0:T(8,128)(2,1)S(1)}, u32[]{:S(2)}, u32[]{:S(2)}) collective-permute-start(bf16[256,1024]{1,0:T(8,128)(2,1)S(1)} %collective-permute-done.1.refs_2_), channel_id=1, source_target_pairs={{2,1},{1,0},{6,5},{5,4},{10,9},{9,8},{14,13},{13,12},{18,17},{17,1... | collective-permute-start | bytes 1572872 | tf_op jit(solution)/shard_map/ppermute | solution.py:575
  22.5 11.2 %collective-permute-start.6 = (bf16[256,1024]{1,0:T(8,128)(2,1)S(1)}, bf16[256,1024]{1,0:T(8,128)(2,1)S(1)}, u32[]{:S(2)}, u32[]{:S(2)}) collective-permute-start(bf16[256,1024]{1,0:T(8,128)(2,1)S(1)} %collective-permute-done.refs_1_), channel_id=1, source_target_pairs={{1,2},{2,3},{5,6},{6,7},{9,10},{10,11},{13,14},{14,15},{17,18},{18... | collective-permute-start | bytes 1572872 | tf_op jit(solution)/shard_map/ppermute | solution.py:576
  25.5 7.5 %collective-permute-start.7 = (bf16[4,32,384]{2,1,0:T(8,128)(2,1)S(1)}, bf16[4,32,384]{2,1,0:T(8,128)(2,1)S(1)}, u32[]{:S(2)}, u32[]{:S(2)}) collective-permute-start(bf16[4,32,384]{2,1,0:T(8,128)(2,1)S(1)} %get-tuple-element.82.refs_0_), channel_id=1, source_target_pairs={{0,8},{4,12},{8,16},{12,20},{16,24},{20,28},{24,0},{28,4},{1,9},{5... | collective-permute-start | bytes 294920 | tf_op jit(solution)/shard_map/ppermute | solution.py:628
  26.8 6.3 %collective-permute-start.8 = (bf16[4,32,384]{2,1,0:T(8,128)(2,1)S(1)}, bf16[4,32,384]{2,1,0:T(8,128)(2,1)S(1)}, u32[]{:S(2)}, u32[]{:S(2)}) collective-permute-start(bf16[4,32,384]{2,1,0:T(8,128)(2,1)S(1)} %get-tuple-element.82.refs_0_), channel_id=1, source_target_pairs={{0,16},{4,20},{8,24},{12,28},{16,0},{20,4},{24,8},{28,12},{1,17},{... | collective-permute-start | bytes 294920 | tf_op jit(solution)/shard_map/ppermute | solution.py:628
  28.0 5.0 %collective-permute-start.9 = (bf16[4,32,384]{2,1,0:T(8,128)(2,1)S(1)}, bf16[4,32,384]{2,1,0:T(8,128)(2,1)S(1)}, u32[]{:S(2)}, u32[]{:S(2)}) collective-permute-start(bf16[4,32,384]{2,1,0:T(8,128)(2,1)S(1)} %get-tuple-element.82.refs_0_), channel_id=1, source_target_pairs={{0,24},{4,28},{8,0},{12,4},{16,8},{20,12},{24,16},{28,20},{1,25},{... | collective-permute-start | bytes 294920 | tf_op jit(solution)/shard_map/ppermute | solution.py:628
  33.7 19.2 %collective-permute-start.10 = (bf16[256,1024]{1,0:T(8,128)(2,1)S(1)}, bf16[256,1024]{1,0:T(8,128)(2,1)S(1)}, u32[]{:S(2)}, u32[]{:S(2)}) collective-permute-start(bf16[256,1024]{1,0:T(8,128)(2,1)S(1)} %collective-permute-done.5.refs_0_.refs_3_), channel_id=1, source_target_pairs={{1,0},{5,4},{9,8},{13,12},{17,16},{21,20},{25,24},{29,28}} | collective-permute-start | bytes 1572872 | tf_op jit(solution)/shard_map/ppermute | solution.py:575
  35.0 17.9 %collective-permute-start.11 = (bf16[256,1024]{1,0:T(8,128)(2,1)S(1)}, bf16[256,1024]{1,0:T(8,128)(2,1)S(1)}, u32[]{:S(2)}, u32[]{:S(2)}) collective-permute-start(bf16[256,1024]{1,0:T(8,128)(2,1)S(1)} %collective-permute-done.6.refs_1_.refs_4_), channel_id=1, source_target_pairs={{2,3},{6,7},{10,11},{14,15},{18,19},{22,23},{26,27},{30,31}} | collective-permute-start | bytes 1572872 | tf_op jit(solution)/shard_map/ppermute | solution.py:576
  35.7 12.3 %collective-permute-start.12 = (bf16[4,4,32,384]{3,2,1,0:T(8,128)(2,1)S(1)}, bf16[4,4,32,384]{3,2,1,0:T(8,128)(2,1)S(1)}, u32[]{:S(2)}, u32[]{:S(2)}) collective-permute-start(bf16[4,4,32,384]{3,2,1,0:T(8,128)(2,1)S(1)} %combine.1.refs_5_), channel_id=1, source_target_pairs={{0,4},{4,0},{8,12},{12,8},{16,20},{20,16},{24,28},{28,24},{1,5},{5... | collective-permute-start | bytes 1179656 | tf_op jit(solution)/shard_map/ppermute | solution.py:640
  49.8 10.1 %collective-permute-start.14 = (bf16[512,256]{1,0:T(8,128)(2,1)S(1)}, bf16[512,256]{1,0:T(8,128)(2,1)S(1)}, u32[]{:S(2)}, u32[]{:S(2)}) collective-permute-start(bf16[512,256]{1,0:T(8,128)(2,1)S(1)} %get-tuple-element.102), channel_id=1, source_target_pairs={{0,4},{4,8},{8,12},{12,16},{16,20},{20,24},{24,28},{1,5},{5,9},{9,... | collective-permute-start | bytes 786440 | tf_op jit(solution)/shard_map/ppermute | solution.py:21
  52.9 7.0 %collective-permute-start.13 = (bf16[512,128]{1,0:T(8,128)(2,1)S(1)}, bf16[512,128]{1,0:T(8,128)(2,1)S(1)}, u32[]{:S(2)}, u32[]{:S(2)}) collective-permute-start(bf16[512,128]{1,0:T(8,128)(2,1)S(1)} %get-tuple-element.101), channel_id=1, source_target_pairs={{0,16},{4,20},{8,24},{12,28},{1,17},{5,21},{9,25},{13,29},{2,18},{... | collective-permute-start | bytes 393224 | tf_op jit(solution)/shard_map/ppermute | solution.py:678
  59.9 4.8 %collective-permute-start.15 = (bf16[512,128]{1,0:T(8,128)(2,1)S(1)}, bf16[512,128]{1,0:T(8,128)(2,1)S(1)}, u32[]{:S(2)}, u32[]{:S(2)}) collective-permute-start(bf16[512,128]{1,0:T(8,128)(2,1)S(1)} %get-tuple-element.105), channel_id=1, source_target_pairs={{0,8},{4,12},{8,0},{12,4},{16,24},{20,28},{24,16},{28,20},{1,9},{5... | collective-permute-start | bytes 393224 | tf_op jit(solution)/shard_map/ppermute | solution.py:693
  60.3 5.7 %collective-permute-start.16 = (bf16[256,256]{1,0:T(8,128)(2,1)S(1)}, bf16[256,256]{1,0:T(8,128)(2,1)S(1)}, u32[]{:S(2)}, u32[]{:S(2)}) collective-permute-start(bf16[256,256]{1,0:T(8,128)(2,1)S(1)} %get-tuple-element.119), channel_id=1, source_target_pairs={{0,4},{4,8},{8,12},{12,16},{16,20},{20,24},{24,28}} | collective-permute-start | bytes 393224 | tf_op jit(solution)/shard_map/ppermute | solution.py:704
  64.8 3.6 %collective-permute-start.17 = (bf16[512,128]{1,0:T(8,128)(2,1)S(1)}, bf16[512,128]{1,0:T(8,128)(2,1)S(1)}, u32[]{:S(2)}, u32[]{:S(2)}) collective-permute-start(bf16[512,128]{1,0:T(8,128)(2,1)S(1)} %get-tuple-element.122), channel_id=1, source_target_pairs={{0,4},{4,0},{8,12},{12,8},{16,20},{20,16},{24,28},{28,24},{1,5},{5... | collective-permute-start | bytes 393224 | tf_op jit(solution)/shard_map/ppermute | solution.py:693
  68.9 17.3 %collective-permute-start.20 = (bf16[256,512]{1,0:T(8,128)(2,1)S(1)}, bf16[256,512]{1,0:T(8,128)(2,1)S(1)}, u32[]{:S(2)}, u32[]{:S(2)}) collective-permute-start(bf16[256,512]{1,0:T(8,128)(2,1)S(1)} %finish2.1), channel_id=1, source_target_pairs={{0,2},{1,3},{2,0},{3,1},{4,6},{5,7},{6,4},{7,5},{8,10},{9,11},{10,... | collective-permute-start | bytes 786440 | tf_op jit(solution)/shard_map/ppermute | solution.py:733
  69.4 25.6 %collective-permute-start.19 = (bf16[256,512]{1,0:T(8,128)(2,1)S(1)}, bf16[256,512]{1,0:T(8,128)(2,1)S(1)}, u32[]{:S(2)}, u32[]{:S(2)}) collective-permute-start(bf16[256,512]{1,0:T(8,128)(2,1)S(1)} %finish3.1), channel_id=1, source_target_pairs={{0,3},{1,0},{2,1},{3,2},{4,7},{5,4},{6,5},{7,6},{8,11},{9,8},{10,9... | collective-permute-start | bytes 786440 | tf_op jit(solution)/shard_map/ppermute | solution.py:733
  74.1 20.9 %collective-permute-start.18 = (bf16[256,512]{1,0:T(8,128)(2,1)S(1)}, bf16[256,512]{1,0:T(8,128)(2,1)S(1)}, u32[]{:S(2)}, u32[]{:S(2)}) collective-permute-start(bf16[256,512]{1,0:T(8,128)(2,1)S(1)} %finish1.1), channel_id=1, source_target_pairs={{0,1},{1,2},{2,3},{3,0},{4,5},{5,6},{6,7},{7,4},{8,9},{9,10},{10,1... | collective-permute-start | bytes 786440 | tf_op jit(solution)/shard_map/ppermute | solution.py:733
  (2 other events, 1.4 us)

commit v15 on v11

--- a/solution.py
+++ b/solution.py
@@ -334,31 +334,37 @@
     def present(group):
         return jnp.abs(mine - group) <= hops
 
-    def block(queries_at, keys_at, head, causal=None):
-        return pair(
-            proj_ref[rows_of(queries_at, count), head_columns(head)],
-            proj_ref[rows_of(keys_at, count), head_columns(head, 1)],
-            proj_ref[rows_of(keys_at, count), head_columns(head, 2)],
-            causal,
-        )
-
-    @pl.loop(0, n_mem)
-    def _(group):
-        @pl.when(present(group))
-        def _():
-            for head in range(HEADS):
-                intra_ref[rows_of(group, count), head_columns(head)] = block(
-                    group, group, head, triangle(count)
+    def queries_of(group, first):
+        here = slice(group * count, (group + 1) * count)
+        before = slice(first * count, group * count)
+        causal = triangle(count)
+        for head in range(HEADS):
+            queries = proj_ref[here, head_columns(head)]
+            summed = pair(
+                queries,
+                proj_ref[here, head_columns(head, 1)],
+                proj_ref[here, head_columns(head, 2)],
+                causal,
+            )
+            if first < group:
+                summed += pair(
+                    queries,
+                    proj_ref[before, head_columns(head, 1)],
+                    proj_ref[before, head_columns(head, 2)],
                 )
-
-        @pl.loop(0, group)
-        def _(other):
-            @pl.when(present(group) & present(other))
-            def _():
-                for head in range(HEADS):
-                    intra_ref[rows_of(group, count), head_columns(head)] += block(
-                        group, other, head
-                    )
+            intra_ref[here, head_columns(head)] = summed
+
+    for group in range(n_mem):
+
+        @pl.when(present(group) & (mine < n_mem - 1))
+        def _(group=group):
+            queries_of(group, 0)
+
+        if group:
+
+            @pl.when(mine == n_mem - 1)
+            def _(group=group):
+                queries_of(group, 1)
 
 
 def last_keys_body(n_mem, above_ref, below_ref, routes_ref, weight_ref, before_ref, *refs):

time: 95.1 us -> 93.4 us (0.982)
  Pallas kernels: 19.8 us -> 17.4 us
  starting transfers between devices: 37.4 us -> 39.6 us
  waiting for transfers between devices: 30.8 us -> 29.5 us
    pallas_call x1, Pallas kernels: 8.17 us -> 5.94 us  [dense_shards(): kernel_call(functools.partial(arrivals_body, n_mem, 3, early, True), 'mid...]
    ppermute x3, starting transfers between devices: 4.74 us -> 6.92 us  [dense_shards(): lax.ppermute(part, 'mem', [(i, (i + shift) % n_mem) for i in range(n_mem)])]
    ppermute x3, waiting for transfers between devices: 20.5 us -> 19 us  [dense_shards(): lax.ppermute(part, 'mem', [(i, (i + shift) % n_mem) for i in range(n_mem)])]
  transfers between devices with their start and end apart: 21 -> 21, of which waited for: 6 -> 6; matrix products, arithmetic and copies ran while one was open for 0% -> 0% of each run, Pallas kernels for 20% -> 17%
where the time goes in v15:
time: 93.4 us; the launch traced here: 92.3 us
  starting transfers between devices  39.6 us (42%)
  waiting for transfers between devices  29.5 us (32%)
  Pallas kernels  17.4 us (19%)
  local copies, waits for them, and re-layouts  5.43 us (6%)
    ppermute x3, waiting for transfers between devices, dense_shards(): lax.ppermute(part, 'mem', [(i, (i + shift) % n_mem) for i in range(n_mem)])  19 us
    ppermute x3, starting transfers between devices, dense_shards(): lax.ppermute(part, 'mem', [(i, (i + shift) % n_mem) for i in range(n_mem)])  6.92 us
    pallas_call x1, Pallas kernels, dense_shards(): kernel_call(functools.partial(arrivals_body, n_mem, 3, early, True), 'mid...  5.94 us
    unnamed x10, local copies, waits for them, and re-layouts  5.43 us
    ppermute x3, waiting for transfers between devices, dense_shards(): lax.ppermute(packed[s], 'mem', [(i, (i + s) % n_mem) for i in range(n_mem)])  5.1 us
    ppermute x2, waiting for transfers between devices, dense_shards(): got = lax.ppermute(sent, 'ctx', [(i, i ^ bit) for i in range(n_ctx)])  4.81 us
    ppermute x1, starting transfers between devices, dense_shards(): lax.ppermute(of_core, 'ctx', [(i, i ^ 1) for i in range(n_ctx)])  4.08 us
    pallas_call x1, Pallas kernels, dense_shards(): kernel_call(functools.partial(arrivals_body, n_mem, 0, 3, False), 'near_r...  3.87 us
  transfers between devices with their start and end apart: 21, of which 6 were waited for; matrix products, arithmetic and copies ran while one was open for 0% of the time, Pallas kernels for 17%

profile of v15, /device:TPU:9, one launch (start us, length us, event | category | flops | bytes accessed | tf_op | source)
XLA Modules:
  0.0 92.3 jit_solution(3979385654637769866)
XLA Ops:
  0.0 3.2 %collective-permute-start = (bf16[256,1024]{1,0:T(8,128)(2,1)}, bf16[256,1024]{1,0:T(8,128)(2,1)S(1)}, u32[]{:S(2)}, u32[]{:S(2)}) collective-permute-start(bf16[256,1024]{1,0:T(8,128)(2,1)} %refs_0_.1), channel_id=1, source_target_pairs={{0,1},{1,2},{2,3},{4,5},{5,6},{6,7},{8,9},{9,10},{10,11},{12,13},{... | collective-permute-start | bytes 1572872 | tf_op jit(solution)/shard_map/ppermute | solution.py:579
  3.2 2.1 %collective-permute-start.1 = (bf16[256,1024]{1,0:T(8,128)(2,1)}, bf16[256,1024]{1,0:T(8,128)(2,1)S(1)}, u32[]{:S(2)}, u32[]{:S(2)}) collective-permute-start(bf16[256,1024]{1,0:T(8,128)(2,1)} %refs_0_.1), channel_id=1, source_target_pairs={{3,2},{2,1},{1,0},{7,6},{6,5},{5,4},{11,10},{10,9},{9,8},{15,14},{... | collective-permute-start | bytes 1572872 | tf_op jit(solution)/shard_map/ppermute | solution.py:580
  7.3 1.3 %collective-permute-start.2 = (bf16[48,384]{1,0:T(8,128)(2,1)S(1)}, bf16[48,384]{1,0:T(8,128)(2,1)S(1)}, u32[]{:S(2)}, u32[]{:S(2)}) collective-permute-start(bf16[48,384]{1,0:T(8,128)(2,1)S(1)} %get-tuple-element.66), channel_id=1, source_target_pairs={{0,1},{1,2},{2,3},{3,0},{4,5},{5,6},{6,7},{7,4},{8,9},{9,10},{10,1... | collective-permute-start | bytes 110600 | tf_op jit(solution)/shard_map/ppermute | solution.py:594
  9.7 1.4 %collective-permute-start.4 = (bf16[48,384]{1,0:T(8,128)(2,1)S(1)}, bf16[48,384]{1,0:T(8,128)(2,1)S(1)}, u32[]{:S(2)}, u32[]{:S(2)}) collective-permute-start(bf16[48,384]{1,0:T(8,128)(2,1)S(1)} %get-tuple-element.68), channel_id=1, source_target_pairs={{0,3},{1,0},{2,1},{3,2},{4,7},{5,4},{6,5},{7,6},{8,11},{9,8},{10,9... | collective-permute-start | bytes 110600 | tf_op jit(solution)/shard_map/ppermute | solution.py:594
  11.1 1.9 %copy-done = bf16[1,1024,1536]{2,1,0:T(8,128)(2,1)S(1)} copy-done((bf16[1,1024,1536]{2,1,0:T(8,128)(2,1)S(1)}, bf16[1,1024,1536]{2,1,0:T(8,128)(2,1)}, u32[]{:S(2)}) %copy-start) | copy-done | bytes 3145752
  15.7 4.4 %collective-permute-done.3.refs_2_ = bf16[48,384]{1,0:T(8,128)(2,1)S(1)} collective-permute-done((bf16[48,384]{1,0:T(8,128)(2,1)S(1)}, bf16[48,384]{1,0:T(8,128)(2,1)S(1)}, u32[]{:S(2)}, u32[]{:S(2)}) %collective-permute-start.3) | collective-permute-done | bytes 36896 | tf_op jit(solution)/shard_map/ppermute | solution.py:594
  20.1 2.3 %collective-permute-start.5 = (bf16[256,1024]{1,0:T(8,128)(2,1)S(1)}, bf16[256,1024]{1,0:T(8,128)(2,1)S(1)}, u32[]{:S(2)}, u32[]{:S(2)}) collective-permute-start(bf16[256,1024]{1,0:T(8,128)(2,1)S(1)} %collective-permute-done.1.refs_2_), channel_id=1, source_target_pairs={{2,1},{1,0},{6,5},{5,4},{10,9},{9,8},{14,13},{13,12},{18,17},{17,1... | collective-permute-start | bytes 1572872 | tf_op jit(solution)/shard_map/ppermute | solution.py:581
  22.5 3.0 %collective-permute-start.6 = (bf16[256,1024]{1,0:T(8,128)(2,1)S(1)}, bf16[256,1024]{1,0:T(8,128)(2,1)S(1)}, u32[]{:S(2)}, u32[]{:S(2)}) collective-permute-start(bf16[256,1024]{1,0:T(8,128)(2,1)S(1)} %collective-permute-done.refs_1_), channel_id=1, source_target_pairs={{1,2},{2,3},{5,6},{6,7},{9,10},{10,11},{13,14},{14,15},{17,18},{18... | collective-permute-start | bytes 1572872 | tf_op jit(solution)/shard_map/ppermute | solution.py:582
  25.5 1.3 %collective-permute-start.7 = (bf16[4,32,384]{2,1,0:T(8,128)(2,1)S(1)}, bf16[4,32,384]{2,1,0:T(8,128)(2,1)S(1)}, u32[]{:S(2)}, u32[]{:S(2)}) collective-permute-start(bf16[4,32,384]{2,1,0:T(8,128)(2,1)S(1)} %get-tuple-element.80.refs_0_), channel_id=1, source_target_pairs={{0,8},{4,12},{8,16},{12,20},{16,24},{20,28},{24,0},{28,4},{1,9},{5... | collective-permute-start | bytes 294920 | tf_op jit(solution)/shard_map/ppermute | solution.py:634
  26.8 1.2 %collective-permute-start.8 = (bf16[4,32,384]{2,1,0:T(8,128)(2,1)S(1)}, bf16[4,32,384]{2,1,0:T(8,128)(2,1)S(1)}, u32[]{:S(2)}, u32[]{:S(2)}) collective-permute-start(bf16[4,32,384]{2,1,0:T(8,128)(2,1)S(1)} %get-tuple-element.80.refs_0_), channel_id=1, source_target_pairs={{0,16},{4,20},{8,24},{12,28},{16,0},{20,4},{24,8},{28,12},{1,17},{... | collective-permute-start | bytes 294920 | tf_op jit(solution)/shard_map/ppermute | solution.py:634
  28.0 1.2 %collective-permute-start.9 = (bf16[4,32,384]{2,1,0:T(8,128)(2,1)S(1)}, bf16[4,32,384]{2,1,0:T(8,128)(2,1)S(1)}, u32[]{:S(2)}, u32[]{:S(2)}) collective-permute-start(bf16[4,32,384]{2,1,0:T(8,128)(2,1)S(1)} %get-tuple-element.80.refs_0_), channel_id=1, source_target_pairs={{0,24},{4,28},{8,0},{12,4},{16,8},{20,12},{24,16},{28,20},{1,25},{... | collective-permute-start | bytes 294920 | tf_op jit(solution)/shard_map/ppermute | solution.py:634
  29.1 3.9 %near_rows.1 = (bf16[1024,1536]{1,0:T(8,128)(2,1)S(1)}, f32[1024,128]{1,0:T(8,128)S(1)}, f32[512,128]{1,0:T(8,128)S(1)}) custom-call(bf16[256,1024]{1,0:T(8,128)(2,1)S(1)} %get-tuple-element.76.refs_0_, bf16[256,1024]{1,0:T(8,128)(2,1)S(1)} %collective-permute-done.refs_1_, bf16[256,1024]{1,0:T(8,128)(2,1)S(1)} %collective-permute-done.1.refs_2_, ...), custom_call_target="tpu_custom_call" | custom-call | flops 2415919104 | bytes 6291456 | tf_op jit(solution)/shard_map/near_rows/pallas_call | solution.py:625
  33.7 1.3 %collective-permute-start.10 = (bf16[256,1024]{1,0:T(8,128)(2,1)S(1)}, bf16[256,1024]{1,0:T(8,128)(2,1)S(1)}, u32[]{:S(2)}, u32[]{:S(2)}) collective-permute-start(bf16[256,1024]{1,0:T(8,128)(2,1)S(1)} %collective-permute-done.5.refs_0_.refs_3_), channel_id=1, source_target_pairs={{1,0},{5,4},{9,8},{13,12},{17,16},{21,20},{25,24},{29,28}} | collective-permute-start | bytes 1572872 | tf_op jit(solution)/shard_map/ppermute | solution.py:581
  35.7 4.1 %collective-permute-start.12 = (bf16[4,4,32,384]{3,2,1,0:T(8,128)(2,1)S(1)}, bf16[4,4,32,384]{3,2,1,0:T(8,128)(2,1)S(1)}, u32[]{:S(2)}, u32[]{:S(2)}) collective-permute-start(bf16[4,4,32,384]{3,2,1,0:T(8,128)(2,1)S(1)} %combine.1.refs_5_), channel_id=1, source_target_pairs={{0,4},{4,0},{8,12},{12,8},{16,20},{20,16},{24,28},{28,24},{1,5},{5... | collective-permute-start | bytes 1179656 | tf_op jit(solution)/shard_map/ppermute | solution.py:646
  39.8 5.9 %middle_rows.1 = (bf16[1024,1536]{1,0:T(8,128)(2,1)S(1)}, f32[1024,128]{1,0:T(8,128)S(1)}, f32[512,128]{1,0:T(8,128)S(1)}, f32[1024,512]{1,0:T(8,128)S(1)}) custom-call(bf16[256,1024]{1,0:T(8,128)(2,1)S(1)} %collective-permute-done.5.refs_0_.refs_3_, bf16[256,1024]{1,0:T(8,128)(2,1)S(1)} %collective-permute-done.6.refs_1_.refs_4_, ...), custom_call_target="tpu_custom_call" | custom-call | flops 2415919104 | bytes 6291456 | tf_op jit(solution)/shard_map/middle_rows/pallas_call | solution.py:652
  45.7 1.9 %window_early.1 = (bf16[1024,384]{1,0:T(8,128)(2,1)S(1)}, bf16[1024,384]{1,0:T(8,128)(2,1)S(1)}, bf16[512,256]{1,0:T(8,128)(2,1)S(1)}) custom-call(bf16[256,1024]{1,0:T(8,128)(2,1)S(1)} %get-tuple-element.76.refs_0_, bf16[256,1024]{1,0:T(8,128)(2,1)S(1)} %collective-permute-done.refs_1_, bf16[256,1024]{1,0:T(8,128)(2,1)S(1)} %collective-permute-done.1.refs_2_, ...), custom_call_target="tpu_custom_call" | custom-call | flops 805306368 | bytes 5242880 | tf_op jit(solution)/shard_map/window_early/pallas_call | solution.py:659
  47.6 3.1 %collective-permute-start.13 = (bf16[512,128]{1,0:T(8,128)(2,1)S(1)}, bf16[512,128]{1,0:T(8,128)(2,1)S(1)}, u32[]{:S(2)}, u32[]{:S(2)}) collective-permute-start(bf16[512,128]{1,0:T(8,128)(2,1)S(1)} %get-tuple-element.99), channel_id=1, source_target_pairs={{0,16},{4,20},{8,24},{12,28},{1,17},{5,21},{9,25},{13,29},{2,18},{... | collective-permute-start | bytes 393224 | tf_op jit(solution)/shard_map/ppermute | solution.py:684
  50.8 3.3 %collective-permute-start.15 = (bf16[512,256]{1,0:T(8,128)(2,1)S(1)}, bf16[512,256]{1,0:T(8,128)(2,1)S(1)}, u32[]{:S(2)}, u32[]{:S(2)}) collective-permute-start(bf16[512,256]{1,0:T(8,128)(2,1)S(1)} %get-tuple-element.114), channel_id=1, source_target_pairs={{0,4},{4,8},{8,12},{12,16},{16,20},{20,24},{24,28},{1,5},{5,9},{9,... | collective-permute-start | bytes 786440 | tf_op jit(solution)/shard_map/ppermute | solution.py:21
  55.8 4.8 %collective-permute-done.14.refs_1_ = bf16[512,128]{1,0:T(8,128)(2,1)S(1)} collective-permute-done((bf16[512,128]{1,0:T(8,128)(2,1)S(1)}, bf16[512,128]{1,0:T(8,128)(2,1)S(1)}, u32[]{:S(2)}, u32[]{:S(2)}) %collective-permute-start.14) | collective-permute-done | bytes 131104 | tf_op jit(solution)/shard_map/ppermute | solution.py:698
  61.2 2.3 %window_attend.1.refs_6_ = f32[1024,128]{1,0:T(8,128)S(1)} custom-call(bf16[1024,384]{1,0:T(8,128)(2,1)S(1)} %get-tuple-element.113.win_ref, bf16[512,256]{1,0:T(8,128)(2,1)S(1)} %collective-permute-done.15.halo_ref, bf16[256,256]{1,0:T(8,128)(2,1)S(1)} %collective-permute-done.16.late_ref), custom_call_target="tpu_custom_call" | custom-call | flops 402653184 | bytes 3145728 | tf_op jit(solution)/shard_map/window_attend/pallas_call | solution.py:711
  64.0 5.4 %collective-permute-start.20 = (bf16[256,512]{1,0:T(8,128)(2,1)S(1)}, bf16[256,512]{1,0:T(8,128)(2,1)S(1)}, u32[]{:S(2)}, u32[]{:S(2)}) collective-permute-start(bf16[256,512]{1,0:T(8,128)(2,1)S(1)} %finish2.1), channel_id=1, source_target_pairs={{0,2},{1,3},{2,0},{3,1},{4,6},{5,7},{6,4},{7,5},{8,10},{9,11},{10,... | collective-permute-start | bytes 786440 | tf_op jit(solution)/shard_map/ppermute | solution.py:738
  70.5 1.5 %collective-permute-start.18 = (bf16[256,512]{1,0:T(8,128)(2,1)S(1)}, bf16[256,512]{1,0:T(8,128)(2,1)S(1)}, u32[]{:S(2)}, u32[]{:S(2)}) collective-permute-start(bf16[256,512]{1,0:T(8,128)(2,1)S(1)} %finish1.1), channel_id=1, source_target_pairs={{0,1},{1,2},{2,3},{3,0},{4,5},{5,6},{6,7},{7,4},{8,9},{9,10},{10,1... | collective-permute-start | bytes 786440 | tf_op jit(solution)/shard_map/ppermute | solution.py:738
  72.4 13.0 %collective-permute-done.20.refs_3_ = bf16[256,512]{1,0:T(8,128)(2,1)S(1)} collective-permute-done((bf16[256,512]{1,0:T(8,128)(2,1)S(1)}, bf16[256,512]{1,0:T(8,128)(2,1)S(1)}, u32[]{:S(2)}, u32[]{:S(2)}) %collective-permute-start.20) | collective-permute-done | bytes 262176 | tf_op jit(solution)/shard_map/ppermute | solution.py:738
  85.4 6.1 %collective-permute-done.19.refs_2_ = bf16[256,512]{1,0:T(8,128)(2,1)S(1)} collective-permute-done((bf16[256,512]{1,0:T(8,128)(2,1)S(1)}, bf16[256,512]{1,0:T(8,128)(2,1)S(1)}, u32[]{:S(2)}, u32[]{:S(2)}) %collective-permute-start.19) | collective-permute-done | bytes 262176 | tf_op jit(solution)/shard_map/ppermute | solution.py:738
  (46 shorter events, 12.1 us)
Async XLA Ops:
  0.0 20.1 %collective-permute-start = (bf16[256,1024]{1,0:T(8,128)(2,1)}, bf16[256,1024]{1,0:T(8,128)(2,1)S(1)}, u32[]{:S(2)}, u32[]{:S(2)}) collective-permute-start(bf16[256,1024]{1,0:T(8,128)(2,1)} %refs_0_.1), channel_id=1, source_target_pairs={{0,1},{1,2},{2,3},{4,5},{5,6},{6,7},{8,9},{9,10},{10,11},{12,13},{... | collective-permute-start | bytes 1572872 | tf_op jit(solution)/shard_map/ppermute | solution.py:579
  3.2 16.9 %collective-permute-start.1 = (bf16[256,1024]{1,0:T(8,128)(2,1)}, bf16[256,1024]{1,0:T(8,128)(2,1)S(1)}, u32[]{:S(2)}, u32[]{:S(2)}) collective-permute-start(bf16[256,1024]{1,0:T(8,128)(2,1)} %refs_0_.1), channel_id=1, source_target_pairs={{3,2},{2,1},{1,0},{7,6},{6,5},{5,4},{11,10},{10,9},{9,8},{15,14},{... | collective-permute-start | bytes 1572872 | tf_op jit(solution)/shard_map/ppermute | solution.py:580
  5.3 1.1 %copy-start.1 = (bf16[256,1536]{1,0:T(8,128)(2,1)S(1)}, bf16[256,1536]{1,0:T(8,128)(2,1)}, u32[]{:S(2)}) copy-start(bf16[256,1536]{1,0:T(8,128)(2,1)} %weight_ref.1) | copy-start | bytes 2359300
  7.3 8.4 %collective-permute-start.2 = (bf16[48,384]{1,0:T(8,128)(2,1)S(1)}, bf16[48,384]{1,0:T(8,128)(2,1)S(1)}, u32[]{:S(2)}, u32[]{:S(2)}) collective-permute-start(bf16[48,384]{1,0:T(8,128)(2,1)S(1)} %get-tuple-element.66), channel_id=1, source_target_pairs={{0,1},{1,2},{2,3},{3,0},{4,5},{5,6},{6,7},{7,4},{8,9},{9,10},{10,1... | collective-permute-start | bytes 110600 | tf_op jit(solution)/shard_map/ppermute | solution.py:594
  8.6 11.5 %collective-permute-start.3 = (bf16[48,384]{1,0:T(8,128)(2,1)S(1)}, bf16[48,384]{1,0:T(8,128)(2,1)S(1)}, u32[]{:S(2)}, u32[]{:S(2)}) collective-permute-start(bf16[48,384]{1,0:T(8,128)(2,1)S(1)} %get-tuple-element.67), channel_id=1, source_target_pairs={{0,2},{1,3},{2,0},{3,1},{4,6},{5,7},{6,4},{7,5},{8,10},{9,11},{10,... | collective-permute-start | bytes 110600 | tf_op jit(solution)/shard_map/ppermute | solution.py:594
  9.7 10.4 %collective-permute-start.4 = (bf16[48,384]{1,0:T(8,128)(2,1)S(1)}, bf16[48,384]{1,0:T(8,128)(2,1)S(1)}, u32[]{:S(2)}, u32[]{:S(2)}) collective-permute-start(bf16[48,384]{1,0:T(8,128)(2,1)S(1)} %get-tuple-element.68), channel_id=1, source_target_pairs={{0,3},{1,0},{2,1},{3,2},{4,7},{5,4},{6,5},{7,6},{8,11},{9,8},{10,9... | collective-permute-start | bytes 110600 | tf_op jit(solution)/shard_map/ppermute | solution.py:594
  11.1 1.9 %copy-start = (bf16[1,1024,1536]{2,1,0:T(8,128)(2,1)S(1)}, bf16[1,1024,1536]{2,1,0:T(8,128)(2,1)}, u32[]{:S(2)}) copy-start(bf16[1,1024,1536]{2,1,0:T(8,128)(2,1)} %param.8) | copy-start | bytes 9437188
  13.0 1.0 %copy-start.2 = (bf16[256,1024]{1,0:T(8,128)(2,1)S(1)}, bf16[256,1024]{1,0:T(8,128)(2,1)}, u32[]{:S(2)}) copy-start(bf16[256,1024]{1,0:T(8,128)(2,1)} %refs_0_.1) | copy-start | bytes 1572868
  20.1 13.0 %collective-permute-start.5 = (bf16[256,1024]{1,0:T(8,128)(2,1)S(1)}, bf16[256,1024]{1,0:T(8,128)(2,1)S(1)}, u32[]{:S(2)}, u32[]{:S(2)}) collective-permute-start(bf16[256,1024]{1,0:T(8,128)(2,1)S(1)} %collective-permute-done.1.refs_2_), channel_id=1, source_target_pairs={{2,1},{1,0},{6,5},{5,4},{10,9},{9,8},{14,13},{13,12},{18,17},{17,1... | collective-permute-start | bytes 1572872 | tf_op jit(solution)/shard_map/ppermute | solution.py:581
  22.5 11.2 %collective-permute-start.6 = (bf16[256,1024]{1,0:T(8,128)(2,1)S(1)}, bf16[256,1024]{1,0:T(8,128)(2,1)S(1)}, u32[]{:S(2)}, u32[]{:S(2)}) collective-permute-start(bf16[256,1024]{1,0:T(8,128)(2,1)S(1)} %collective-permute-done.refs_1_), channel_id=1, source_target_pairs={{1,2},{2,3},{5,6},{6,7},{9,10},{10,11},{13,14},{14,15},{17,18},{18... | collective-permute-start | bytes 1572872 | tf_op jit(solution)/shard_map/ppermute | solution.py:582
  25.5 7.5 %collective-permute-start.7 = (bf16[4,32,384]{2,1,0:T(8,128)(2,1)S(1)}, bf16[4,32,384]{2,1,0:T(8,128)(2,1)S(1)}, u32[]{:S(2)}, u32[]{:S(2)}) collective-permute-start(bf16[4,32,384]{2,1,0:T(8,128)(2,1)S(1)} %get-tuple-element.80.refs_0_), channel_id=1, source_target_pairs={{0,8},{4,12},{8,16},{12,20},{16,24},{20,28},{24,0},{28,4},{1,9},{5... | collective-permute-start | bytes 294920 | tf_op jit(solution)/shard_map/ppermute | solution.py:634
  26.8 6.3 %collective-permute-start.8 = (bf16[4,32,384]{2,1,0:T(8,128)(2,1)S(1)}, bf16[4,32,384]{2,1,0:T(8,128)(2,1)S(1)}, u32[]{:S(2)}, u32[]{:S(2)}) collective-permute-start(bf16[4,32,384]{2,1,0:T(8,128)(2,1)S(1)} %get-tuple-element.80.refs_0_), channel_id=1, source_target_pairs={{0,16},{4,20},{8,24},{12,28},{16,0},{20,4},{24,8},{28,12},{1,17},{... | collective-permute-start | bytes 294920 | tf_op jit(solution)/shard_map/ppermute | solution.py:634
  28.0 5.1 %collective-permute-start.9 = (bf16[4,32,384]{2,1,0:T(8,128)(2,1)S(1)}, bf16[4,32,384]{2,1,0:T(8,128)(2,1)S(1)}, u32[]{:S(2)}, u32[]{:S(2)}) collective-permute-start(bf16[4,32,384]{2,1,0:T(8,128)(2,1)S(1)} %get-tuple-element.80.refs_0_), channel_id=1, source_target_pairs={{0,24},{4,28},{8,0},{12,4},{16,8},{20,12},{24,16},{28,20},{1,25},{... | collective-permute-start | bytes 294920 | tf_op jit(solution)/shard_map/ppermute | solution.py:634
  33.7 13.9 %collective-permute-start.10 = (bf16[256,1024]{1,0:T(8,128)(2,1)S(1)}, bf16[256,1024]{1,0:T(8,128)(2,1)S(1)}, u32[]{:S(2)}, u32[]{:S(2)}) collective-permute-start(bf16[256,1024]{1,0:T(8,128)(2,1)S(1)} %collective-permute-done.5.refs_0_.refs_3_), channel_id=1, source_target_pairs={{1,0},{5,4},{9,8},{13,12},{17,16},{21,20},{25,24},{29,28}} | collective-permute-start | bytes 1572872 | tf_op jit(solution)/shard_map/ppermute | solution.py:581
  35.0 12.6 %collective-permute-start.11 = (bf16[256,1024]{1,0:T(8,128)(2,1)S(1)}, bf16[256,1024]{1,0:T(8,128)(2,1)S(1)}, u32[]{:S(2)}, u32[]{:S(2)}) collective-permute-start(bf16[256,1024]{1,0:T(8,128)(2,1)S(1)} %collective-permute-done.6.refs_1_.refs_4_), channel_id=1, source_target_pairs={{2,3},{6,7},{10,11},{14,15},{18,19},{22,23},{26,27},{30,31}} | collective-permute-start | bytes 1572872 | tf_op jit(solution)/shard_map/ppermute | solution.py:582
  35.7 10.0 %collective-permute-start.12 = (bf16[4,4,32,384]{3,2,1,0:T(8,128)(2,1)S(1)}, bf16[4,4,32,384]{3,2,1,0:T(8,128)(2,1)S(1)}, u32[]{:S(2)}, u32[]{:S(2)}) collective-permute-start(bf16[4,4,32,384]{3,2,1,0:T(8,128)(2,1)S(1)} %combine.1.refs_5_), channel_id=1, source_target_pairs={{0,4},{4,0},{8,12},{12,8},{16,20},{20,16},{24,28},{28,24},{1,5},{5... | collective-permute-start | bytes 1179656 | tf_op jit(solution)/shard_map/ppermute | solution.py:646
  47.6 6.5 %collective-permute-start.13 = (bf16[512,128]{1,0:T(8,128)(2,1)S(1)}, bf16[512,128]{1,0:T(8,128)(2,1)S(1)}, u32[]{:S(2)}, u32[]{:S(2)}) collective-permute-start(bf16[512,128]{1,0:T(8,128)(2,1)S(1)} %get-tuple-element.99), channel_id=1, source_target_pairs={{0,16},{4,20},{8,24},{12,28},{1,17},{5,21},{9,25},{13,29},{2,18},{... | collective-permute-start | bytes 393224 | tf_op jit(solution)/shard_map/ppermute | solution.py:684
  50.8 10.4 %collective-permute-start.15 = (bf16[512,256]{1,0:T(8,128)(2,1)S(1)}, bf16[512,256]{1,0:T(8,128)(2,1)S(1)}, u32[]{:S(2)}, u32[]{:S(2)}) collective-permute-start(bf16[512,256]{1,0:T(8,128)(2,1)S(1)} %get-tuple-element.114), channel_id=1, source_target_pairs={{0,4},{4,8},{8,12},{12,16},{16,20},{20,24},{24,28},{1,5},{5,9},{9,... | collective-permute-start | bytes 786440 | tf_op jit(solution)/shard_map/ppermute | solution.py:21
  54.2 6.5 %collective-permute-start.14 = (bf16[512,128]{1,0:T(8,128)(2,1)S(1)}, bf16[512,128]{1,0:T(8,128)(2,1)S(1)}, u32[]{:S(2)}, u32[]{:S(2)}) collective-permute-start(bf16[512,128]{1,0:T(8,128)(2,1)S(1)} %get-tuple-element.101), channel_id=1, source_target_pairs={{0,8},{4,12},{8,0},{12,4},{16,24},{20,28},{24,16},{28,20},{1,9},{5... | collective-permute-start | bytes 393224 | tf_op jit(solution)/shard_map/ppermute | solution.py:698
  55.1 6.0 %collective-permute-start.16 = (bf16[256,256]{1,0:T(8,128)(2,1)S(1)}, bf16[256,256]{1,0:T(8,128)(2,1)S(1)}, u32[]{:S(2)}, u32[]{:S(2)}) collective-permute-start(bf16[256,256]{1,0:T(8,128)(2,1)S(1)} %get-tuple-element.115), channel_id=1, source_target_pairs={{0,4},{4,8},{8,12},{12,16},{16,20},{20,24},{24,28}} | collective-permute-start | bytes 393224 | tf_op jit(solution)/shard_map/ppermute | solution.py:709
  60.7 2.8 %collective-permute-start.17 = (bf16[512,128]{1,0:T(8,128)(2,1)S(1)}, bf16[512,128]{1,0:T(8,128)(2,1)S(1)}, u32[]{:S(2)}, u32[]{:S(2)}) collective-permute-start(bf16[512,128]{1,0:T(8,128)(2,1)S(1)} %get-tuple-element.118), channel_id=1, source_target_pairs={{0,4},{4,0},{8,12},{12,8},{16,20},{20,16},{24,28},{28,24},{1,5},{5... | collective-permute-start | bytes 393224 | tf_op jit(solution)/shard_map/ppermute | solution.py:698
  64.0 21.3 %collective-permute-start.20 = (bf16[256,512]{1,0:T(8,128)(2,1)S(1)}, bf16[256,512]{1,0:T(8,128)(2,1)S(1)}, u32[]{:S(2)}, u32[]{:S(2)}) collective-permute-start(bf16[256,512]{1,0:T(8,128)(2,1)S(1)} %finish2.1), channel_id=1, source_target_pairs={{0,2},{1,3},{2,0},{3,1},{4,6},{5,7},{6,4},{7,5},{8,10},{9,11},{10,... | collective-permute-start | bytes 786440 | tf_op jit(solution)/shard_map/ppermute | solution.py:738
  69.9 21.5 %collective-permute-start.19 = (bf16[256,512]{1,0:T(8,128)(2,1)S(1)}, bf16[256,512]{1,0:T(8,128)(2,1)S(1)}, u32[]{:S(2)}, u32[]{:S(2)}) collective-permute-start(bf16[256,512]{1,0:T(8,128)(2,1)S(1)} %finish3.1), channel_id=1, source_target_pairs={{0,3},{1,0},{2,1},{3,2},{4,7},{5,4},{6,5},{7,6},{8,11},{9,8},{10,9... | collective-permute-start | bytes 786440 | tf_op jit(solution)/shard_map/ppermute | solution.py:738
  70.5 21.0 %collective-permute-start.18 = (bf16[256,512]{1,0:T(8,128)(2,1)S(1)}, bf16[256,512]{1,0:T(8,128)(2,1)S(1)}, u32[]{:S(2)}, u32[]{:S(2)}) collective-permute-start(bf16[256,512]{1,0:T(8,128)(2,1)S(1)} %finish1.1), channel_id=1, source_target_pairs={{0,1},{1,2},{2,3},{3,0},{4,5},{5,6},{6,7},{7,4},{8,9},{9,10},{10,1... | collective-permute-start | bytes 786440 | tf_op jit(solution)/shard_map/ppermute | solution.py:738
  (2 other events, 1.4 us)

commit v16 on v15

--- a/solution.py
+++ b/solution.py
@@ -498,7 +498,8 @@
         masked = jnp.where(allowed, scores, -1e30)
         highest = jnp.max(masked, axis=-1, keepdims=True)
         expo = jnp.exp(masked - highest)
-        probs = (expo / jnp.sum(expo, axis=-1, keepdims=True)).astype(jnp.bfloat16)
+        share = 1.0 / jnp.sum(expo, axis=-1, keepdims=True)
+        probs = (expo * share).astype(jnp.bfloat16)
         out_ref[start : start + count, :] = jnp.dot(
             probs, values, preferred_element_type=jnp.float32
         )

time: 93.4 us -> 93.4 us (level)
  no operation moved by 1% of the time
where the time goes in v16:
time: 93.4 us; the launch traced here: 92.3 us
  starting transfers between devices  39.6 us (42%)
  waiting for transfers between devices  29.5 us (32%)
  Pallas kernels  17.4 us (19%)
  local copies, waits for them, and re-layouts  5.43 us (6%)
    ppermute x3, waiting for transfers between devices, dense_shards(): lax.ppermute(part, 'mem', [(i, (i + shift) % n_mem) for i in range(n_mem)])  19 us
    ppermute x3, starting transfers between devices, dense_shards(): lax.ppermute(part, 'mem', [(i, (i + shift) % n_mem) for i in range(n_mem)])  6.92 us
    pallas_call x1, Pallas kernels, dense_shards(): kernel_call(functools.partial(arrivals_body, n_mem, 3, early, True), 'mid...  5.94 us
    unnamed x10, local copies, waits for them, and re-layouts  5.43 us
    ppermute x3, waiting for transfers between devices, dense_shards(): lax.ppermute(packed[s], 'mem', [(i, (i + s) % n_mem) for i in range(n_mem)])  5.1 us
    ppermute x2, waiting for transfers between devices, dense_shards(): got = lax.ppermute(sent, 'ctx', [(i, i ^ bit) for i in range(n_ctx)])  4.81 us
    ppermute x1, starting transfers between devices, dense_shards(): lax.ppermute(of_core, 'ctx', [(i, i ^ 1) for i in range(n_ctx)])  4.08 us
    pallas_call x1, Pallas kernels, dense_shards(): kernel_call(functools.partial(arrivals_body, n_mem, 0, 3, False), 'near_r...  3.87 us
  transfers between devices with their start and end apart: 21, of which 6 were waited for; matrix products, arithmetic and copies ran while one was open for 0% of the time, Pallas kernels for 17%

profile of v16, /device:TPU:9, one launch (start us, length us, event | category | flops | bytes accessed | tf_op | source)
XLA Modules:
  0.0 92.3 jit_solution(3979385654637769866)
XLA Ops:
  0.0 3.2 %collective-permute-start = (bf16[256,1024]{1,0:T(8,128)(2,1)}, bf16[256,1024]{1,0:T(8,128)(2,1)S(1)}, u32[]{:S(2)}, u32[]{:S(2)}) collective-permute-start(bf16[256,1024]{1,0:T(8,128)(2,1)} %refs_0_.1), channel_id=1, source_target_pairs={{0,1},{1,2},{2,3},{4,5},{5,6},{6,7},{8,9},{9,10},{10,11},{12,13},{... | collective-permute-start | bytes 1572872 | tf_op jit(solution)/shard_map/ppermute | solution.py:580
  3.2 2.1 %collective-permute-start.1 = (bf16[256,1024]{1,0:T(8,128)(2,1)}, bf16[256,1024]{1,0:T(8,128)(2,1)S(1)}, u32[]{:S(2)}, u32[]{:S(2)}) collective-permute-start(bf16[256,1024]{1,0:T(8,128)(2,1)} %refs_0_.1), channel_id=1, source_target_pairs={{3,2},{2,1},{1,0},{7,6},{6,5},{5,4},{11,10},{10,9},{9,8},{15,14},{... | collective-permute-start | bytes 1572872 | tf_op jit(solution)/shard_map/ppermute | solution.py:581
  7.3 1.3 %collective-permute-start.2 = (bf16[48,384]{1,0:T(8,128)(2,1)S(1)}, bf16[48,384]{1,0:T(8,128)(2,1)S(1)}, u32[]{:S(2)}, u32[]{:S(2)}) collective-permute-start(bf16[48,384]{1,0:T(8,128)(2,1)S(1)} %get-tuple-element.66), channel_id=1, source_target_pairs={{0,1},{1,2},{2,3},{3,0},{4,5},{5,6},{6,7},{7,4},{8,9},{9,10},{10,1... | collective-permute-start | bytes 110600 | tf_op jit(solution)/shard_map/ppermute | solution.py:595
  9.7 1.4 %collective-permute-start.4 = (bf16[48,384]{1,0:T(8,128)(2,1)S(1)}, bf16[48,384]{1,0:T(8,128)(2,1)S(1)}, u32[]{:S(2)}, u32[]{:S(2)}) collective-permute-start(bf16[48,384]{1,0:T(8,128)(2,1)S(1)} %get-tuple-element.68), channel_id=1, source_target_pairs={{0,3},{1,0},{2,1},{3,2},{4,7},{5,4},{6,5},{7,6},{8,11},{9,8},{10,9... | collective-permute-start | bytes 110600 | tf_op jit(solution)/shard_map/ppermute | solution.py:595
  11.1 1.9 %copy-done = bf16[1,1024,1536]{2,1,0:T(8,128)(2,1)S(1)} copy-done((bf16[1,1024,1536]{2,1,0:T(8,128)(2,1)S(1)}, bf16[1,1024,1536]{2,1,0:T(8,128)(2,1)}, u32[]{:S(2)}) %copy-start) | copy-done | bytes 3145752
  15.7 4.4 %collective-permute-done.3.refs_2_ = bf16[48,384]{1,0:T(8,128)(2,1)S(1)} collective-permute-done((bf16[48,384]{1,0:T(8,128)(2,1)S(1)}, bf16[48,384]{1,0:T(8,128)(2,1)S(1)}, u32[]{:S(2)}, u32[]{:S(2)}) %collective-permute-start.3) | collective-permute-done | bytes 36896 | tf_op jit(solution)/shard_map/ppermute | solution.py:595
  20.1 2.3 %collective-permute-start.5 = (bf16[256,1024]{1,0:T(8,128)(2,1)S(1)}, bf16[256,1024]{1,0:T(8,128)(2,1)S(1)}, u32[]{:S(2)}, u32[]{:S(2)}) collective-permute-start(bf16[256,1024]{1,0:T(8,128)(2,1)S(1)} %collective-permute-done.1.refs_2_), channel_id=1, source_target_pairs={{2,1},{1,0},{6,5},{5,4},{10,9},{9,8},{14,13},{13,12},{18,17},{17,1... | collective-permute-start | bytes 1572872 | tf_op jit(solution)/shard_map/ppermute | solution.py:582
  22.5 3.0 %collective-permute-start.6 = (bf16[256,1024]{1,0:T(8,128)(2,1)S(1)}, bf16[256,1024]{1,0:T(8,128)(2,1)S(1)}, u32[]{:S(2)}, u32[]{:S(2)}) collective-permute-start(bf16[256,1024]{1,0:T(8,128)(2,1)S(1)} %collective-permute-done.refs_1_), channel_id=1, source_target_pairs={{1,2},{2,3},{5,6},{6,7},{9,10},{10,11},{13,14},{14,15},{17,18},{18... | collective-permute-start | bytes 1572872 | tf_op jit(solution)/shard_map/ppermute | solution.py:583
  25.5 1.3 %collective-permute-start.7 = (bf16[4,32,384]{2,1,0:T(8,128)(2,1)S(1)}, bf16[4,32,384]{2,1,0:T(8,128)(2,1)S(1)}, u32[]{:S(2)}, u32[]{:S(2)}) collective-permute-start(bf16[4,32,384]{2,1,0:T(8,128)(2,1)S(1)} %get-tuple-element.80.refs_0_), channel_id=1, source_target_pairs={{0,8},{4,12},{8,16},{12,20},{16,24},{20,28},{24,0},{28,4},{1,9},{5... | collective-permute-start | bytes 294920 | tf_op jit(solution)/shard_map/ppermute | solution.py:635
  26.8 1.2 %collective-permute-start.8 = (bf16[4,32,384]{2,1,0:T(8,128)(2,1)S(1)}, bf16[4,32,384]{2,1,0:T(8,128)(2,1)S(1)}, u32[]{:S(2)}, u32[]{:S(2)}) collective-permute-start(bf16[4,32,384]{2,1,0:T(8,128)(2,1)S(1)} %get-tuple-element.80.refs_0_), channel_id=1, source_target_pairs={{0,16},{4,20},{8,24},{12,28},{16,0},{20,4},{24,8},{28,12},{1,17},{... | collective-permute-start | bytes 294920 | tf_op jit(solution)/shard_map/ppermute | solution.py:635
  28.0 1.2 %collective-permute-start.9 = (bf16[4,32,384]{2,1,0:T(8,128)(2,1)S(1)}, bf16[4,32,384]{2,1,0:T(8,128)(2,1)S(1)}, u32[]{:S(2)}, u32[]{:S(2)}) collective-permute-start(bf16[4,32,384]{2,1,0:T(8,128)(2,1)S(1)} %get-tuple-element.80.refs_0_), channel_id=1, source_target_pairs={{0,24},{4,28},{8,0},{12,4},{16,8},{20,12},{24,16},{28,20},{1,25},{... | collective-permute-start | bytes 294920 | tf_op jit(solution)/shard_map/ppermute | solution.py:635
  29.1 3.9 %near_rows.1 = (bf16[1024,1536]{1,0:T(8,128)(2,1)S(1)}, f32[1024,128]{1,0:T(8,128)S(1)}, f32[512,128]{1,0:T(8,128)S(1)}) custom-call(bf16[256,1024]{1,0:T(8,128)(2,1)S(1)} %get-tuple-element.76.refs_0_, bf16[256,1024]{1,0:T(8,128)(2,1)S(1)} %collective-permute-done.refs_1_, bf16[256,1024]{1,0:T(8,128)(2,1)S(1)} %collective-permute-done.1.refs_2_, ...), custom_call_target="tpu_custom_call" | custom-call | flops 2415919104 | bytes 6291456 | tf_op jit(solution)/shard_map/near_rows/pallas_call | solution.py:626
  33.7 1.3 %collective-permute-start.10 = (bf16[256,1024]{1,0:T(8,128)(2,1)S(1)}, bf16[256,1024]{1,0:T(8,128)(2,1)S(1)}, u32[]{:S(2)}, u32[]{:S(2)}) collective-permute-start(bf16[256,1024]{1,0:T(8,128)(2,1)S(1)} %collective-permute-done.5.refs_0_.refs_3_), channel_id=1, source_target_pairs={{1,0},{5,4},{9,8},{13,12},{17,16},{21,20},{25,24},{29,28}} | collective-permute-start | bytes 1572872 | tf_op jit(solution)/shard_map/ppermute | solution.py:582
  35.7 4.1 %collective-permute-start.12 = (bf16[4,4,32,384]{3,2,1,0:T(8,128)(2,1)S(1)}, bf16[4,4,32,384]{3,2,1,0:T(8,128)(2,1)S(1)}, u32[]{:S(2)}, u32[]{:S(2)}) collective-permute-start(bf16[4,4,32,384]{3,2,1,0:T(8,128)(2,1)S(1)} %combine.1.refs_5_), channel_id=1, source_target_pairs={{0,4},{4,0},{8,12},{12,8},{16,20},{20,16},{24,28},{28,24},{1,5},{5... | collective-permute-start | bytes 1179656 | tf_op jit(solution)/shard_map/ppermute | solution.py:647
  39.8 5.9 %middle_rows.1 = (bf16[1024,1536]{1,0:T(8,128)(2,1)S(1)}, f32[1024,128]{1,0:T(8,128)S(1)}, f32[512,128]{1,0:T(8,128)S(1)}, f32[1024,512]{1,0:T(8,128)S(1)}) custom-call(bf16[256,1024]{1,0:T(8,128)(2,1)S(1)} %collective-permute-done.5.refs_0_.refs_3_, bf16[256,1024]{1,0:T(8,128)(2,1)S(1)} %collective-permute-done.6.refs_1_.refs_4_, ...), custom_call_target="tpu_custom_call" | custom-call | flops 2415919104 | bytes 6291456 | tf_op jit(solution)/shard_map/middle_rows/pallas_call | solution.py:653
  45.7 1.9 %window_early.1 = (bf16[1024,384]{1,0:T(8,128)(2,1)S(1)}, bf16[1024,384]{1,0:T(8,128)(2,1)S(1)}, bf16[512,256]{1,0:T(8,128)(2,1)S(1)}) custom-call(bf16[256,1024]{1,0:T(8,128)(2,1)S(1)} %get-tuple-element.76.refs_0_, bf16[256,1024]{1,0:T(8,128)(2,1)S(1)} %collective-permute-done.refs_1_, bf16[256,1024]{1,0:T(8,128)(2,1)S(1)} %collective-permute-done.1.refs_2_, ...), custom_call_target="tpu_custom_call" | custom-call | flops 805306368 | bytes 5242880 | tf_op jit(solution)/shard_map/window_early/pallas_call | solution.py:660
  47.6 3.1 %collective-permute-start.13 = (bf16[512,128]{1,0:T(8,128)(2,1)S(1)}, bf16[512,128]{1,0:T(8,128)(2,1)S(1)}, u32[]{:S(2)}, u32[]{:S(2)}) collective-permute-start(bf16[512,128]{1,0:T(8,128)(2,1)S(1)} %get-tuple-element.99), channel_id=1, source_target_pairs={{0,16},{4,20},{8,24},{12,28},{1,17},{5,21},{9,25},{13,29},{2,18},{... | collective-permute-start | bytes 393224 | tf_op jit(solution)/shard_map/ppermute | solution.py:685
  50.8 3.3 %collective-permute-start.15 = (bf16[512,256]{1,0:T(8,128)(2,1)S(1)}, bf16[512,256]{1,0:T(8,128)(2,1)S(1)}, u32[]{:S(2)}, u32[]{:S(2)}) collective-permute-start(bf16[512,256]{1,0:T(8,128)(2,1)S(1)} %get-tuple-element.114), channel_id=1, source_target_pairs={{0,4},{4,8},{8,12},{12,16},{16,20},{20,24},{24,28},{1,5},{5,9},{9,... | collective-permute-start | bytes 786440 | tf_op jit(solution)/shard_map/ppermute | solution.py:21
  55.8 4.8 %collective-permute-done.14.refs_1_ = bf16[512,128]{1,0:T(8,128)(2,1)S(1)} collective-permute-done((bf16[512,128]{1,0:T(8,128)(2,1)S(1)}, bf16[512,128]{1,0:T(8,128)(2,1)S(1)}, u32[]{:S(2)}, u32[]{:S(2)}) %collective-permute-start.14) | collective-permute-done | bytes 131104 | tf_op jit(solution)/shard_map/ppermute | solution.py:699
  61.2 2.3 %window_attend.1.refs_6_ = f32[1024,128]{1,0:T(8,128)S(1)} custom-call(bf16[1024,384]{1,0:T(8,128)(2,1)S(1)} %get-tuple-element.113.win_ref, bf16[512,256]{1,0:T(8,128)(2,1)S(1)} %collective-permute-done.15.halo_ref, bf16[256,256]{1,0:T(8,128)(2,1)S(1)} %collective-permute-done.16.late_ref), custom_call_target="tpu_custom_call" | custom-call | flops 402653184 | bytes 3145728 | tf_op jit(solution)/shard_map/window_attend/pallas_call | solution.py:712
  64.0 5.4 %collective-permute-start.20 = (bf16[256,512]{1,0:T(8,128)(2,1)S(1)}, bf16[256,512]{1,0:T(8,128)(2,1)S(1)}, u32[]{:S(2)}, u32[]{:S(2)}) collective-permute-start(bf16[256,512]{1,0:T(8,128)(2,1)S(1)} %finish2.1), channel_id=1, source_target_pairs={{0,2},{1,3},{2,0},{3,1},{4,6},{5,7},{6,4},{7,5},{8,10},{9,11},{10,... | collective-permute-start | bytes 786440 | tf_op jit(solution)/shard_map/ppermute | solution.py:739
  70.5 1.5 %collective-permute-start.18 = (bf16[256,512]{1,0:T(8,128)(2,1)S(1)}, bf16[256,512]{1,0:T(8,128)(2,1)S(1)}, u32[]{:S(2)}, u32[]{:S(2)}) collective-permute-start(bf16[256,512]{1,0:T(8,128)(2,1)S(1)} %finish1.1), channel_id=1, source_target_pairs={{0,1},{1,2},{2,3},{3,0},{4,5},{5,6},{6,7},{7,4},{8,9},{9,10},{10,1... | collective-permute-start | bytes 786440 | tf_op jit(solution)/shard_map/ppermute | solution.py:739
  72.4 13.0 %collective-permute-done.20.refs_3_ = bf16[256,512]{1,0:T(8,128)(2,1)S(1)} collective-permute-done((bf16[256,512]{1,0:T(8,128)(2,1)S(1)}, bf16[256,512]{1,0:T(8,128)(2,1)S(1)}, u32[]{:S(2)}, u32[]{:S(2)}) %collective-permute-start.20) | collective-permute-done | bytes 262176 | tf_op jit(solution)/shard_map/ppermute | solution.py:739
  85.4 6.1 %collective-permute-done.19.refs_2_ = bf16[256,512]{1,0:T(8,128)(2,1)S(1)} collective-permute-done((bf16[256,512]{1,0:T(8,128)(2,1)S(1)}, bf16[256,512]{1,0:T(8,128)(2,1)S(1)}, u32[]{:S(2)}, u32[]{:S(2)}) %collective-permute-start.19) | collective-permute-done | bytes 262176 | tf_op jit(solution)/shard_map/ppermute | solution.py:739
  (46 shorter events, 12.1 us)
Async XLA Ops:
  0.0 20.1 %collective-permute-start = (bf16[256,1024]{1,0:T(8,128)(2,1)}, bf16[256,1024]{1,0:T(8,128)(2,1)S(1)}, u32[]{:S(2)}, u32[]{:S(2)}) collective-permute-start(bf16[256,1024]{1,0:T(8,128)(2,1)} %refs_0_.1), channel_id=1, source_target_pairs={{0,1},{1,2},{2,3},{4,5},{5,6},{6,7},{8,9},{9,10},{10,11},{12,13},{... | collective-permute-start | bytes 1572872 | tf_op jit(solution)/shard_map/ppermute | solution.py:580
  3.2 16.9 %collective-permute-start.1 = (bf16[256,1024]{1,0:T(8,128)(2,1)}, bf16[256,1024]{1,0:T(8,128)(2,1)S(1)}, u32[]{:S(2)}, u32[]{:S(2)}) collective-permute-start(bf16[256,1024]{1,0:T(8,128)(2,1)} %refs_0_.1), channel_id=1, source_target_pairs={{3,2},{2,1},{1,0},{7,6},{6,5},{5,4},{11,10},{10,9},{9,8},{15,14},{... | collective-permute-start | bytes 1572872 | tf_op jit(solution)/shard_map/ppermute | solution.py:581
  5.3 1.1 %copy-start.1 = (bf16[256,1536]{1,0:T(8,128)(2,1)S(1)}, bf16[256,1536]{1,0:T(8,128)(2,1)}, u32[]{:S(2)}) copy-start(bf16[256,1536]{1,0:T(8,128)(2,1)} %weight_ref.1) | copy-start | bytes 2359300
  7.3 8.4 %collective-permute-start.2 = (bf16[48,384]{1,0:T(8,128)(2,1)S(1)}, bf16[48,384]{1,0:T(8,128)(2,1)S(1)}, u32[]{:S(2)}, u32[]{:S(2)}) collective-permute-start(bf16[48,384]{1,0:T(8,128)(2,1)S(1)} %get-tuple-element.66), channel_id=1, source_target_pairs={{0,1},{1,2},{2,3},{3,0},{4,5},{5,6},{6,7},{7,4},{8,9},{9,10},{10,1... | collective-permute-start | bytes 110600 | tf_op jit(solution)/shard_map/ppermute | solution.py:595
  8.6 11.5 %collective-permute-start.3 = (bf16[48,384]{1,0:T(8,128)(2,1)S(1)}, bf16[48,384]{1,0:T(8,128)(2,1)S(1)}, u32[]{:S(2)}, u32[]{:S(2)}) collective-permute-start(bf16[48,384]{1,0:T(8,128)(2,1)S(1)} %get-tuple-element.67), channel_id=1, source_target_pairs={{0,2},{1,3},{2,0},{3,1},{4,6},{5,7},{6,4},{7,5},{8,10},{9,11},{10,... | collective-permute-start | bytes 110600 | tf_op jit(solution)/shard_map/ppermute | solution.py:595
  9.7 10.4 %collective-permute-start.4 = (bf16[48,384]{1,0:T(8,128)(2,1)S(1)}, bf16[48,384]{1,0:T(8,128)(2,1)S(1)}, u32[]{:S(2)}, u32[]{:S(2)}) collective-permute-start(bf16[48,384]{1,0:T(8,128)(2,1)S(1)} %get-tuple-element.68), channel_id=1, source_target_pairs={{0,3},{1,0},{2,1},{3,2},{4,7},{5,4},{6,5},{7,6},{8,11},{9,8},{10,9... | collective-permute-start | bytes 110600 | tf_op jit(solution)/shard_map/ppermute | solution.py:595
  11.1 1.9 %copy-start = (bf16[1,1024,1536]{2,1,0:T(8,128)(2,1)S(1)}, bf16[1,1024,1536]{2,1,0:T(8,128)(2,1)}, u32[]{:S(2)}) copy-start(bf16[1,1024,1536]{2,1,0:T(8,128)(2,1)} %param.8) | copy-start | bytes 9437188
  13.0 1.0 %copy-start.2 = (bf16[256,1024]{1,0:T(8,128)(2,1)S(1)}, bf16[256,1024]{1,0:T(8,128)(2,1)}, u32[]{:S(2)}) copy-start(bf16[256,1024]{1,0:T(8,128)(2,1)} %refs_0_.1) | copy-start | bytes 1572868
  20.1 13.0 %collective-permute-start.5 = (bf16[256,1024]{1,0:T(8,128)(2,1)S(1)}, bf16[256,1024]{1,0:T(8,128)(2,1)S(1)}, u32[]{:S(2)}, u32[]{:S(2)}) collective-permute-start(bf16[256,1024]{1,0:T(8,128)(2,1)S(1)} %collective-permute-done.1.refs_2_), channel_id=1, source_target_pairs={{2,1},{1,0},{6,5},{5,4},{10,9},{9,8},{14,13},{13,12},{18,17},{17,1... | collective-permute-start | bytes 1572872 | tf_op jit(solution)/shard_map/ppermute | solution.py:582
  22.5 11.2 %collective-permute-start.6 = (bf16[256,1024]{1,0:T(8,128)(2,1)S(1)}, bf16[256,1024]{1,0:T(8,128)(2,1)S(1)}, u32[]{:S(2)}, u32[]{:S(2)}) collective-permute-start(bf16[256,1024]{1,0:T(8,128)(2,1)S(1)} %collective-permute-done.refs_1_), channel_id=1, source_target_pairs={{1,2},{2,3},{5,6},{6,7},{9,10},{10,11},{13,14},{14,15},{17,18},{18... | collective-permute-start | bytes 1572872 | tf_op jit(solution)/shard_map/ppermute | solution.py:583
  25.5 7.5 %collective-permute-start.7 = (bf16[4,32,384]{2,1,0:T(8,128)(2,1)S(1)}, bf16[4,32,384]{2,1,0:T(8,128)(2,1)S(1)}, u32[]{:S(2)}, u32[]{:S(2)}) collective-permute-start(bf16[4,32,384]{2,1,0:T(8,128)(2,1)S(1)} %get-tuple-element.80.refs_0_), channel_id=1, source_target_pairs={{0,8},{4,12},{8,16},{12,20},{16,24},{20,28},{24,0},{28,4},{1,9},{5... | collective-permute-start | bytes 294920 | tf_op jit(solution)/shard_map/ppermute | solution.py:635
  26.8 6.3 %collective-permute-start.8 = (bf16[4,32,384]{2,1,0:T(8,128)(2,1)S(1)}, bf16[4,32,384]{2,1,0:T(8,128)(2,1)S(1)}, u32[]{:S(2)}, u32[]{:S(2)}) collective-permute-start(bf16[4,32,384]{2,1,0:T(8,128)(2,1)S(1)} %get-tuple-element.80.refs_0_), channel_id=1, source_target_pairs={{0,16},{4,20},{8,24},{12,28},{16,0},{20,4},{24,8},{28,12},{1,17},{... | collective-permute-start | bytes 294920 | tf_op jit(solution)/shard_map/ppermute | solution.py:635
  28.0 5.1 %collective-permute-start.9 = (bf16[4,32,384]{2,1,0:T(8,128)(2,1)S(1)}, bf16[4,32,384]{2,1,0:T(8,128)(2,1)S(1)}, u32[]{:S(2)}, u32[]{:S(2)}) collective-permute-start(bf16[4,32,384]{2,1,0:T(8,128)(2,1)S(1)} %get-tuple-element.80.refs_0_), channel_id=1, source_target_pairs={{0,24},{4,28},{8,0},{12,4},{16,8},{20,12},{24,16},{28,20},{1,25},{... | collective-permute-start | bytes 294920 | tf_op jit(solution)/shard_map/ppermute | solution.py:635
  33.7 13.9 %collective-permute-start.10 = (bf16[256,1024]{1,0:T(8,128)(2,1)S(1)}, bf16[256,1024]{1,0:T(8,128)(2,1)S(1)}, u32[]{:S(2)}, u32[]{:S(2)}) collective-permute-start(bf16[256,1024]{1,0:T(8,128)(2,1)S(1)} %collective-permute-done.5.refs_0_.refs_3_), channel_id=1, source_target_pairs={{1,0},{5,4},{9,8},{13,12},{17,16},{21,20},{25,24},{29,28}} | collective-permute-start | bytes 1572872 | tf_op jit(solution)/shard_map/ppermute | solution.py:582
  35.0 12.6 %collective-permute-start.11 = (bf16[256,1024]{1,0:T(8,128)(2,1)S(1)}, bf16[256,1024]{1,0:T(8,128)(2,1)S(1)}, u32[]{:S(2)}, u32[]{:S(2)}) collective-permute-start(bf16[256,1024]{1,0:T(8,128)(2,1)S(1)} %collective-permute-done.6.refs_1_.refs_4_), channel_id=1, source_target_pairs={{2,3},{6,7},{10,11},{14,15},{18,19},{22,23},{26,27},{30,31}} | collective-permute-start | bytes 1572872 | tf_op jit(solution)/shard_map/ppermute | solution.py:583
  35.7 10.0 %collective-permute-start.12 = (bf16[4,4,32,384]{3,2,1,0:T(8,128)(2,1)S(1)}, bf16[4,4,32,384]{3,2,1,0:T(8,128)(2,1)S(1)}, u32[]{:S(2)}, u32[]{:S(2)}) collective-permute-start(bf16[4,4,32,384]{3,2,1,0:T(8,128)(2,1)S(1)} %combine.1.refs_5_), channel_id=1, source_target_pairs={{0,4},{4,0},{8,12},{12,8},{16,20},{20,16},{24,28},{28,24},{1,5},{5... | collective-permute-start | bytes 1179656 | tf_op jit(solution)/shard_map/ppermute | solution.py:647
  47.6 6.5 %collective-permute-start.13 = (bf16[512,128]{1,0:T(8,128)(2,1)S(1)}, bf16[512,128]{1,0:T(8,128)(2,1)S(1)}, u32[]{:S(2)}, u32[]{:S(2)}) collective-permute-start(bf16[512,128]{1,0:T(8,128)(2,1)S(1)} %get-tuple-element.99), channel_id=1, source_target_pairs={{0,16},{4,20},{8,24},{12,28},{1,17},{5,21},{9,25},{13,29},{2,18},{... | collective-permute-start | bytes 393224 | tf_op jit(solution)/shard_map/ppermute | solution.py:685
  50.8 10.4 %collective-permute-start.15 = (bf16[512,256]{1,0:T(8,128)(2,1)S(1)}, bf16[512,256]{1,0:T(8,128)(2,1)S(1)}, u32[]{:S(2)}, u32[]{:S(2)}) collective-permute-start(bf16[512,256]{1,0:T(8,128)(2,1)S(1)} %get-tuple-element.114), channel_id=1, source_target_pairs={{0,4},{4,8},{8,12},{12,16},{16,20},{20,24},{24,28},{1,5},{5,9},{9,... | collective-permute-start | bytes 786440 | tf_op jit(solution)/shard_map/ppermute | solution.py:21
  54.2 6.5 %collective-permute-start.14 = (bf16[512,128]{1,0:T(8,128)(2,1)S(1)}, bf16[512,128]{1,0:T(8,128)(2,1)S(1)}, u32[]{:S(2)}, u32[]{:S(2)}) collective-permute-start(bf16[512,128]{1,0:T(8,128)(2,1)S(1)} %get-tuple-element.101), channel_id=1, source_target_pairs={{0,8},{4,12},{8,0},{12,4},{16,24},{20,28},{24,16},{28,20},{1,9},{5... | collective-permute-start | bytes 393224 | tf_op jit(solution)/shard_map/ppermute | solution.py:699
  55.1 6.0 %collective-permute-start.16 = (bf16[256,256]{1,0:T(8,128)(2,1)S(1)}, bf16[256,256]{1,0:T(8,128)(2,1)S(1)}, u32[]{:S(2)}, u32[]{:S(2)}) collective-permute-start(bf16[256,256]{1,0:T(8,128)(2,1)S(1)} %get-tuple-element.115), channel_id=1, source_target_pairs={{0,4},{4,8},{8,12},{12,16},{16,20},{20,24},{24,28}} | collective-permute-start | bytes 393224 | tf_op jit(solution)/shard_map/ppermute | solution.py:710
  60.7 2.8 %collective-permute-start.17 = (bf16[512,128]{1,0:T(8,128)(2,1)S(1)}, bf16[512,128]{1,0:T(8,128)(2,1)S(1)}, u32[]{:S(2)}, u32[]{:S(2)}) collective-permute-start(bf16[512,128]{1,0:T(8,128)(2,1)S(1)} %get-tuple-element.118), channel_id=1, source_target_pairs={{0,4},{4,0},{8,12},{12,8},{16,20},{20,16},{24,28},{28,24},{1,5},{5... | collective-permute-start | bytes 393224 | tf_op jit(solution)/shard_map/ppermute | solution.py:699
  64.0 21.3 %collective-permute-start.20 = (bf16[256,512]{1,0:T(8,128)(2,1)S(1)}, bf16[256,512]{1,0:T(8,128)(2,1)S(1)}, u32[]{:S(2)}, u32[]{:S(2)}) collective-permute-start(bf16[256,512]{1,0:T(8,128)(2,1)S(1)} %finish2.1), channel_id=1, source_target_pairs={{0,2},{1,3},{2,0},{3,1},{4,6},{5,7},{6,4},{7,5},{8,10},{9,11},{10,... | collective-permute-start | bytes 786440 | tf_op jit(solution)/shard_map/ppermute | solution.py:739
  69.9 21.5 %collective-permute-start.19 = (bf16[256,512]{1,0:T(8,128)(2,1)S(1)}, bf16[256,512]{1,0:T(8,128)(2,1)S(1)}, u32[]{:S(2)}, u32[]{:S(2)}) collective-permute-start(bf16[256,512]{1,0:T(8,128)(2,1)S(1)} %finish3.1), channel_id=1, source_target_pairs={{0,3},{1,0},{2,1},{3,2},{4,7},{5,4},{6,5},{7,6},{8,11},{9,8},{10,9... | collective-permute-start | bytes 786440 | tf_op jit(solution)/shard_map/ppermute | solution.py:739
  70.5 21.0 %collective-permute-start.18 = (bf16[256,512]{1,0:T(8,128)(2,1)S(1)}, bf16[256,512]{1,0:T(8,128)(2,1)S(1)}, u32[]{:S(2)}, u32[]{:S(2)}) collective-permute-start(bf16[256,512]{1,0:T(8,128)(2,1)S(1)} %finish1.1), channel_id=1, source_target_pairs={{0,1},{1,2},{2,3},{3,0},{4,5},{5,6},{6,7},{7,4},{8,9},{9,10},{10,1... | collective-permute-start | bytes 786440 | tf_op jit(solution)/shard_map/ppermute | solution.py:739
  (2 other events, 1.4 us)
